TPU v7x, 32 devices: a whole 2x2x4 slice. The times are simulated.
32 devices in a mesh: seq: 8 (over z, x), stream: 4 (over y, core).
Axes of the slice: x: 2, y: 2, z: 4, core: 2. Of those that a mesh axis runs over, the one named last changes fastest.
Arguments:
- inputs: bfloat16 [8, 1024, 2048], P('stream', 'seq'), may hold values from -6 to 6
- start_state: float32 [8, 2048], P('stream'), may hold values from -6 to 6
- lengths: int32 [8], P('stream'), may hold values from 512 to 1024, as said below
- weights: bfloat16 [2048, 6144], P('seq', 'stream'), may hold values from -0.125 to 0.125
- peep_forget: float32 [2048], replicated, may hold values from -1 to 1
- peep_reset: float32 [2048], replicated, may hold values from -1 to 1
- bias_forget: float32 [2048], replicated, may hold values from 2 to 7
- bias_reset: float32 [2048], replicated, may hold values from -1.5 to 1.5
- norm_gain: float32 [2048], replicated, may hold values from 0.5 to 1.5
- norm_bias: float32 [2048], replicated, may hold values from -3 to 3
- out_grad: bfloat16 [8, 1024, 2048], P('stream', 'seq'), may hold values from -6 to 6
Outputs:
- outputs: bfloat16 [8, 1024, 2048], P('stream', 'seq')
- final_state: float32 [8, 2048], P('stream', 'seq')
- input_grad: bfloat16 [8, 1024, 2048], P('stream', 'seq')
- weight_grad: float32 [2048, 6144], P('seq', 'stream')
- peep_forget_grad: float32 [2048], replicated
- peep_reset_grad: float32 [2048], replicated
- bias_forget_grad: float32 [2048], replicated
- bias_reset_grad: float32 [2048], replicated
- norm_gain_grad: float32 [2048], replicated
- norm_bias_grad: float32 [2048], replicated
Inputs may be any that keep to these rules, and one draw needn't show every extreme that they name: `lengths`: among the 2 sequences of each index of stream, one drawn from the seed has length 1024.
All inputs are finite; a program needn't handle non-finite values.
Results may differ from a plain program's by a relative error of at most 0.0079.
Values may be sent and summed in bfloat16 or wider, within the bound.
No kernel may reach another device: no remote copies, remote signals or barrier semaphores. Data moves between devices by JAX's collectives and lax.ppermute only.
A program may use at most 128 MiB of HBM per device.

v0:
```python
import jax
import jax.numpy as jnp
from jax import lax
from jax.sharding import PartitionSpec as P

epsilon = 1e-05


def passed_along(value, axis, steps):
    count = lax.axis_size(axis)
    leading, last = (max(0, -steps), min(count, count - steps))
    return lax.ppermute(value, axis, [(source, source + steps) for source in range(leading, last)])


def carried_in(array, axis, combine, identity, reverse):
    count, here = (lax.axis_size(axis), lax.axis_index(axis))
    everything = jax.tree.map(lambda part: lax.all_gather(part, axis), array)
    start = jax.tree.map(
        lambda part, zero: jnp.broadcast_to(jnp.asarray(zero, part.dtype), part.shape),
        array,
        identity,
    )

    def turn(k, before):
        at = count - 1 - k if reverse else k
        reached = at > here if reverse else at < here
        new = combine(before, jax.tree.map(lambda part: part[at], everything))
        return jax.tree.map(lambda a, b: jnp.where(reached, a, b), new, before)

    return lax.fori_loop(0, count, turn, start)


def compose(earlier, later):
    return (earlier[0] * later[0], later[0] * earlier[1] + later[1])


def compose_back(earlier, later):
    return (
        earlier[0] * later[0],
        earlier[0] * later[1] + earlier[1],
        later[0] * earlier[2] + later[2],
    )


def local(
    inputs,
    start_state,
    lengths,
    weights,
    peep_forget,
    peep_reset,
    bias_forget,
    bias_reset,
    norm_gain,
    norm_bias,
    out_grad,
):
    batch_size, span_len, model_width = inputs.shape
    seq_count = lax.axis_size("seq")
    span_index = lax.axis_index("seq")
    weight_rows = lax.all_gather(weights, "seq", axis=0, tiled=True)
    source = inputs.astype(jnp.float32)
    centered = source - jnp.mean(source, axis=2, keepdims=True)
    variance = jnp.mean(centered * centered, axis=2, keepdims=True)
    inv_scale = lax.rsqrt(variance + epsilon)
    scaled = centered * inv_scale
    normed = (scaled * norm_gain + norm_bias).astype(jnp.bfloat16)
    gathered = lax.all_gather(normed, "stream", axis=0, tiled=True)
    slab = jnp.einsum(
        "nck,ko->nco", gathered, weight_rows, preferred_element_type=jnp.float32
    ).astype(jnp.bfloat16)
    projected = lax.all_to_all(slab, "stream", split_axis=0, concat_axis=2, tiled=True)
    candidate = projected[:, :, :model_width].astype(jnp.float32)
    forget_pre = projected[:, :, model_width : 2 * model_width].astype(jnp.float32)
    reset_pre = projected[:, :, 2 * model_width :].astype(jnp.float32)
    arrived = passed_along(projected[:, -1, :model_width], "seq", 1)
    first_prev = jnp.where(span_index == 0, start_state, arrived.astype(jnp.float32))
    previous = jnp.concatenate([first_prev[:, None, :], candidate[:, :-1, :]], axis=1)
    forget = jax.nn.sigmoid(forget_pre + peep_forget * previous + bias_forget)
    reset = jax.nn.sigmoid(reset_pre + peep_reset * previous + bias_reset)
    positions = span_index * span_len + jnp.arange(span_len, dtype=jnp.int32)
    live = (positions[None, :] < lengths[:, None])[:, :, None]
    decay = jnp.where(live, forget, 1.0)
    inject = jnp.where(live, (1.0 - forget) * candidate, 0.0)
    running_decay, running_inject = lax.associative_scan(compose, (decay, inject), axis=1)
    span_decay = running_decay[:, -1, :]
    span_inject = running_inject[:, -1, :]
    unit_map = jnp.ones_like(span_decay)
    empty_map = jnp.zeros_like(span_decay)
    before_decay, before_inject = carried_in(
        (span_decay, span_inject), "seq", compose, (unit_map, empty_map), False
    )
    state_in = before_decay * start_state + before_inject
    states = running_decay * state_in[:, None, :] + running_inject
    prior_states = jnp.concatenate([state_in[:, None, :], states[:, :-1, :]], axis=1)
    outputs = jnp.where(live, reset * states + (1.0 - reset) * source, source).astype(jnp.bfloat16)
    grad_out = out_grad.astype(jnp.float32)
    grad_state = jnp.where(live, reset * grad_out, 0.0)
    grad_reset = jnp.where(live, grad_out * (states - source), 0.0)
    next_decay = jnp.concatenate([decay[:, 1:, :], jnp.ones_like(decay[:, :1, :])], axis=1)
    reach_decay, reach_local = lax.associative_scan(
        compose, (next_decay, grad_state), axis=1, reverse=True
    )
    handed = decay[:, 0, :] * reach_local[:, 0, :]
    after_decay, after_inject, after_adjoint = carried_in(
        (span_decay, span_inject, handed),
        "seq",
        compose_back,
        (unit_map, empty_map, empty_map),
        True,
    )
    adjoint = reach_decay * after_adjoint[:, None, :] + reach_local
    final_full = after_decay * states[:, -1, :] + after_inject
    slice_width = model_width // seq_count
    final_state = lax.dynamic_slice_in_dim(final_full, span_index * slice_width, slice_width, 1)
    grad_forget = jnp.where(live, adjoint * (prior_states - candidate), 0.0)
    direct_candidate = jnp.where(live, adjoint * (1.0 - forget), 0.0)
    forget_term = forget * (1.0 - forget) * grad_forget
    reset_term = reset * (1.0 - reset) * grad_reset
    grad_previous = forget_term * peep_forget + reset_term * peep_reset
    returned = passed_along(grad_previous[:, 0, :], "seq", -1)
    grad_candidate = direct_candidate + jnp.concatenate(
        [grad_previous[:, 1:, :], returned[:, None, :]], axis=1
    )
    grad_projected = jnp.concatenate([grad_candidate, forget_term, reset_term], axis=2).astype(
        jnp.bfloat16
    )
    peep_forget_part = jnp.sum(forget_term * previous, axis=(0, 1))
    peep_reset_part = jnp.sum(reset_term * previous, axis=(0, 1))
    bias_forget_part = jnp.sum(forget_term, axis=(0, 1))
    bias_reset_part = jnp.sum(reset_term, axis=(0, 1))
    returned_slab = lax.all_to_all(
        grad_projected, "stream", split_axis=2, concat_axis=0, tiled=True
    )
    piece_rows = gathered
    weight_grad = lax.psum_scatter(
        jnp.einsum("nck,nco->ko", piece_rows, returned_slab, preferred_element_type=jnp.float32),
        "seq",
        scatter_dimension=0,
        tiled=True,
    )
    piece_rows = returned_slab
    grad_normed = lax.psum_scatter(
        jnp.einsum("nco,ko->nck", piece_rows, weight_rows, preferred_element_type=jnp.float32),
        "stream",
        scatter_dimension=0,
        tiled=True,
    )
    gain_part = jnp.sum(grad_normed * scaled, axis=(0, 1))
    shift_part = jnp.sum(grad_normed, axis=(0, 1))
    grad_scaled = grad_normed * norm_gain
    grad_source = inv_scale * (
        grad_scaled
        - jnp.mean(grad_scaled, axis=2, keepdims=True)
        - scaled * jnp.mean(grad_scaled * scaled, axis=2, keepdims=True)
    )
    input_grad = (grad_source + jnp.where(live, (1.0 - reset) * grad_out, grad_out)).astype(
        jnp.bfloat16
    )
    summed = lax.psum(
        (
            peep_forget_part,
            peep_reset_part,
            bias_forget_part,
            bias_reset_part,
            gain_part,
            shift_part,
        ),
        ("seq", "stream"),
    )
    return (
        outputs,
        final_state,
        input_grad,
        weight_grad,
        summed[0],
        summed[1],
        summed[2],
        summed[3],
        summed[4],
        summed[5],
    )


def solution(mesh):
    return jax.shard_map(
        local,
        mesh=mesh,
        in_specs=(
            P("stream", "seq", None),
            P("stream", None),
            P("stream"),
            P("seq", "stream"),
            P(),
            P(),
            P(),
            P(),
            P(),
            P(),
            P("stream", "seq", None),
        ),
        out_specs=(
            P("stream", "seq", None),
            P("stream", "seq"),
            P("stream", "seq", None),
            P("seq", "stream"),
            P(),
            P(),
            P(),
            P(),
            P(),
            P(),
        ),
        check_vma=False,
    )
```

profile of v0, /device:TPU:0, one launch (start us, length us, event | category | flops | bytes accessed | tf_op | source)
XLA Modules:
  0.0 1169.6 jit_solution(16618115762325208491)
XLA Ops:
  12.7 36.6 %all-gather.6.cloned.1.call-done = bf16[8,128,2048]{2,1,0:T(8,128)(2,1)} async-done(((bf16[2,128,2048]{2,1,0:T(8,128)(2,1)}), bf16[8,128,2048]{2,1,0:T(8,128)(2,1)}) %all-gather.6.cloned.1.call-update) | async-done | bytes 4194320 | tf_op jit(solution)/shard_map/all_gather | solution.py:68
  49.3 101.2 %all-gather.8.cloned.1.call-done = bf16[2048,1536]{1,0:T(8,128)(2,1)} async-done(((bf16[256,1536]{1,0:T(8,128)(2,1)}), bf16[2048,1536]{1,0:T(8,128)(2,1)}) %all-gather.8.cloned.1.call-update) | async-done | bytes 6291472 | tf_op jit(solution)/shard_map/all_gather | solution.py:61
  150.5 11.2 fusion.6
  166.7 36.8 %all-to-all-done = bf16[8,128,1536]{2,1,0:T(8,128)(2,1)} async-done(((bf16[8,128,1536]{2,1,0:T(8,128)(2,1)}), bf16[8,128,1536]{2,1,0:T(8,128)(2,1)}, u32[]{:S(2)}, u32[]{:S(2)}) %all-to-all-start) | async-done | bytes 3145760 | tf_op jit(solution)/shard_map/all_to_all | solution.py:72
  203.5 6.1 copy.140
  209.6 6.9 all_to_all.29
  226.3 5.5 slice.528
  231.8 5.4 slice.499
  237.2 5.4 slice.498
  244.1 5.5 slice.495
  249.6 5.4 slice.466
  255.0 5.4 slice.465
  379.5 5.3 pad.200
  387.1 5.5 pad.186
  392.6 5.3 pad.187
  398.9 31.0 %all-gather = f32[16,1,2048]{2,1,0:T(1,128)S(1)} all-gather(f32[2,1,2048]{2,1,0:T(1,128)S(1)} %slice_add_fusion.5), channel_id=2, replica_groups=mesh['seq'=8,'stream'=4] {'seq'}, dimensions={0}, use_global_device_ids=true | all-gather | bytes 147456 | tf_op jit(solution)/shard_map/all_gather | solution.py:17
  430.4 5.3 pad.201
  436.7 30.7 %all-gather.1 = f32[16,1,2048]{2,1,0:T(1,128)S(1)} all-gather(f32[2,1,2048]{2,1,0:T(1,128)S(1)} %slice_add_fusion.2), channel_id=3, replica_groups=mesh['seq'=8,'stream'=4] {'seq'}, dimensions={0}, use_global_device_ids=true | all-gather | bytes 147456 | tf_op jit(solution)/shard_map/all_gather | solution.py:17
  470.6 6.0 fusion.33
  478.5 5.4 slice.586
  483.9 5.4 slice.538
  489.3 5.4 slice.536
  497.9 5.4 slice.541
  503.3 5.4 slice.534
  508.7 5.4 slice.532
  514.1 8.9 slice.537
  523.0 8.9 slice.539
  531.9 8.9 slice.542
  540.8 8.9 slice.535
  605.7 9.0 slice.587
  614.7 9.0 slice.533
  689.4 5.3 pad.214
  694.7 5.3 pad.215
  706.1 16.7 %rev.9 = f32[2,128,2048]{2,1,0:T(8,128)} reverse(f32[2,128,2048]{2,1,0:T(8,128)} %add.522), dimensions={1} | reverse | bytes 4194304 | tf_op jit(solution)/shard_map/rev | solution.py:101
  722.9 30.8 %all-gather.2 = f32[16,1,2048]{2,1,0:T(1,128)S(1)} all-gather(f32[2,1,2048]{2,1,0:T(1,128)S(1)} %add_multiply_fusion.20), channel_id=4, replica_groups=mesh['seq'=8,'stream'=4] {'seq'}, dimensions={0}, use_global_device_ids=true | all-gather | bytes 147456 | tf_op jit(solution)/shard_map/all_gather | solution.py:17
  754.0 6.5 while.37
  760.5 5.3 pad.228
  765.8 5.3 pad.229
  775.1 16.8 %rev.8 = f32[2,128,2048]{2,1,0:T(8,128)} reverse(f32[2,128,2048]{2,1,0:T(8,128)} %add.531), dimensions={1} | reverse | bytes 4194304 | tf_op jit(solution)/shard_map/rev | solution.py:101
  791.9 7.4 multiply_reduce_fusion
  810.2 8.7 copy.124
  818.9 42.3 %all_to_all.36 = bf16[2,128,6144]{1,0,2:T(2,128)(2,1)} all-to-all(bf16[2,128,6144]{1,0,2:T(2,128)(2,1)} %copy.124), channel_id=1, replica_groups=mesh['seq'=8,'stream'=4] {'stream'}, dimensions={2} | all-to-all | bytes 6291456 | tf_op jit(solution)/shard_map/all_to_all | solution.py:132
  861.1 8.7 copy.125
  869.8 11.7 %fusion.2 = f32[8,128,2048]{2,1,0:T(8,128)} fusion(bf16[8,128,1536]{2,1,0:T(8,128)(2,1)} %bitcast.83, bf16[2048,1536]{1,0:T(8,128)(2,1)} %all-gather.8.cloned.1.call-done), kind=kOutput, calls=%fused_computation.12 | convolution fusion | flops 6442450944 | bytes 17825792 | tf_op jit(solution)/shard_map/nco,ko->nck/dot_general | solution.py:144
  881.6 13.2 %convolution_bitcast_fusion = f32[2048,1536]{1,0:T(8,128)} fusion(bf16[8,128,2048]{2,1,0:T(8,128)(2,1)} %all-gather.6.cloned.1.call-done, bf16[8,128,1536]{2,1,0:T(8,128)(2,1)} %bitcast.84), kind=kOutput, calls=%fused_computation.11 | convolution fusion | flops 6442450944 | bytes 19922944 | tf_op jit(solution)/shard_map/nck,nco->ko/dot_general | solution.py:137
  896.4 53.5 %reduce-scatter.3.cloned.1.call-done = f32[2,128,2048]{2,1,0:T(8,128)} async-done(((f32[8,128,2048]{2,1,0:T(8,128)}), f32[2,128,2048]{2,1,0:T(8,128)}) %reduce-scatter.3.cloned.1.call-update) | async-done | bytes 2097168 | tf_op jit(solution)/shard_map/reduce_scatter | solution.py:143
  952.4 45.3 %all-reduce.58 = (f32[2048]{0:T(1024)}, f32[2048]{0:T(1024)}, f32[2048]{0:T(1024)}, f32[2048]{0:T(1024)}, f32[2048]{0:T(1024)}, /*index=5*/f32[2048]{0:T(1024)}) all-reduce(f32[2048]{0:T(1024)S(1)} %get-tuple-element.406, f32[2048]{0:T(1024)S(1)} %get-tuple-element.405, ...), channel_id=1, replica_groups=mesh['seq'=8,'stream'=4] {'seq','stream'}, use_global_device_ids=true, to_apply=%region_11.12 | all-reduce | flops 12288 | bytes 98304 | tf_op jit(solution)/shard_map/psum | solution.py:160
  1002.0 160.6 %reduce-scatter.5.cloned.1.call-done = f32[256,1536]{1,0:T(8,128)} async-done(((f32[2048,1536]{1,0:T(8,128)}), f32[256,1536]{1,0:T(8,128)}) %reduce-scatter.5.cloned.1.call-update) | async-done | bytes 1572880 | tf_op jit(solution)/shard_map/reduce_scatter | solution.py:136
  (434 shorter events, 310.9 us)
Async XLA Ops:
  7.2 42.1 %all-gather.6.cloned.1.call-start = ((), (), s32[]{:S(2)}) async-start(), calls=%async_computation.4 | async-start | bytes 5242880 | tf_op jit(solution)/shard_map/all_gather | solution.py:68
  10.5 151.2 %copy-start.78 = (f32[2,128]{1,0:T(2,128)}, f32[2,128]{1,0:T(2,128)S(1)}, u32[]{:S(2)}) copy-start(f32[2,128]{1,0:T(2,128)S(1)} %add_rsqrt_fusion) | copy-start | bytes 3076
  12.0 138.6 %all-gather.8.cloned.1.call-start = ((), (), s32[]{:S(2)}) async-start(), calls=%async_computation.5 | async-start | bytes 7077888 | tf_op jit(solution)/shard_map/all_gather | solution.py:61
  161.7 5.0 copy-start.84
  161.7 41.8 %all-to-all-start = ((bf16[8,128,1536]{2,1,0:T(8,128)(2,1)}), bf16[8,128,1536]{2,1,0:T(8,128)(2,1)}, u32[]{:S(2)}, u32[]{:S(2)}) async-start(bf16[8,128,1536]{2,1,0:T(8,128)(2,1)} %fusion.6), calls=%async_computation | async-start | bytes 6291456 | tf_op jit(solution)/shard_map/all_to_all | solution.py:72
  166.5 783.4 %reduce-scatter.3.cloned.1.call-start = ((), (), s32[]{:S(2)}) async-start(), calls=%async_computation.6 | async-start | bytes 10485760 | tf_op jit(solution)/shard_map/reduce_scatter | solution.py:143
  166.7 55.0 %copy-start.80 = (pred[2,128]{1,0:T(4,128)(4,1)}, pred[2,128]{1,0:T(4,128)(4,1)S(1)}, u32[]{:S(2)}) copy-start(pred[2,128]{1,0:T(4,128)(4,1)S(1)} %broadcast_compare_fusion) | copy-start | bytes 772
  216.5 5.2 copy-start.74
  216.5 5.2 copy-start.1
  216.6 5.3 copy-start.52
  216.6 5.3 copy-start.56
  217.6 4.1 collective-permute-start
  332.3 7.8 copy-start.70
  336.3 7.1 copy-start.68
  340.1 10.0 copy-start.37
  379.5 5.3 copy-start.63
  430.2 39.1 %copy-start.44 = (f32[2,2048]{1,0:T(2,128)S(1)}, f32[2,2048]{1,0:T(2,128)}, u32[]{:S(2)}) copy-start(f32[2,2048]{1,0:T(2,128)} %custom-call.1) | copy-start | bytes 49156
  430.2 39.1 %copy-start.45 = (f32[2,2048]{1,0:T(2,128)S(1)}, f32[2,2048]{1,0:T(2,128)}, u32[]{:S(2)}) copy-start(f32[2,2048]{1,0:T(2,128)} %custom-call) | copy-start | bytes 49156
  430.3 39.6 %copy-start.75 = (f32[2,2048]{1,0:T(2,128)S(1)}, f32[2,2048]{1,0:T(2,128)}, u32[]{:S(2)}) copy-start(f32[2,2048]{1,0:T(2,128)} %param.16) | copy-start | bytes 49156
  430.3 40.2 %copy-start.42 = (f32[2,1,2048]{2,1,0:T(1,128)S(1)}, f32[2,1,2048]{2,1,0:T(1,128)}, u32[]{:S(2)}) copy-start(f32[2,1,2048]{2,1,0:T(1,128)} %copy-done.41) | copy-start | bytes 49156
  430.3 40.2 %copy-start.50 = (f32[2048]{0:T(1024)S(1)}, f32[2048]{0:T(1024)}, u32[]{:S(2)}) copy-start(f32[2048]{0:T(1024)} %param.20) | copy-start | bytes 24580
  430.3 40.2 %copy-start.54 = (f32[2048]{0:T(1024)S(1)}, f32[2048]{0:T(1024)}, u32[]{:S(2)}) copy-start(f32[2048]{0:T(1024)} %param.22) | copy-start | bytes 24580
  430.4 40.2 %copy-start.81 = (pred[2,128]{1,0:T(4,128)(4,1)S(1)}, pred[2,128]{1,0:T(4,128)(4,1)}, u32[]{:S(2)}) copy-start(pred[2,128]{1,0:T(4,128)(4,1)} %copy-done.80) | copy-start | bytes 772
  469.9 6.7 copy-start.39
  469.9 6.7 copy-start.40
  605.7 18.1 %copy-start.72 = (f32[2,1,2048]{2,1,0:T(1,128)S(1)}, f32[2,1,2048]{2,1,0:T(1,128)}, u32[]{:S(2)}) copy-start(f32[2,1,2048]{2,1,0:T(1,128)} %get-tuple-element.494) | copy-start | bytes 49156
  605.7 18.0 %copy-start.73 = (f32[2,1,2048]{2,1,0:T(1,128)S(1)}, f32[2,1,2048]{2,1,0:T(1,128)}, u32[]{:S(2)}) copy-start(f32[2,1,2048]{2,1,0:T(1,128)} %get-tuple-element.495) | copy-start | bytes 49156
  605.7 21.7 %copy-start.48 = (f32[2,3,2048]{2,1,0:T(4,128)S(1)}, f32[2,3,2048]{2,1,0:T(4,128)}, u32[]{:S(2)}) copy-start(f32[2,3,2048]{2,1,0:T(4,128)} %slice.561) | copy-start | bytes 147460
  605.7 21.7 %copy-start.49 = (f32[2,3,2048]{2,1,0:T(4,128)S(1)}, f32[2,3,2048]{2,1,0:T(4,128)}, u32[]{:S(2)}) copy-start(f32[2,3,2048]{2,1,0:T(4,128)} %slice.578) | copy-start | bytes 147460
  642.2 7.8 copy-start.71
  646.1 7.1 copy-start.69
  649.9 10.0 copy-start.38
  706.1 47.9 %copy-start.46 = (f32[2,2048]{1,0:T(2,128)S(1)}, f32[2,2048]{1,0:T(2,128)}, u32[]{:S(2)}) copy-start(f32[2,2048]{1,0:T(2,128)} %custom-call.3) | copy-start | bytes 49156
  706.1 47.9 %copy-start.47 = (f32[2,2048]{1,0:T(2,128)S(1)}, f32[2,2048]{1,0:T(2,128)}, u32[]{:S(2)}) copy-start(f32[2,2048]{1,0:T(2,128)} %custom-call.2) | copy-start | bytes 49156
  775.0 16.8 %copy-start.43 = (f32[2,1,2048]{2,1,0:T(1,128)S(1)}, f32[2,1,2048]{2,1,0:T(1,128)}, u32[]{:S(2)}) copy-start(f32[2,1,2048]{2,1,0:T(1,128)} %copy-done.41) | copy-start | bytes 49156
  775.0 16.8 %copy-start.51 = (f32[2048]{0:T(1024)S(1)}, f32[2048]{0:T(1024)}, u32[]{:S(2)}) copy-start(f32[2048]{0:T(1024)} %param.20) | copy-start | bytes 24580
  775.0 16.8 %copy-start.53 = (f32[2048]{0:T(1024)S(1)}, f32[2048]{0:T(1024)}, u32[]{:S(2)}) copy-start(f32[2048]{0:T(1024)} %param.19) | copy-start | bytes 24580
  775.0 16.8 %copy-start.55 = (f32[2048]{0:T(1024)S(1)}, f32[2048]{0:T(1024)}, u32[]{:S(2)}) copy-start(f32[2048]{0:T(1024)} %param.22) | copy-start | bytes 24580
  775.0 16.8 %copy-start.57 = (f32[2048]{0:T(1024)S(1)}, f32[2048]{0:T(1024)}, u32[]{:S(2)}) copy-start(f32[2048]{0:T(1024)} %param.21) | copy-start | bytes 24580
  775.0 16.8 %copy-start.60 = (f32[2,1,2048]{2,1,0:T(1,128)S(1)}, f32[2,1,2048]{2,1,0:T(1,128)}, u32[]{:S(2)}) copy-start(f32[2,1,2048]{2,1,0:T(1,128)} %broadcast_in_dim.80) | copy-start | bytes 49156
  775.0 16.8 %copy-start.82 = (pred[2,128]{1,0:T(4,128)(4,1)S(1)}, pred[2,128]{1,0:T(4,128)(4,1)}, u32[]{:S(2)}) copy-start(pred[2,128]{1,0:T(4,128)(4,1)} %copy-done.80) | copy-start | bytes 772
  799.9 5.9 copy-start.2
  799.9 5.9 copy-start.3
  799.9 5.9 collective-permute-start.1
  881.6 281.0 %reduce-scatter.5.cloned.1.call-start = ((), (), s32[]{:S(2)}) async-start(), calls=%async_computation.7 | async-start | bytes 14155776 | tf_op jit(solution)/shard_map/reduce_scatter | solution.py:136
  894.8 55.1 %copy-start.59 = (f32[2048]{0:T(1024)S(1)}, f32[2048]{0:T(1024)}, u32[]{:S(2)}) copy-start(f32[2048]{0:T(1024)} %param.23) | copy-start | bytes 24580
  894.8 55.1 %copy-start.77 = (f32[2,128]{1,0:T(2,128)S(1)}, f32[2,128]{1,0:T(2,128)}, u32[]{:S(2)}) copy-start(f32[2,128]{1,0:T(2,128)} %copy-done.76) | copy-start | bytes 3076
  894.8 55.1 %copy-start.79 = (f32[2,128]{1,0:T(2,128)S(1)}, f32[2,128]{1,0:T(2,128)}, u32[]{:S(2)}) copy-start(f32[2,128]{1,0:T(2,128)} %copy-done.78) | copy-start | bytes 3076
  (44 other events, 122.7 us)
Sparse Core Ops, SparseCore 0:
  12.1 37.1 all-gather.5
  51.5 99.0 all-gather.7
  881.7 68.1 reduce-scatter.2
  954.3 208.1 reduce-scatter.4
where the time goes:
time: 1190 us; the launch traced here: 1170 us
  local copies, waits for them, and re-layouts  397 us (33%)
  waiting for transfers between devices  394 us (33%)
  blocking collectives  180 us (15%)
  other arithmetic  138 us (12%)
  matrix products  36.1 us (3%)
  between operations  15.5 us (1%)
    reduce_scatter x1, waiting for transfers between devices, local(): lax.psum_scatter(jnp.einsum('nck,nco->ko', piece_rows, returned_slab, pre...  161 us
    slice x49, local copies, waits for them, and re-layouts, local(): lax.associative_scan(compose, (next_decay, grad_state), axis=1, reverse=T...  131 us
    all_gather x1, waiting for transfers between devices, local(): weight_rows = lax.all_gather(weights, 'seq', axis=0, tiled=True)  101 us
    all_gather x3, blocking collectives, carried_in(): everything = jax.tree.map(lambda part: lax.all_gather(part, axis), array)  92.5 us
    slice x44, local copies, waits for them, and re-layouts, local(): lax.associative_scan(compose, (decay, inject), axis=1)  79.2 us
    reduce_scatter x1, waiting for transfers between devices, local(): lax.psum_scatter(jnp.einsum('nco,ko->nck', piece_rows, weight_rows, prefe...  53.5 us
    pad x24, local copies, waits for them, and re-layouts, local(): lax.associative_scan(compose, (next_decay, grad_state), axis=1, reverse=T...  52.4 us
    pad x24, local copies, waits for them, and re-layouts, local(): lax.associative_scan(compose, (decay, inject), axis=1)  51.7 us
  transfers between devices with their start and end apart: 7, of which 6 were waited for; matrix products, arithmetic and copies ran while one was open for 2% of the time, Pallas kernels for 0%

commit v1 on v0

v1 whole, which is shorter than its diff:
```python
import functools

import jax
import jax.numpy as jnp
import numpy as np
from jax import lax
from jax.experimental import pallas as pl
from jax.experimental.pallas import tpu as pltpu
from jax.sharding import PartitionSpec as P

epsilon = 1e-05
f32 = jnp.float32
bf16 = jnp.bfloat16
GROUPS = 2
PAD = 8
VMEM_BYTES = 56 * 1024 * 1024


def vmem_spec():
    return pl.BlockSpec(memory_space=pltpu.VMEM)


def smem_spec():
    return pl.BlockSpec(memory_space=pltpu.SMEM)


def call(kernel, out_shape, operands, scratch=(), scalars=0, flops=0, touched=0):
    specs = [smem_spec()] * scalars + [vmem_spec()] * (len(operands) - scalars)
    return pl.pallas_call(
        kernel,
        out_shape=out_shape,
        in_specs=specs,
        out_specs=jax.tree.map(lambda _: vmem_spec(), out_shape),
        scratch_shapes=list(scratch),
        compiler_params=pltpu.CompilerParams(vmem_limit_bytes=VMEM_BYTES),
        cost_estimate=pl.CostEstimate(flops=flops, bytes_accessed=touched, transcendentals=0),
    )(*operands)


def ring_order(count):
    if count == 8:
        return [0, 2, 4, 6, 7, 5, 3, 1]
    return list(range(count))


def along_ring(value, steps):
    order = ring_order(lax.axis_size("seq"))
    count = len(order)
    return lax.ppermute(value, "seq", [(order[i], order[(i + steps) % count]) for i in range(count)])


def swapped(value, axis, bit):
    return lax.ppermute(value, axis, [(i, i ^ bit) for i in range(lax.axis_size(axis))])


def norm_kernel(count, rows, *refs):
    pieces = refs[:count]
    gain, bias, normed, means, scales = refs[count:]
    step = 32
    gain_row, bias_row = gain[...], bias[...]
    for k in range(count):

        def body(i, _, k=k):
            at = pl.multiple_of(i * step, step)
            x = pieces[k][pl.ds(at, step), :].astype(f32)
            mean = jnp.mean(x, axis=1, keepdims=True)
            centered = x - mean
            scale = lax.rsqrt(jnp.mean(centered * centered, axis=1, keepdims=True) + epsilon)
            out = (centered * scale * gain_row + bias_row).astype(bf16)
            to = pl.multiple_of(k * rows + i * step, step)
            normed[pl.ds(to, step), :] = out
            means[pl.ds(to, step), :] = jnp.broadcast_to(mean, (step, 128))
            scales[pl.ds(to, step), :] = jnp.broadcast_to(scale, (step, 128))
            return 0

        lax.fori_loop(0, rows // step, body, 0)


def strided(ref, row, seqs, stride):
    tiles = [ref[lane, pl.ds(row, seqs, stride=stride), :] for lane in range(ref.shape[0])]
    return jnp.concatenate(tiles, axis=1)


def put_strided(ref, row, seqs, stride, value):
    for lane in range(ref.shape[0]):
        ref[lane, pl.ds(row, seqs, stride=stride), :] = value[:, lane * 128 : (lane + 1) * 128]


def put_rows(ref, row, count, value):
    for lane in range(ref.shape[0]):
        ref[lane, pl.ds(row, count), :] = value[:, lane * 128 : (lane + 1) * 128]


def get_rows(ref, row, count):
    return jnp.concatenate([ref[lane, pl.ds(row, count), :] for lane in range(ref.shape[0])], axis=1)


def first_kernel(dims, part, sources, place, normed, halo, start, lens, vecs, *refs):
    seqs, span, width, slots, blocks, depth, split = dims
    stride = span + PAD
    w = refs[:blocks + (1 if split else 0)]
    g_in, x_in = refs[len(w) : len(w) + slots], refs[len(w) + slots : len(w) + 2 * slots]
    cand, forg, rese, maps, planes, gs, xs = refs[len(w) + 2 * slots :]
    per = seqs // slots
    lane0 = part * width
    for k in range(slots):
        for j in range(per):
            to = (k * per + j) * stride + PAD
            put_rows(gs, to, span, g_in[k][j, :, lane0 : lane0 + width].astype(f32))
            put_rows(xs, to, span, x_in[k][j, :, lane0 : lane0 + width].astype(f32))

    def block(b):
        if split and b == blocks - 1:
            return jnp.concatenate([w[b][...], w[b + 1][...]], axis=0)
        return w[b][...]

    rows = per * span
    for k in range(slots):
        total = None
        for b in range(blocks):
            at = pl.multiple_of(sources[b] * depth, depth)
            term = jnp.dot(
                normed[k * rows : (k + 1) * rows, pl.ds(at, depth)],
                block(b),
                preferred_element_type=f32,
            )
            total = term if total is None else total + term
        total = total.astype(bf16).astype(f32)
        for j in range(per):
            to = (k * per + j) * stride + PAD
            for ref, gate in ((cand, 0), (forg, 1), (rese, 2)):
                here = total[j * span : (j + 1) * span, gate * width : (gate + 1) * width]
                put_rows(ref, to, span, here)
    last = None
    for b in range(blocks):
        at = pl.multiple_of(sources[b] * depth, depth)
        term = jnp.dot(halo[:, pl.ds(at, depth)], block(b)[:, :width], preferred_element_type=f32)
        last = term if last is None else last + term
    last = last.astype(bf16).astype(f32)[:seqs]
    before = jnp.where(place[1] == 0, start[...], last)
    put_strided(cand, PAD - 1, seqs, stride, before)
    peep_f, peep_r, bias_f, bias_r = (vecs[i : i + 1, :] for i in range(4))
    ends = lens[...]
    base = place[0]

    def turn(t, carry):
        previous, decays, injects, handed = carry
        row = t + PAD
        c = strided(cand, row, seqs, stride)
        f = jax.nn.sigmoid(strided(forg, row, seqs, stride) + peep_f * previous + bias_f)
        r = jax.nn.sigmoid(strided(rese, row, seqs, stride) + peep_r * previous + bias_r)
        put_strided(forg, row, seqs, stride, f)
        put_strided(rese, row, seqs, stride, r)
        live = base + t < ends
        d = jnp.where(live, f, 1.0)
        inject = jnp.where(live, (1.0 - f) * c, 0.0)
        pulled = jnp.where(live, r * strided(gs, row, seqs, stride), 0.0)
        decays = decays * d
        return c, decays, d * injects + inject, handed + decays * pulled

    one, zero = jnp.ones((seqs, width), f32), jnp.zeros((seqs, width), f32)
    _, decays, injects, handed = lax.fori_loop(0, span, turn, (before, one, zero, zero), unroll=4)
    maps[0], maps[1], maps[2] = decays, injects, handed
    c, f, r, g, x = (strided(ref, PAD, seqs, stride) for ref in (cand, forg, rese, gs, xs))
    live = base < ends
    d = jnp.where(live, f, 1.0)
    inject = jnp.where(live, (1.0 - f) * c, 0.0)
    via_adjoint = jnp.where(live, (1.0 - f) * peep_f, 0.0)
    via_state = jnp.where(live, r * (1.0 - r) * g * peep_r, 0.0)
    planes[0], planes[1] = via_adjoint, via_adjoint * c
    planes[2], planes[3] = via_state * d, via_state * (inject - x)


def second_kernel(dims, part, place, lens, vecs, links, cand, forg, rese, *refs):
    seqs, span, width, slots = dims
    stride = span + PAD
    g_in, x_in = refs[:slots], refs[slots : 2 * slots]
    grads, moved = refs[2 * slots], refs[2 * slots + 1 : 3 * slots + 1]
    final, sums = refs[3 * slots + 1 : 3 * slots + 3]
    gs, xs, states, outs, gcs, fts, rts = refs[3 * slots + 3 :]
    per = seqs // slots
    lane0 = part * width
    for k in range(slots):
        for j in range(per):
            to = (k * per + j) * stride + PAD
            put_rows(gs, to, span, g_in[k][j, :, lane0 : lane0 + width].astype(f32))
            put_rows(xs, to, span, x_in[k][j, :, lane0 : lane0 + width].astype(f32))
    peep_f, peep_r = vecs[0:1, :], vecs[1:2, :]
    ends = lens[...]
    base = place[0]
    begin, after = links[0], links[1]
    put_strided(states, PAD - 1, seqs, stride, begin)

    def forward(t, state):
        row = t + PAD
        c, f, r, x = (strided(ref, row, seqs, stride) for ref in (cand, forg, rese, xs))
        live = base + t < ends
        state = jnp.where(live, f * state + (1.0 - f) * c, state)
        put_strided(states, row, seqs, stride, state)
        put_strided(outs, row, seqs, stride, jnp.where(live, r * state + (1.0 - r) * x, x))
        return state

    end = lax.fori_loop(0, span, forward, begin, unroll=4)
    final[...] = links[2] * end + links[3]
    upcoming = end * (links[4] * after + links[6]) - links[5] * after + links[7]

    def backward(i, carry):
        reached, upcoming, pf, pr, bf, br = carry
        row = span - 1 - i + PAD
        c, f, r, x, g = (strided(ref, row, seqs, stride) for ref in (cand, forg, rese, xs, gs))
        state = strided(states, row, seqs, stride)
        prior = strided(states, row - 1, seqs, stride)
        previous = strided(cand, row - 1, seqs, stride)
        live = base + (span - 1 - i) < ends
        zero = jnp.zeros_like(f)
        adjoint = jnp.where(live, r * g, 0.0) + reached
        kept = jnp.where(live, (1.0 - f) * adjoint, zero)
        ft = f * kept * (prior - c)
        rt = jnp.where(live, r * (1.0 - r) * g * (state - x), zero)
        put_strided(gcs, row, seqs, stride, kept + upcoming)
        put_strided(fts, row, seqs, stride, ft)
        put_strided(rts, row, seqs, stride, rt)
        put_strided(gs, row, seqs, stride, jnp.where(live, (1.0 - r) * g, g))
        reached = jnp.where(live, f * adjoint, adjoint)
        return (
            reached,
            ft * peep_f + rt * peep_r,
            pf + ft * previous,
            pr + rt * previous,
            bf + ft,
            br + rt,
        )

    zero = jnp.zeros((seqs, width), f32)
    done = lax.fori_loop(0, span, backward, (after, upcoming, zero, zero, zero, zero), unroll=4)
    sums[...] = jnp.zeros_like(sums)
    for i in range(4):
        sums[i : i + 1, :] = jnp.sum(done[2 + i], axis=0, keepdims=True)
    for n in range(seqs):
        at = n * stride + PAD
        for gate, ref in enumerate((gcs, fts, rts)):
            lanes = slice(gate * width, (gate + 1) * width)
            grads[n * span : (n + 1) * span, lanes] = get_rows(ref, at, span).astype(bf16)
        k, j = n // per, n % per
        moved[k][0, j] = get_rows(outs, at, span).astype(bf16)
        moved[k][1, j] = get_rows(gs, at, span).astype(bf16)


def token_kernel(dims, sources, *refs):
    slots, blocks, depth, rows, groups, split = dims
    n_w = blocks + (1 if split else 0)
    grads = refs[:groups]
    w = [refs[groups + a * n_w : groups + (a + 1) * n_w] for a in range(groups)]
    at0 = groups + groups * n_w
    pieces = refs[at0 : at0 + slots]
    means, scales = refs[at0 + slots : at0 + slots + 2]
    own = refs[at0 + slots + 2]
    others = refs[at0 + slots + 3 : at0 + 2 * slots + 2]
    sums = refs[at0 + 2 * slots + 2]

    def block(a, b):
        if split and b == blocks - 1:
            return jnp.concatenate([w[a][b][...], w[a][b + 1][...]], axis=0)
        return w[a][b][...]

    sums[...] = jnp.zeros_like(sums)
    for b in range(blocks):
        at = pl.multiple_of(sources[b] * depth, depth)
        lanes = pl.ds(at, depth)
        gain_sum, bias_sum = jnp.zeros((8, depth), f32), jnp.zeros((8, depth), f32)
        weights = [block(a, b) for a in range(groups)]
        for k in range(slots):
            here = pl.ds(k * rows, rows)
            total = None
            for a in range(groups):
                term = lax.dot_general(
                    grads[a][here, :],
                    weights[a],
                    (((1,), (1,)), ((), ())),
                    preferred_element_type=f32,
                )
                total = term if total is None else total + term
            copies = depth // 128
            mean = jnp.concatenate([means[here, :]] * copies, axis=1)
            scale = jnp.concatenate([scales[here, :]] * copies, axis=1)
            scaled = (pieces[k][:, lanes].astype(f32) - mean) * scale
            gain_sum += jnp.sum((total * scaled).reshape(rows // 8, 8, depth), axis=0)
            bias_sum += jnp.sum(total.reshape(rows // 8, 8, depth), axis=0)
            if k == 0:
                own[:, lanes] = total
            else:
                others[k - 1][:, lanes] = total.astype(bf16)
        sums[0:1, lanes] = jnp.sum(gain_sum, axis=0, keepdims=True)
        sums[1:2, lanes] = jnp.sum(bias_sum, axis=0, keepdims=True)


def pick(table, index):
    return jnp.take(jnp.asarray(np.asarray(table), jnp.int32), index, axis=0)


def chosen(options, index):
    result = options[0]
    for i in range(1, len(options)):
        result = jnp.where(index == i, options[i], result)
    return result


def gates_of_units(weights, width, lane0, lanes):
    count, here = lax.axis_size("stream"), lax.axis_index("stream")
    if count == 4:
        pieces = [weights[:, s * width + lane0 : s * width + lane0 + lanes] for s in range(3)]
        even = here % 2 == 0
        own = jnp.where(even, pieces[0], pieces[2])
        near = swapped(pieces[1], "stream", 1)
        far = swapped(jnp.where(even, pieces[2], pieces[0]), "stream", 2)
        got = [own, near, far]
        order = ((0, 1, 2), (1, 0, 2), (2, 0, 1), (2, 1, 0))
        return jnp.concatenate(
            [chosen([got[order[d][gate]] for d in range(4)], here) for gate in range(3)], axis=1
        )
    everything = lax.all_gather(weights, "stream", axis=1, tiled=True)
    model = count * width
    return jnp.concatenate(
        [
            lax.dynamic_slice_in_dim(everything, gate * model + here * width + lane0, lanes, 1)
            for gate in range(3)
        ],
        axis=1,
    )


def columns_as_stored(gates):
    count, here = lax.axis_size("stream"), lax.axis_index("stream")
    if count == 4:
        own = chosen([gates[0], gates[1], gates[1], gates[2]], here)
        near = swapped(
            chosen([gates[1], gates[0], gates[2], gates[1]], here).astype(bf16), "stream", 1
        ).astype(f32)
        far = swapped(
            chosen([gates[2], gates[2], gates[0], gates[0]], here).astype(bf16), "stream", 2
        ).astype(f32)
        even = here % 2 == 0
        return [jnp.where(even, own, far), near, jnp.where(even, far, own)]
    everything = lax.all_gather(jnp.stack(gates).astype(bf16), "stream", axis=1).astype(f32)
    flat = everything.reshape((3 * count,) + gates[0].shape)
    return [lax.dynamic_index_in_dim(flat, 3 * here + s, 0, keepdims=False) for s in range(3)]


def gathered_blocks(block):
    count = lax.axis_size("seq")
    half = block.shape[0] // 2
    up = down = block
    blocks = [block]
    for _ in range(count // 2 - 1):
        up, down = along_ring(up, 1), along_ring(down, -1)
        blocks += [up, down]
    blocks += [along_ring(up[:half], 1), along_ring(down[half:], -1)]
    return blocks


def exchanged_maps(maps):
    count, here = lax.axis_size("seq"), lax.axis_index("seq")
    decay, inject, handed = maps[0], maps[1], maps[2]
    one, zero = jnp.ones_like(decay), jnp.zeros_like(decay)
    before = (one, zero)
    after = (one, zero, zero)
    bit = 1
    while bit < count:
        other = swapped(jnp.stack([decay, inject, handed]), "seq", bit)
        theirs = (other[0], other[1], other[2])
        first = (here & bit) == 0
        before_new = (theirs[0] * before[0], before[0] * theirs[1] + before[1])
        after_new = (
            after[0] * theirs[0],
            theirs[0] * after[1] + theirs[1],
            after[2] + after[0] * theirs[2],
        )
        before = tuple(jnp.where(first, a, b) for a, b in zip(before, before_new))
        after = tuple(jnp.where(first, b, a) for a, b in zip(after, after_new))
        together = decay * theirs[0]
        inject_new = jnp.where(
            first, theirs[0] * inject + theirs[1], decay * theirs[1] + inject
        )
        handed_new = jnp.where(
            first, handed + decay * theirs[2], theirs[2] + theirs[0] * handed
        )
        decay, inject, handed = together, inject_new, handed_new
        bit *= 2
    return before, after


def local(
    inputs,
    start_state,
    lengths,
    weights,
    peep_forget,
    peep_reset,
    bias_forget,
    bias_reset,
    norm_gain,
    norm_bias,
    out_grad,
):
    per, span, model = inputs.shape
    n_seq, slots = lax.axis_size("seq"), lax.axis_size("stream")
    at_seq, at_stream = lax.axis_index("seq"), lax.axis_index("stream")
    seqs = per * slots
    units = model // slots
    width = units // GROUPS
    depth = model // n_seq
    rows = per * span
    tokens = seqs * span
    order = ring_order(n_seq)
    spot = pick(np.argsort(order), at_seq)
    far = n_seq // 2
    steps = [0]
    for k in range(1, far):
        steps += [-k, k]
    steps.append(far)
    sources = pick(order, (spot + jnp.asarray(steps, jnp.int32)) % n_seq)
    place = jnp.stack([at_seq * span, at_seq]).astype(jnp.int32)

    bits = []
    bit = slots // 2
    while bit:
        bits.append(bit)
        bit //= 2

    def everyone(own):
        pieces = {0: own}
        for bit in bits:
            for k in list(pieces):
                pieces[k ^ bit] = swapped(pieces[k], "stream", bit)
        return [pieces[k] for k in range(slots)]

    def owner_units(array, k, lanes=units, lane0=0):
        return lax.dynamic_slice_in_dim(
            array, (at_stream ^ k) * units + lane0, lanes, array.ndim - 1
        )

    ordered_weights = [
        gates_of_units(weights, units, a * width, width) for a in range(GROUPS)
    ]
    blocks = [gathered_blocks(block) for block in ordered_weights]

    held_depth, split = depth, True
    if depth % 128:
        places = jnp.stack([sources[b] for b in range(n_seq)] + [sources[n_seq - 1]]) * depth
        places = places.at[n_seq].add(depth // 2)
        held_depth, split = 2 * 128, False
        for a in range(GROUPS):
            whole = jnp.zeros((model, 3 * width), bf16)
            for b, block in enumerate(blocks[a]):
                whole = lax.dynamic_update_slice_in_dim(whole, block, places[b], 0)
            blocks[a] = [whole[i : i + held_depth] for i in range(0, model, held_depth)]
        sources = jnp.arange(model // held_depth, dtype=jnp.int32)
    n_blocks = model // held_depth

    pieces = everyone(inputs.reshape(rows, model))
    ahead = lax.ppermute(
        inputs[:, -1, :], "seq", [(i, i + 1) for i in range(n_seq - 1)]
    )
    halo = jnp.concatenate(everyone(ahead), axis=0)
    halo = jnp.concatenate([halo, jnp.zeros((-seqs % 16, model), bf16)], axis=0)
    small = []
    for k in range(slots):
        message = jnp.concatenate(
            [
                owner_units(start_state, k),
                jnp.broadcast_to(lengths.astype(f32)[:, None], (per, 128)),
            ],
            axis=1,
        )
        small.append(swapped(message, "stream", k) if k else message)
    small = jnp.concatenate(small, axis=0)
    start_units = small[:, :units]
    ends = small[:, units : units + 1].astype(jnp.int32)
    ends = jnp.broadcast_to(ends, (seqs, width))
    grads_in = []
    for k in range(slots):
        message = owner_units(out_grad, k)
        grads_in.append(swapped(message, "stream", k) if k else message)
    sources_in = [
        lax.dynamic_slice_in_dim(piece, at_stream * units, units, 1).reshape(per, span, units)
        for piece in pieces
    ]

    gain_row, bias_row = norm_gain.reshape(1, model), norm_bias.reshape(1, model)
    normed, means, scales = call(
        functools.partial(norm_kernel, slots, rows),
        [
            jax.ShapeDtypeStruct((tokens, model), bf16),
            jax.ShapeDtypeStruct((tokens, 128), f32),
            jax.ShapeDtypeStruct((tokens, 128), f32),
        ],
        [*pieces, gain_row, bias_row],
        flops=tokens * model * 10,
        touched=tokens * model * 4,
    )
    wide = halo.astype(f32)
    centered = wide - jnp.mean(wide, axis=1, keepdims=True)
    spread = lax.rsqrt(jnp.mean(centered * centered, axis=1, keepdims=True) + epsilon)
    halo = (centered * spread * gain_row + bias_row).astype(bf16)

    vectors = jnp.stack([peep_forget, peep_reset, bias_forget, bias_reset])
    vectors = lax.dynamic_slice_in_dim(vectors, at_stream * units, units, 1)
    vectors = jnp.concatenate([vectors, jnp.zeros_like(vectors)], axis=0)

    tall = seqs * (span + PAD)
    field = jax.ShapeDtypeStruct((width // 128, tall, 128), f32)
    space = pltpu.VMEM((width // 128, tall, 128), f32)
    grad_groups, sum_groups, final_groups, moved_groups, parts_groups = [], [], [], [], []
    for a in range(GROUPS):
        vecs = vectors[:, a * width : (a + 1) * width]
        start = start_units[:, a * width : (a + 1) * width]
        cand, forg, rese, maps, planes = call(
            functools.partial(
                first_kernel, (seqs, span, width, slots, n_blocks, held_depth, split), a
            ),
            [
                field,
                field,
                field,
                jax.ShapeDtypeStruct((3, seqs, width), f32),
                jax.ShapeDtypeStruct((4, seqs, width), f32),
            ],
            [sources, place, normed, halo, start, ends, vecs, *blocks[a], *grads_in, *sources_in],
            scratch=[space, space],
            scalars=2,
            flops=2 * tokens * model * 3 * width,
            touched=tokens * model * 2,
        )
        linked = lax.ppermute(planes, "seq", [(i + 1, i) for i in range(n_seq - 1)])
        before, after = exchanged_maps(maps)
        begin = before[0] * start + before[1]
        links = jnp.concatenate(
            [jnp.stack([begin, after[2], after[0], after[1]]), linked], axis=0
        )
        out = call(
            functools.partial(second_kernel, (seqs, span, width, slots), a),
            [
                jax.ShapeDtypeStruct((tokens, 3 * width), bf16),
                *[jax.ShapeDtypeStruct((2, per, span, width), bf16)] * slots,
                jax.ShapeDtypeStruct((seqs, width), f32),
                jax.ShapeDtypeStruct((8, width), f32),
            ],
            [place, ends, vecs, links, cand, forg, rese, *grads_in, *sources_in],
            scratch=[space] * 7,
            scalars=1,
            flops=tokens * width * 60,
            touched=tokens * width * 24,
        )
        grads = out[0]
        grad_groups.append(grads)
        final_groups.append(out[slots + 1])
        sum_groups.append(out[slots + 2][:4])
        moved = [
            swapped(out[1 + k], "stream", k) if k else out[1 + k] for k in range(slots)
        ]
        moved_groups.append(moved)

        def partial(dest, grads=grads):
            columns = lax.dynamic_slice_in_dim(normed, dest * depth, depth, 1)
            return lax.dot_general(
                columns, grads, (((0,), (0,)), ((), ())), preferred_element_type=f32
            )

        def owner(distance):
            return pick(order, (spot + distance) % n_seq)

        half = depth // 2
        farthest = partial(owner(far)).astype(bf16)
        up = along_ring(farthest[:half], 1)
        down = along_ring(farthest[half:], -1)
        for distance in range(far - 1, 0, -1):
            mine_up = partial(owner(distance))
            mine_down = partial(owner(-distance))
            if distance == far - 1:
                mine_up = jnp.concatenate(
                    [mine_up[:half] + up.astype(f32), mine_up[half:]], axis=0
                )
                mine_down = jnp.concatenate(
                    [mine_down[:half], mine_down[half:] + down.astype(f32)], axis=0
                )
            else:
                mine_up = mine_up + up.astype(f32)
                mine_down = mine_down + down.astype(f32)
            up = along_ring(mine_up.astype(bf16), 1)
            down = along_ring(mine_down.astype(bf16), -1)
        mine = partial(at_seq) + up.astype(f32) + down.astype(f32)
        parts_groups.append(
            columns_as_stored([mine[:, g * width : (g + 1) * width] for g in range(3)])
        )

    weight_grad = jnp.concatenate(
        [parts_groups[a][s] for s in range(3) for a in range(GROUPS)], axis=1
    )

    token_out = call(
        functools.partial(token_kernel, (slots, n_blocks, held_depth, rows, GROUPS, split)),
        [
            jax.ShapeDtypeStruct((rows, model), f32),
            *[jax.ShapeDtypeStruct((rows, model), bf16)] * (slots - 1),
            jax.ShapeDtypeStruct((8, model), f32),
        ],
        [
            sources,
            *grad_groups,
            *[block for group in blocks for block in group],
            *pieces,
            means,
            scales,
        ],
        scalars=1,
        flops=2 * tokens * model * 3 * units,
        touched=tokens * model * 4,
    )
    held = {k: token_out[k] for k in range(slots)}
    for bit in reversed(bits):
        for k in sorted(held):
            if k & bit:
                got = swapped(held.pop(k).astype(bf16), "stream", bit)
                held[k ^ bit] = held[k ^ bit].astype(f32) + got.astype(f32)
    grad_normed = held[0]

    outputs = jnp.zeros((per, span, model), bf16)
    direct = jnp.zeros((per, span, model), bf16)
    for a in range(GROUPS):
        for k in range(slots):
            at = (at_stream ^ k) * units + a * width
            outputs = lax.dynamic_update_slice_in_dim(outputs, moved_groups[a][k][0], at, 2)
            direct = lax.dynamic_update_slice_in_dim(direct, moved_groups[a][k][1], at, 2)

    source = inputs.astype(f32).reshape(rows, model)
    scale = scales[:rows, :1]
    scaled = (source - means[:rows, :1]) * scale
    grad_scaled = grad_normed * norm_gain
    grad_source = scale * (
        grad_scaled
        - jnp.mean(grad_scaled, axis=1, keepdims=True)
        - scaled * jnp.mean(grad_scaled * scaled, axis=1, keepdims=True)
    )
    input_grad = (grad_source.reshape(per, span, model) + direct.astype(f32)).astype(bf16)

    gate_sums = jnp.concatenate(sum_groups, axis=1)
    summed = jnp.concatenate(
        [
            lax.dynamic_update_slice_in_dim(
                jnp.zeros((4, model), f32), gate_sums, at_stream * units, 1
            ),
            token_out[slots][:2],
        ],
        axis=0,
    )
    for bit in reversed(bits):
        summed = summed + swapped(summed, "stream", bit)
    bit = 1
    while bit < n_seq:
        summed = summed + swapped(summed, "seq", bit)
        bit *= 2

    final_units = jnp.concatenate(final_groups, axis=1)
    share = model // n_seq
    holder = at_seq * share // units
    within = at_seq * share % units
    mine = lax.dynamic_slice_in_dim(final_units, within, share, 1)
    mine = jnp.where(at_stream == holder, mine, 0.0)
    ordered = jnp.zeros_like(mine)
    for k in range(slots):
        ordered = lax.dynamic_update_slice_in_dim(
            ordered, mine[k * per : (k + 1) * per], (at_stream ^ k) * per, 0
        )
    for bit in reversed(bits):
        ordered = ordered + swapped(ordered, "stream", bit)
    final_state = lax.dynamic_slice_in_dim(ordered, at_stream * per, per, 0)

    return (
        outputs,
        final_state,
        input_grad,
        weight_grad,
        summed[0],
        summed[1],
        summed[2],
        summed[3],
        summed[4],
        summed[5],
    )


def solution(mesh):
    return jax.shard_map(
        local,
        mesh=mesh,
        in_specs=(
            P("stream", "seq", None),
            P("stream", None),
            P("stream"),
            P("seq", "stream"),
            P(),
            P(),
            P(),
            P(),
            P(),
            P(),
            P("stream", "seq", None),
        ),
        out_specs=(
            P("stream", "seq", None),
            P("stream", "seq"),
            P("stream", "seq", None),
            P("seq", "stream"),
            P(),
            P(),
            P(),
            P(),
            P(),
            P(),
        ),
        check_vma=False,
    )
```

time: 1190 us -> 324 us (0.27); the launches traced: 1170 us -> 324 us
  local copies, waits for them, and re-layouts: 397 us -> 23.4 us
  waiting for transfers between devices: 394 us -> 124 us
  blocking collectives: 180 us -> 0 us
  other arithmetic: 138 us -> 12.5 us
  starting transfers between devices: 9.19 us -> 78.3 us
  Pallas kernels: 0 us -> 63.3 us
  matrix products: 36.1 us -> 14.8 us
    reduce_scatter x2 -> x0, waiting for transfers between devices: 214 us -> none  [the longest x1 161 us: local(): lax.psum_scatter(jnp.einsum('nck,nco->ko', piece_rows, returned_slab, pre...]
    slice x98 -> x17, local copies, waits for them, and re-layouts: 214 us -> 4.31 us  [the longest x1 1.11 us: local(): scaled = (source - means[:rows, :1]) * scale]
    all_gather x2 -> x0, waiting for transfers between devices: 138 us -> none  [the longest x1 101 us: local(): weight_rows = lax.all_gather(weights, 'seq', axis=0, tiled=True)]
    ppermute x2 -> x77, waiting for transfers between devices: 4.07 us -> 124 us  [the longest x42 67.9 us: swapped(): lax.ppermute(value, axis, [(i, i ^ bit) for i in range(lax.axis_size(axis...]
    pad x48 -> x0, local copies, waits for them, and re-layouts: 104 us -> none  [the longest x24 52.4 us: local(): lax.associative_scan(compose, (next_decay, grad_state), axis=1, reverse=T...]
    all_gather x3 -> x0, blocking collectives: 92.5 us -> none  [carried_in(): everything = jax.tree.map(lambda part: lax.all_gather(part, axis), array)]
    ppermute x2 -> x77, starting transfers between devices: 4.2 us -> 78.3 us  [the longest x42 38.5 us: swapped(): lax.ppermute(value, axis, [(i, i ^ bit) for i in range(lax.axis_size(axis...]
    pallas_call x0 -> x6, Pallas kernels: none -> 63.3 us  [call(): pl.pallas_call(kernel, out_shape=out_shape, in_specs=specs, out_specs=jax...]
  transfers between devices with their start and end apart: 7 -> 77, of which waited for: 6 -> 31; matrix products, arithmetic and copies ran while one was open for 2% -> 11% of each run, Pallas kernels for 0% -> 13%
where the time goes in v1:
time: 324 us
  waiting for transfers between devices  124 us (38%)
  starting transfers between devices  78.3 us (24%)
  Pallas kernels  63.3 us (20%)
  local copies, waits for them, and re-layouts  23.4 us (7%)
  matrix products  14.8 us (5%)
  other arithmetic  12.5 us (4%)
  between operations  7.26 us (2%)
    ppermute x42, waiting for transfers between devices, swapped(): lax.ppermute(value, axis, [(i, i ^ bit) for i in range(lax.axis_size(axis...  67.9 us
    pallas_call x6, Pallas kernels, call(): pl.pallas_call(kernel, out_shape=out_shape, in_specs=specs, out_specs=jax...  63.3 us
    ppermute x32, waiting for transfers between devices, along_ring(): lax.ppermute(value, 'seq', [(order[i], order[(i + steps) % count]) for i...  56 us
    ppermute x42, starting transfers between devices, swapped(): lax.ppermute(value, axis, [(i, i ^ bit) for i in range(lax.axis_size(axis...  38.5 us
    ppermute x32, starting transfers between devices, along_ring(): lax.ppermute(value, 'seq', [(order[i], order[(i + steps) % count]) for i...  33.3 us
    dot_general x16, matrix products, partial(): lax.dot_general(columns, grads, (((0,), (0,)), ((), ())), preferred_eleme...  14.8 us
  transfers between devices with their start and end apart: 77, of which 31 were waited for; matrix products, arithmetic and copies ran while one was open for 11% of the time, Pallas kernels for 13%

profile of v1, /device:TPU:0, one launch (start us, length us, event | category | flops | bytes accessed | tf_op | source)
XLA Modules:
  0.0 323.6 jit_solution(17326890630303696963)
XLA Ops:
  1.9 3.0 collective-permute-start.30
  7.5 1.9 collective-permute-start.4
  17.9 3.8 %collective-permute-start.6 = (bf16[2,2048]{1,0:T(2,128)(2,1)S(1)}, bf16[2,2048]{1,0:T(2,128)(2,1)S(1)}, u32[]{:S(2)}, u32[]{:S(2)}) collective-permute-start(bf16[2,2048]{1,0:T(2,128)(2,1)S(1)} %bitcast.183), channel_id=1, source_target_pairs={{0,4},{4,8},{8,12},{12,16},{16,20},{20,24},{24,28},{1,5},{5,9},{9,... | collective-permute-start | bytes 24584 | tf_op jit(solution)/shard_map/ppermute | solution.py:461
  21.7 13.9 %collective-permute-done.10 = bf16[256,256]{1,0:T(8,128)(2,1)S(1)} collective-permute-done((bf16[256,256]{1,0:T(8,128)(2,1)S(1)}, bf16[256,256]{1,0:T(8,128)(2,1)S(1)}, u32[]{:S(2)}, u32[]{:S(2)}) %collective-permute-start.10) | collective-permute-done | bytes 131104 | tf_op jit(solution)/shard_map/ppermute | solution.py:53
  35.6 1.8 collective-permute-start.32
  37.8 1.7 collective-permute-start.8
  43.3 1.6 collective-permute-start.12
  55.2 2.1 constant_dynamic-slice_fusion.6
  61.1 2.7 collective-permute-done.34.refs_3_.refs_14_
  65.5 5.1 %collective-permute-done.35.refs_4_.refs_15_ = bf16[256,768]{1,0:T(8,128)(2,1)S(1)} collective-permute-done((bf16[256,768]{1,0:T(8,128)(2,1)}, bf16[256,768]{1,0:T(8,128)(2,1)S(1)}, u32[]{:S(2)}, u32[]{:S(2)}) %collective-permute-start.35) | collective-permute-done | bytes 393248 | tf_op jit(solution)/shard_map/ppermute | solution.py:49
  72.6 1.6 collective-permute-start.16
  74.2 4.8 %collective-permute-done.15.refs_4_.refs_6_ = bf16[256,768]{1,0:T(8,128)(2,1)S(1)} collective-permute-done((bf16[256,768]{1,0:T(8,128)(2,1)}, bf16[256,768]{1,0:T(8,128)(2,1)S(1)}, u32[]{:S(2)}, u32[]{:S(2)}) %collective-permute-start.15) | collective-permute-done | bytes 393248 | tf_op jit(solution)/shard_map/ppermute | solution.py:49
  79.8 3.1 collective-permute-done.36.refs_5_.refs_16_
  82.9 4.6 %collective-permute-done.37.refs_6_.refs_17_ = bf16[256,768]{1,0:T(8,128)(2,1)S(1)} collective-permute-done((bf16[256,768]{1,0:T(8,128)(2,1)S(1)}, bf16[256,768]{1,0:T(8,128)(2,1)S(1)}, u32[]{:S(2)}, u32[]{:S(2)}) %collective-permute-start.37) | collective-permute-done | bytes 393248 | tf_op jit(solution)/shard_map/ppermute | solution.py:49
  89.7 3.7 %collective-permute-done.17.refs_6_.refs_8_ = bf16[256,768]{1,0:T(8,128)(2,1)S(1)} collective-permute-done((bf16[256,768]{1,0:T(8,128)(2,1)S(1)}, bf16[256,768]{1,0:T(8,128)(2,1)S(1)}, u32[]{:S(2)}, u32[]{:S(2)}) %collective-permute-start.17) | collective-permute-done | bytes 393248 | tf_op jit(solution)/shard_map/ppermute | solution.py:49
  95.4 1.7 constant_dynamic-slice_fusion.4
  97.1 12.1 %shard_map.339 = (bf16[1024,2048]{1,0:T(8,128)(2,1)}, f32[1024,128]{1,0:T(8,128)}, f32[1024,128]{1,0:T(8,128)}) custom-call(bf16[256,2048]{1,0:T(8,128)(2,1)} %bitcast.154, bf16[256,2048]{1,0:T(8,128)(2,1)} %collective-permute-done.3.refs_1_.refs_21_, bf16[256,2048]{1,0:T(8,128)(2,1)} %copy-done.12, bf16[256,2048]{1,0:T(8,128)(2,1)} %copy-done.13, ...), custom_call_target="tpu_custom_call" | custom-call | flops 20971520 | bytes 8388608 | tf_op jit(solution)/shard_map/pallas_call | solution.py:29
  109.2 1.7 constant_dynamic-slice_fusion.2
  110.9 1.6 collective-permute-start.18
  113.9 10.4 %shard_map.342 = (f32[2,1088,128]{2,1,0:T(8,128)}, f32[2,1088,128]{2,1,0:T(8,128)}, f32[2,1088,128]{2,1,0:T(8,128)}, f32[3,8,256]{2,1,0:T(8,128)}, f32[4,8,256]{2,1,0:T(8,128)}) custom-call(s32[8]{0:T(128)} %and_select_fusion.sources, s32[2]{0:T(128)} %pad_add_fusion.place, bf16[1024,2048]{1,0:T(8,128)(2,1)} %get-tuple-element.42.normed, ...), custom_call_target="tpu_custom_call" | custom-call | flops 3221225472 | bytes 4194304 | tf_op jit(solution)/shard_map/pallas_call | solution.py:29
  127.1 10.4 %shard_map.340 = (f32[2,1088,128]{2,1,0:T(8,128)}, f32[2,1088,128]{2,1,0:T(8,128)}, f32[2,1088,128]{2,1,0:T(8,128)}, f32[3,8,256]{2,1,0:T(8,128)}, f32[4,8,256]{2,1,0:T(8,128)}) custom-call(s32[8]{0:T(128)} %and_select_fusion.sources, s32[2]{0:T(128)} %pad_add_fusion.place, bf16[1024,2048]{1,0:T(8,128)(2,1)} %get-tuple-element.42.normed, ...), custom_call_target="tpu_custom_call" | custom-call | flops 3221225472 | bytes 4194304 | tf_op jit(solution)/shard_map/pallas_call | solution.py:29
  137.5 2.7 collective-permute-start.23
  142.7 2.2 collective-permute-start.41
  146.9 4.3 %collective-permute-start.42 = (f32[3,8,256]{2,1,0:T(8,128)S(1)}, f32[3,8,256]{2,1,0:T(8,128)S(1)}, u32[]{:S(2)}, u32[]{:S(2)}) collective-permute-start(f32[3,8,256]{2,1,0:T(8,128)S(1)} %pad_maximum_fusion.10), channel_id=1, source_target_pairs={{0,16},{4,20},{8,24},{12,28},{16,0},{20,4},{24,8},{28,12},{1,17},{... | collective-permute-start | bytes 73736 | tf_op jit(solution)/shard_map/ppermute | solution.py:53
  151.2 2.4 collective-permute-start.25
  154.3 8.1 %shard_map.343 = (bf16[1024,768]{1,0:T(8,128)(2,1)}, bf16[2,2,128,256]{3,2,1,0:T(8,128)(2,1)}, bf16[2,2,128,256]{3,2,1,0:T(8,128)(2,1)}, bf16[2,2,128,256]{3,2,1...) custom-call(s32[2]{0:T(128)} %pad_add_fusion.place, ...), custom_call_target="tpu_custom_call" | custom-call | flops 15728640 | bytes 6291456 | tf_op jit(solution)/shard_map/pallas_call | solution.py:29
  162.4 3.0 fusion.20
  166.9 8.0 %shard_map.341 = (bf16[1024,768]{1,0:T(8,128)(2,1)}, bf16[2,2,128,256]{3,2,1,0:T(8,128)(2,1)}, bf16[2,2,128,256]{3,2,1,0:T(8,128)(2,1)}, bf16[2,2,128,256]{3,2,1...) custom-call(s32[2]{0:T(128)} %pad_add_fusion.place, ...), custom_call_target="tpu_custom_call" | custom-call | flops 15728640 | bytes 6291456 | tf_op jit(solution)/shard_map/pallas_call | solution.py:29
  174.9 3.1 fusion.22
  179.9 14.4 %shard_map.344 = (f32[256,2048]{1,0:T(8,128)}, bf16[256,2048]{1,0:T(8,128)(2,1)}, bf16[256,2048]{1,0:T(8,128)(2,1)}, bf16[256,2048]{1,0:T(8,128)(2,1)}, f32[8,2048]{1,0:T(8,128)}) custom-call(s32[8]{0:T(128)} %and_select_fusion.sources, bf16[1024,768]{1,0:T(8,128)(2,1)} %get-tuple-element.64.refs_0_, bf16[1024,768]{1,0:T(8,128)(2,1)} %get-tuple-element.65.refs_1_, ...), custom_call_target="tpu_custom_call" | custom-call | flops 6442450944 | bytes 8388608 | tf_op jit(solution)/shard_map/pallas_call | solution.py:29
  205.8 5.1 %collective-permute-done.74 = f32[6,2048]{1,0:T(8,128)S(1)} collective-permute-done((f32[6,2048]{1,0:T(8,128)S(1)}, f32[6,2048]{1,0:T(8,128)S(1)}, u32[]{:S(2)}, u32[]{:S(2)}) %collective-permute-start.74) | collective-permute-done | bytes 49184 | tf_op jit(solution)/shard_map/ppermute | solution.py:53
  211.0 4.4 %collective-permute-done.75 = f32[6,2048]{1,0:T(8,128)S(1)} collective-permute-done((f32[6,2048]{1,0:T(8,128)S(1)}, f32[6,2048]{1,0:T(8,128)S(1)}, u32[]{:S(2)}, u32[]{:S(2)}) %collective-permute-start.75) | collective-permute-done | bytes 49184 | tf_op jit(solution)/shard_map/ppermute | solution.py:53
  217.4 3.8 %collective-permute-start.76 = (f32[6,2048]{1,0:T(8,128)S(1)}, f32[6,2048]{1,0:T(8,128)S(1)}, u32[]{:S(2)}, u32[]{:S(2)}) collective-permute-start(f32[6,2048]{1,0:T(8,128)S(1)} %add.592), channel_id=1, source_target_pairs={{0,16},{4,20},{8,24},{12,28},{16,0},{20,4},{24,8},{28,12},{1,17},{... | collective-permute-start | bytes 147464 | tf_op jit(solution)/shard_map/ppermute | solution.py:53
  221.3 3.6 %collective-permute-done.76 = f32[6,2048]{1,0:T(8,128)S(1)} collective-permute-done((f32[6,2048]{1,0:T(8,128)S(1)}, f32[6,2048]{1,0:T(8,128)S(1)}, u32[]{:S(2)}, u32[]{:S(2)}) %collective-permute-start.76) | collective-permute-done | bytes 49184 | tf_op jit(solution)/shard_map/ppermute | solution.py:53
  227.9 5.6 %collective-permute-done.29 = bf16[2,2,128,256]{3,2,1,0:T(8,128)(2,1)S(1)} collective-permute-done((bf16[2,2,128,256]{3,2,1,0:T(8,128)(2,1)S(1)}, bf16[2,2,128,256]{3,2,1,0:T(8,128)(2,1)S(1)}, u32[]{:S(2)}, u32[]{:S(2)}) %collective-permute-start.29) | collective-permute-done | bytes 262176 | tf_op jit(solution)/shard_map/ppermute | solution.py:53
  234.3 3.2 collective-permute-done.45
  237.5 1.8 collective-permute-start.66
  239.4 4.5 %collective-permute-done.46 = bf16[2,2,128,256]{3,2,1,0:T(8,128)(2,1)S(1)} collective-permute-done((bf16[2,2,128,256]{3,2,1,0:T(8,128)(2,1)S(1)}, bf16[2,2,128,256]{3,2,1,0:T(8,128)(2,1)S(1)}, u32[]{:S(2)}, u32[]{:S(2)}) %collective-permute-start.46) | collective-permute-done | bytes 262176 | tf_op jit(solution)/shard_map/ppermute | solution.py:53
  247.1 1.7 collective-permute-done.66
  249.9 6.0 %collective-permute-done.53 = bf16[256,768]{1,0:T(8,128)(2,1)S(1)} collective-permute-done((bf16[256,768]{1,0:T(8,128)(2,1)S(1)}, bf16[256,768]{1,0:T(8,128)(2,1)S(1)}, u32[]{:S(2)}, u32[]{:S(2)}) %collective-permute-start.53) | collective-permute-done | bytes 393248 | tf_op jit(solution)/shard_map/ppermute | solution.py:49
  259.5 4.9 %collective-permute-done.63 = bf16[256,768]{1,0:T(8,128)(2,1)S(1)} collective-permute-done((bf16[256,768]{1,0:T(8,128)(2,1)S(1)}, bf16[256,768]{1,0:T(8,128)(2,1)S(1)}, u32[]{:S(2)}, u32[]{:S(2)}) %collective-permute-start.63) | collective-permute-done | bytes 393248 | tf_op jit(solution)/shard_map/ppermute | solution.py:49
  266.3 1.7 collective-permute-done.67
  268.8 4.0 %collective-permute-done.54 = bf16[256,768]{1,0:T(8,128)(2,1)S(1)} collective-permute-done((bf16[256,768]{1,0:T(8,128)(2,1)S(1)}, bf16[256,768]{1,0:T(8,128)(2,1)S(1)}, u32[]{:S(2)}, u32[]{:S(2)}) %collective-permute-start.54) | collective-permute-done | bytes 393248 | tf_op jit(solution)/shard_map/ppermute | solution.py:49
  274.7 1.7 collective-permute-done.58
  277.3 1.9 collective-permute-start.59
  279.5 8.5 %collective-permute-done.55 = bf16[256,768]{1,0:T(8,128)(2,1)S(1)} collective-permute-done((bf16[256,768]{1,0:T(8,128)(2,1)S(1)}, bf16[256,768]{1,0:T(8,128)(2,1)S(1)}, u32[]{:S(2)}, u32[]{:S(2)}) %collective-permute-start.55) | collective-permute-done | bytes 393248 | tf_op jit(solution)/shard_map/ppermute | solution.py:49
  288.1 2.0 collective-permute-start.51
  295.2 21.6 %collective-permute-done.60 = bf16[256,256]{1,0:T(8,128)(2,1)S(1)} collective-permute-done((bf16[256,256]{1,0:T(8,128)(2,1)S(1)}, bf16[256,256]{1,0:T(8,128)(2,1)S(1)}, u32[]{:S(2)}, u32[]{:S(2)}) %collective-permute-start.60) | collective-permute-done | bytes 131104 | tf_op jit(solution)/shard_map/ppermute | solution.py:53
  (379 shorter events, 89.1 us)
Async XLA Ops:
  1.9 15.7 %collective-permute-start.30 = (bf16[256,256]{1,0:T(8,128)(2,1)S(1)}, bf16[256,256]{1,0:T(8,128)(2,1)S(1)}, u32[]{:S(2)}, u32[]{:S(2)}) collective-permute-start(bf16[256,256]{1,0:T(8,128)(2,1)S(1)} %get-tuple-element.256), channel_id=1, source_target_pairs={{0,2},{1,3},{2,0},{3,1},{4,6},{5,7},{6,4},{7,5},{8,10},{9,11},{10,... | collective-permute-start | bytes 393224 | tf_op jit(solution)/shard_map/ppermute | solution.py:53
  4.9 12.7 %collective-permute-start.31 = (bf16[256,256]{1,0:T(8,128)(2,1)S(1)}, bf16[256,256]{1,0:T(8,128)(2,1)S(1)}, u32[]{:S(2)}, u32[]{:S(2)}) collective-permute-start(bf16[256,256]{1,0:T(8,128)(2,1)S(1)} %get-tuple-element.255), channel_id=1, source_target_pairs={{0,1},{1,0},{2,3},{3,2},{4,5},{5,4},{6,7},{7,6},{8,9},{9,8},{10,11... | collective-permute-start | bytes 393224 | tf_op jit(solution)/shard_map/ppermute | solution.py:53
  7.4 30.2 %collective-permute-start.1 = (f32[2,640]{1,0:T(2,128)S(1)}, f32[2,640]{1,0:T(2,128)S(1)}, u32[]{:S(2)}, u32[]{:S(2)}) collective-permute-start(f32[2,640]{1,0:T(2,128)S(1)} %get-tuple-element.306), channel_id=1, source_target_pairs={{0,2},{1,3},{2,0},{3,1},{4,6},{5,7},{6,4},{7,5},{8,10},{9,11},{10,... | collective-permute-start | bytes 15368 | tf_op jit(solution)/shard_map/ppermute | solution.py:53
  7.5 57.7 %collective-permute-start.4 = (bf16[256,2048]{1,0:T(8,128)(2,1)}, bf16[256,2048]{1,0:T(8,128)(2,1)S(1)}, u32[]{:S(2)}, u32[]{:S(2)}) collective-permute-start(bf16[256,2048]{1,0:T(8,128)(2,1)} %bitcast.153), channel_id=1, source_target_pairs={{0,2},{1,3},{2,0},{3,1},{4,6},{5,7},{6,4},{7,5},{8,10},{9,11},{10,... | collective-permute-start | bytes 3145736 | tf_op jit(solution)/shard_map/ppermute | solution.py:53
  17.6 18.0 %collective-permute-start.10 = (bf16[256,256]{1,0:T(8,128)(2,1)S(1)}, bf16[256,256]{1,0:T(8,128)(2,1)S(1)}, u32[]{:S(2)}, u32[]{:S(2)}) collective-permute-start(bf16[256,256]{1,0:T(8,128)(2,1)S(1)} %get-tuple-element.254), channel_id=1, source_target_pairs={{0,2},{1,3},{2,0},{3,1},{4,6},{5,7},{6,4},{7,5},{8,10},{9,11},{10,... | collective-permute-start | bytes 393224 | tf_op jit(solution)/shard_map/ppermute | solution.py:53
  17.8 19.6 %collective-permute-start.11 = (bf16[256,256]{1,0:T(8,128)(2,1)S(1)}, bf16[256,256]{1,0:T(8,128)(2,1)S(1)}, u32[]{:S(2)}, u32[]{:S(2)}) collective-permute-start(bf16[256,256]{1,0:T(8,128)(2,1)S(1)} %get-tuple-element.253), channel_id=1, source_target_pairs={{0,1},{1,0},{2,3},{3,2},{4,5},{5,4},{6,7},{7,6},{8,9},{9,8},{10,11... | collective-permute-start | bytes 393224 | tf_op jit(solution)/shard_map/ppermute | solution.py:53
  17.9 19.9 %collective-permute-start.6 = (bf16[2,2048]{1,0:T(2,128)(2,1)S(1)}, bf16[2,2048]{1,0:T(2,128)(2,1)S(1)}, u32[]{:S(2)}, u32[]{:S(2)}) collective-permute-start(bf16[2,2048]{1,0:T(2,128)(2,1)S(1)} %bitcast.183), channel_id=1, source_target_pairs={{0,4},{4,8},{8,12},{12,16},{16,20},{20,24},{24,28},{1,5},{5,9},{9,... | collective-permute-start | bytes 24584 | tf_op jit(solution)/shard_map/ppermute | solution.py:461
  42.5 29.6 %collective-permute-start.3 = (bf16[256,2048]{1,0:T(8,128)(2,1)S(1)}, bf16[256,2048]{1,0:T(8,128)(2,1)}, u32[]{:S(2)}, u32[]{:S(2)}) collective-permute-start(bf16[256,2048]{1,0:T(8,128)(2,1)S(1)} %bitcast.157), channel_id=1, source_target_pairs={{0,1},{1,0},{2,3},{3,2},{4,5},{5,4},{6,7},{7,6},{8,9},{9,8},{10,11... | collective-permute-start | bytes 3145736 | tf_op jit(solution)/shard_map/ppermute | solution.py:53
  43.3 15.7 %collective-permute-start.12 = (bf16[256,768]{1,0:T(8,128)(2,1)S(1)}, bf16[256,768]{1,0:T(8,128)(2,1)}, u32[]{:S(2)}, u32[]{:S(2)}) collective-permute-start(bf16[256,768]{1,0:T(8,128)(2,1)S(1)} %pad_maximum_fusion.refs_0_.refs_2_), channel_id=1, source_target_pairs={{0,8},{8,16},{16,24},{24,28},{28,20},{20,12},{12,4},{4,0},{1,9},{9... | collective-permute-start | bytes 1179656 | tf_op jit(solution)/shard_map/ppermute | solution.py:49
  45.9 13.9 %collective-permute-start.13 = (bf16[256,768]{1,0:T(8,128)(2,1)S(1)}, bf16[256,768]{1,0:T(8,128)(2,1)}, u32[]{:S(2)}, u32[]{:S(2)}) collective-permute-start(bf16[256,768]{1,0:T(8,128)(2,1)S(1)} %pad_maximum_fusion.refs_0_.refs_2_), channel_id=1, source_target_pairs={{0,4},{8,0},{16,8},{24,16},{28,24},{20,28},{12,20},{4,12},{1,5},{9... | collective-permute-start | bytes 1179656 | tf_op jit(solution)/shard_map/ppermute | solution.py:49
  48.1 15.7 %collective-permute-start.34 = (bf16[256,768]{1,0:T(8,128)(2,1)}, bf16[256,768]{1,0:T(8,128)(2,1)}, u32[]{:S(2)}, u32[]{:S(2)}) collective-permute-start(bf16[256,768]{1,0:T(8,128)(2,1)} %collective-permute-done.32.refs_1_.refs_12_), channel_id=1, source_target_pairs={{0,8},{8,16},{16,24},{24,28},{28,20},{20,12},{12,4},{4,0},{1,9},{9... | collective-permute-start | bytes 1179656 | tf_op jit(solution)/shard_map/ppermute | solution.py:49
  59.8 12.8 %collective-permute-start.14 = (bf16[256,768]{1,0:T(8,128)(2,1)}, bf16[256,768]{1,0:T(8,128)(2,1)S(1)}, u32[]{:S(2)}, u32[]{:S(2)}) collective-permute-start(bf16[256,768]{1,0:T(8,128)(2,1)} %collective-permute-done.12.refs_1_.refs_3_), channel_id=1, source_target_pairs={{0,8},{8,16},{16,24},{24,28},{28,20},{20,12},{12,4},{4,0},{1,9},{9... | collective-permute-start | bytes 1179656 | tf_op jit(solution)/shard_map/ppermute | solution.py:49
  63.8 15.3 %collective-permute-start.15 = (bf16[256,768]{1,0:T(8,128)(2,1)}, bf16[256,768]{1,0:T(8,128)(2,1)S(1)}, u32[]{:S(2)}, u32[]{:S(2)}) collective-permute-start(bf16[256,768]{1,0:T(8,128)(2,1)} %collective-permute-done.13.refs_2_.refs_4_), channel_id=1, source_target_pairs={{0,4},{8,0},{16,8},{24,16},{28,24},{20,28},{12,20},{4,12},{1,5},{9... | collective-permute-start | bytes 1179656 | tf_op jit(solution)/shard_map/ppermute | solution.py:49
  65.2 29.7 %collective-permute-start.5 = (bf16[256,2048]{1,0:T(8,128)(2,1)S(1)}, bf16[256,2048]{1,0:T(8,128)(2,1)S(1)}, u32[]{:S(2)}, u32[]{:S(2)}) collective-permute-start(bf16[256,2048]{1,0:T(8,128)(2,1)S(1)} %collective-permute-done.4.refs_2_.refs_22_), channel_id=1, source_target_pairs={{0,1},{1,0},{2,3},{3,2},{4,5},{5,4},{6,7},{7,6},{8,9},{9,8},{10,11... | collective-permute-start | bytes 3145736 | tf_op jit(solution)/shard_map/ppermute | solution.py:53
  70.6 12.3 %collective-permute-start.36 = (bf16[256,768]{1,0:T(8,128)(2,1)}, bf16[256,768]{1,0:T(8,128)(2,1)S(1)}, u32[]{:S(2)}, u32[]{:S(2)}) collective-permute-start(bf16[256,768]{1,0:T(8,128)(2,1)} %collective-permute-done.34.refs_3_.refs_14_), channel_id=1, source_target_pairs={{0,8},{8,16},{16,24},{24,28},{28,20},{20,12},{12,4},{4,0},{1,9},{9... | collective-permute-start | bytes 1179656 | tf_op jit(solution)/shard_map/ppermute | solution.py:49
  72.2 15.3 %collective-permute-start.37 = (bf16[256,768]{1,0:T(8,128)(2,1)S(1)}, bf16[256,768]{1,0:T(8,128)(2,1)S(1)}, u32[]{:S(2)}, u32[]{:S(2)}) collective-permute-start(bf16[256,768]{1,0:T(8,128)(2,1)S(1)} %collective-permute-done.35.refs_4_.refs_15_), channel_id=1, source_target_pairs={{0,4},{8,0},{16,8},{24,16},{28,24},{20,28},{12,20},{4,12},{1,5},{9... | collective-permute-start | bytes 1179656 | tf_op jit(solution)/shard_map/ppermute | solution.py:49
  72.6 16.2 %collective-permute-start.16 = (bf16[256,768]{1,0:T(8,128)(2,1)S(1)}, bf16[256,768]{1,0:T(8,128)(2,1)S(1)}, u32[]{:S(2)}, u32[]{:S(2)}) collective-permute-start(bf16[256,768]{1,0:T(8,128)(2,1)S(1)} %collective-permute-done.14.refs_3_.refs_5_), channel_id=1, source_target_pairs={{0,8},{8,16},{16,24},{24,28},{28,20},{20,12},{12,4},{4,0},{1,9},{9... | collective-permute-start | bytes 1179656 | tf_op jit(solution)/shard_map/ppermute | solution.py:49
  79.0 14.4 %collective-permute-start.17 = (bf16[256,768]{1,0:T(8,128)(2,1)S(1)}, bf16[256,768]{1,0:T(8,128)(2,1)S(1)}, u32[]{:S(2)}, u32[]{:S(2)}) collective-permute-start(bf16[256,768]{1,0:T(8,128)(2,1)S(1)} %collective-permute-done.15.refs_4_.refs_6_), channel_id=1, source_target_pairs={{0,4},{8,0},{16,8},{24,16},{28,24},{20,28},{12,20},{4,12},{1,5},{9... | collective-permute-start | bytes 1179656 | tf_op jit(solution)/shard_map/ppermute | solution.py:49
  82.9 28.1 %collective-permute-start.20 = (bf16[2,128,512]{2,1,0:T(8,128)(2,1)}, bf16[2,128,512]{2,1,0:T(8,128)(2,1)S(1)}, u32[]{:S(2)}, u32[]{:S(2)}) collective-permute-start(bf16[2,128,512]{2,1,0:T(8,128)(2,1)} %get-tuple-element.246), channel_id=1, source_target_pairs={{0,1},{1,0},{2,3},{3,2},{4,5},{5,4},{6,7},{7,6},{8,9},{9,8},{10,11... | collective-permute-start | bytes 786440 | tf_op jit(solution)/shard_map/ppermute | solution.py:53
  87.4 25.1 %collective-permute-start.21 = (bf16[2,128,512]{2,1,0:T(8,128)(2,1)S(1)}, bf16[2,128,512]{2,1,0:T(8,128)(2,1)S(1)}, u32[]{:S(2)}, u32[]{:S(2)}) collective-permute-start(bf16[2,128,512]{2,1,0:T(8,128)(2,1)S(1)} %get-tuple-element.248), channel_id=1, source_target_pairs={{0,2},{1,3},{2,0},{3,1},{4,6},{5,7},{6,4},{7,5},{8,10},{9,11},{10,... | collective-permute-start | bytes 786440 | tf_op jit(solution)/shard_map/ppermute | solution.py:53
  88.9 24.1 %collective-permute-start.22 = (bf16[2,128,512]{2,1,0:T(8,128)(2,1)S(1)}, bf16[2,128,512]{2,1,0:T(8,128)(2,1)S(1)}, u32[]{:S(2)}, u32[]{:S(2)}) collective-permute-start(bf16[2,128,512]{2,1,0:T(8,128)(2,1)S(1)} %get-tuple-element.245), channel_id=1, source_target_pairs={{0,3},{1,2},{2,1},{3,0},{4,7},{5,6},{6,5},{7,4},{8,11},{9,10},{10,... | collective-permute-start | bytes 786440 | tf_op jit(solution)/shard_map/ppermute | solution.py:53
  93.4 19.6 %collective-permute-start.38 = (bf16[128,768]{1,0:T(8,128)(2,1)S(1)}, bf16[128,768]{1,0:T(8,128)(2,1)S(1)}, u32[]{:S(2)}, u32[]{:S(2)}) collective-permute-start(bf16[128,768]{1,0:T(8,128)(2,1)S(1)} %slice.421), channel_id=1, source_target_pairs={{0,8},{8,16},{16,24},{24,28},{28,20},{20,12},{12,4},{4,0},{1,9},{9... | collective-permute-start | bytes 589832 | tf_op jit(solution)/shard_map/ppermute | solution.py:49
  95.0 18.0 %collective-permute-start.39 = (bf16[128,768]{1,0:T(8,128)(2,1)S(1)}, bf16[128,768]{1,0:T(8,128)(2,1)S(1)}, u32[]{:S(2)}, u32[]{:S(2)}) collective-permute-start(bf16[128,768]{1,0:T(8,128)(2,1)S(1)} %slice.422), channel_id=1, source_target_pairs={{0,4},{8,0},{16,8},{24,16},{28,24},{20,28},{12,20},{4,12},{1,5},{9... | collective-permute-start | bytes 589832 | tf_op jit(solution)/shard_map/ppermute | solution.py:49
  110.9 15.4 %collective-permute-start.18 = (bf16[128,768]{1,0:T(8,128)(2,1)S(1)}, bf16[128,768]{1,0:T(8,128)(2,1)S(1)}, u32[]{:S(2)}, u32[]{:S(2)}) collective-permute-start(bf16[128,768]{1,0:T(8,128)(2,1)S(1)} %slice.407), channel_id=1, source_target_pairs={{0,8},{8,16},{16,24},{24,28},{28,20},{20,12},{12,4},{4,0},{1,9},{9... | collective-permute-start | bytes 589832 | tf_op jit(solution)/shard_map/ppermute | solution.py:49
  112.5 13.8 %collective-permute-start.19 = (bf16[128,768]{1,0:T(8,128)(2,1)S(1)}, bf16[128,768]{1,0:T(8,128)(2,1)S(1)}, u32[]{:S(2)}, u32[]{:S(2)}) collective-permute-start(bf16[128,768]{1,0:T(8,128)(2,1)S(1)} %slice.408), channel_id=1, source_target_pairs={{0,4},{8,0},{16,8},{24,16},{28,24},{20,28},{12,20},{4,12},{1,5},{9... | collective-permute-start | bytes 589832 | tf_op jit(solution)/shard_map/ppermute | solution.py:49
  124.3 18.3 %collective-permute-start.40 = (f32[3,8,256]{2,1,0:T(8,128)}, f32[3,8,256]{2,1,0:T(8,128)S(1)}, u32[]{:S(2)}, u32[]{:S(2)}) collective-permute-start(f32[3,8,256]{2,1,0:T(8,128)} %get-tuple-element.52), channel_id=1, source_target_pairs={{0,4},{4,0},{8,12},{12,8},{16,20},{20,16},{24,28},{28,24},{1,5},{5... | collective-permute-start | bytes 73736 | tf_op jit(solution)/shard_map/ppermute | solution.py:53
  124.8 28.8 %collective-permute-start.43 = (f32[4,8,256]{2,1,0:T(8,128)}, f32[4,8,256]{2,1,0:T(8,128)S(1)}, u32[]{:S(2)}, u32[]{:S(2)}) collective-permute-start(f32[4,8,256]{2,1,0:T(8,128)} %get-tuple-element.53), channel_id=1, source_target_pairs={{4,0},{8,4},{12,8},{16,12},{20,16},{24,20},{28,24},{5,1},{9,5},{13... | collective-permute-start | bytes 98312 | tf_op jit(solution)/shard_map/ppermute | solution.py:534
  140.2 26.0 %collective-permute-start.26 = (f32[4,8,256]{2,1,0:T(8,128)}, f32[4,8,256]{2,1,0:T(8,128)S(1)}, u32[]{:S(2)}, u32[]{:S(2)}) collective-permute-start(f32[4,8,256]{2,1,0:T(8,128)} %get-tuple-element.44), channel_id=1, source_target_pairs={{4,0},{8,4},{12,8},{16,12},{20,16},{24,20},{28,24},{5,1},{9,5},{13... | collective-permute-start | bytes 98312 | tf_op jit(solution)/shard_map/ppermute | solution.py:534
  151.2 14.9 %collective-permute-start.25 = (f32[3,8,256]{2,1,0:T(8,128)S(1)}, f32[3,8,256]{2,1,0:T(8,128)S(1)}, u32[]{:S(2)}, u32[]{:S(2)}) collective-permute-start(f32[3,8,256]{2,1,0:T(8,128)S(1)} %pad_maximum_fusion.8), channel_id=1, source_target_pairs={{0,16},{4,20},{8,24},{12,28},{16,0},{20,4},{24,8},{28,12},{1,17},{... | collective-permute-start | bytes 73736 | tf_op jit(solution)/shard_map/ppermute | solution.py:53
  195.4 15.5 %collective-permute-start.61 = (bf16[128,768]{1,0:T(8,128)(2,1)S(1)}, bf16[128,768]{1,0:T(8,128)(2,1)S(1)}, u32[]{:S(2)}, u32[]{:S(2)}) collective-permute-start(bf16[128,768]{1,0:T(8,128)(2,1)S(1)} %get-tuple-element.257), channel_id=1, source_target_pairs={{0,8},{8,16},{16,24},{24,28},{28,20},{20,12},{12,4},{4,0},{1,9},{9... | collective-permute-start | bytes 589832 | tf_op jit(solution)/shard_map/ppermute | solution.py:49
  200.1 15.4 %collective-permute-start.65 = (bf16[128,768]{1,0:T(8,128)(2,1)S(1)}, bf16[128,768]{1,0:T(8,128)(2,1)S(1)}, u32[]{:S(2)}, u32[]{:S(2)}) collective-permute-start(bf16[128,768]{1,0:T(8,128)(2,1)S(1)} %get-tuple-element.258), channel_id=1, source_target_pairs={{0,4},{8,0},{16,8},{24,16},{28,24},{20,28},{12,20},{4,12},{1,5},{9... | collective-permute-start | bytes 589832 | tf_op jit(solution)/shard_map/ppermute | solution.py:49
  201.3 14.8 %collective-permute-start.52 = (bf16[128,768]{1,0:T(8,128)(2,1)S(1)}, bf16[128,768]{1,0:T(8,128)(2,1)S(1)}, u32[]{:S(2)}, u32[]{:S(2)}) collective-permute-start(bf16[128,768]{1,0:T(8,128)(2,1)S(1)} %get-tuple-element.259), channel_id=1, source_target_pairs={{0,8},{8,16},{16,24},{24,28},{28,20},{20,12},{12,4},{4,0},{1,9},{9... | collective-permute-start | bytes 589832 | tf_op jit(solution)/shard_map/ppermute | solution.py:49
  203.2 14.2 %collective-permute-start.56 = (bf16[128,768]{1,0:T(8,128)(2,1)S(1)}, bf16[128,768]{1,0:T(8,128)(2,1)S(1)}, u32[]{:S(2)}, u32[]{:S(2)}) collective-permute-start(bf16[128,768]{1,0:T(8,128)(2,1)S(1)} %get-tuple-element.260), channel_id=1, source_target_pairs={{0,4},{8,0},{16,8},{24,16},{28,24},{20,28},{12,20},{4,12},{1,5},{9... | collective-permute-start | bytes 589832 | tf_op jit(solution)/shard_map/ppermute | solution.py:49
  210.8 66.4 %collective-permute-start.50 = (bf16[256,2048]{1,0:T(8,128)(2,1)S(1)}, bf16[256,2048]{1,0:T(8,128)(2,1)S(1)}, u32[]{:S(2)}, u32[]{:S(2)}) collective-permute-start(bf16[256,2048]{1,0:T(8,128)(2,1)S(1)} %copy-done.51), channel_id=1, source_target_pairs={{0,1},{1,0},{2,3},{3,2},{4,5},{5,4},{6,7},{7,6},{8,9},{9,8},{10,11... | collective-permute-start | bytes 3145736 | tf_op jit(solution)/shard_map/ppermute | solution.py:53
  215.4 103.0 %collective-permute-start.49 = (bf16[256,2048]{1,0:T(8,128)(2,1)S(1)}, bf16[256,2048]{1,0:T(8,128)(2,1)S(1)}, u32[]{:S(2)}, u32[]{:S(2)}) collective-permute-start(bf16[256,2048]{1,0:T(8,128)(2,1)S(1)} %copy-done.50), channel_id=1, source_target_pairs={{0,1},{1,0},{2,3},{3,2},{4,5},{5,4},{6,7},{7,6},{8,9},{9,8},{10,11... | collective-permute-start | bytes 3145736 | tf_op jit(solution)/shard_map/ppermute | solution.py:53
  243.9 12.1 %collective-permute-start.53 = (bf16[256,768]{1,0:T(8,128)(2,1)S(1)}, bf16[256,768]{1,0:T(8,128)(2,1)S(1)}, u32[]{:S(2)}, u32[]{:S(2)}) collective-permute-start(bf16[256,768]{1,0:T(8,128)(2,1)S(1)} %pad_maximum_fusion.2), channel_id=1, source_target_pairs={{0,8},{8,16},{16,24},{24,28},{28,20},{20,12},{12,4},{4,0},{1,9},{9... | collective-permute-start | bytes 1179656 | tf_op jit(solution)/shard_map/ppermute | solution.py:49
  245.4 12.5 %collective-permute-start.57 = (bf16[256,768]{1,0:T(8,128)(2,1)S(1)}, bf16[256,768]{1,0:T(8,128)(2,1)S(1)}, u32[]{:S(2)}, u32[]{:S(2)}) collective-permute-start(bf16[256,768]{1,0:T(8,128)(2,1)S(1)} %pad_maximum_fusion.3), channel_id=1, source_target_pairs={{0,4},{8,0},{16,8},{24,16},{28,24},{20,28},{12,20},{4,12},{1,5},{9... | collective-permute-start | bytes 1179656 | tf_op jit(solution)/shard_map/ppermute | solution.py:49
  248.8 15.5 %collective-permute-start.63 = (bf16[256,768]{1,0:T(8,128)(2,1)S(1)}, bf16[256,768]{1,0:T(8,128)(2,1)S(1)}, u32[]{:S(2)}, u32[]{:S(2)}) collective-permute-start(bf16[256,768]{1,0:T(8,128)(2,1)S(1)} %fusion.7), channel_id=1, source_target_pairs={{0,8},{8,16},{16,24},{24,28},{28,20},{20,12},{12,4},{4,0},{1,9},{9... | collective-permute-start | bytes 1179656 | tf_op jit(solution)/shard_map/ppermute | solution.py:49
  255.9 12.1 %collective-permute-start.67 = (bf16[256,768]{1,0:T(8,128)(2,1)S(1)}, bf16[256,768]{1,0:T(8,128)(2,1)S(1)}, u32[]{:S(2)}, u32[]{:S(2)}) collective-permute-start(bf16[256,768]{1,0:T(8,128)(2,1)S(1)} %fusion.9), channel_id=1, source_target_pairs={{0,4},{8,0},{16,8},{24,16},{28,24},{20,28},{12,20},{4,12},{1,5},{9... | collective-permute-start | bytes 1179656 | tf_op jit(solution)/shard_map/ppermute | solution.py:49
  257.9 14.9 %collective-permute-start.54 = (bf16[256,768]{1,0:T(8,128)(2,1)S(1)}, bf16[256,768]{1,0:T(8,128)(2,1)S(1)}, u32[]{:S(2)}, u32[]{:S(2)}) collective-permute-start(bf16[256,768]{1,0:T(8,128)(2,1)S(1)} %fusion.3), channel_id=1, source_target_pairs={{0,8},{8,16},{16,24},{24,28},{28,20},{20,12},{12,4},{4,0},{1,9},{9... | collective-permute-start | bytes 1179656 | tf_op jit(solution)/shard_map/ppermute | solution.py:49
  264.4 12.1 %collective-permute-start.58 = (bf16[256,768]{1,0:T(8,128)(2,1)S(1)}, bf16[256,768]{1,0:T(8,128)(2,1)S(1)}, u32[]{:S(2)}, u32[]{:S(2)}) collective-permute-start(bf16[256,768]{1,0:T(8,128)(2,1)S(1)} %fusion.5), channel_id=1, source_target_pairs={{0,4},{8,0},{16,8},{24,16},{28,24},{20,28},{12,20},{4,12},{1,5},{9... | collective-permute-start | bytes 1179656 | tf_op jit(solution)/shard_map/ppermute | solution.py:49
  268.0 25.8 %collective-permute-start.64 = (bf16[256,768]{1,0:T(8,128)(2,1)S(1)}, bf16[256,768]{1,0:T(8,128)(2,1)S(1)}, u32[]{:S(2)}, u32[]{:S(2)}) collective-permute-start(bf16[256,768]{1,0:T(8,128)(2,1)S(1)} %fusion.6), channel_id=1, source_target_pairs={{0,8},{8,16},{16,24},{24,28},{28,20},{20,12},{12,4},{4,0},{1,9},{9... | collective-permute-start | bytes 1179656 | tf_op jit(solution)/shard_map/ppermute | solution.py:49
  272.8 21.0 %collective-permute-start.68 = (bf16[256,768]{1,0:T(8,128)(2,1)S(1)}, bf16[256,768]{1,0:T(8,128)(2,1)S(1)}, u32[]{:S(2)}, u32[]{:S(2)}) collective-permute-start(bf16[256,768]{1,0:T(8,128)(2,1)S(1)} %fusion.8), channel_id=1, source_target_pairs={{0,4},{8,0},{16,8},{24,16},{28,24},{20,28},{12,20},{4,12},{1,5},{9... | collective-permute-start | bytes 1179656 | tf_op jit(solution)/shard_map/ppermute | solution.py:49
  277.3 14.4 %collective-permute-start.59 = (bf16[256,768]{1,0:T(8,128)(2,1)S(1)}, bf16[256,768]{1,0:T(8,128)(2,1)S(1)}, u32[]{:S(2)}, u32[]{:S(2)}) collective-permute-start(bf16[256,768]{1,0:T(8,128)(2,1)S(1)} %fusion.4), channel_id=1, source_target_pairs={{0,4},{8,0},{16,8},{24,16},{28,24},{20,28},{12,20},{4,12},{1,5},{9... | collective-permute-start | bytes 1179656 | tf_op jit(solution)/shard_map/ppermute | solution.py:49
  288.1 30.4 %collective-permute-start.51 = (bf16[256,2048]{1,0:T(8,128)(2,1)S(1)}, bf16[256,2048]{1,0:T(8,128)(2,1)S(1)}, u32[]{:S(2)}, u32[]{:S(2)}) collective-permute-start(bf16[256,2048]{1,0:T(8,128)(2,1)S(1)} %add_convert_fusion.1), channel_id=1, source_target_pairs={{0,2},{1,3},{2,0},{3,1},{4,6},{5,7},{6,4},{7,5},{8,10},{9,11},{10,... | collective-permute-start | bytes 3145736 | tf_op jit(solution)/shard_map/ppermute | solution.py:53
  292.3 24.5 %collective-permute-start.60 = (bf16[256,256]{1,0:T(8,128)(2,1)S(1)}, bf16[256,256]{1,0:T(8,128)(2,1)S(1)}, u32[]{:S(2)}, u32[]{:S(2)}) collective-permute-start(bf16[256,256]{1,0:T(8,128)(2,1)S(1)} %get-tuple-element.252), channel_id=1, source_target_pairs={{0,2},{1,3},{2,0},{3,1},{4,6},{5,7},{6,4},{7,5},{8,10},{9,11},{10,... | collective-permute-start | bytes 393224 | tf_op jit(solution)/shard_map/ppermute | solution.py:53
  294.4 23.8 %collective-permute-start.69 = (bf16[256,256]{1,0:T(8,128)(2,1)S(1)}, bf16[256,256]{1,0:T(8,128)(2,1)S(1)}, u32[]{:S(2)}, u32[]{:S(2)}) collective-permute-start(bf16[256,256]{1,0:T(8,128)(2,1)S(1)} %get-tuple-element.250), channel_id=1, source_target_pairs={{0,2},{1,3},{2,0},{3,1},{4,6},{5,7},{6,4},{7,5},{8,10},{9,11},{10,... | collective-permute-start | bytes 393224 | tf_op jit(solution)/shard_map/ppermute | solution.py:53
  295.2 23.1 %collective-permute-start.70 = (bf16[256,256]{1,0:T(8,128)(2,1)S(1)}, bf16[256,256]{1,0:T(8,128)(2,1)S(1)}, u32[]{:S(2)}, u32[]{:S(2)}) collective-permute-start(bf16[256,256]{1,0:T(8,128)(2,1)S(1)} %get-tuple-element.251), channel_id=1, source_target_pairs={{0,1},{1,0},{2,3},{3,2},{4,5},{5,4},{6,7},{7,6},{8,9},{9,8},{10,11... | collective-permute-start | bytes 393224 | tf_op jit(solution)/shard_map/ppermute | solution.py:53
  (95 other events, 1102.2 us)

commit v2 on v1

v2 whole, which is shorter than its diff:
```python
import functools

import jax
import jax.numpy as jnp
from jax import lax
from jax.experimental import pallas as pl
from jax.experimental.pallas import tpu as pltpu
from jax.sharding import PartitionSpec as P

epsilon = 1e-05
f32 = jnp.float32
bf16 = jnp.bfloat16
GROUPS = 1
PAD = 8
PINNED = True
MIB = 1024 * 1024


def vmem_spec():
    return pl.BlockSpec(memory_space=pltpu.VMEM)


def smem_spec():
    return pl.BlockSpec(memory_space=pltpu.SMEM)


def call(kernel, out_shape, operands, scratch=(), scalars=0, room=6):
    specs = [smem_spec()] * scalars + [vmem_spec()] * (len(operands) - scalars)
    if PINNED:
        out_shape = jax.tree.map(lambda out: pltpu.VMEM(out.shape, out.dtype), out_shape)
        operands = operands[:scalars] + [
            pltpu.with_memory_space_constraint(x, pltpu.VMEM) for x in operands[scalars:]
        ]
    return pl.pallas_call(
        kernel,
        out_shape=out_shape,
        in_specs=specs,
        out_specs=jax.tree.map(lambda _: vmem_spec(), out_shape),
        scratch_shapes=list(scratch),
        compiler_params=pltpu.CompilerParams(vmem_limit_bytes=room * MIB),
        cost_estimate=pl.CostEstimate(flops=0, bytes_accessed=0, transcendentals=0),
    )(*operands)


def at_spot(spot, count):
    if count != 8:
        return spot
    return spot * 2 if isinstance(spot, int) and spot < 4 else (
        15 - spot * 2 if isinstance(spot, int) else jnp.where(spot < 4, spot * 2, 15 - spot * 2)
    )


def spot_of(index, count):
    if count != 8:
        return index
    return jnp.where(index % 2 == 0, index // 2, (15 - index) // 2)


def wrapped(value, count):
    value = jnp.where(value >= count, value - count, value)
    return jnp.where(value < 0, value + count, value)


def along_ring(value, steps):
    count = lax.axis_size("seq")
    order = [at_spot(i, count) for i in range(count)]
    return lax.ppermute(value, "seq", [(order[i], order[(i + steps) % count]) for i in range(count)])


def swapped(value, axis, bit):
    return lax.ppermute(value, axis, [(i, i ^ bit) for i in range(lax.axis_size(axis))])


def norm_kernel(parts, rows, tail, units, place, *refs):
    flat = sum(len(slot) for slot in parts)
    pieces = refs[:flat]
    gain, bias, normed, means, scales, picked = refs[flat:]
    gain_row, bias_row = gain[...], bias[...]
    lanes = pl.ds(pl.multiple_of(place[2], units), units)
    at = 0
    for k, slot in enumerate(parts):
        for low, high in slot:
            x = pieces[at][...].astype(f32)
            mean = jnp.mean(x, axis=1, keepdims=True)
            centered = x - mean
            scale = lax.rsqrt(jnp.mean(centered * centered, axis=1, keepdims=True) + epsilon)
            base = k * (rows + tail)
            normed[base + low : base + high, :] = (centered * scale * gain_row + bias_row).astype(bf16)
            count = min(high, rows) - low
            here = slice(k * rows + low, k * rows + low + count)
            means[here, :] = jnp.broadcast_to(mean[:count], (count, 128))
            scales[here, :] = jnp.broadcast_to(scale[:count], (count, 128))
            picked[here, :] = pieces[at][:count, lanes]
            at += 1


def strided(ref, row, seqs, stride):
    tiles = [ref[lane, pl.ds(row, seqs, stride=stride), :] for lane in range(ref.shape[0])]
    return jnp.concatenate(tiles, axis=1)


def put_strided(ref, row, seqs, stride, value):
    for lane in range(ref.shape[0]):
        ref[lane, pl.ds(row, seqs, stride=stride), :] = value[:, lane * 128 : (lane + 1) * 128]


def put_rows(ref, row, count, value):
    for lane in range(ref.shape[0]):
        ref[lane, pl.ds(row, count), :] = value[:, lane * 128 : (lane + 1) * 128]


def get_rows(ref, row, count):
    return jnp.concatenate([ref[lane, pl.ds(row, count), :] for lane in range(ref.shape[0])], axis=1)


def message_kernel(slots, units, tail, where, grads, start, lengths, *outs):
    rows, per = grads.shape[0], start.shape[0]
    for k in range(slots):
        lanes = pl.ds(pl.multiple_of(where[k], units), units)
        outs[k][:rows, :] = grads[:, lanes]
        left = start[:, lanes]
        extra = []
        for _ in range(3):
            part = left.astype(bf16).astype(f32)
            extra.append(part)
            left = left - part
        counts = lengths[...]
        high = counts // 256
        extra += [
            jnp.broadcast_to(n.astype(f32)[:, :1], (per, units)) for n in (high, counts - high * 256)
        ]
        extra.append(jnp.zeros((tail - 5 * per, units), f32))
        outs[k][rows:, :] = jnp.concatenate(extra, axis=0).astype(bf16)


def merge_kernel(mine_up, mine_down, up, down, out_up, out_down):
    count, total = up.shape[0], mine_up.shape[0]
    out_up[:count, :] = (mine_up[:count, :] + up[...].astype(f32)).astype(bf16)
    out_down[total - count :, :] = (mine_down[total - count :, :] + down[...].astype(f32)).astype(bf16)
    if count < total:
        out_up[count:, :] = mine_up[count:, :].astype(bf16)
        out_down[: total - count, :] = mine_down[: total - count, :].astype(bf16)


def spread_rows(dims, part, g_in, picked, gs, xs):
    seqs, span, width, slots = dims
    per, lanes = seqs // slots, slice(part * width, (part + 1) * width)
    for n in range(seqs):
        to = n * (span + PAD) + PAD
        put_rows(gs, to, span, g_in[n // per][n % per * span : n % per * span + span, lanes].astype(f32))
        put_rows(xs, to, span, picked[n * span : (n + 1) * span, lanes].astype(f32))


def begin_kernel(blocks, depth, rows, count, sources, normed, *refs):
    total = refs[blocks]
    for k in range(count):
        here = slice(k * rows, (k + 1) * rows)
        sum_ = None
        for b in range(blocks):
            at = pl.multiple_of(sources[b] * depth, depth)
            term = jnp.dot(
                normed[here, pl.ds(at, depth)], refs[b][...], preferred_element_type=f32
            )
            sum_ = term if sum_ is None else sum_ + term
        total[here, :] = sum_


def first_kernel(dims, part, sources, place, normed, start, lens, vecs, picked, *refs):
    seqs, span, width, slots, blocks, depth, split, tail = dims
    stride = span + PAD
    late = 2 if split else 1
    w, begun = refs[:late], refs[late]
    g_in = refs[late + 1 : late + 1 + slots]
    cand, forg, rese, maps, planes, gs, xs = refs[late + 1 + slots :]
    per = seqs // slots
    spread_rows((seqs, span, width, slots), part, g_in, picked, gs, xs)

    rows = per * span
    ext = rows + tail
    lead = w[len(w) - late][...] if late == 1 else jnp.concatenate([w[-2][...], w[-1][...]], axis=0)
    at = pl.multiple_of(sources[blocks - 1] * depth, depth)
    for k in range(slots):
        total = begun[k * ext : (k + 1) * ext, :] + jnp.dot(
            normed[k * ext : (k + 1) * ext, pl.ds(at, depth)], lead, preferred_element_type=f32
        )
        total = total.astype(bf16).astype(f32)
        for j in range(per):
            n = k * per + j
            put_rows(cand, n * stride + PAD - 8, 8, jnp.broadcast_to(total[rows + j : rows + j + 1, :width], (8, width)))
            for ref, gate in ((cand, 0), (forg, 1), (rese, 2)):
                here = total[j * span : (j + 1) * span, gate * width : (gate + 1) * width]
                put_rows(ref, n * stride + PAD, span, here)
    last = strided(cand, PAD - 1, seqs, stride)
    before = jnp.where(place[1] == 0, start[...], last)
    put_strided(cand, PAD - 1, seqs, stride, before)
    peep_f, peep_r, bias_f, bias_r = (vecs[i : i + 1, :] for i in range(4))
    ends = lens[...]
    base = place[0]

    def turn(t, carry):
        previous, decays, injects, handed = carry
        row = t + PAD
        c = strided(cand, row, seqs, stride)
        f = jax.nn.sigmoid(strided(forg, row, seqs, stride) + peep_f * previous + bias_f)
        r = jax.nn.sigmoid(strided(rese, row, seqs, stride) + peep_r * previous + bias_r)
        put_strided(forg, row, seqs, stride, f)
        put_strided(rese, row, seqs, stride, r)
        live = base + t < ends
        d = jnp.where(live, f, 1.0)
        inject = jnp.where(live, (1.0 - f) * c, 0.0)
        pulled = jnp.where(live, r * strided(gs, row, seqs, stride), 0.0)
        decays = decays * d
        return c, decays, d * injects + inject, handed + decays * pulled

    one, zero = jnp.ones((seqs, width), f32), jnp.zeros((seqs, width), f32)
    _, decays, injects, handed = lax.fori_loop(0, span, turn, (before, one, zero, zero), unroll=4)
    maps[0], maps[1], maps[2] = decays, injects, handed
    c, f, r, g, x = (strided(ref, PAD, seqs, stride) for ref in (cand, forg, rese, gs, xs))
    live = base < ends
    d = jnp.where(live, f, 1.0)
    inject = jnp.where(live, (1.0 - f) * c, 0.0)
    via_adjoint = jnp.where(live, (1.0 - f) * peep_f, 0.0)
    via_state = jnp.where(live, r * (1.0 - r) * g * peep_r, 0.0)
    planes[0], planes[1] = via_adjoint, via_adjoint * c
    planes[2], planes[3] = via_state * d, via_state * (inject - x)


def second_kernel(
    dims, part, place, lens, vecs, earlier, later, start, linked, cand, forg, rese, picked, *refs
):
    seqs, span, width, slots, tail = dims
    stride = span + PAD
    g_in = refs[:slots]
    grads, moved = refs[slots], refs[slots + 1 : 2 * slots + 1]
    final, sums = refs[2 * slots + 1 : 2 * slots + 3]
    gs, xs, states, outs, gcs, fts, rts = refs[2 * slots + 3 :]
    per = seqs // slots
    spread_rows((seqs, span, width, slots), part, g_in, picked, gs, xs)
    peep_f, peep_r = vecs[0:1, :], vecs[1:2, :]
    ends = lens[...]
    base = place[0]
    begin, after = earlier[0] * start[...] + earlier[1], later[2]
    put_strided(states, PAD - 1, seqs, stride, begin)

    def forward(t, state):
        row = t + PAD
        c, f, r, x = (strided(ref, row, seqs, stride) for ref in (cand, forg, rese, xs))
        live = base + t < ends
        state = jnp.where(live, f * state + (1.0 - f) * c, state)
        put_strided(states, row, seqs, stride, state)
        put_strided(outs, row, seqs, stride, jnp.where(live, r * state + (1.0 - r) * x, x))
        return state

    end = lax.fori_loop(0, span, forward, begin, unroll=4)
    final[...] = later[0] * end + later[1]
    upcoming = end * (linked[0] * after + linked[2]) - linked[1] * after + linked[3]

    def backward(i, carry):
        reached, upcoming, pf, pr, bf, br = carry
        row = span - 1 - i + PAD
        c, f, r, x, g = (strided(ref, row, seqs, stride) for ref in (cand, forg, rese, xs, gs))
        state = strided(states, row, seqs, stride)
        prior = strided(states, row - 1, seqs, stride)
        previous = strided(cand, row - 1, seqs, stride)
        live = base + (span - 1 - i) < ends
        zero = jnp.zeros_like(f)
        adjoint = jnp.where(live, r * g, 0.0) + reached
        kept = jnp.where(live, (1.0 - f) * adjoint, zero)
        ft = f * kept * (prior - c)
        rt = jnp.where(live, r * (1.0 - r) * g * (state - x), zero)
        put_strided(gcs, row, seqs, stride, kept + upcoming)
        put_strided(fts, row, seqs, stride, ft)
        put_strided(rts, row, seqs, stride, rt)
        put_strided(gs, row, seqs, stride, jnp.where(live, (1.0 - r) * g, g))
        reached = jnp.where(live, f * adjoint, adjoint)
        return (
            reached,
            ft * peep_f + rt * peep_r,
            pf + ft * previous,
            pr + rt * previous,
            bf + ft,
            br + rt,
        )

    zero = jnp.zeros((seqs, width), f32)
    done = lax.fori_loop(0, span, backward, (after, upcoming, zero, zero, zero, zero), unroll=4)
    sums[...] = jnp.zeros_like(sums)
    for i in range(4):
        sums[i : i + 1, :] = jnp.sum(done[2 + i], axis=0, keepdims=True)
    for n in range(seqs):
        at = n * stride + PAD
        k, j = n // per, n % per
        to = k * (per * span + tail) + j * span
        for gate, ref in enumerate((gcs, fts, rts)):
            lanes = slice(gate * width, (gate + 1) * width)
            grads[to : to + span, lanes] = get_rows(ref, at, span).astype(bf16)
        if j == per - 1:
            grads[to + span : to + span + tail, :] = jnp.zeros((tail, 3 * width), bf16)
        moved[k][0, j] = get_rows(outs, at, span).astype(bf16)
        moved[k][1, j] = get_rows(gs, at, span).astype(bf16)


def partial_kernel(count, depth, owners, normed, grads, *outs):
    for i in range(count):
        lanes = pl.ds(pl.multiple_of(owners[i] * depth, min(depth, 128)), depth)
        outs[i][...] = lax.dot_general(
            normed[:, lanes], grads[...], (((0,), (0,)), ((), ())), preferred_element_type=f32
        ).astype(outs[i].dtype)


def token_kernel(dims, parts, sources, *refs):
    slots, blocks, depth, rows, groups, split, tail = dims
    flat = sum(len(slot) for slot in parts)
    n_w = blocks + (1 if split else 0)
    grads = refs[:groups]
    w = [refs[groups + a * n_w : groups + (a + 1) * n_w] for a in range(groups)]
    at0 = groups + groups * n_w
    pieces = refs[at0 : at0 + flat]
    means, scales, own = refs[at0 + flat : at0 + flat + 3]
    others = refs[at0 + flat + 3 : at0 + flat + slots + 2]
    sums = refs[at0 + flat + slots + 2]
    first_of = [sum(len(slot) for slot in parts[:k]) for k in range(slots)]

    def raw(k, lanes):
        found = [
            pieces[first_of[k] + i][: min(high, rows) - low, lanes]
            for i, (low, high) in enumerate(parts[k])
        ]
        return found[0] if len(found) == 1 else jnp.concatenate(found, axis=0)

    def block(a, b):
        if split and b == blocks - 1:
            return jnp.concatenate([w[a][b][...], w[a][b + 1][...]], axis=0)
        return w[a][b][...]

    sums[...] = jnp.zeros_like(sums)
    for b in range(blocks):
        at = pl.multiple_of(sources[b] * depth, depth)
        lanes = pl.ds(at, depth)
        gain_sum, bias_sum = jnp.zeros((8, depth), f32), jnp.zeros((8, depth), f32)
        weights = [block(a, b) for a in range(groups)]
        for k in range(slots):
            here = pl.ds(k * rows, rows)
            total = None
            for a in range(groups):
                term = lax.dot_general(
                    grads[a][k * (rows + tail) : k * (rows + tail) + rows, :],
                    weights[a],
                    (((1,), (1,)), ((), ())),
                    preferred_element_type=f32,
                )
                total = term if total is None else total + term
            copies = depth // 128
            mean = jnp.concatenate([means[here, :]] * copies, axis=1)
            scale = jnp.concatenate([scales[here, :]] * copies, axis=1)
            scaled = (raw(k, lanes).astype(f32) - mean) * scale
            gain_sum += jnp.sum((total * scaled).reshape(rows // 8, 8, depth), axis=0)
            bias_sum += jnp.sum(total.reshape(rows // 8, 8, depth), axis=0)
            if k == 0:
                own[:, lanes] = total
            else:
                others[k - 1][:, lanes] = total.astype(bf16)
        sums[0:1, lanes] = jnp.sum(gain_sum, axis=0, keepdims=True)
        sums[1:2, lanes] = jnp.sum(bias_sum, axis=0, keepdims=True)


def chosen(options, index):
    result = options[0]
    for i in range(1, len(options)):
        result = jnp.where(index == i, options[i], result)
    return result


def gates_of_units(weights, width, lane0, lanes, take):
    count, here = lax.axis_size("stream"), lax.axis_index("stream")
    if count == 4:
        pieces = [weights[:, s * width + lane0 : s * width + lane0 + lanes] for s in range(3)]
        even = here % 2 == 0
        own = jnp.where(even, pieces[0], pieces[2])
        near = swapped(take(pieces[1]), "stream", 1)
        far = swapped(take(jnp.where(even, pieces[2], pieces[0])), "stream", 2)
        got = [own, near, far]
        order = ((0, 1, 2), (1, 0, 2), (2, 0, 1), (2, 1, 0))
        gates = [chosen([got[order[d][gate]] for d in range(4)], here) for gate in range(3)]
        return jnp.concatenate(gates, axis=1), (near, far)
    everything = lax.all_gather(weights, "stream", axis=1, tiled=True)
    model = count * width
    gates = [
        lax.dynamic_slice_in_dim(everything, gate * model + here * width + lane0, lanes, 1)
        for gate in range(3)
    ]
    return jnp.concatenate(gates, axis=1), ()


def columns_as_stored(gates):
    count, here = lax.axis_size("stream"), lax.axis_index("stream")
    if count == 4:
        own = chosen([gates[0], gates[1], gates[1], gates[2]], here)
        near = swapped(
            chosen([gates[1], gates[0], gates[2], gates[1]], here).astype(bf16), "stream", 1
        ).astype(f32)
        far = swapped(
            chosen([gates[2], gates[2], gates[0], gates[0]], here).astype(bf16), "stream", 2
        ).astype(f32)
        even = here % 2 == 0
        return [jnp.where(even, own, far), near, jnp.where(even, far, own)]
    everything = lax.all_gather(jnp.stack(gates).astype(bf16), "stream", axis=1).astype(f32)
    flat = everything.reshape((3 * count,) + gates[0].shape)
    return [lax.dynamic_index_in_dim(flat, 3 * here + s, 0, keepdims=False) for s in range(3)]


def first_maps(maps):
    one, zero = jnp.ones_like(maps[0]), jnp.zeros_like(maps[0])
    return (maps[0], maps[1], maps[2]), (one, zero), (one, zero, zero)


def joined_maps(known, other, bit):
    (decay, inject, handed), before, later = known
    theirs = (other[0], other[1], other[2])
    first = (lax.axis_index("seq") & bit) == 0
    before_new = (theirs[0] * before[0], before[0] * theirs[1] + before[1])
    later_new = (
        later[0] * theirs[0],
        theirs[0] * later[1] + theirs[1],
        later[2] + later[0] * theirs[2],
    )
    before = tuple(jnp.where(first, a, b) for a, b in zip(before, before_new))
    later = tuple(jnp.where(first, b, a) for a, b in zip(later, later_new))
    inject_new = jnp.where(first, theirs[0] * inject + theirs[1], decay * theirs[1] + inject)
    handed_new = jnp.where(first, handed + decay * theirs[2], theirs[2] + theirs[0] * handed)
    return (decay * theirs[0], inject_new, handed_new), before, later


class Rounds:
    def __init__(self):
        self.before, self.given = [], []

    def take(self, value):
        if not self.before:
            return value
        return lax.optimization_barrier((value, self.before))[0]

    def give(self, *values):
        self.given += values

    def turn(self):
        self.before, self.given = self.given, []


def local(
    inputs,
    start_state,
    lengths,
    weights,
    peep_forget,
    peep_reset,
    bias_forget,
    bias_reset,
    norm_gain,
    norm_bias,
    out_grad,
):
    per, span, model = inputs.shape
    n_seq, slots = lax.axis_size("seq"), lax.axis_size("stream")
    at_seq, at_stream = lax.axis_index("seq"), lax.axis_index("stream")
    seqs = per * slots
    units = model // slots
    width = units // GROUPS
    depth = model // n_seq
    rows = per * span
    tokens = seqs * span
    tail = 16
    half = depth // 2
    spot = spot_of(at_seq, n_seq)
    far = n_seq // 2
    steps = [0]
    for k in range(1, far):
        steps += [-k, k]
    steps.append(far)

    def owner(distance):
        return at_spot(wrapped(spot + distance, n_seq), n_seq)

    sources = jnp.stack([owner(distance) for distance in steps]).astype(jnp.int32)
    place = jnp.stack([at_seq * span, at_seq, at_stream * units]).astype(jnp.int32)
    bits = [1 << b for b in range(slots.bit_length() - 1)]

    def owner_units(array, k):
        return lax.dynamic_slice_in_dim(array, (at_stream ^ k) * units, units, array.ndim - 1)

    vectors = jnp.stack([peep_forget, peep_reset, bias_forget, bias_reset])
    vectors = lax.dynamic_slice_in_dim(vectors, at_stream * units, units, 1)
    vectors = jnp.concatenate([vectors, jnp.zeros_like(vectors)], axis=0)
    group_vectors = [vectors[:, a * width : (a + 1) * width] for a in range(GROUPS)]
    gain_row, bias_row = norm_gain.reshape(1, model), norm_bias.reshape(1, model)
    tall = seqs * (span + PAD)
    field = jax.ShapeDtypeStruct((width // 128, tall, 128), f32)
    space = pltpu.VMEM((width // 128, tall, 128), f32)

    rounds = Rounds()
    take, give = rounds.take, rounds.give
    box = {}

    up, down, blocks = [None] * GROUPS, [None] * GROUPS, [None] * GROUPS

    def gather(a, step):
        if step == 1:
            up[a] = down[a] = take(box["dealt", a])
            blocks[a] = [up[a]]
        if step == far:
            up[a], down[a] = up[a][:half], down[a][half:]
        up[a], down[a] = along_ring(take(up[a]), 1), along_ring(take(down[a]), -1)
        blocks[a] += [up[a], down[a]]
        give(up[a], down[a])

    def partials(a, distances, kind):
        places = [owner(distance) for distance in distances]
        grads = take(box["grads", a])
        if depth % 128:
            return [
                lax.dot_general(
                    lax.dynamic_slice_in_dim(box["normed"], place * depth, depth, 1),
                    grads,
                    (((0,), (0,)), ((), ())),
                    preferred_element_type=f32,
                ).astype(kind)
                for place in places
            ]
        return call(
            functools.partial(partial_kernel, len(places), depth),
            [jax.ShapeDtypeStruct((depth, 3 * width), kind)] * len(places),
            [jnp.stack(places).astype(jnp.int32), box["normed"], grads],
            scalars=1,
        )

    def scatter(a, step):
        if step == 1:
            farthest = take(box["farthest", a])
            to_up, to_down = farthest[:half], farthest[half:]
        else:
            to_up, to_down = call(
                merge_kernel,
                [jax.ShapeDtypeStruct((depth, 3 * width), bf16)] * 2,
                [*box["mine", a], up[a], down[a]],
            )
        up[a], down[a] = along_ring(take(to_up), 1), along_ring(take(to_down), -1)
        give(up[a], down[a])
        if step < far:
            box["mine", a] = partials(a, (far - step, step - far), f32)
            give(*box["mine", a])
        else:
            box["own", a] = partials(a, (0,), f32)[0]
            give(box["own", a])

    def deal(a):
        box["dealt", a], came = gates_of_units(weights, units, a * width, width, take)
        give(*came)

    in_parts = slots == 4
    whole_part = [(0, rows + tail)]
    cuts = [(0, rows // 2), (rows // 2, rows + tail)]
    parts = [whole_part, whole_part, cuts, cuts] if in_parts else [whole_part] * slots
    tokens_of = [[None] * len(slot) for slot in parts]
    flat_inputs = inputs.reshape(rows, model)

    def ahead_tokens():
        box["ahead"] = lax.ppermute(
            take(inputs[:, -1, :]), "seq", [(i, i + 1) for i in range(n_seq - 1)]
        )
        give(box["ahead"])

    def own_tokens():
        tokens_of[0][0] = jnp.concatenate(
            [flat_inputs, box["ahead"], jnp.zeros((tail - per, model), bf16)], axis=0
        )

    def everyones_tokens():
        ahead_tokens()
        own_tokens()
        for bit in reversed(bits):
            for k in range(slots):
                if tokens_of[k][0] is not None and tokens_of[k ^ bit][0] is None:
                    tokens_of[k ^ bit][0] = swapped(tokens_of[k][0], "stream", bit)

    def near_tokens():
        own_tokens()
        tokens_of[1][0] = swapped(take(tokens_of[0][0]), "stream", 1)
        give(tokens_of[1][0])

    def far_tokens(i):
        low, high = cuts[i]
        source = flat_inputs[low:high] if high <= rows else tokens_of[0][0][low:high]
        tokens_of[2][i] = swapped(take(source), "stream", 2)
        give(tokens_of[2][i])

    def passed_tokens(i):
        tokens_of[3][i] = swapped(take(tokens_of[2][i]), "stream", 1)
        give(tokens_of[3][i])

    def messages():
        where = jnp.stack([(at_stream ^ k) * units for k in range(slots)]).astype(jnp.int32)
        box["messages"] = call(
            functools.partial(message_kernel, slots, units, tail),
            [jax.ShapeDtypeStruct((rows + tail, units), bf16)] * slots,
            [
                where,
                take(out_grad.reshape(rows, model)),
                start_state,
                jnp.broadcast_to(lengths[:, None], (per, 128)),
            ],
            scalars=1,
        )

    def out_grads():
        for k in range(slots):
            box["g", k] = box["messages"][k]
            if k:
                box["g", k] = swapped(take(box["g", k]), "stream", k)
                give(box["g", k])

    def normalise():
        flat = [piece for slot in tokens_of for piece in slot]
        box["normed"], box["means"], box["scales"], box["picked"] = call(
            functools.partial(norm_kernel, parts, rows, tail, units),
            [
                jax.ShapeDtypeStruct((slots * (rows + tail), model), bf16),
                jax.ShapeDtypeStruct((tokens, 128), f32),
                jax.ShapeDtypeStruct((tokens, 128), f32),
                jax.ShapeDtypeStruct((tokens, units), bf16),
            ],
            [place, *flat, take(gain_row), bias_row],
            scalars=1,
        )
        give(box["normed"])

    def in_order(a):
        if depth % 128 == 0:
            return blocks[a], sources, n_seq, depth, True
        wide = 2 * 128
        if ("whole", a) not in box:
            whole = jnp.zeros((model, 3 * width), bf16)
            for b, block in enumerate(blocks[a]):
                at = owner(steps[min(b, n_seq - 1)]) * depth + (half if b == n_seq else 0)
                whole = lax.dynamic_update_slice_in_dim(whole, block, at, 0)
            box["whole", a] = [whole[i : i + wide] for i in range(0, model, wide)]
        return box["whole", a], jnp.arange(model // wide, dtype=jnp.int32), model // wide, wide, False

    def from_others():
        extra = [box["g", k][rows : rows + 5 * per].astype(f32) for k in range(slots)]
        extra = [x.reshape(5, per, units) for x in extra]
        box["start"] = jnp.concatenate([x[0] + x[1] + x[2] for x in extra], axis=0)
        ends = jnp.concatenate([x[3] * 256 + x[4] for x in extra], axis=0)
        box["ends"] = ends[:, :width].astype(jnp.int32)

    def begin(a):
        held, places, count, deep, _ = in_order(a)
        box["begun", a] = call(
            functools.partial(begin_kernel, count - 1, deep, rows + tail, slots),
            jax.ShapeDtypeStruct((slots * (rows + tail), 3 * width), f32),
            [places, take(box["normed"]), *held[: count - 1]],
            scalars=1,
        )
        give(box["begun", a])

    def first(a):
        start = box["start"][:, a * width : (a + 1) * width]
        held, places, count, deep, split = in_order(a)
        *fields, maps, planes = call(
            functools.partial(first_kernel, (seqs, span, width, slots, count, deep, split, tail), a),
            [
                field,
                field,
                field,
                jax.ShapeDtypeStruct((3, seqs, width), f32),
                jax.ShapeDtypeStruct((4, seqs, width), f32),
            ],
            [
                places,
                place,
                box["normed"],
                start,
                take(box["ends"]),
                group_vectors[a],
                box["picked"],
                *held[count - 1 :],
                box["begun", a],
                *[box["g", k] for k in range(slots)],
            ],
            scratch=[space, space],
            scalars=2,
            room=7,
        )
        box["fields", a] = fields
        box["linked", a] = lax.ppermute(planes, "seq", [(i + 1, i) for i in range(n_seq - 1)])
        box["known", a], box["maps", a] = first_maps(maps), maps
        join(a, 1)
        give(box["linked", a])

    def join(a, bit):
        mine = box["maps", a] if bit == 1 else take(jnp.stack(box["known", a][0]))
        other = swapped(mine, "seq", bit)
        give(other)
        box["known", a] = joined_maps(box["known", a], other, bit)

    def join_rest(a, low, high):
        for b in range(low, high):
            if 1 << b < n_seq:
                join(a, 1 << b)

    def second(a):
        _, earlier, later = box["known", a]
        start = box["start"][:, a * width : (a + 1) * width]
        out = call(
            functools.partial(second_kernel, (seqs, span, width, slots, tail), a),
            [
                jax.ShapeDtypeStruct((slots * (rows + tail), 3 * width), bf16),
                *[jax.ShapeDtypeStruct((2, per, span, width), bf16)] * slots,
                jax.ShapeDtypeStruct((seqs, width), f32),
                jax.ShapeDtypeStruct((8, width), f32),
            ],
            [
                place,
                take(box["ends"]),
                group_vectors[a],
                jnp.stack(earlier),
                jnp.stack(later),
                start,
                box["linked", a],
                *box["fields", a],
                box["picked"],
                *[box["g", k] for k in range(slots)],
            ],
            scratch=[space] * 7,
            scalars=1,
            room=17,
        )
        box["grads", a] = out[0]
        box["moving", a] = out[1 : slots + 1]
        box["final", a], box["sums", a] = out[slots + 1], out[slots + 2][:4]
        box["farthest", a] = partials(a, (far,), bf16)[0]
        box["grads", a] = lax.optimization_barrier((box["grads", a], box["farthest", a]))[0]

    def moved(a, among):
        for k in among:
            box["moved", a, k] = box["moving", a][k]
            if k:
                box["moved", a, k] = swapped(take(box["moving", a][k]), "stream", k)
                give(box["moved", a, k])

    def stored(a):
        total = box["own", a] + up[a].astype(f32) + down[a].astype(f32)
        total = take(total)
        box["stored", a] = columns_as_stored(
            [total[:, g * width : (g + 1) * width] for g in range(3)]
        )

    def token_grads():
        held = [in_order(a) for a in range(GROUPS)]
        _, places, count, deep, split = held[0]
        out = call(
            functools.partial(
                token_kernel, (slots, count, deep, rows, GROUPS, split, tail), parts
            ),
            [
                jax.ShapeDtypeStruct((rows, model), f32),
                *[jax.ShapeDtypeStruct((rows, model), bf16)] * (slots - 1),
                jax.ShapeDtypeStruct((8, model), f32),
            ],
            [
                places,
                *[take(box["grads", a]) for a in range(GROUPS)],
                *[block for group in held for block in group[0]],
                *[piece for slot in tokens_of for piece in slot],
                box["means"],
                box["scales"],
            ],
            scalars=1,
        )
        box["kept"] = {k: out[k] for k in range(slots)}
        box["token_sums"] = out[slots][:2]
        give(out[0])

    def token_sends(bit):
        kept = box["kept"]
        for k in sorted(kept, reverse=True):
            if k & bit:
                got = swapped(take(kept.pop(k).astype(bf16)), "stream", bit)
                kept[k ^ bit] = kept[k ^ bit].astype(f32) + got.astype(f32)
                give(got)

    def token_part(i, count):
        if i == 0:
            box["sending"] = box["kept"].pop(2).astype(bf16)
            box["arrived"] = []
        low, high = rows * i // count // 16 * 16, rows * (i + 1) // count // 16 * 16
        box["arrived"].append(swapped(take(box["sending"][low:high]), "stream", 2))
        give(box["arrived"][i])
        if i + 1 == count:
            box["kept"][0] = box["kept"][0] + jnp.concatenate(box["arrived"], axis=0).astype(f32)

    def sums():
        gate_sums = jnp.concatenate([box["sums", a] for a in range(GROUPS)], axis=1)
        box["summed"] = jnp.concatenate(
            [
                lax.dynamic_update_slice_in_dim(
                    jnp.zeros((4, model), f32), gate_sums, at_stream * units, 1
                ),
                box["token_sums"],
            ],
            axis=0,
        )

    def seq_sums(low, high):
        for b in range(low, high):
            if 1 << b < n_seq:
                box["summed"] = box["summed"] + swapped(take(box["summed"]), "seq", 1 << b)
                give(box["summed"])

    def stream_sums():
        share = model // n_seq
        final_units = jnp.concatenate([box["final", a] for a in range(GROUPS)], axis=1)
        mine = lax.dynamic_slice_in_dim(final_units, at_seq * share % units, share, 1)
        mine = jnp.where(at_stream == at_seq * share // units, mine, 0.0)
        ordered = jnp.zeros_like(mine)
        for k in range(slots):
            ordered = lax.dynamic_update_slice_in_dim(
                ordered, mine[k * per : (k + 1) * per], (at_stream ^ k) * per, 0
            )
        ordered = jnp.pad(ordered.reshape(-1), (0, -seqs * share % model)).reshape(-1, model)
        summed = jnp.concatenate([box["summed"], ordered], axis=0)
        for bit in bits:
            summed = summed + swapped(take(summed), "stream", bit)
        box["final_state"] = lax.dynamic_slice_in_dim(
            summed[6:].reshape(-1)[: seqs * share].reshape(seqs, share), at_stream * per, per, 0
        )
        box["summed"] = summed[:6]

    def assemble():
        for name, which in (("outputs", 0), ("direct", 1)):
            whole = take(jnp.zeros((per, span, model), bf16))
            for a in range(GROUPS):
                for k in range(slots):
                    at = (at_stream ^ k) * units + a * width
                    whole = lax.dynamic_update_slice_in_dim(whole, box["moved", a, k][which], at, 2)
            box[name] = whole

    group = functools.partial
    if in_parts:
        early = [
            [group(far_tokens, 0)],
            [near_tokens, group(far_tokens, 1), group(passed_tokens, 0), messages],
            [group(passed_tokens, 1), out_grads, normalise],
        ]
    else:
        early = [[everyones_tokens], [messages], [out_grads, normalise]]
    early.append([from_others] + ([group(begin, 0)] if depth % 128 == 0 else []))
    if in_parts:
        ahead_tokens()
    deal(0)
    rounds.turn()
    for step in range(1, far + 1):
        gather(0, step)
        for other in early[step - 1] if step <= len(early) else ():
            other()
        rounds.turn()
    if depth % 128:
        begin(0)
    first(0)
    rounds.turn()
    join_rest(0, 1, 9)
    rounds.turn()
    second(0)
    late = [
        [token_grads, group(moved, 0, range(slots)[:3])],
        [group(token_sends, 1), group(moved, 0, range(slots)[3:]), sums, group(seq_sums, 0, 1)],
        [group(seq_sums, 1, 2)],
        [group(seq_sums, 2, 9), assemble],
    ]
    if in_parts:
        late[2].append(group(token_part, 0, 2))
        late[3].append(group(token_part, 1, 2))
    else:
        late[2] += [group(token_sends, bit) for bit in bits[1:]]
    rounds.before = []
    for step in range(1, far + 1):
        scatter(0, step)
        for other in late[step - 1] if step <= len(late) else ():
            other()
        rounds.turn()
    stored(0)
    stream_sums()
    weight_grad = jnp.concatenate(
        [box["stored", a][s] for s in range(3) for a in range(GROUPS)], axis=1
    )

    grad_normed = box["kept"][0]
    source = inputs.astype(f32).reshape(rows, model)
    scale = box["scales"][:rows, :1]
    scaled = (source - box["means"][:rows, :1]) * scale
    grad_scaled = grad_normed * norm_gain
    grad_source = scale * (
        grad_scaled
        - jnp.mean(grad_scaled, axis=1, keepdims=True)
        - scaled * jnp.mean(grad_scaled * scaled, axis=1, keepdims=True)
    )
    input_grad = (grad_source.reshape(per, span, model) + box["direct"].astype(f32)).astype(bf16)
    outputs, final_state, summed = box["outputs"], box["final_state"], box["summed"]

    return (
        outputs,
        final_state,
        input_grad,
        weight_grad,
        summed[0],
        summed[1],
        summed[2],
        summed[3],
        summed[4],
        summed[5],
    )


def solution(mesh):
    return jax.shard_map(
        local,
        mesh=mesh,
        in_specs=(
            P("stream", "seq", None),
            P("stream", None),
            P("stream"),
            P("seq", "stream"),
            P(),
            P(),
            P(),
            P(),
            P(),
            P(),
            P("stream", "seq", None),
        ),
        out_specs=(
            P("stream", "seq", None),
            P("stream", "seq"),
            P("stream", "seq", None),
            P("seq", "stream"),
            P(),
            P(),
            P(),
            P(),
            P(),
            P(),
        ),
        check_vma=False,
    )
```

time: 324 us -> 248 us (0.77)
  starting transfers between devices: 78.3 us -> 45.5 us
  waiting for transfers between devices: 124 us -> 101 us
  local copies, waits for them, and re-layouts: 23.4 us -> 39.1 us
  matrix products: 14.8 us -> 0 us
  Pallas kernels: 63.3 us -> 51 us
  between operations: 7.26 us -> 1.71 us
  other arithmetic: 12.5 us -> 9.13 us
    ppermute x32 -> x16, waiting for transfers between devices: 56 us -> 23.9 us  [along_ring(): lax.ppermute(value, 'seq', [(order[i], order[(i + steps) % count]) for i...]
    unnamed x133 -> x127, local copies, waits for them, and re-layouts: 6.01 us -> 30 us
    ppermute x32 -> x16, starting transfers between devices: 33.3 us -> 17.3 us  [along_ring(): lax.ppermute(value, 'seq', [(order[i], order[(i + steps) % count]) for i...]
    ppermute x42 -> x27, starting transfers between devices: 38.5 us -> 23.3 us  [swapped(): lax.ppermute(value, axis, [(i, i ^ bit) for i in range(lax.axis_size(axis...]
    dot_general x16 -> x0, matrix products: 14.8 us -> none  [partial(): lax.dot_general(columns, grads, (((0,), (0,)), ((), ())), preferred_eleme...]
    pallas_call x6 -> x14, Pallas kernels: 63.3 us -> 51 us  [call(): pl.pallas_call(kernel, out_shape=out_shape, in_specs=specs, out_specs=jax...]
    dynamic_slice x6 -> x1, local copies, waits for them, and re-layouts: 7.76 us -> 0.59 us  [stream_sums(): lax.dynamic_slice_in_dim(summed[6:].reshape(-1)[:seqs * share].reshape(se...]
    ppermute x42 -> x27, waiting for transfers between devices: 67.9 us -> 73.2 us  [swapped(): lax.ppermute(value, axis, [(i, i ^ bit) for i in range(lax.axis_size(axis...]
  transfers between devices with their start and end apart: 77 -> 45, of which waited for: 31 -> 25; matrix products, arithmetic and copies ran while one was open for 11% -> 6% of each run, Pallas kernels for 13% -> 13%
where the time goes in v2:
time: 248 us; the launch traced here: 247 us
  waiting for transfers between devices  101 us (41%)
  Pallas kernels  51 us (21%)
  starting transfers between devices  45.5 us (18%)
  local copies, waits for them, and re-layouts  39.1 us (16%)
  other arithmetic  9.13 us (4%)
    ppermute x27, waiting for transfers between devices, swapped(): lax.ppermute(value, axis, [(i, i ^ bit) for i in range(lax.axis_size(axis...  73.2 us
    pallas_call x14, Pallas kernels, call(): pl.pallas_call(kernel, out_shape=out_shape, in_specs=specs, out_specs=jax...  51 us
    unnamed x127, local copies, waits for them, and re-layouts  30 us
    ppermute x16, waiting for transfers between devices, along_ring(): lax.ppermute(value, 'seq', [(order[i], order[(i + steps) % count]) for i...  23.9 us
    ppermute x27, starting transfers between devices, swapped(): lax.ppermute(value, axis, [(i, i ^ bit) for i in range(lax.axis_size(axis...  23.3 us
    ppermute x16, starting transfers between devices, along_ring(): lax.ppermute(value, 'seq', [(order[i], order[(i + steps) % count]) for i...  17.3 us
  transfers between devices with their start and end apart: 45, of which 25 were waited for; matrix products, arithmetic and copies ran while one was open for 6% of the time, Pallas kernels for 13%

profile of v2, /device:TPU:0, one launch (start us, length us, event | category | flops | bytes accessed | tf_op | source)
XLA Modules:
  0.0 247.2 jit_solution(17810767329193374821)
XLA Ops:
  1.8 3.0 %collective-permute-start.1 = (bf16[256,512]{1,0:T(8,128)(2,1)S(1)}, bf16[256,512]{1,0:T(8,128)(2,1)S(1)}, u32[]{:S(2)}, u32[]{:S(2)}) collective-permute-start(bf16[256,512]{1,0:T(8,128)(2,1)S(1)} %get-tuple-element.190), channel_id=1, source_target_pairs={{0,2},{1,3},{2,0},{3,1},{4,6},{5,7},{6,4},{7,5},{8,10},{9,11},{10,... | collective-permute-start | bytes 786440 | tf_op jit(solution)/shard_map/ppermute | solution.py:71
  5.7 3.4 %collective-permute-start = (bf16[2,2048]{1,0:T(2,128)(2,1)S(1)}, bf16[2,2048]{1,0:T(2,128)(2,1)S(1)}, u32[]{:S(2)}, u32[]{:S(2)}) collective-permute-start(bf16[2,2048]{1,0:T(2,128)(2,1)S(1)} %bitcast.85), channel_id=1, source_target_pairs={{0,4},{4,8},{8,12},{12,16},{16,20},{20,24},{24,28},{1,5},{5,9},{9,... | collective-permute-start | bytes 24584 | tf_op jit(solution)/shard_map/ppermute | solution.py:567
  9.2 2.0 collective-permute-done.1
  12.4 1.8 collective-permute-start.3
  14.6 1.8 collective-permute-start.5
  16.7 10.5 %collective-permute-done.5.refs_2_.refs_12_ = bf16[128,2048]{1,0:T(8,128)(2,1)S(1)} collective-permute-done((bf16[128,2048]{1,0:T(8,128)(2,1)S(1)}, bf16[128,2048]{1,0:T(8,128)(2,1)S(1)}, u32[]{:S(2)}, u32[]{:S(2)}) %collective-permute-start.5) | collective-permute-done | bytes 524320 | tf_op jit(solution)/shard_map/ppermute | solution.py:71
  27.2 4.1 %collective-permute-done.3.refs_1_.refs_2_ = bf16[256,1536]{1,0:T(8,128)(2,1)} collective-permute-done((bf16[256,1536]{1,0:T(8,128)(2,1)S(1)}, bf16[256,1536]{1,0:T(8,128)(2,1)}, u32[]{:S(2)}, u32[]{:S(2)}) %collective-permute-start.3) | collective-permute-done | bytes 786464 | tf_op jit(solution)/shard_map/ppermute | solution.py:67
  33.1 1.5 collective-permute-start.9
  35.4 1.5 collective-permute-start.7
  41.9 9.0 %collective-permute-done.7.refs_3_.refs_13_ = bf16[144,2048]{1,0:T(8,128)(2,1)} collective-permute-done((bf16[144,2048]{1,0:T(8,128)(2,1)}, bf16[144,2048]{1,0:T(8,128)(2,1)}, u32[]{:S(2)}, u32[]{:S(2)}) %collective-permute-start.7) | collective-permute-done | bytes 589856 | tf_op jit(solution)/shard_map/ppermute | solution.py:71
  50.9 1.9 collective-permute-done.10.refs_4_.refs_5_
  53.1 1.5 collective-permute-start.13
  54.6 1.5 collective-permute-start.16
  57.4 5.2 %collective-permute-done.13.refs_5_.refs_2_ = bf16[272,512]{1,0:T(8,128)(2,1)S(1)} collective-permute-done((bf16[272,512]{1,0:T(8,128)(2,1)S(1)}, bf16[272,512]{1,0:T(8,128)(2,1)S(1)}, u32[]{:S(2)}, u32[]{:S(2)}) %collective-permute-start.13) | collective-permute-done | bytes 278560 | tf_op jit(solution)/shard_map/ppermute | solution.py:71
  62.6 5.0 %collective-permute-done.14.refs_6_.refs_3_ = bf16[272,512]{1,0:T(8,128)(2,1)S(1)} collective-permute-done((bf16[272,512]{1,0:T(8,128)(2,1)S(1)}, bf16[272,512]{1,0:T(8,128)(2,1)S(1)}, u32[]{:S(2)}, u32[]{:S(2)}) %collective-permute-start.14) | collective-permute-done | bytes 278560 | tf_op jit(solution)/shard_map/ppermute | solution.py:71
  69.1 4.3 %shard_map.186 = (bf16[1088,2048]{1,0:T(8,128)(2,1)S(1)}, f32[1024,128]{1,0:T(8,128)S(1)}, f32[1024,128]{1,0:T(8,128)S(1)}, bf16[1024,512]{1,0:T(8,128)(2,1)S(1)}) custom-call(s32[3]{0:T(128)S(1)} %pad_add_fusion.1.place, bf16[272,2048]{1,0:T(8,128)(2,1)S(1)} %maximum_maximum_fusion.refs_0_.refs_10_, ...), custom_call_target="tpu_custom_call" | custom-call | tf_op jit(solution)/shard_map/pallas_call | solution.py:34
  75.7 1.6 collective-permute-start.18
  77.9 8.1 %shard_map.188.refs_2_ = f32[1088,1536]{1,0:T(8,128)S(1)} custom-call(s32[8]{0:T(128)S(1)} %copy-done.46, bf16[1088,2048]{1,0:T(8,128)(2,1)S(1)} %get-tuple-element.116.normed, bf16[256,1536]{1,0:T(8,128)(2,1)S(1)} %pad_maximum_fusion.1.refs_0_.refs_1_, bf16[256,1536]{1,0:T(8,128)(2,1)} %collective-permute-done.3.refs_1_.refs_2_, ...), custom_call_target="tpu_custom_call" | custom-call | tf_op jit(solution)/shard_map/pallas_call | solution.py:34
  88.1 4.4 %shard_map.189 = (f32[4,1088,128]{2,1,0:T(8,128)S(1)}, f32[4,1088,128]{2,1,0:T(8,128)S(1)}, f32[4,1088,128]{2,1,0:T(8,128)S(1)}, f32[3,8,512]{2,1,0:T(8,128)S(1)}, f32[4,8,512]{2,1,0:T(8,128)S(1)}) custom-call(s32[8]{0:T(128)S(1)} %copy-done.46, s32[3]{0:T(128)S(1)} %pad_add_fusion.1.place, bf16[1088,2048]{1,0:T(8,128)(2,1)S(1)} %get-tuple-element.116.normed, ...), custom_call_target="tpu_custom_call" | custom-call | tf_op jit(solution)/shard_map/pallas_call | solution.py:34
  92.5 1.4 copy-done.16
  93.9 1.4 copy-done.18
  96.7 1.6 collective-permute-start.19
  98.3 1.5 collective-permute-start.20
  100.9 3.6 %collective-permute-done.20.linked = f32[4,8,512]{2,1,0:T(8,128)S(1)} collective-permute-done((f32[4,8,512]{2,1,0:T(8,128)S(1)}, f32[4,8,512]{2,1,0:T(8,128)S(1)}, u32[]{:S(2)}, u32[]{:S(2)}) %collective-permute-start.20) | collective-permute-done | bytes 65568 | tf_op jit(solution)/shard_map/ppermute | solution.py:694
  104.5 1.6 collective-permute-start.21
  106.1 2.5 %collective-permute-done.21 = f32[3,8,512]{2,1,0:T(8,128)S(1)} collective-permute-done((f32[3,8,512]{2,1,0:T(8,128)S(1)}, f32[3,8,512]{2,1,0:T(8,128)S(1)}, u32[]{:S(2)}, u32[]{:S(2)}) %collective-permute-start.21) | collective-permute-done | bytes 49184 | tf_op jit(solution)/shard_map/ppermute | solution.py:71
  108.6 2.7 %collective-permute-start.22 = (f32[3,8,512]{2,1,0:T(8,128)S(1)}, f32[3,8,512]{2,1,0:T(8,128)S(1)}, u32[]{:S(2)}, u32[]{:S(2)}) collective-permute-start(f32[3,8,512]{2,1,0:T(8,128)S(1)} %pad_maximum_fusion.5), channel_id=1, source_target_pairs={{0,16},{4,20},{8,24},{12,28},{16,0},{20,4},{24,8},{28,12},{1,17},{... | collective-permute-start | bytes 147464 | tf_op jit(solution)/shard_map/ppermute | solution.py:71
  111.2 2.4 collective-permute-done.22
  115.1 1.8 copy-done.17
  116.9 1.6 copy-done.19
  118.5 1.6 copy-done.21
  124.6 11.5 %shard_map.190 = (bf16[1088,1536]{1,0:T(8,128)(2,1)S(1)}, bf16[2,2,128,512]{3,2,1,0:T(8,128)(2,1)S(1)}, bf16[2,2,128,512]{3,2,1,0:T(8,128)(2,1)}, bf16[2,2,128,5...) custom-call(s32[3]{0:T(128)S(1)} %copy-done.50, ...), custom_call_target="tpu_custom_call" | custom-call | tf_op jit(solution)/shard_map/pallas_call | solution.py:34
  137.5 1.7 collective-permute-start.26
  140.2 1.4 collective-permute-start.23
  143.5 2.3 copy-done.1
  145.8 2.8 %shard_map.192 = (f32[256,1536]{1,0:T(8,128)S(1)}, f32[256,1536]{1,0:T(8,128)S(1)}) custom-call(s32[2]{0:T(128)S(1)} %get-tuple-element.226.owners, bf16[1088,2048]{1,0:T(8,128)(2,1)S(1)} %copy-done.1, bf16[1088,1536]{1,0:T(8,128)(2,1)S(1)} %get-tuple-element.171.grads.refs_0_), custom_call_target="tpu_custom_call" | custom-call | tf_op jit(solution)/shard_map/pallas_call | solution.py:34
  156.0 9.3 %shard_map.193 = (f32[256,2048]{1,0:T(8,128)S(1)}, bf16[256,2048]{1,0:T(8,128)(2,1)S(1)}, bf16[256,2048]{1,0:T(8,128)(2,1)S(1)}, bf16[256,2048]{1,0:T(8,128)(2,1)S(1)}, f32[8,2048]{1,0:T(8,128)S(1)}) custom-call(s32[8]{0:T(128)S(1)} %copy-done.47, bf16[1088,1536]{1,0:T(8,128)(2,1)S(1)} %get-tuple-element.171.grads.refs_0_, bf16[256,1536]{1,0:T(8,128)(2,1)S(1)} %copy-done.5, ...), custom_call_target="tpu_custom_call" | custom-call | tf_op jit(solution)/shard_map/pallas_call | solution.py:34
  172.0 2.8 %shard_map.194 = (f32[256,1536]{1,0:T(8,128)S(1)}, f32[256,1536]{1,0:T(8,128)S(1)}) custom-call(s32[2]{0:T(128)S(1)} %get-tuple-element.225.owners, bf16[1088,2048]{1,0:T(8,128)(2,1)S(1)} %bitcast.70, bf16[1088,1536]{1,0:T(8,128)(2,1)S(1)} %get-tuple-element.171.grads.refs_0_), custom_call_target="tpu_custom_call" | custom-call | tf_op jit(solution)/shard_map/pallas_call | solution.py:34
  174.8 13.1 %collective-permute-done.28.down = bf16[256,1536]{1,0:T(8,128)(2,1)S(1)} collective-permute-done((bf16[256,1536]{1,0:T(8,128)(2,1)S(1)}, bf16[256,1536]{1,0:T(8,128)(2,1)S(1)}, u32[]{:S(2)}, u32[]{:S(2)}) %collective-permute-start.28) | collective-permute-done | bytes 786464 | tf_op jit(solution)/shard_map/ppermute | solution.py:67
  188.9 1.7 collective-permute-start.34
  193.2 2.8 %shard_map.197 = (f32[256,1536]{1,0:T(8,128)S(1)}, f32[256,1536]{1,0:T(8,128)S(1)}) custom-call(s32[2]{0:T(128)S(1)} %pad_add_fusion.4.owners, bf16[1088,2048]{1,0:T(8,128)(2,1)S(1)} %bitcast.70, bf16[1088,1536]{1,0:T(8,128)(2,1)S(1)} %get-tuple-element.171.grads.refs_0_), custom_call_target="tpu_custom_call" | custom-call | tf_op jit(solution)/shard_map/pallas_call | solution.py:34
  196.0 12.6 %collective-permute-done.35 = f32[6,2048]{1,0:T(8,128)S(1)} collective-permute-done((f32[6,2048]{1,0:T(8,128)S(1)}, f32[6,2048]{1,0:T(8,128)S(1)}, u32[]{:S(2)}, u32[]{:S(2)}) %collective-permute-start.35) | collective-permute-done | bytes 49184 | tf_op jit(solution)/shard_map/ppermute | solution.py:71
  210.5 2.9 %collective-permute-start.39 = (bf16[256,1536]{1,0:T(8,128)(2,1)S(1)}, bf16[256,1536]{1,0:T(8,128)(2,1)S(1)}, u32[]{:S(2)}, u32[]{:S(2)}) collective-permute-start(bf16[256,1536]{1,0:T(8,128)(2,1)S(1)} %get-tuple-element.170), channel_id=1, source_target_pairs={{0,4},{8,0},{16,8},{24,16},{28,24},{20,28},{12,20},{4,12},{1,5},{9... | collective-permute-start | bytes 2359304 | tf_op jit(solution)/shard_map/ppermute | solution.py:67
  213.4 1.4 collective-permute-start.37
  217.2 14.4 %collective-permute-done.37 = f32[6,2048]{1,0:T(8,128)S(1)} collective-permute-done((f32[6,2048]{1,0:T(8,128)S(1)}, f32[6,2048]{1,0:T(8,128)S(1)}, u32[]{:S(2)}, u32[]{:S(2)}) %collective-permute-start.37) | collective-permute-done | bytes 49184 | tf_op jit(solution)/shard_map/ppermute | solution.py:71
  236.2 1.9 collective-permute-start.43
  238.1 2.8 %collective-permute-done.42 = f32[7,2048]{1,0:T(8,128)S(1)} collective-permute-done((f32[7,2048]{1,0:T(8,128)S(1)}, f32[7,2048]{1,0:T(8,128)S(1)}, u32[]{:S(2)}, u32[]{:S(2)}) %collective-permute-start.42) | collective-permute-done | bytes 57376 | tf_op jit(solution)/shard_map/ppermute | solution.py:71
  242.1 3.6 %collective-permute-done.43 = bf16[256,512]{1,0:T(8,128)(2,1)S(1)} collective-permute-done((bf16[256,512]{1,0:T(8,128)(2,1)S(1)}, bf16[256,512]{1,0:T(8,128)(2,1)S(1)}, u32[]{:S(2)}, u32[]{:S(2)}) %collective-permute-start.43) | collective-permute-done | bytes 262176 | tf_op jit(solution)/shard_map/ppermute | solution.py:71
  (263 shorter events, 60.6 us)
Async XLA Ops:
  1.8 9.3 %collective-permute-start.1 = (bf16[256,512]{1,0:T(8,128)(2,1)S(1)}, bf16[256,512]{1,0:T(8,128)(2,1)S(1)}, u32[]{:S(2)}, u32[]{:S(2)}) collective-permute-start(bf16[256,512]{1,0:T(8,128)(2,1)S(1)} %get-tuple-element.190), channel_id=1, source_target_pairs={{0,2},{1,3},{2,0},{3,1},{4,6},{5,7},{6,4},{7,5},{8,10},{9,11},{10,... | collective-permute-start | bytes 786440 | tf_op jit(solution)/shard_map/ppermute | solution.py:71
  4.9 6.3 %collective-permute-start.2 = (bf16[256,512]{1,0:T(8,128)(2,1)S(1)}, bf16[256,512]{1,0:T(8,128)(2,1)S(1)}, u32[]{:S(2)}, u32[]{:S(2)}) collective-permute-start(bf16[256,512]{1,0:T(8,128)(2,1)S(1)} %get-tuple-element.189), channel_id=1, source_target_pairs={{0,1},{1,0},{2,3},{3,2},{4,5},{5,4},{6,7},{7,6},{8,9},{9,8},{10,11... | collective-permute-start | bytes 786440 | tf_op jit(solution)/shard_map/ppermute | solution.py:71
  5.7 6.7 %collective-permute-start = (bf16[2,2048]{1,0:T(2,128)(2,1)S(1)}, bf16[2,2048]{1,0:T(2,128)(2,1)S(1)}, u32[]{:S(2)}, u32[]{:S(2)}) collective-permute-start(bf16[2,2048]{1,0:T(2,128)(2,1)S(1)} %bitcast.85), channel_id=1, source_target_pairs={{0,4},{4,8},{8,12},{12,16},{16,20},{20,24},{24,28},{1,5},{5,9},{9,... | collective-permute-start | bytes 24584 | tf_op jit(solution)/shard_map/ppermute | solution.py:567
  12.4 65.5 %copy-start.4 = (bf16[256,1536]{1,0:T(8,128)(2,1)}, bf16[256,1536]{1,0:T(8,128)(2,1)S(1)}, u32[]{:S(2)}) copy-start(bf16[256,1536]{1,0:T(8,128)(2,1)S(1)} %pad_maximum_fusion.1.refs_0_.refs_1_) | copy-start | bytes 2359300
  12.4 18.9 %collective-permute-start.3 = (bf16[256,1536]{1,0:T(8,128)(2,1)S(1)}, bf16[256,1536]{1,0:T(8,128)(2,1)}, u32[]{:S(2)}, u32[]{:S(2)}) collective-permute-start(bf16[256,1536]{1,0:T(8,128)(2,1)S(1)} %pad_maximum_fusion.1.refs_0_.refs_1_), channel_id=1, source_target_pairs={{0,8},{8,16},{16,24},{24,28},{28,20},{20,12},{12,4},{4,0},{1,9},{9... | collective-permute-start | bytes 2359304 | tf_op jit(solution)/shard_map/ppermute | solution.py:67
  14.3 18.2 %collective-permute-start.4 = (bf16[256,1536]{1,0:T(8,128)(2,1)S(1)}, bf16[256,1536]{1,0:T(8,128)(2,1)}, u32[]{:S(2)}, u32[]{:S(2)}) collective-permute-start(bf16[256,1536]{1,0:T(8,128)(2,1)S(1)} %pad_maximum_fusion.1.refs_0_.refs_1_), channel_id=1, source_target_pairs={{0,4},{8,0},{16,8},{24,16},{28,24},{20,28},{12,20},{4,12},{1,5},{9... | collective-permute-start | bytes 2359304 | tf_op jit(solution)/shard_map/ppermute | solution.py:67
  14.6 12.6 %collective-permute-start.5 = (bf16[128,2048]{1,0:T(8,128)(2,1)S(1)}, bf16[128,2048]{1,0:T(8,128)(2,1)S(1)}, u32[]{:S(2)}, u32[]{:S(2)}) collective-permute-start(bf16[128,2048]{1,0:T(8,128)(2,1)S(1)} %slice_bitcast_fusion), channel_id=1, source_target_pairs={{0,2},{1,3},{2,0},{3,1},{4,6},{5,7},{6,4},{7,5},{8,10},{9,11},{10,... | collective-permute-start | bytes 1572872 | tf_op jit(solution)/shard_map/ppermute | solution.py:71
  16.7 56.8 %copy-start.2 = (bf16[272,2048]{1,0:T(8,128)(2,1)}, bf16[272,2048]{1,0:T(8,128)(2,1)S(1)}, u32[]{:S(2)}) copy-start(bf16[272,2048]{1,0:T(8,128)(2,1)S(1)} %maximum_maximum_fusion.refs_0_.refs_10_) | copy-start | bytes 3342340
  32.5 20.5 %collective-permute-start.6 = (bf16[272,2048]{1,0:T(8,128)(2,1)S(1)}, bf16[272,2048]{1,0:T(8,128)(2,1)S(1)}, u32[]{:S(2)}, u32[]{:S(2)}) collective-permute-start(bf16[272,2048]{1,0:T(8,128)(2,1)S(1)} %maximum_maximum_fusion.refs_0_.refs_10_), channel_id=1, source_target_pairs={{0,1},{1,0},{2,3},{3,2},{4,5},{5,4},{6,7},{7,6},{8,9},{9,8},{10,11... | collective-permute-start | bytes 3342344 | tf_op jit(solution)/shard_map/ppermute | solution.py:71
  32.5 20.3 %collective-permute-start.10 = (bf16[256,1536]{1,0:T(8,128)(2,1)}, bf16[256,1536]{1,0:T(8,128)(2,1)}, u32[]{:S(2)}, u32[]{:S(2)}) collective-permute-start(bf16[256,1536]{1,0:T(8,128)(2,1)} %collective-permute-done.4.refs_2_.refs_3_), channel_id=1, source_target_pairs={{0,4},{8,0},{16,8},{24,16},{28,24},{20,28},{12,20},{4,12},{1,5},{9... | collective-permute-start | bytes 2359304 | tf_op jit(solution)/shard_map/ppermute | solution.py:67
  33.1 20.0 %collective-permute-start.9 = (bf16[256,1536]{1,0:T(8,128)(2,1)}, bf16[256,1536]{1,0:T(8,128)(2,1)}, u32[]{:S(2)}, u32[]{:S(2)}) collective-permute-start(bf16[256,1536]{1,0:T(8,128)(2,1)} %collective-permute-done.3.refs_1_.refs_2_), channel_id=1, source_target_pairs={{0,8},{8,16},{16,24},{24,28},{28,20},{20,12},{12,4},{4,0},{1,9},{9... | collective-permute-start | bytes 2359304 | tf_op jit(solution)/shard_map/ppermute | solution.py:67
  35.4 15.5 %collective-permute-start.7 = (bf16[144,2048]{1,0:T(8,128)(2,1)}, bf16[144,2048]{1,0:T(8,128)(2,1)}, u32[]{:S(2)}, u32[]{:S(2)}) collective-permute-start(bf16[144,2048]{1,0:T(8,128)(2,1)} %slice.327), channel_id=1, source_target_pairs={{0,2},{1,3},{2,0},{3,1},{4,6},{5,7},{6,4},{7,5},{8,10},{9,11},{10,... | collective-permute-start | bytes 1769480 | tf_op jit(solution)/shard_map/ppermute | solution.py:71
  36.9 4.9 %collective-permute-start.8 = (bf16[128,2048]{1,0:T(8,128)(2,1)S(1)}, bf16[128,2048]{1,0:T(8,128)(2,1)}, u32[]{:S(2)}, u32[]{:S(2)}) collective-permute-start(bf16[128,2048]{1,0:T(8,128)(2,1)S(1)} %collective-permute-done.5.refs_2_.refs_12_), channel_id=1, source_target_pairs={{0,1},{1,0},{2,3},{3,2},{4,5},{5,4},{6,7},{7,6},{8,9},{9,8},{10,11... | collective-permute-start | bytes 1572872 | tf_op jit(solution)/shard_map/ppermute | solution.py:71
  38.4 49.6 %copy-start.49 = (s32[3]{0:T(128)}, s32[3]{0:T(128)S(1)}, u32[]{:S(2)}) copy-start(s32[3]{0:T(128)S(1)} %pad_add_fusion.1.place) | copy-start | bytes 40
  53.1 3.6 %collective-permute-start.12 = (bf16[272,512]{1,0:T(8,128)(2,1)S(1)}, bf16[272,512]{1,0:T(8,128)(2,1)S(1)}, u32[]{:S(2)}, u32[]{:S(2)}) collective-permute-start(bf16[272,512]{1,0:T(8,128)(2,1)S(1)} %get-tuple-element.107), channel_id=1, source_target_pairs={{0,1},{1,0},{2,3},{3,2},{4,5},{5,4},{6,7},{7,6},{8,9},{9,8},{10,11... | collective-permute-start | bytes 835592 | tf_op jit(solution)/shard_map/ppermute | solution.py:71
  53.1 9.5 %collective-permute-start.13 = (bf16[272,512]{1,0:T(8,128)(2,1)S(1)}, bf16[272,512]{1,0:T(8,128)(2,1)S(1)}, u32[]{:S(2)}, u32[]{:S(2)}) collective-permute-start(bf16[272,512]{1,0:T(8,128)(2,1)S(1)} %get-tuple-element.109), channel_id=1, source_target_pairs={{0,2},{1,3},{2,0},{3,1},{4,6},{5,7},{6,4},{7,5},{8,10},{9,11},{10,... | collective-permute-start | bytes 835592 | tf_op jit(solution)/shard_map/ppermute | solution.py:71
  54.6 20.5 %collective-permute-start.16 = (bf16[256,1536]{1,0:T(8,128)(2,1)}, bf16[256,1536]{1,0:T(8,128)(2,1)S(1)}, u32[]{:S(2)}, u32[]{:S(2)}) collective-permute-start(bf16[256,1536]{1,0:T(8,128)(2,1)} %collective-permute-done.10.refs_4_.refs_5_), channel_id=1, source_target_pairs={{0,4},{8,0},{16,8},{24,16},{28,24},{20,28},{12,20},{4,12},{1,5},{9... | collective-permute-start | bytes 2359304 | tf_op jit(solution)/shard_map/ppermute | solution.py:67
  56.1 19.5 %collective-permute-start.15 = (bf16[256,1536]{1,0:T(8,128)(2,1)}, bf16[256,1536]{1,0:T(8,128)(2,1)S(1)}, u32[]{:S(2)}, u32[]{:S(2)}) collective-permute-start(bf16[256,1536]{1,0:T(8,128)(2,1)} %collective-permute-done.9.refs_3_.refs_4_), channel_id=1, source_target_pairs={{0,8},{8,16},{16,24},{24,28},{28,20},{20,12},{12,4},{4,0},{1,9},{9... | collective-permute-start | bytes 2359304 | tf_op jit(solution)/shard_map/ppermute | solution.py:67
  56.7 11.0 %collective-permute-start.14 = (bf16[272,512]{1,0:T(8,128)(2,1)S(1)}, bf16[272,512]{1,0:T(8,128)(2,1)S(1)}, u32[]{:S(2)}, u32[]{:S(2)}) collective-permute-start(bf16[272,512]{1,0:T(8,128)(2,1)S(1)} %get-tuple-element.111), channel_id=1, source_target_pairs={{0,3},{1,2},{2,1},{3,0},{4,7},{5,6},{6,5},{7,4},{8,11},{9,10},{10,... | collective-permute-start | bytes 835592 | tf_op jit(solution)/shard_map/ppermute | solution.py:71
  56.7 11.0 %collective-permute-start.11 = (bf16[144,2048]{1,0:T(8,128)(2,1)}, bf16[144,2048]{1,0:T(8,128)(2,1)S(1)}, u32[]{:S(2)}, u32[]{:S(2)}) collective-permute-start(bf16[144,2048]{1,0:T(8,128)(2,1)} %collective-permute-done.7.refs_3_.refs_13_), channel_id=1, source_target_pairs={{0,1},{1,0},{2,3},{3,2},{4,5},{5,4},{6,7},{7,6},{8,9},{9,8},{10,11... | collective-permute-start | bytes 1769480 | tf_op jit(solution)/shard_map/ppermute | solution.py:71
  75.7 11.1 %collective-permute-start.18 = (bf16[128,1536]{1,0:T(8,128)(2,1)S(1)}, bf16[128,1536]{1,0:T(8,128)(2,1)S(1)}, u32[]{:S(2)}, u32[]{:S(2)}) collective-permute-start(bf16[128,1536]{1,0:T(8,128)(2,1)S(1)} %slice.352), channel_id=1, source_target_pairs={{0,4},{8,0},{16,8},{24,16},{28,24},{20,28},{12,20},{4,12},{1,5},{9... | collective-permute-start | bytes 1179656 | tf_op jit(solution)/shard_map/ppermute | solution.py:67
  77.3 10.7 %collective-permute-start.17 = (bf16[128,1536]{1,0:T(8,128)(2,1)S(1)}, bf16[128,1536]{1,0:T(8,128)(2,1)S(1)}, u32[]{:S(2)}, u32[]{:S(2)}) collective-permute-start(bf16[128,1536]{1,0:T(8,128)(2,1)S(1)} %slice.351), channel_id=1, source_target_pairs={{0,8},{8,16},{16,24},{24,28},{28,20},{20,12},{12,4},{4,0},{1,9},{9... | collective-permute-start | bytes 1179656 | tf_op jit(solution)/shard_map/ppermute | solution.py:67
  96.7 4.1 %collective-permute-start.19 = (f32[3,8,512]{2,1,0:T(8,128)S(1)}, f32[3,8,512]{2,1,0:T(8,128)S(1)}, u32[]{:S(2)}, u32[]{:S(2)}) collective-permute-start(f32[3,8,512]{2,1,0:T(8,128)S(1)} %get-tuple-element.119), channel_id=1, source_target_pairs={{0,4},{4,0},{8,12},{12,8},{16,20},{20,16},{24,28},{28,24},{1,5},{5... | collective-permute-start | bytes 147464 | tf_op jit(solution)/shard_map/ppermute | solution.py:71
  98.3 6.1 %collective-permute-start.20 = (f32[4,8,512]{2,1,0:T(8,128)S(1)}, f32[4,8,512]{2,1,0:T(8,128)S(1)}, u32[]{:S(2)}, u32[]{:S(2)}) collective-permute-start(f32[4,8,512]{2,1,0:T(8,128)S(1)} %get-tuple-element.120), channel_id=1, source_target_pairs={{4,0},{8,4},{12,8},{16,12},{20,16},{24,20},{28,24},{5,1},{9,5},{13... | collective-permute-start | bytes 196616 | tf_op jit(solution)/shard_map/ppermute | solution.py:694
  104.5 4.1 %collective-permute-start.21 = (f32[3,8,512]{2,1,0:T(8,128)S(1)}, f32[3,8,512]{2,1,0:T(8,128)S(1)}, u32[]{:S(2)}, u32[]{:S(2)}) collective-permute-start(f32[3,8,512]{2,1,0:T(8,128)S(1)} %pad_maximum_fusion.4), channel_id=1, source_target_pairs={{0,8},{4,12},{8,0},{12,4},{16,24},{20,28},{24,16},{28,20},{1,9},{5... | collective-permute-start | bytes 147464 | tf_op jit(solution)/shard_map/ppermute | solution.py:71
  108.6 5.1 %collective-permute-start.22 = (f32[3,8,512]{2,1,0:T(8,128)S(1)}, f32[3,8,512]{2,1,0:T(8,128)S(1)}, u32[]{:S(2)}, u32[]{:S(2)}) collective-permute-start(f32[3,8,512]{2,1,0:T(8,128)S(1)} %pad_maximum_fusion.5), channel_id=1, source_target_pairs={{0,16},{4,20},{8,24},{12,28},{16,0},{20,4},{24,8},{28,12},{1,17},{... | collective-permute-start | bytes 147464 | tf_op jit(solution)/shard_map/ppermute | solution.py:71
  137.4 28.0 %collective-permute-start.25 = (bf16[2,2,128,512]{3,2,1,0:T(8,128)(2,1)}, bf16[2,2,128,512]{3,2,1,0:T(8,128)(2,1)}, u32[]{:S(2)}, u32[]{:S(2)}) collective-permute-start(bf16[2,2,128,512]{3,2,1,0:T(8,128)(2,1)} %get-tuple-element.135), channel_id=1, source_target_pairs={{0,1},{1,0},{2,3},{3,2},{4,5},{5,4},{6,7},{7,6},{8,9},{9,8},{10,11... | collective-permute-start | bytes 1572872 | tf_op jit(solution)/shard_map/ppermute | solution.py:71
  137.5 27.9 %collective-permute-start.26 = (bf16[2,2,128,512]{3,2,1,0:T(8,128)(2,1)}, bf16[2,2,128,512]{3,2,1,0:T(8,128)(2,1)}, u32[]{:S(2)}, u32[]{:S(2)}) collective-permute-start(bf16[2,2,128,512]{3,2,1,0:T(8,128)(2,1)} %get-tuple-element.136), channel_id=1, source_target_pairs={{0,2},{1,3},{2,0},{3,1},{4,6},{5,7},{6,4},{7,5},{8,10},{9,11},{10,... | collective-permute-start | bytes 1572872 | tf_op jit(solution)/shard_map/ppermute | solution.py:71
  140.2 25.2 %collective-permute-start.23 = (bf16[128,1536]{1,0:T(8,128)(2,1)}, bf16[128,1536]{1,0:T(8,128)(2,1)}, u32[]{:S(2)}, u32[]{:S(2)}) collective-permute-start(bf16[128,1536]{1,0:T(8,128)(2,1)} %get-tuple-element.188), channel_id=1, source_target_pairs={{0,8},{8,16},{16,24},{24,28},{28,20},{20,12},{12,4},{4,0},{1,9},{9... | collective-permute-start | bytes 1179656 | tf_op jit(solution)/shard_map/ppermute | solution.py:67
  141.6 23.7 %collective-permute-start.24 = (bf16[128,1536]{1,0:T(8,128)(2,1)}, bf16[128,1536]{1,0:T(8,128)(2,1)}, u32[]{:S(2)}, u32[]{:S(2)}) collective-permute-start(bf16[128,1536]{1,0:T(8,128)(2,1)} %get-tuple-element.187), channel_id=1, source_target_pairs={{0,4},{8,0},{16,8},{24,16},{28,24},{20,28},{12,20},{4,12},{1,5},{9... | collective-permute-start | bytes 1179656 | tf_op jit(solution)/shard_map/ppermute | solution.py:67
  165.4 23.5 %collective-permute-start.29 = (bf16[256,2048]{1,0:T(8,128)(2,1)S(1)}, bf16[256,2048]{1,0:T(8,128)(2,1)S(1)}, u32[]{:S(2)}, u32[]{:S(2)}) collective-permute-start(bf16[256,2048]{1,0:T(8,128)(2,1)S(1)} %get-tuple-element.146), channel_id=1, source_target_pairs={{0,1},{1,0},{2,3},{3,2},{4,5},{5,4},{6,7},{7,6},{8,9},{9,8},{10,11... | collective-permute-start | bytes 3145736 | tf_op jit(solution)/shard_map/ppermute | solution.py:71
  165.5 23.4 %collective-permute-start.30 = (bf16[256,2048]{1,0:T(8,128)(2,1)S(1)}, bf16[256,2048]{1,0:T(8,128)(2,1)S(1)}, u32[]{:S(2)}, u32[]{:S(2)}) collective-permute-start(bf16[256,2048]{1,0:T(8,128)(2,1)S(1)} %get-tuple-element.148), channel_id=1, source_target_pairs={{0,1},{1,0},{2,3},{3,2},{4,5},{5,4},{6,7},{7,6},{8,9},{9,8},{10,11... | collective-permute-start | bytes 3145736 | tf_op jit(solution)/shard_map/ppermute | solution.py:71
  167.4 4.5 %collective-permute-start.32 = (f32[6,2048]{1,0:T(8,128)S(1)}, f32[6,2048]{1,0:T(8,128)S(1)}, u32[]{:S(2)}, u32[]{:S(2)}) collective-permute-start(f32[6,2048]{1,0:T(8,128)S(1)} %pad_maximum_fusion.2), channel_id=1, source_target_pairs={{0,4},{4,0},{8,12},{12,8},{16,20},{20,16},{24,28},{28,24},{1,5},{5... | collective-permute-start | bytes 147464 | tf_op jit(solution)/shard_map/ppermute | solution.py:71
  168.7 19.2 %collective-permute-start.28 = (bf16[256,1536]{1,0:T(8,128)(2,1)S(1)}, bf16[256,1536]{1,0:T(8,128)(2,1)S(1)}, u32[]{:S(2)}, u32[]{:S(2)}) collective-permute-start(bf16[256,1536]{1,0:T(8,128)(2,1)S(1)} %get-tuple-element.143), channel_id=1, source_target_pairs={{0,4},{8,0},{16,8},{24,16},{28,24},{20,28},{12,20},{4,12},{1,5},{9... | collective-permute-start | bytes 2359304 | tf_op jit(solution)/shard_map/ppermute | solution.py:67
  169.5 19.1 %collective-permute-start.27 = (bf16[256,1536]{1,0:T(8,128)(2,1)S(1)}, bf16[256,1536]{1,0:T(8,128)(2,1)S(1)}, u32[]{:S(2)}, u32[]{:S(2)}) collective-permute-start(bf16[256,1536]{1,0:T(8,128)(2,1)S(1)} %get-tuple-element.141), channel_id=1, source_target_pairs={{0,8},{8,16},{16,24},{24,28},{28,20},{20,12},{12,4},{4,0},{1,9},{9... | collective-permute-start | bytes 2359304 | tf_op jit(solution)/shard_map/ppermute | solution.py:67
  171.9 17.0 %collective-permute-start.31 = (bf16[2,2,128,512]{3,2,1,0:T(8,128)(2,1)S(1)}, bf16[2,2,128,512]{3,2,1,0:T(8,128)(2,1)S(1)}, u32[]{:S(2)}, u32[]{:S(2)}) collective-permute-start(bf16[2,2,128,512]{3,2,1,0:T(8,128)(2,1)S(1)} %copy-done.52), channel_id=1, source_target_pairs={{0,3},{1,2},{2,1},{3,0},{4,7},{5,6},{6,5},{7,4},{8,11},{9,10},{10,... | collective-permute-start | bytes 1572872 | tf_op jit(solution)/shard_map/ppermute | solution.py:71
  188.9 19.7 %collective-permute-start.34 = (bf16[256,1536]{1,0:T(8,128)(2,1)S(1)}, bf16[256,1536]{1,0:T(8,128)(2,1)S(1)}, u32[]{:S(2)}, u32[]{:S(2)}) collective-permute-start(bf16[256,1536]{1,0:T(8,128)(2,1)S(1)} %get-tuple-element.156), channel_id=1, source_target_pairs={{0,4},{8,0},{16,8},{24,16},{28,24},{20,28},{12,20},{4,12},{1,5},{9... | collective-permute-start | bytes 2359304 | tf_op jit(solution)/shard_map/ppermute | solution.py:67
  190.6 18.1 %collective-permute-start.33 = (bf16[256,1536]{1,0:T(8,128)(2,1)S(1)}, bf16[256,1536]{1,0:T(8,128)(2,1)S(1)}, u32[]{:S(2)}, u32[]{:S(2)}) collective-permute-start(bf16[256,1536]{1,0:T(8,128)(2,1)S(1)} %get-tuple-element.154), channel_id=1, source_target_pairs={{0,8},{8,16},{16,24},{24,28},{28,20},{20,12},{12,4},{4,0},{1,9},{9... | collective-permute-start | bytes 2359304 | tf_op jit(solution)/shard_map/ppermute | solution.py:67
  191.5 17.1 %collective-permute-start.36 = (bf16[128,2048]{1,0:T(8,128)(2,1)S(1)}, bf16[128,2048]{1,0:T(8,128)(2,1)S(1)}, u32[]{:S(2)}, u32[]{:S(2)}) collective-permute-start(bf16[128,2048]{1,0:T(8,128)(2,1)S(1)} %get-tuple-element.162), channel_id=1, source_target_pairs={{0,2},{1,3},{2,0},{3,1},{4,6},{5,7},{6,4},{7,5},{8,10},{9,11},{10,... | collective-permute-start | bytes 1572872 | tf_op jit(solution)/shard_map/ppermute | solution.py:71
  191.9 16.6 %collective-permute-start.35 = (f32[6,2048]{1,0:T(8,128)S(1)}, f32[6,2048]{1,0:T(8,128)S(1)}, u32[]{:S(2)}, u32[]{:S(2)}) collective-permute-start(f32[6,2048]{1,0:T(8,128)S(1)} %fusion.12), channel_id=1, source_target_pairs={{0,8},{4,12},{8,0},{12,4},{16,24},{20,28},{24,16},{28,20},{1,9},{5... | collective-permute-start | bytes 147464 | tf_op jit(solution)/shard_map/ppermute | solution.py:71
  210.5 24.0 %collective-permute-start.39 = (bf16[256,1536]{1,0:T(8,128)(2,1)S(1)}, bf16[256,1536]{1,0:T(8,128)(2,1)S(1)}, u32[]{:S(2)}, u32[]{:S(2)}) collective-permute-start(bf16[256,1536]{1,0:T(8,128)(2,1)S(1)} %get-tuple-element.170), channel_id=1, source_target_pairs={{0,4},{8,0},{16,8},{24,16},{28,24},{20,28},{12,20},{4,12},{1,5},{9... | collective-permute-start | bytes 2359304 | tf_op jit(solution)/shard_map/ppermute | solution.py:67
  213.4 21.1 %collective-permute-start.38 = (bf16[256,1536]{1,0:T(8,128)(2,1)S(1)}, bf16[256,1536]{1,0:T(8,128)(2,1)S(1)}, u32[]{:S(2)}, u32[]{:S(2)}) collective-permute-start(bf16[256,1536]{1,0:T(8,128)(2,1)S(1)} %get-tuple-element.168), channel_id=1, source_target_pairs={{0,8},{8,16},{16,24},{24,28},{28,20},{20,12},{12,4},{4,0},{1,9},{9... | collective-permute-start | bytes 2359304 | tf_op jit(solution)/shard_map/ppermute | solution.py:67
  213.4 18.2 %collective-permute-start.40 = (bf16[128,2048]{1,0:T(8,128)(2,1)S(1)}, bf16[128,2048]{1,0:T(8,128)(2,1)S(1)}, u32[]{:S(2)}, u32[]{:S(2)}) collective-permute-start(bf16[128,2048]{1,0:T(8,128)(2,1)S(1)} %get-tuple-element.172), channel_id=1, source_target_pairs={{0,2},{1,3},{2,0},{3,1},{4,6},{5,7},{6,4},{7,5},{8,10},{9,11},{10,... | collective-permute-start | bytes 1572872 | tf_op jit(solution)/shard_map/ppermute | solution.py:71
  213.4 18.1 %collective-permute-start.37 = (f32[6,2048]{1,0:T(8,128)S(1)}, f32[6,2048]{1,0:T(8,128)S(1)}, u32[]{:S(2)}, u32[]{:S(2)}) collective-permute-start(f32[6,2048]{1,0:T(8,128)S(1)} %add.311), channel_id=1, source_target_pairs={{0,16},{4,20},{8,24},{12,28},{16,0},{20,4},{24,8},{28,12},{1,17},{... | collective-permute-start | bytes 147464 | tf_op jit(solution)/shard_map/ppermute | solution.py:71
  234.5 1.3 collective-permute-start.41
  235.8 5.0 %collective-permute-start.42 = (f32[7,2048]{1,0:T(8,128)S(1)}, f32[7,2048]{1,0:T(8,128)S(1)}, u32[]{:S(2)}, u32[]{:S(2)}) collective-permute-start(f32[7,2048]{1,0:T(8,128)S(1)} %fusion.19), channel_id=1, source_target_pairs={{0,2},{1,3},{2,0},{3,1},{4,6},{5,7},{6,4},{7,5},{8,10},{9,11},{10,... | collective-permute-start | bytes 172040 | tf_op jit(solution)/shard_map/ppermute | solution.py:71
  236.2 9.5 %collective-permute-start.43 = (bf16[256,512]{1,0:T(8,128)(2,1)S(1)}, bf16[256,512]{1,0:T(8,128)(2,1)S(1)}, u32[]{:S(2)}, u32[]{:S(2)}) collective-permute-start(bf16[256,512]{1,0:T(8,128)(2,1)S(1)} %get-tuple-element.184), channel_id=1, source_target_pairs={{0,2},{1,3},{2,0},{3,1},{4,6},{5,7},{6,4},{7,5},{8,10},{9,11},{10,... | collective-permute-start | bytes 786440 | tf_op jit(solution)/shard_map/ppermute | solution.py:71
  238.1 7.9 %collective-permute-start.44 = (bf16[256,512]{1,0:T(8,128)(2,1)S(1)}, bf16[256,512]{1,0:T(8,128)(2,1)S(1)}, u32[]{:S(2)}, u32[]{:S(2)}) collective-permute-start(bf16[256,512]{1,0:T(8,128)(2,1)S(1)} %get-tuple-element.183), channel_id=1, source_target_pairs={{0,1},{1,0},{2,3},{3,2},{4,5},{5,4},{6,7},{7,6},{8,9},{9,8},{10,11... | collective-permute-start | bytes 786440 | tf_op jit(solution)/shard_map/ppermute | solution.py:71
  (59 other events, 515.1 us)

commit v3 on v2

v3 whole, which is shorter than its diff:
```python
import functools

import jax
import jax.numpy as jnp
from jax import lax
from jax.experimental import pallas as pl
from jax.experimental.pallas import tpu as pltpu
from jax.sharding import PartitionSpec as P

epsilon = 1e-05
f32 = jnp.float32
bf16 = jnp.bfloat16
PAD = 8
STEP = 256
ROOM = 5 * 512 * 1024


def vmem_spec():
    return pl.BlockSpec(memory_space=pltpu.VMEM)


def smem_spec():
    return pl.BlockSpec(memory_space=pltpu.SMEM)


def call(kernel, out_shape, operands, scratch=(), scalars=0, cost=0):
    return pl.pallas_call(
        kernel,
        out_shape=jax.tree.map(lambda out: pltpu.VMEM(out.shape, out.dtype), out_shape),
        in_specs=[smem_spec()] * scalars + [vmem_spec()] * (len(operands) - scalars),
        out_specs=jax.tree.map(lambda _: vmem_spec(), out_shape),
        scratch_shapes=list(scratch),
        compiler_params=pltpu.CompilerParams(vmem_limit_bytes=lax.axis_size("stream") * ROOM),
        cost_estimate=pl.CostEstimate(flops=int(cost * 1e9), bytes_accessed=0, transcendentals=0),
    )(
        *operands[:scalars],
        *[pltpu.with_memory_space_constraint(x, pltpu.VMEM) for x in operands[scalars:]],
    )


def at_spot(spot, count):
    if count != 8:
        return spot
    return spot * 2 if isinstance(spot, int) and spot < 4 else (
        15 - spot * 2 if isinstance(spot, int) else jnp.where(spot < 4, spot * 2, 15 - spot * 2)
    )


def spot_of(index, count):
    if count != 8:
        return index
    return jnp.where(index % 2 == 0, index // 2, (15 - index) // 2)


def wrapped(value, count):
    value = jnp.where(value >= count, value - count, value)
    return jnp.where(value < 0, value + count, value)


def along_ring(value, steps):
    count = lax.axis_size("seq")
    order = [at_spot(i, count) for i in range(count)]
    return lax.ppermute(value, "seq", [(order[i], order[(i + steps) % count]) for i in range(count)])


def cut(array, start, size, axis):
    starts = [jnp.int32(0)] * array.ndim
    sizes = list(array.shape)
    starts[axis], sizes[axis] = start, size
    return lax.dynamic_slice(array, starts, sizes, allow_negative_indices=False)


def pasted(array, piece, start, axis):
    starts = [jnp.int32(0)] * array.ndim
    starts[axis] = start
    return lax.dynamic_update_slice(array, piece, starts, allow_negative_indices=False)


def swapped(value, axis, bit):
    return lax.ppermute(value, axis, [(i, i ^ bit) for i in range(lax.axis_size(axis))])


def norm_kernel(parts, rows, tail, units, place, *refs):
    flat = sum(len(slot) for slot in parts)
    pieces = refs[:flat]
    gain, bias, normed, means, scales, picked = refs[flat:]
    gain_row, bias_row = gain[...], bias[...]
    lanes = pl.ds(pl.multiple_of(place[2], units), units)
    at = 0
    for k, slot in enumerate(parts):
        for low, high in slot:
            x = pieces[at][...].astype(f32)
            mean = jnp.mean(x, axis=1, keepdims=True)
            centered = x - mean
            scale = lax.rsqrt(jnp.mean(centered * centered, axis=1, keepdims=True) + epsilon)
            base = k * (rows + tail)
            normed[base + low : base + high, :] = (centered * scale * gain_row + bias_row).astype(bf16)
            count = min(high, rows) - low
            here = slice(k * rows + low, k * rows + low + count)
            means[here, :] = jnp.broadcast_to(mean[:count], (count, 128))
            scales[here, :] = jnp.broadcast_to(scale[:count], (count, 128))
            picked[here, :] = pieces[at][:count, lanes]
            at += 1


def strided(ref, row, seqs, stride, low=0, count=None):
    count = ref.shape[0] if count is None else count
    tiles = [ref[low + lane, pl.ds(row, seqs, stride=stride), :] for lane in range(count)]
    return jnp.concatenate(tiles, axis=1)


def put_strided(ref, row, seqs, stride, value, low=0):
    for lane in range(value.shape[1] // 128):
        ref[low + lane, pl.ds(row, seqs, stride=stride), :] = value[:, lane * 128 : (lane + 1) * 128]


def put_rows(ref, row, count, value):
    for lane in range(value.shape[1] // 128):
        ref[lane, pl.ds(row, count), :] = value[:, lane * 128 : (lane + 1) * 128]


def get_rows(ref, row, count):
    return jnp.concatenate([ref[lane, pl.ds(row, count), :] for lane in range(ref.shape[0])], axis=1)


def message_kernel(slots, units, tail, where, grads, start, lengths, *outs):
    rows, per = grads.shape[0], start.shape[0]
    for k in range(slots):
        lanes = pl.ds(pl.multiple_of(where[k], units), units)
        outs[k][:rows, :] = grads[:, lanes]
        left = start[:, lanes]
        extra = []
        for _ in range(3):
            part = left.astype(bf16).astype(f32)
            extra.append(part)
            left = left - part
        counts = lengths[...]
        high = counts // 256
        extra += [
            jnp.broadcast_to(n.astype(f32)[:, :1], (per, units)) for n in (high, counts - high * 256)
        ]
        extra.append(jnp.zeros((tail - 5 * per, units), f32))
        outs[k][rows:, :] = jnp.concatenate(extra, axis=0).astype(bf16)


def merge_kernel(cuts, mine_up, mine_down, up, down, *outs):
    count, total = up.shape[0], mine_up.shape[0]
    for n, (low, high) in enumerate(cuts):
        lanes = slice(low, high)
        out_up, out_down = outs[2 * n], outs[2 * n + 1]
        first, last = slice(0, count), slice(total - count, total)
        out_up[first, :] = (mine_up[first, lanes] + up[:, lanes].astype(f32)).astype(bf16)
        out_down[last, :] = (mine_down[last, lanes] + down[:, lanes].astype(f32)).astype(bf16)
        if count < total:
            out_up[count:, :] = mine_up[count:, lanes].astype(bf16)
            out_down[: total - count, :] = mine_down[: total - count, lanes].astype(bf16)


def assemble_kernel(slots, width, where, *refs):
    for k in range(slots):
        lanes = pl.ds(pl.multiple_of(where[k], width), width)
        for which in range(2):
            refs[slots + which][:, :, lanes] = refs[k][which]


def spread_rows(dims, low, width, g_in, picked, gs, xs):
    seqs, span, slots = dims
    per = seqs // slots
    for n in range(seqs):
        to, lanes = n * (span + PAD) + PAD, slice(low, low + width)
        at = n % per * span
        put_rows(gs, to, span, g_in[n // per][at : at + span, lanes].astype(f32))
        put_rows(xs, to, span, picked[n * span : (n + 1) * span, lanes].astype(f32))


def joined(refs):
    return refs[0][...] if len(refs) == 1 else jnp.concatenate([ref[...] for ref in refs], axis=0)


def begin_kernel(blocks, depth, rows, count, sources, normed, *refs):
    total = refs[blocks]
    for k in range(count):
        here = slice(k * rows, (k + 1) * rows)
        sum_ = None
        for b in range(blocks):
            at = pl.multiple_of(sources[b] * depth, depth)
            term = jnp.dot(normed[here, pl.ds(at, depth)], refs[b][...], preferred_element_type=f32)
            sum_ = term if sum_ is None else sum_ + term
        total[here, :] = sum_


def first_kernel(dims, sources, place, normed, start, lens, v0, v1, v2, v3, picked, begun, *refs):
    vecs = (v0, v1, v2, v3)
    seqs, span, width, slots, blocks, depth, late, tail = dims
    stride = span + PAD
    g_in = refs[late : late + slots]
    fields, maps, planes, gs, xs = refs[late + slots :]
    cand, forg, rese = fields.at[0], fields.at[1], fields.at[2]
    per = seqs // slots
    rows = per * span
    ext = rows + tail
    at = pl.multiple_of(sources[blocks - 1] * depth, depth)
    lead = joined(refs[:late])
    for k in range(slots):
        here = slice(k * ext, (k + 1) * ext)
        for piece in range(3):
            field = fields.at[place[3 + piece]]
            columns = slice(piece * width, (piece + 1) * width)
            total = begun[here, columns] + jnp.dot(
                normed[here, pl.ds(at, depth)], lead[:, columns], preferred_element_type=f32
            )
            total = total.astype(bf16).astype(f32)
            for j in range(per):
                to = (k * per + j) * stride + PAD
                before = jnp.broadcast_to(total[rows + j : rows + j + 1, :], (8, width))
                put_rows(field, to - 8, 8, before)
                put_rows(field, to, span, total[j * span : (j + 1) * span, :])
    before = jnp.where(place[1] == 0, start[...], strided(cand, PAD - 1, seqs, stride))
    put_strided(cand, PAD - 1, seqs, stride, before)
    ends = lens[...]
    base = place[0]
    step = min(width, STEP)
    ends = ends[:, :step]
    for low in range(0, width, step):
        units = slice(low, low + step)
        lane, lanes = low // 128, step // 128
        spread_rows((seqs, span, slots), low, step, g_in, picked, gs, xs)
        own = pl.ds(pl.multiple_of(place[2] + low, 128), step)
        peep_f, peep_r, bias_f, bias_r = (row[:, own] for row in vecs)

        def turn(t, carry):
            previous, decays, injects, handed = carry
            row = t + PAD
            c, f, r = (strided(ref, row, seqs, stride, lane, lanes) for ref in (cand, forg, rese))
            f = jax.nn.sigmoid(f + peep_f * previous + bias_f)
            r = jax.nn.sigmoid(r + peep_r * previous + bias_r)
            put_strided(forg, row, seqs, stride, f, lane)
            put_strided(rese, row, seqs, stride, r, lane)
            live = base + t < ends
            d = jnp.where(live, f, 1.0)
            inject = jnp.where(live, (1.0 - f) * c, 0.0)
            pulled = jnp.where(live, r * strided(gs, row, seqs, stride), 0.0)
            decays = decays * d
            return c, decays, d * injects + inject, handed + decays * pulled

        one, zero = jnp.ones((seqs, step), f32), jnp.zeros((seqs, step), f32)
        _, decays, injects, handed = lax.fori_loop(
            0, span, turn, (before[:, units], one, zero, zero), unroll=8
        )
        maps[0, :, units], maps[1, :, units], maps[2, :, units] = decays, injects, handed
        c, f, r = (strided(ref, PAD, seqs, stride, lane, lanes) for ref in (cand, forg, rese))
        g, x = (strided(ref, PAD, seqs, stride) for ref in (gs, xs))
        live = base < ends
        d = jnp.where(live, f, 1.0)
        inject = jnp.where(live, (1.0 - f) * c, 0.0)
        via_adjoint = jnp.where(live, (1.0 - f) * peep_f, 0.0)
        via_state = jnp.where(live, r * (1.0 - r) * g * peep_r, 0.0)
        planes[0, :, units], planes[1, :, units] = via_adjoint, via_adjoint * c
        planes[2, :, units], planes[3, :, units] = via_state * d, via_state * (inject - x)


def second_kernel(
    dims, place, lens, v0, v1, earlier, later, start, linked, fields, picked, *refs
):
    vecs = (v0, v1)
    seqs, span, width, slots, tail = dims
    stride = span + PAD
    g_in = refs[:slots]
    grads, moved = refs[slots], refs[slots + 1 : 2 * slots + 1]
    final, sums = refs[2 * slots + 1 : 2 * slots + 3]
    gs, xs, states, outs, gcs, fts, rts = refs[2 * slots + 3 :]
    cand, forg, rese = fields.at[0], fields.at[1], fields.at[2]
    per = seqs // slots
    base = place[0]
    step = min(width, STEP)
    ends = lens[:, :step]
    sums[...] = jnp.zeros_like(sums)
    for k in range(slots):
        to = k * (per * span + tail) + per * span
        grads[to : to + tail, :] = jnp.zeros((tail, 3 * width), bf16)
    for low in range(0, width, step):
        units = slice(low, low + step)
        lane, lanes = low // 128, step // 128
        spread_rows((seqs, span, slots), low, step, g_in, picked, gs, xs)
        own = pl.ds(pl.multiple_of(place[2] + low, 128), step)
        peep_f, peep_r = (row[:, own] for row in vecs[:2])
        begin = earlier[0, :, units] * start[:, units] + earlier[1, :, units]
        after = later[2, :, units]
        put_strided(states, PAD - 1, seqs, stride, begin)

        def forward(t, state):
            row = t + PAD
            c, f, r = (strided(ref, row, seqs, stride, lane, lanes) for ref in (cand, forg, rese))
            x = strided(xs, row, seqs, stride)
            live = base + t < ends
            state = jnp.where(live, f * state + (1.0 - f) * c, state)
            put_strided(states, row, seqs, stride, state)
            put_strided(outs, row, seqs, stride, jnp.where(live, r * state + (1.0 - r) * x, x))
            return state

        end = lax.fori_loop(0, span, forward, begin, unroll=8)
        final[:, units] = later[0, :, units] * end + later[1, :, units]
        link = [linked[i, :, units] for i in range(4)]
        upcoming = end * (link[0] * after + link[2]) - link[1] * after + link[3]

        def backward(i, carry):
            reached, upcoming, pf, pr, bf, br = carry
            row = span - 1 - i + PAD
            c, f, r = (strided(ref, row, seqs, stride, lane, lanes) for ref in (cand, forg, rese))
            x, g, state = (strided(ref, row, seqs, stride) for ref in (xs, gs, states))
            prior = strided(states, row - 1, seqs, stride)
            previous = strided(cand, row - 1, seqs, stride, lane, lanes)
            live = base + (span - 1 - i) < ends
            zero = jnp.zeros_like(f)
            adjoint = jnp.where(live, r * g, 0.0) + reached
            kept = jnp.where(live, (1.0 - f) * adjoint, zero)
            ft = f * kept * (prior - c)
            rt = jnp.where(live, r * (1.0 - r) * g * (state - x), zero)
            put_strided(gcs, row, seqs, stride, kept + upcoming)
            put_strided(fts, row, seqs, stride, ft)
            put_strided(rts, row, seqs, stride, rt)
            put_strided(gs, row, seqs, stride, jnp.where(live, (1.0 - r) * g, g))
            reached = jnp.where(live, f * adjoint, adjoint)
            return (
                reached,
                ft * peep_f + rt * peep_r,
                pf + ft * previous,
                pr + rt * previous,
                bf + ft,
                br + rt,
            )

        zero = jnp.zeros((seqs, step), f32)
        done = lax.fori_loop(
            0, span, backward, (after, upcoming, zero, zero, zero, zero), unroll=4
        )
        for i in range(4):
            sums[i : i + 1, units] = jnp.sum(done[2 + i], axis=0, keepdims=True)
        for n in range(seqs):
            at = n * stride + PAD
            k, j = n // per, n % per
            to = k * (per * span + tail) + j * span
            for gate, ref in enumerate((gcs, fts, rts)):
                here = slice(gate * width + low, gate * width + low + step)
                grads[to : to + span, here] = get_rows(ref, at, span).astype(bf16)
            moved[k][0, j, :, units] = get_rows(outs, at, span).astype(bf16)
            moved[k][1, j, :, units] = get_rows(gs, at, span).astype(bf16)


def partial_kernel(distances, depth, width, owners, place, normed, grads, *outs):
    for i, distance in enumerate(distances):
        lanes = pl.ds(pl.multiple_of(owners[distance] * depth, min(depth, 128)), depth)
        columns = normed[:, lanes]
        for piece in range(3):
            gate = pl.ds(pl.multiple_of(place[3 + piece] * width, width), width)
            sum_ = lax.dot_general(
                columns, grads[:, gate], (((0,), (0,)), ((), ())), preferred_element_type=f32
            )
            outs[i][:, piece * width : (piece + 1) * width] = sum_.astype(outs[i].dtype)


def token_kernel(dims, parts, sources, place, grads, gate_sums, *refs):
    slots, blocks, depth, rows, width, split, tail = dims
    flat = sum(len(slot) for slot in parts)
    n_w = blocks + (1 if split else 0)
    pieces = refs[n_w : n_w + flat]
    means, scales, own = refs[n_w + flat : n_w + flat + 3]
    others = refs[n_w + flat + 3 : n_w + flat + slots + 2]
    sums = refs[n_w + flat + slots + 2]
    first_of = [sum(len(slot) for slot in parts[:k]) for k in range(slots)]

    def raw(k, lanes):
        found = [
            pieces[first_of[k] + i][: min(high, rows) - low, lanes]
            for i, (low, high) in enumerate(parts[k])
        ]
        return found[0] if len(found) == 1 else jnp.concatenate(found, axis=0)

    def block(b):
        return joined(refs[b : b + 2] if split and b == blocks - 1 else refs[b : b + 1])

    sums[...] = jnp.zeros_like(sums)
    sums[:4, pl.ds(pl.multiple_of(place[2], width), width)] = gate_sums[:4, :]
    for b in range(blocks):
        at = pl.multiple_of(sources[b] * depth, depth)
        lanes = pl.ds(at, depth)
        gain_sum, bias_sum = jnp.zeros((8, depth), f32), jnp.zeros((8, depth), f32)
        weights = block(b)
        for k in range(slots):
            here = pl.ds(k * rows, rows)
            total = None
            for piece in range(3):
                gate = pl.ds(pl.multiple_of(place[3 + piece] * width, width), width)
                term = lax.dot_general(
                    grads[k * (rows + tail) : k * (rows + tail) + rows, gate],
                    weights[:, piece * width : (piece + 1) * width],
                    (((1,), (1,)), ((), ())),
                    preferred_element_type=f32,
                )
                total = term if total is None else total + term
            copies = depth // 128
            mean = jnp.concatenate([means[here, :]] * copies, axis=1)
            scale = jnp.concatenate([scales[here, :]] * copies, axis=1)
            scaled = (raw(k, lanes).astype(f32) - mean) * scale
            gain_sum += jnp.sum((total * scaled).reshape(rows // 8, 8, depth), axis=0)
            bias_sum += jnp.sum(total.reshape(rows // 8, 8, depth), axis=0)
            if k == 0:
                own[:, lanes] = total
            else:
                others[k - 1][:, lanes] = total.astype(bf16)
        sums[4:5, lanes] = jnp.sum(gain_sum, axis=0, keepdims=True)
        sums[5:6, lanes] = jnp.sum(bias_sum, axis=0, keepdims=True)


def first_maps(maps):
    one, zero = jnp.ones_like(maps[0]), jnp.zeros_like(maps[0])
    return (maps[0], maps[1], maps[2]), (one, zero), (one, zero, zero)


def joined_maps(known, other, first):
    (decay, inject, handed), before, later = known
    theirs = (other[0], other[1], other[2])
    before_new = (theirs[0] * before[0], before[0] * theirs[1] + before[1])
    later_new = (
        later[0] * theirs[0],
        theirs[0] * later[1] + theirs[1],
        later[2] + later[0] * theirs[2],
    )
    before = tuple(jnp.where(first, a, b) for a, b in zip(before, before_new))
    later = tuple(jnp.where(first, b, a) for a, b in zip(later, later_new))
    inject_new = jnp.where(first, theirs[0] * inject + theirs[1], decay * theirs[1] + inject)
    handed_new = jnp.where(first, handed + decay * theirs[2], theirs[2] + theirs[0] * handed)
    return (decay * theirs[0], inject_new, handed_new), before, later


class Rounds:
    def __init__(self):
        self.before, self.given = [], []

    def take(self, value):
        if not self.before:
            return value
        return lax.optimization_barrier((value, self.before))[0]

    def give(self, *values):
        self.given += values

    def turn(self):
        self.before, self.given = self.given, []


def local(
    inputs,
    start_state,
    lengths,
    weights,
    peep_forget,
    peep_reset,
    bias_forget,
    bias_reset,
    norm_gain,
    norm_bias,
    out_grad,
):
    per, span, model = inputs.shape
    n_seq, slots = lax.axis_size("seq"), lax.axis_size("stream")
    at_seq, at_stream = lax.axis_index("seq"), lax.axis_index("stream")
    seqs = per * slots
    width = model // slots
    depth = model // n_seq
    rows = per * span
    tokens = seqs * span
    tail = 16
    half = depth // 2
    spot = spot_of(at_seq, n_seq)
    far = n_seq // 2
    steps = [0]
    for k in range(1, far):
        steps += [-k, k]
    steps.append(far)
    dealing = slots == 4

    def owner(distance):
        return at_spot(wrapped(spot + distance, n_seq), n_seq)

    def per_stream(table):
        found = table[0]
        for d in range(1, len(table)):
            found = jnp.where(at_stream == d, table[d], found)
        return found

    gates = ((0, 1, 2), (1, 0, 2), (1, 2, 0), (2, 1, 0)) if dealing else ((0, 1, 2),)
    gate_of = [per_stream([table[piece] for table in gates]) for piece in range(3)]
    bits = [1 << b for b in range(slots.bit_length() - 1)]
    seq_bits = [1 << b for b in range(n_seq.bit_length() - 1)]
    share = model // n_seq
    index = {
        "sources": jnp.stack([owner(distance) for distance in steps]).astype(jnp.int32),
        "place": jnp.stack([at_seq * span, at_seq, at_stream * width, *gate_of]).astype(jnp.int32),
        "owners": jnp.stack([owner(distance) for distance in range(n_seq)]).astype(jnp.int32),
        "where": jnp.stack([(at_stream ^ k) * width for k in range(slots)]).astype(jnp.int32),
        "lanes": [(at_stream ^ k) * width for k in range(slots)],
        "rows": [(at_stream ^ k) * per for k in range(slots)],
        "first": [(at_seq & bit) == 0 for bit in seq_bits],
        "even": at_stream % 2 == 0,
        "share": at_seq * share % width,
        "holds": at_stream == at_seq * share // width,
    }
    index, inputs, weights, out_grad, start_state, lengths = lax.optimization_barrier(
        (index, inputs, weights, out_grad, start_state, lengths)
    )
    sources, place, even = index["sources"], index["place"], index["even"]

    vectors = [
        row.reshape(1, model) for row in (peep_forget, peep_reset, bias_forget, bias_reset)
    ]
    gain_row, bias_row = norm_gain.reshape(1, model), norm_bias.reshape(1, model)
    tall = seqs * (span + PAD)
    fields = jax.ShapeDtypeStruct((3, width // 128, tall, 128), f32)
    space = pltpu.VMEM((min(width, STEP) // 128, tall, 128), f32)

    rounds = Rounds()
    take, give = rounds.take, rounds.give
    box = {}

    def deal():
        if dealing:
            pieces = [weights[:, i * width : (i + 1) * width] for i in range(3)]
            own = jnp.where(even, pieces[0], pieces[2])
            near = swapped(pieces[1], "stream", 1)
            distant = swapped(jnp.where(even, pieces[2], pieces[0]), "stream", 2)
            box["dealt"] = jnp.concatenate([own, near, distant], axis=1)
            give(near, distant)
            return
        everything = lax.all_gather(weights, "stream", axis=1, tiled=True)
        found = [
            lax.dynamic_slice_in_dim(everything, gate * model + at_stream * width, width, 1)
            for gate in range(3)
        ]
        box["dealt"] = jnp.concatenate(found, axis=1)

    def stored():
        own, rest = box["total"]
        near, distant = rest[:, :width], rest[:, width:]
        if dealing:
            distant = swapped(distant.astype(bf16), "stream", 2).astype(f32)
            near = swapped(near.astype(bf16), "stream", 1).astype(f32)
            found = [jnp.where(even, own, distant), near, jnp.where(even, distant, own)]
        else:
            flat = lax.all_gather(
                jnp.concatenate(box["total"], axis=1).astype(bf16), "stream", axis=0
            ).astype(f32)
            flat = jnp.swapaxes(flat.reshape(slots, depth, 3, width), 0, 2)
            flat = jnp.swapaxes(flat, 1, 2).reshape(3 * slots, depth, width)
            found = [
                lax.dynamic_index_in_dim(flat, 3 * at_stream + i, 0, keepdims=False)
                for i in range(3)
            ]
        return jnp.concatenate(found, axis=1)

    def gather(step):
        if step == 1:
            box["up"] = box["down"] = take(box["dealt"])
            box["blocks"] = [box["dealt"]]
        if step == far:
            box["up"], box["down"] = box["up"][:half], box["down"][half:]
        box["up"] = along_ring(take(box["up"]), 1)
        box["down"] = along_ring(take(box["down"]), -1)
        box["blocks"] += [box["up"], box["down"]]
        give(box["up"], box["down"])

    def partials(distances, kind):
        grads = take(box["grads"])
        if depth % 128:
            found = []
            for distance in distances:
                at = owner(distance)
                sum_ = lax.dot_general(
                    lax.dynamic_slice_in_dim(box["normed"], at * depth, depth, 1),
                    grads,
                    (((0,), (0,)), ((), ())),
                    preferred_element_type=f32,
                ).astype(kind)
                found.append(sum_)
            return found
        return call(
            functools.partial(
                partial_kernel, [distance % n_seq for distance in distances], depth, width
            ),
            [jax.ShapeDtypeStruct((depth, 3 * width), kind)] * len(distances),
            [index["owners"], place, box["normed"], grads],
            scalars=2,
        )

    def scatter(step):
        cuts_of = [(0, 3 * width)]
        if step == 1:
            sent = [box["farthest"][:half], box["farthest"][half:]]
        else:
            sent = call(
                functools.partial(merge_kernel, cuts_of),
                [jax.ShapeDtypeStruct((depth, b - a), bf16) for a, b in cuts_of for _ in range(2)],
                [*box["mine"], box["up"], box["down"]],
            )
        came = [along_ring(take(value), 1 - 2 * (i % 2)) for i, value in enumerate(sent)]
        box["up"], box["down"] = came
        give(*came)
        box["mine"] = partials((far - step, step - far) if step < far else (0,), f32)
        give(*box["mine"])

    whole_part = [(0, rows + tail)]
    cuts = [(0, rows // 2), (rows // 2, rows + tail)]
    parts = [whole_part, whole_part, cuts, cuts] if dealing else [whole_part] * slots
    tokens_of = [[None] * len(slot) for slot in parts]
    flat_inputs = inputs.reshape(rows, model)

    def ahead_tokens():
        box["ahead"] = lax.ppermute(
            take(inputs[:, -1, :]), "seq", [(i, i + 1) for i in range(n_seq - 1)]
        )
        give(box["ahead"])

    def own_tokens():
        tokens_of[0][0] = jnp.concatenate(
            [flat_inputs, box["ahead"], jnp.zeros((tail - per, model), bf16)], axis=0
        )

    def everyones_tokens():
        ahead_tokens()
        own_tokens()
        for bit in reversed(bits):
            for k in range(slots):
                if tokens_of[k][0] is not None and tokens_of[k ^ bit][0] is None:
                    tokens_of[k ^ bit][0] = swapped(tokens_of[k][0], "stream", bit)

    def near_tokens():
        own_tokens()
        tokens_of[1][0] = swapped(take(tokens_of[0][0]), "stream", 1)
        give(tokens_of[1][0])

    def far_tokens(i):
        low, high = cuts[i]
        source = flat_inputs[low:high] if high <= rows else tokens_of[0][0][low:high]
        tokens_of[2][i] = swapped(take(source), "stream", 2)
        give(tokens_of[2][i])

    def passed_tokens(i):
        tokens_of[3][i] = swapped(take(tokens_of[2][i]), "stream", 1)
        give(tokens_of[3][i])

    def messages():
        box["messages"] = call(
            functools.partial(message_kernel, slots, width, tail),
            [jax.ShapeDtypeStruct((rows + tail, width), bf16)] * slots,
            [
                index["where"],
                take(out_grad.reshape(rows, model)),
                start_state,
                jnp.broadcast_to(lengths[:, None], (per, 128)),
            ],
            scalars=1,
        )

    def out_grads():
        for k in range(slots):
            box["g", k] = box["messages"][k]
            if k:
                box["g", k] = swapped(take(box["g", k]), "stream", k)
                give(box["g", k])

    def normalise():
        flat = [piece for slot in tokens_of for piece in slot]
        box["normed"], box["means"], box["scales"], box["picked"] = call(
            functools.partial(norm_kernel, parts, rows, tail, width),
            [
                jax.ShapeDtypeStruct((slots * (rows + tail), model), bf16),
                jax.ShapeDtypeStruct((tokens, 128), f32),
                jax.ShapeDtypeStruct((tokens, 128), f32),
                jax.ShapeDtypeStruct((tokens, width), bf16),
            ],
            [place, *flat, take(gain_row), bias_row],
            scalars=1,
        )
        give(box["normed"])

    def from_others():
        extra = [box["g", k][rows : rows + 5 * per].astype(f32) for k in range(slots)]
        extra = [x.reshape(5, per, width) for x in extra]
        box["start"] = jnp.concatenate([x[0] + x[1] + x[2] for x in extra], axis=0)
        ends = jnp.concatenate([x[3] * 256 + x[4] for x in extra], axis=0)
        box["ends"] = ends.astype(jnp.int32)

    def in_order():
        if depth % 128 == 0:
            return box["blocks"], sources, n_seq, depth, True
        deep = 2 * 128
        if "whole" not in box:
            whole = jnp.zeros((model, 3 * width), bf16)
            for b, block in enumerate(box["blocks"]):
                at = owner(steps[min(b, n_seq - 1)]) * depth + (half if b == n_seq else 0)
                whole = lax.dynamic_update_slice_in_dim(whole, block, at, 0)
            box["whole"] = [whole[i : i + deep] for i in range(0, model, deep)]
        count = model // deep
        return box["whole"], jnp.arange(count, dtype=jnp.int32), count, deep, False

    def begin():
        held, places, count, deep, _ = in_order()
        box["begun"] = call(
            functools.partial(begin_kernel, count - 1, deep, rows + tail, slots),
            jax.ShapeDtypeStruct((slots * (rows + tail), 3 * width), f32),
            [places, take(box["normed"]), *held[: count - 1]],
            scalars=1,
        )
        give(box["begun"])

    def first():
        held, places, count, deep, split = in_order()
        box["fields"], maps, planes = call(
            functools.partial(
                first_kernel, (seqs, span, width, slots, count, deep, 2 if split else 1, tail)
            ),
            [
                fields,
                jax.ShapeDtypeStruct((3, seqs, width), f32),
                jax.ShapeDtypeStruct((4, seqs, width), f32),
            ],
            [
                places,
                place,
                box["normed"],
                box["start"],
                take(box["ends"]),
                *vectors,
                box["picked"],
                box["begun"],
                *held[count - 1 :],
                *[box["g", k] for k in range(slots)],
            ],
            scratch=[space, space],
            scalars=2,
        )
        box["linked"] = lax.ppermute(planes, "seq", [(i + 1, i) for i in range(n_seq - 1)])
        box["known"], box["maps"] = first_maps(maps), maps
        join(1)

    def join(bit):
        mine = box["maps"] if bit == 1 else take(jnp.stack(box["known"][0]))
        other = swapped(mine, "seq", bit)
        give(other)
        box["known"] = joined_maps(box["known"], other, index["first"][seq_bits.index(bit)])

    def join_rest():
        bit = 2
        while bit < n_seq:
            join(bit)
            bit *= 2

    def second():
        _, earlier, later = box["known"]
        out = call(
            functools.partial(second_kernel, (seqs, span, width, slots, tail)),
            [
                jax.ShapeDtypeStruct((slots * (rows + tail), 3 * width), bf16),
                *[jax.ShapeDtypeStruct((2, per, span, width), bf16)] * slots,
                jax.ShapeDtypeStruct((seqs, width), f32),
                jax.ShapeDtypeStruct((8, width), f32),
            ],
            [
                place,
                take(box["ends"]),
                *vectors[:2],
                jnp.stack(earlier),
                jnp.stack(later),
                box["start"],
                box["linked"],
                box["fields"],
                box["picked"],
                *[box["g", k] for k in range(slots)],
            ],
            scratch=[space] * 7,
            scalars=1,
        )
        box["grads"], box["moving"] = out[0], out[1 : slots + 1]
        box["final"], box["sums"] = out[slots + 1], out[slots + 2]
        rounds.before = []
        box["farthest"] = partials((far,), bf16)[0]
        box["grads"] = lax.optimization_barrier((box["grads"], box["farthest"]))[0]

    def moved(among):
        for k in among:
            box["moved", k] = box["moving"][k]
            if k:
                box["moved", k] = swapped(take(box["moving"][k]), "stream", k)
                give(box["moved", k])

    def token_grads():
        held, places, count, deep, split = in_order()
        out = call(
            functools.partial(
                token_kernel, (slots, count, deep, rows, width, split, tail), parts
            ),
            [
                jax.ShapeDtypeStruct((rows, model), f32),
                *[jax.ShapeDtypeStruct((rows, model), bf16)] * (slots - 1),
                jax.ShapeDtypeStruct((8, model), f32),
            ],
            [
                places,
                place,
                take(box["grads"]),
                box["sums"],
                *held,
                *[piece for slot in tokens_of for piece in slot],
                box["means"],
                box["scales"],
            ],
            scalars=2,
        )
        box["kept"] = {k: out[k] for k in range(slots)}
        box["summed"] = out[slots]
        give(out[0])

    def token_sends(bit):
        kept = box["kept"]
        for k in sorted(kept, reverse=True):
            if k & bit:
                got = swapped(take(kept.pop(k).astype(bf16)), "stream", bit)
                kept[k ^ bit] = kept[k ^ bit].astype(f32) + got.astype(f32)
                give(got)

    def token_part(i, count):
        if i == 0:
            box["sending"] = box["kept"].pop(2).astype(bf16)
            box["arrived"] = []
        low, high = rows * i // count // 16 * 16, rows * (i + 1) // count // 16 * 16
        box["arrived"].append(swapped(take(box["sending"][low:high]), "stream", 2))
        give(box["arrived"][i])
        if i + 1 == count:
            box["kept"][0] = box["kept"][0] + jnp.concatenate(box["arrived"], axis=0).astype(f32)

    def sums(axis, bit):
        if "states" not in box:
            mine = jnp.where(index["holds"], cut(box["final"], index["share"], share, 1), 0.0)
            box["states"] = {k: mine[k * per : (k + 1) * per] for k in range(slots)}
        states, summed = box["states"], box["summed"][:6]
        going = [k for k in sorted(states) if k & bit] if axis == "stream" else []
        if going:
            row = jnp.concatenate([states[k] for k in going], axis=1)
            row = jnp.pad(row, ((0, 0), (0, model - row.shape[1])))
            summed = jnp.concatenate([summed, row], axis=0)
        got = swapped(take(summed), axis, bit)
        box["summed"] = box["summed"][:6] + got[:6]
        for i, k in enumerate(going):
            states.pop(k)
            states[k ^ bit] = states[k ^ bit] + got[6:, i * share : (i + 1) * share]

    def assemble():
        box["outputs"], box["direct"] = call(
            functools.partial(assemble_kernel, slots, width),
            [jax.ShapeDtypeStruct((per, span, model), bf16)] * 2,
            [index["where"], *[take(box["moved", k]) for k in range(slots)]],
            scalars=1,
        )

    part = functools.partial
    if dealing:
        early = [
            [part(far_tokens, 0)],
            [near_tokens, part(far_tokens, 1), part(passed_tokens, 0), messages],
            [part(passed_tokens, 1), out_grads, normalise],
        ]
    else:
        early = [[everyones_tokens], [messages], [out_grads, normalise]]
    early.append([from_others] + ([begin] if depth % 128 == 0 else []))
    deal()
    if dealing:
        ahead_tokens()
    rounds.turn()
    for step in range(1, far + 1):
        gather(step)
        for other in early[step - 1] if step <= len(early) else ():
            other()
        rounds.turn()
    if depth % 128:
        begin()
    first()
    rounds.turn()
    join_rest()
    rounds.turn()
    second()
    late = [
        [part(moved, range(slots)[:3])],
        [part(moved, range(slots)[3:]), token_grads],
        [part(token_sends, 1), part(sums, "stream", 1), part(sums, "seq", 1)],
        [part(sums, "seq", 2), assemble],
    ]
    if dealing:
        late[3] += [part(token_part, 0, 2), part(token_part, 1, 2)]
    else:
        late[3] += [part(token_sends, bit) for bit in bits[1:]]
    for step in range(1, far + 1):
        scatter(step)
        for other in late[step - 1] if step <= len(late) else ():
            other()
        rounds.turn()
    total = box["mine"][0] + box["up"].astype(f32) + box["down"].astype(f32)
    box["total"] = total[:, :width], total[:, width:]
    weight_grad = stored()
    for bit in seq_bits[2:]:
        sums("seq", bit)
    for bit in bits[1:]:
        sums("stream", bit)

    grad_normed = box["kept"][0]
    source = inputs.astype(f32).reshape(rows, model)
    scale = box["scales"][:rows, :1]
    scaled = (source - box["means"][:rows, :1]) * scale
    grad_scaled = grad_normed * norm_gain
    grad_source = scale * (
        grad_scaled
        - jnp.mean(grad_scaled, axis=1, keepdims=True)
        - scaled * jnp.mean(grad_scaled * scaled, axis=1, keepdims=True)
    )
    input_grad = (grad_source.reshape(per, span, model) + box["direct"].astype(f32)).astype(bf16)
    outputs, final_state, summed = box["outputs"], box["states"][0], box["summed"]

    return (
        outputs,
        final_state,
        input_grad,
        weight_grad,
        summed[0],
        summed[1],
        summed[2],
        summed[3],
        summed[4],
        summed[5],
    )


def solution(mesh):
    return jax.shard_map(
        local,
        mesh=mesh,
        in_specs=(
            P("stream", "seq", None),
            P("stream", None),
            P("stream"),
            P("seq", "stream"),
            P(),
            P(),
            P(),
            P(),
            P(),
            P(),
            P("stream", "seq", None),
        ),
        out_specs=(
            P("stream", "seq", None),
            P("stream", "seq"),
            P("stream", "seq", None),
            P("seq", "stream"),
            P(),
            P(),
            P(),
            P(),
            P(),
            P(),
        ),
        check_vma=False,
    )
```

time: 248 us -> 218 us (0.88)
  local copies, waits for them, and re-layouts: 39.1 us -> 3.61 us
  waiting for transfers between devices: 101 us -> 116 us
  Pallas kernels: 51 us -> 44.8 us
    unnamed x127 -> x21, local copies, waits for them, and re-layouts: 30 us -> 1.03 us
    ppermute x16, waiting for transfers between devices: 23.9 us -> 43.8 us  [along_ring(): lax.ppermute(value, 'seq', [(order[i], order[(i + steps) % count]) for i...]
    pallas_call x14 -> x15, Pallas kernels: 51 us -> 44.8 us  [call(): pl.pallas_call(kernel, out_shape=jax.tree.map(lambda out: pltpu.VMEM(out....]
    ppermute x27, waiting for transfers between devices: 73.2 us -> 70.6 us  [swapped(): lax.ppermute(value, axis, [(i, i ^ bit) for i in range(lax.axis_size(axis...]
  transfers between devices with their start and end apart: 45 -> 45, of which waited for: 25 -> 31; matrix products, arithmetic and copies ran while one was open for 6% -> 4% of each run, Pallas kernels for 13% -> 15%
where the time goes in v3:
time: 218 us
  waiting for transfers between devices  116 us (53%)
  Pallas kernels  44.8 us (21%)
  starting transfers between devices  44.5 us (20%)
  other arithmetic  7.37 us (3%)
  local copies, waits for them, and re-layouts  3.61 us (2%)
    ppermute x27, waiting for transfers between devices, swapped(): lax.ppermute(value, axis, [(i, i ^ bit) for i in range(lax.axis_size(axis...  70.6 us
    pallas_call x15, Pallas kernels, call(): pl.pallas_call(kernel, out_shape=jax.tree.map(lambda out: pltpu.VMEM(out....  44.8 us
    ppermute x16, waiting for transfers between devices, along_ring(): lax.ppermute(value, 'seq', [(order[i], order[(i + steps) % count]) for i...  43.8 us
    ppermute x27, starting transfers between devices, swapped(): lax.ppermute(value, axis, [(i, i ^ bit) for i in range(lax.axis_size(axis...  22 us
    ppermute x16, starting transfers between devices, along_ring(): lax.ppermute(value, 'seq', [(order[i], order[(i + steps) % count]) for i...  17.8 us
  transfers between devices with their start and end apart: 45, of which 31 were waited for; matrix products, arithmetic and copies ran while one was open for 4% of the time, Pallas kernels for 15%

profile of v3, /device:TPU:0, one launch (start us, length us, event | category | flops | bytes accessed | tf_op | source)
XLA Modules:
  0.0 217.9 jit_solution(1799179041709511798)
XLA Ops:
  3.0 2.6 %collective-permute-start.1 = (bf16[256,512]{1,0:T(8,128)(2,1)S(1)}, bf16[256,512]{1,0:T(8,128)(2,1)S(1)}, u32[]{:S(2)}, u32[]{:S(2)}) collective-permute-start(bf16[256,512]{1,0:T(8,128)(2,1)S(1)} %get-tuple-element.223), channel_id=1, source_target_pairs={{0,2},{1,3},{2,0},{3,1},{4,6},{5,7},{6,4},{7,5},{8,10},{9,11},{10,... | collective-permute-start | bytes 786440 | tf_op jit(solution)/shard_map/ppermute | solution.py:80
  6.7 3.4 %collective-permute-start.2 = (bf16[2,2048]{1,0:T(2,128)(2,1)S(1)}, bf16[2,2048]{1,0:T(2,128)(2,1)S(1)}, u32[]{:S(2)}, u32[]{:S(2)}) collective-permute-start(bf16[2,2048]{1,0:T(2,128)(2,1)S(1)} %slice_bitcast_fusion.1), channel_id=1, source_target_pairs={{0,4},{4,8},{8,12},{12,16},{16,20},{20,24},{24,28},{1,5},{5,9},{9,... | collective-permute-start | bytes 24584 | tf_op jit(solution)/shard_map/ppermute | solution.py:618
  10.1 2.4 %collective-permute-done.1 = bf16[256,512]{1,0:T(8,128)(2,1)S(1)} collective-permute-done((bf16[256,512]{1,0:T(8,128)(2,1)S(1)}, bf16[256,512]{1,0:T(8,128)(2,1)S(1)}, u32[]{:S(2)}, u32[]{:S(2)}) %collective-permute-start.1) | collective-permute-done | bytes 262176 | tf_op jit(solution)/shard_map/ppermute | solution.py:80
  12.6 2.1 collective-permute-start.3
  14.8 1.8 collective-permute-start.5
  16.9 11.0 %collective-permute-done.5.refs_2_.refs_11_ = bf16[128,2048]{1,0:T(8,128)(2,1)S(1)} collective-permute-done((bf16[128,2048]{1,0:T(8,128)(2,1)S(1)}, bf16[128,2048]{1,0:T(8,128)(2,1)S(1)}, u32[]{:S(2)}, u32[]{:S(2)}) %collective-permute-start.5) | collective-permute-done | bytes 524320 | tf_op jit(solution)/shard_map/ppermute | solution.py:80
  27.9 4.0 %collective-permute-done.3.refs_1_ = bf16[256,1536]{1,0:T(8,128)(2,1)S(1)} collective-permute-done((bf16[256,1536]{1,0:T(8,128)(2,1)S(1)}, bf16[256,1536]{1,0:T(8,128)(2,1)S(1)}, u32[]{:S(2)}, u32[]{:S(2)}) %collective-permute-start.3) | collective-permute-done | bytes 786464 | tf_op jit(solution)/shard_map/ppermute | solution.py:63
  31.9 1.3 collective-permute-done.4.refs_2_
  33.7 1.6 collective-permute-start.6
  35.4 1.6 collective-permute-start.9
  38.9 11.7 %collective-permute-done.9.refs_3_.refs_12_ = bf16[144,2048]{1,0:T(8,128)(2,1)S(1)} collective-permute-done((bf16[144,2048]{1,0:T(8,128)(2,1)S(1)}, bf16[144,2048]{1,0:T(8,128)(2,1)S(1)}, u32[]{:S(2)}, u32[]{:S(2)}) %collective-permute-start.9) | collective-permute-done | bytes 589856 | tf_op jit(solution)/shard_map/ppermute | solution.py:80
  50.6 2.6 %collective-permute-done.7.refs_4_ = bf16[256,1536]{1,0:T(8,128)(2,1)S(1)} collective-permute-done((bf16[256,1536]{1,0:T(8,128)(2,1)S(1)}, bf16[256,1536]{1,0:T(8,128)(2,1)S(1)}, u32[]{:S(2)}, u32[]{:S(2)}) %collective-permute-start.7) | collective-permute-done | bytes 786464 | tf_op jit(solution)/shard_map/ppermute | solution.py:63
  53.4 1.6 collective-permute-start.12
  55.0 1.5 collective-permute-start.16
  57.7 5.2 %collective-permute-done.12.refs_4_.refs_2_ = bf16[272,512]{1,0:T(8,128)(2,1)S(1)} collective-permute-done((bf16[272,512]{1,0:T(8,128)(2,1)S(1)}, bf16[272,512]{1,0:T(8,128)(2,1)S(1)}, u32[]{:S(2)}, u32[]{:S(2)}) %collective-permute-start.12) | collective-permute-done | bytes 278560 | tf_op jit(solution)/shard_map/ppermute | solution.py:80
  62.9 5.0 %collective-permute-done.13.refs_5_.refs_3_ = bf16[272,512]{1,0:T(8,128)(2,1)S(1)} collective-permute-done((bf16[272,512]{1,0:T(8,128)(2,1)S(1)}, bf16[272,512]{1,0:T(8,128)(2,1)S(1)}, u32[]{:S(2)}, u32[]{:S(2)}) %collective-permute-start.13) | collective-permute-done | bytes 278560 | tf_op jit(solution)/shard_map/ppermute | solution.py:80
  68.0 3.7 %shard_map.187 = (bf16[1088,2048]{1,0:T(8,128)(2,1)S(1)}, f32[1024,128]{1,0:T(8,128)S(1)}, f32[1024,128]{1,0:T(8,128)S(1)}, bf16[1024,512]{1,0:T(8,128)(2,1)S(1)}) custom-call(s32[6]{0:T(128)S(1)} %stack.116.place, bf16[272,2048]{1,0:T(8,128)(2,1)S(1)} %maximum_maximum_fusion.refs_0_.refs_9_, bf16[272,2048]{1,0:T(8,128)(2,1)S(1)} %collective-permute-done.8.refs_1_.refs_10_, ...), custom_call_target="tpu_custom_call" | custom-call | tf_op jit(solution)/shard_map/pallas_call | solution.py:27
  71.7 3.0 %collective-permute-done.16.refs_6_ = bf16[256,1536]{1,0:T(8,128)(2,1)S(1)} collective-permute-done((bf16[256,1536]{1,0:T(8,128)(2,1)S(1)}, bf16[256,1536]{1,0:T(8,128)(2,1)S(1)}, u32[]{:S(2)}, u32[]{:S(2)}) %collective-permute-start.16) | collective-permute-done | bytes 786464 | tf_op jit(solution)/shard_map/ppermute | solution.py:63
  75.9 1.6 collective-permute-start.18
  78.3 6.8 %shard_map.188.begun = f32[1088,1536]{1,0:T(8,128)S(1)} custom-call(s32[8]{0:T(128)S(1)} %stack.120.sources, bf16[1088,2048]{1,0:T(8,128)(2,1)S(1)} %get-tuple-element.141.normed, bf16[256,1536]{1,0:T(8,128)(2,1)S(1)} %pad_maximum_fusion.1.refs_0_, bf16[256,1536]{1,0:T(8,128)(2,1)S(1)} %collective-permute-done.3.refs_1_, ...), custom_call_target="tpu_custom_call" | custom-call | tf_op jit(solution)/shard_map/pallas_call | solution.py:27
  85.9 1.6 collective-permute-done.17.refs_0_.refs_7_
  87.5 4.1 %shard_map.189 = (f32[3,4,1088,128]{3,2,1,0:T(8,128)S(1)}, f32[3,8,512]{2,1,0:T(8,128)S(1)}, f32[4,8,512]{2,1,0:T(8,128)S(1)}) custom-call(s32[8]{0:T(128)S(1)} %stack.120.sources, s32[6]{0:T(128)S(1)} %stack.116.place, bf16[1088,2048]{1,0:T(8,128)(2,1)S(1)} %get-tuple-element.141.normed, f32[8,512]{1,0:T(8,128)S(1)} %pad_maximum_fusion.7.start, ...), custom_call_target="tpu_custom_call" | custom-call | tf_op jit(solution)/shard_map/pallas_call | solution.py:27
  91.6 1.6 collective-permute-start.19
  93.2 2.5 %collective-permute-done.19 = f32[3,8,512]{2,1,0:T(8,128)S(1)} collective-permute-done((f32[3,8,512]{2,1,0:T(8,128)S(1)}, f32[3,8,512]{2,1,0:T(8,128)S(1)}, u32[]{:S(2)}, u32[]{:S(2)}) %collective-permute-start.19) | collective-permute-done | bytes 49184 | tf_op jit(solution)/shard_map/ppermute | solution.py:80
  96.9 3.5 %collective-permute-done.20 = f32[3,8,512]{2,1,0:T(8,128)S(1)} collective-permute-done((f32[3,8,512]{2,1,0:T(8,128)S(1)}, f32[3,8,512]{2,1,0:T(8,128)S(1)}, u32[]{:S(2)}, u32[]{:S(2)}) %collective-permute-start.20) | collective-permute-done | bytes 49184 | tf_op jit(solution)/shard_map/ppermute | solution.py:80
  103.0 3.0 %collective-permute-done.21 = f32[3,8,512]{2,1,0:T(8,128)S(1)} collective-permute-done((f32[3,8,512]{2,1,0:T(8,128)S(1)}, f32[3,8,512]{2,1,0:T(8,128)S(1)}, u32[]{:S(2)}, u32[]{:S(2)}) %collective-permute-start.21) | collective-permute-done | bytes 49184 | tf_op jit(solution)/shard_map/ppermute | solution.py:80
  106.1 1.8 collective-permute-done.22.linked
  107.8 8.8 %shard_map.190 = (bf16[1088,1536]{1,0:T(8,128)(2,1)S(1)}, bf16[2,2,128,512]{3,2,1,0:T(8,128)(2,1)S(1)}, bf16[2,2,128,512]{3,2,1,0:T(8,128)(2,1)S(1)}, bf16[2,2,1...) custom-call(s32[6]{0:T(128)S(1)} %stack.116.place, ...), custom_call_target="tpu_custom_call" | custom-call | tf_op jit(solution)/shard_map/pallas_call | solution.py:27
  117.3 1.8 shard_map.191
  120.3 1.7 collective-permute-start.24
  122.0 2.8 %shard_map.192 = (f32[256,1536]{1,0:T(8,128)S(1)}, f32[256,1536]{1,0:T(8,128)S(1)}) custom-call(s32[8]{0:T(128)S(1)} %stack.109.owners, s32[6]{0:T(128)S(1)} %stack.116.place, bf16[1088,2048]{1,0:T(8,128)(2,1)S(1)} %get-tuple-element.141.normed, bf16[1088,1536]{1,0:T(8,128)(2,1)S(1)} %get-tuple-element.201.grads), custom_call_target="tpu_custom_call" | custom-call | tf_op jit(solution)/shard_map/pallas_call | solution.py:27
  124.8 6.6 %collective-permute-done.23.up = bf16[128,1536]{1,0:T(8,128)(2,1)S(1)} collective-permute-done((bf16[128,1536]{1,0:T(8,128)(2,1)S(1)}, bf16[128,1536]{1,0:T(8,128)(2,1)S(1)}, u32[]{:S(2)}, u32[]{:S(2)}) %collective-permute-start.23) | collective-permute-done | bytes 393248 | tf_op jit(solution)/shard_map/ppermute | solution.py:63
  131.6 2.2 %collective-permute-start.28 = (bf16[256,1536]{1,0:T(8,128)(2,1)S(1)}, bf16[256,1536]{1,0:T(8,128)(2,1)S(1)}, u32[]{:S(2)}, u32[]{:S(2)}) collective-permute-start(bf16[256,1536]{1,0:T(8,128)(2,1)S(1)} %get-tuple-element.167), channel_id=1, source_target_pairs={{0,4},{8,0},{16,8},{24,16},{28,24},{20,28},{12,20},{4,12},{1,5},{9... | collective-permute-start | bytes 2359304 | tf_op jit(solution)/shard_map/ppermute | solution.py:63
  133.9 2.8 %shard_map.193 = (f32[256,1536]{1,0:T(8,128)S(1)}, f32[256,1536]{1,0:T(8,128)S(1)}) custom-call(s32[8]{0:T(128)S(1)} %stack.109.owners, s32[6]{0:T(128)S(1)} %stack.116.place, bf16[1088,2048]{1,0:T(8,128)(2,1)S(1)} %get-tuple-element.141.normed, bf16[1088,1536]{1,0:T(8,128)(2,1)S(1)} %get-tuple-element.201.grads), custom_call_target="tpu_custom_call" | custom-call | tf_op jit(solution)/shard_map/pallas_call | solution.py:27
  136.7 7.5 %shard_map.196 = (f32[256,2048]{1,0:T(8,128)S(1)}, bf16[256,2048]{1,0:T(8,128)(2,1)S(1)}, bf16[256,2048]{1,0:T(8,128)(2,1)S(1)}, bf16[256,2048]{1,0:T(8,128)(2,1)S(1)}, f32[8,2048]{1,0:T(8,128)S(1)}) custom-call(s32[8]{0:T(128)S(1)} %stack.120.sources, s32[6]{0:T(128)S(1)} %stack.116.place, bf16[1088,1536]{1,0:T(8,128)(2,1)S(1)} %get-tuple-element.201.grads, ...), custom_call_target="tpu_custom_call" | custom-call | tf_op jit(solution)/shard_map/pallas_call | solution.py:27
  144.2 3.8 %collective-permute-done.29.refs_3_ = bf16[2,2,128,512]{3,2,1,0:T(8,128)(2,1)S(1)} collective-permute-done((bf16[2,2,128,512]{3,2,1,0:T(8,128)(2,1)S(1)}, bf16[2,2,128,512]{3,2,1,0:T(8,128)(2,1)S(1)}, u32[]{:S(2)}, u32[]{:S(2)}) %collective-permute-start.29) | collective-permute-done | bytes 524320 | tf_op jit(solution)/shard_map/ppermute | solution.py:80
  148.0 2.8 %collective-permute-done.28.down = bf16[256,1536]{1,0:T(8,128)(2,1)S(1)} collective-permute-done((bf16[256,1536]{1,0:T(8,128)(2,1)S(1)}, bf16[256,1536]{1,0:T(8,128)(2,1)S(1)}, u32[]{:S(2)}, u32[]{:S(2)}) %collective-permute-start.28) | collective-permute-done | bytes 786464 | tf_op jit(solution)/shard_map/ppermute | solution.py:63
  150.8 1.9 collective-permute-done.27.up
  153.4 2.8 %shard_map.197 = (f32[256,1536]{1,0:T(8,128)S(1)}, f32[256,1536]{1,0:T(8,128)S(1)}) custom-call(s32[8]{0:T(128)S(1)} %stack.109.owners, s32[6]{0:T(128)S(1)} %stack.116.place, bf16[1088,2048]{1,0:T(8,128)(2,1)S(1)} %get-tuple-element.141.normed, bf16[1088,1536]{1,0:T(8,128)(2,1)S(1)} %get-tuple-element.201.grads), custom_call_target="tpu_custom_call" | custom-call | tf_op jit(solution)/shard_map/pallas_call | solution.py:27
  159.0 16.9 %collective-permute-done.31.down = bf16[256,1536]{1,0:T(8,128)(2,1)S(1)} collective-permute-done((bf16[256,1536]{1,0:T(8,128)(2,1)S(1)}, bf16[256,1536]{1,0:T(8,128)(2,1)S(1)}, u32[]{:S(2)}, u32[]{:S(2)}) %collective-permute-start.31) | collective-permute-done | bytes 786464 | tf_op jit(solution)/shard_map/ppermute | solution.py:63
  176.5 1.4 collective-permute-start.40
  179.9 2.9 %collective-permute-done.35 = f32[6,2048]{1,0:T(8,128)S(1)} collective-permute-done((f32[6,2048]{1,0:T(8,128)S(1)}, f32[6,2048]{1,0:T(8,128)S(1)}, u32[]{:S(2)}, u32[]{:S(2)}) %collective-permute-start.35) | collective-permute-done | bytes 49184 | tf_op jit(solution)/shard_map/ppermute | solution.py:80
  184.4 1.8 shard_map.200
  186.9 1.4 collective-permute-start.37
  191.3 9.1 %collective-permute-done.39 = bf16[128,2048]{1,0:T(8,128)(2,1)S(1)} collective-permute-done((bf16[128,2048]{1,0:T(8,128)(2,1)S(1)}, bf16[128,2048]{1,0:T(8,128)(2,1)S(1)}, u32[]{:S(2)}, u32[]{:S(2)}) %collective-permute-start.39) | collective-permute-done | bytes 524320 | tf_op jit(solution)/shard_map/ppermute | solution.py:80
  205.1 3.6 %collective-permute-done.41 = f32[6,2048]{1,0:T(8,128)S(1)} collective-permute-done((f32[6,2048]{1,0:T(8,128)S(1)}, f32[6,2048]{1,0:T(8,128)S(1)}, u32[]{:S(2)}, u32[]{:S(2)}) %collective-permute-start.41) | collective-permute-done | bytes 49184 | tf_op jit(solution)/shard_map/ppermute | solution.py:80
  211.0 2.3 %collective-permute-done.42 = f32[8,2048]{1,0:T(8,128)S(1)} collective-permute-done((f32[8,2048]{1,0:T(8,128)S(1)}, f32[8,2048]{1,0:T(8,128)S(1)}, u32[]{:S(2)}, u32[]{:S(2)}) %collective-permute-start.42) | collective-permute-done | bytes 65568 | tf_op jit(solution)/shard_map/ppermute | solution.py:80
  214.6 1.9 collective-permute-done.43
  (139 shorter events, 36.9 us)
Async XLA Ops:
  2.5 7.6 %collective-permute-start = (bf16[256,512]{1,0:T(8,128)(2,1)S(1)}, bf16[256,512]{1,0:T(8,128)(2,1)S(1)}, u32[]{:S(2)}, u32[]{:S(2)}) collective-permute-start(bf16[256,512]{1,0:T(8,128)(2,1)S(1)} %get-tuple-element.222), channel_id=1, source_target_pairs={{0,1},{1,0},{2,3},{3,2},{4,5},{5,4},{6,7},{7,6},{8,9},{9,8},{10,11... | collective-permute-start | bytes 786440 | tf_op jit(solution)/shard_map/ppermute | solution.py:80
  3.0 9.5 %collective-permute-start.1 = (bf16[256,512]{1,0:T(8,128)(2,1)S(1)}, bf16[256,512]{1,0:T(8,128)(2,1)S(1)}, u32[]{:S(2)}, u32[]{:S(2)}) collective-permute-start(bf16[256,512]{1,0:T(8,128)(2,1)S(1)} %get-tuple-element.223), channel_id=1, source_target_pairs={{0,2},{1,3},{2,0},{3,1},{4,6},{5,7},{6,4},{7,5},{8,10},{9,11},{10,... | collective-permute-start | bytes 786440 | tf_op jit(solution)/shard_map/ppermute | solution.py:80
  6.7 5.9 %collective-permute-start.2 = (bf16[2,2048]{1,0:T(2,128)(2,1)S(1)}, bf16[2,2048]{1,0:T(2,128)(2,1)S(1)}, u32[]{:S(2)}, u32[]{:S(2)}) collective-permute-start(bf16[2,2048]{1,0:T(2,128)(2,1)S(1)} %slice_bitcast_fusion.1), channel_id=1, source_target_pairs={{0,4},{4,8},{8,12},{12,16},{16,20},{20,24},{24,28},{1,5},{5,9},{9,... | collective-permute-start | bytes 24584 | tf_op jit(solution)/shard_map/ppermute | solution.py:618
  12.5 24.5 %copy-start = (bf16[2,128,2048]{2,1,0:T(8,128)(2,1)S(1)}, bf16[2,128,2048]{2,1,0:T(8,128)(2,1)}, u32[]{:S(2)}) copy-start(bf16[2,128,2048]{2,1,0:T(8,128)(2,1)} %param.21) | copy-start | bytes 3145732
  12.6 19.4 %collective-permute-start.3 = (bf16[256,1536]{1,0:T(8,128)(2,1)S(1)}, bf16[256,1536]{1,0:T(8,128)(2,1)S(1)}, u32[]{:S(2)}, u32[]{:S(2)}) collective-permute-start(bf16[256,1536]{1,0:T(8,128)(2,1)S(1)} %pad_maximum_fusion.1.refs_0_), channel_id=1, source_target_pairs={{0,8},{8,16},{16,24},{24,28},{28,20},{20,12},{12,4},{4,0},{1,9},{9... | collective-permute-start | bytes 2359304 | tf_op jit(solution)/shard_map/ppermute | solution.py:63
  14.7 18.6 %collective-permute-start.4 = (bf16[256,1536]{1,0:T(8,128)(2,1)S(1)}, bf16[256,1536]{1,0:T(8,128)(2,1)S(1)}, u32[]{:S(2)}, u32[]{:S(2)}) collective-permute-start(bf16[256,1536]{1,0:T(8,128)(2,1)S(1)} %pad_maximum_fusion.1.refs_0_), channel_id=1, source_target_pairs={{0,4},{8,0},{16,8},{24,16},{28,24},{20,28},{12,20},{4,12},{1,5},{9... | collective-permute-start | bytes 2359304 | tf_op jit(solution)/shard_map/ppermute | solution.py:63
  14.8 13.1 %collective-permute-start.5 = (bf16[128,2048]{1,0:T(8,128)(2,1)S(1)}, bf16[128,2048]{1,0:T(8,128)(2,1)S(1)}, u32[]{:S(2)}, u32[]{:S(2)}) collective-permute-start(bf16[128,2048]{1,0:T(8,128)(2,1)S(1)} %slice_bitcast_fusion), channel_id=1, source_target_pairs={{0,2},{1,3},{2,0},{3,1},{4,6},{5,7},{6,4},{7,5},{8,10},{9,11},{10,... | collective-permute-start | bytes 1572872 | tf_op jit(solution)/shard_map/ppermute | solution.py:80
  16.6 51.3 %copy-start.3 = (f32[2048]{0:T(1024)S(1)}, f32[2048]{0:T(1024)}, u32[]{:S(2)}) copy-start(f32[2048]{0:T(1024)} %param.19) | copy-start | bytes 24580
  16.6 51.4 %copy-start.7 = (f32[2048]{0:T(1024)S(1)}, f32[2048]{0:T(1024)}, u32[]{:S(2)}) copy-start(f32[2048]{0:T(1024)} %param.20) | copy-start | bytes 24580
  33.3 20.1 %collective-permute-start.8 = (bf16[272,2048]{1,0:T(8,128)(2,1)S(1)}, bf16[272,2048]{1,0:T(8,128)(2,1)S(1)}, u32[]{:S(2)}, u32[]{:S(2)}) collective-permute-start(bf16[272,2048]{1,0:T(8,128)(2,1)S(1)} %maximum_maximum_fusion.refs_0_.refs_9_), channel_id=1, source_target_pairs={{0,1},{1,0},{2,3},{3,2},{4,5},{5,4},{6,7},{7,6},{8,9},{9,8},{10,11... | collective-permute-start | bytes 3342344 | tf_op jit(solution)/shard_map/ppermute | solution.py:80
  33.3 20.0 %collective-permute-start.7 = (bf16[256,1536]{1,0:T(8,128)(2,1)S(1)}, bf16[256,1536]{1,0:T(8,128)(2,1)S(1)}, u32[]{:S(2)}, u32[]{:S(2)}) collective-permute-start(bf16[256,1536]{1,0:T(8,128)(2,1)S(1)} %collective-permute-done.4.refs_2_), channel_id=1, source_target_pairs={{0,4},{8,0},{16,8},{24,16},{28,24},{20,28},{12,20},{4,12},{1,5},{9... | collective-permute-start | bytes 2359304 | tf_op jit(solution)/shard_map/ppermute | solution.py:63
  33.7 19.7 %collective-permute-start.6 = (bf16[256,1536]{1,0:T(8,128)(2,1)S(1)}, bf16[256,1536]{1,0:T(8,128)(2,1)S(1)}, u32[]{:S(2)}, u32[]{:S(2)}) collective-permute-start(bf16[256,1536]{1,0:T(8,128)(2,1)S(1)} %collective-permute-done.3.refs_1_), channel_id=1, source_target_pairs={{0,8},{8,16},{16,24},{24,28},{28,20},{20,12},{12,4},{4,0},{1,9},{9... | collective-permute-start | bytes 2359304 | tf_op jit(solution)/shard_map/ppermute | solution.py:63
  35.4 15.2 %collective-permute-start.9 = (bf16[144,2048]{1,0:T(8,128)(2,1)S(1)}, bf16[144,2048]{1,0:T(8,128)(2,1)S(1)}, u32[]{:S(2)}, u32[]{:S(2)}) collective-permute-start(bf16[144,2048]{1,0:T(8,128)(2,1)S(1)} %slice.309), channel_id=1, source_target_pairs={{0,2},{1,3},{2,0},{3,1},{4,6},{5,7},{6,4},{7,5},{8,10},{9,11},{10,... | collective-permute-start | bytes 1769480 | tf_op jit(solution)/shard_map/ppermute | solution.py:80
  36.9 1.9 collective-permute-start.10
  53.4 3.7 %collective-permute-start.11 = (bf16[272,512]{1,0:T(8,128)(2,1)S(1)}, bf16[272,512]{1,0:T(8,128)(2,1)S(1)}, u32[]{:S(2)}, u32[]{:S(2)}) collective-permute-start(bf16[272,512]{1,0:T(8,128)(2,1)S(1)} %get-tuple-element.128), channel_id=1, source_target_pairs={{0,1},{1,0},{2,3},{3,2},{4,5},{5,4},{6,7},{7,6},{8,9},{9,8},{10,11... | collective-permute-start | bytes 835592 | tf_op jit(solution)/shard_map/ppermute | solution.py:80
  53.4 9.5 %collective-permute-start.12 = (bf16[272,512]{1,0:T(8,128)(2,1)S(1)}, bf16[272,512]{1,0:T(8,128)(2,1)S(1)}, u32[]{:S(2)}, u32[]{:S(2)}) collective-permute-start(bf16[272,512]{1,0:T(8,128)(2,1)S(1)} %get-tuple-element.130), channel_id=1, source_target_pairs={{0,2},{1,3},{2,0},{3,1},{4,6},{5,7},{6,4},{7,5},{8,10},{9,11},{10,... | collective-permute-start | bytes 835592 | tf_op jit(solution)/shard_map/ppermute | solution.py:80
  55.0 19.7 %collective-permute-start.16 = (bf16[256,1536]{1,0:T(8,128)(2,1)S(1)}, bf16[256,1536]{1,0:T(8,128)(2,1)S(1)}, u32[]{:S(2)}, u32[]{:S(2)}) collective-permute-start(bf16[256,1536]{1,0:T(8,128)(2,1)S(1)} %collective-permute-done.7.refs_4_), channel_id=1, source_target_pairs={{0,4},{8,0},{16,8},{24,16},{28,24},{20,28},{12,20},{4,12},{1,5},{9... | collective-permute-start | bytes 2359304 | tf_op jit(solution)/shard_map/ppermute | solution.py:63
  56.6 19.3 %collective-permute-start.15 = (bf16[256,1536]{1,0:T(8,128)(2,1)S(1)}, bf16[256,1536]{1,0:T(8,128)(2,1)S(1)}, u32[]{:S(2)}, u32[]{:S(2)}) collective-permute-start(bf16[256,1536]{1,0:T(8,128)(2,1)S(1)} %collective-permute-done.6.refs_3_), channel_id=1, source_target_pairs={{0,8},{8,16},{16,24},{24,28},{28,20},{20,12},{12,4},{4,0},{1,9},{9... | collective-permute-start | bytes 2359304 | tf_op jit(solution)/shard_map/ppermute | solution.py:63
  57.1 10.9 %collective-permute-start.14 = (bf16[144,2048]{1,0:T(8,128)(2,1)S(1)}, bf16[144,2048]{1,0:T(8,128)(2,1)S(1)}, u32[]{:S(2)}, u32[]{:S(2)}) collective-permute-start(bf16[144,2048]{1,0:T(8,128)(2,1)S(1)} %collective-permute-done.9.refs_3_.refs_12_), channel_id=1, source_target_pairs={{0,1},{1,0},{2,3},{3,2},{4,5},{5,4},{6,7},{7,6},{8,9},{9,8},{10,11... | collective-permute-start | bytes 1769480 | tf_op jit(solution)/shard_map/ppermute | solution.py:80
  57.1 10.8 %collective-permute-start.13 = (bf16[272,512]{1,0:T(8,128)(2,1)S(1)}, bf16[272,512]{1,0:T(8,128)(2,1)S(1)}, u32[]{:S(2)}, u32[]{:S(2)}) collective-permute-start(bf16[272,512]{1,0:T(8,128)(2,1)S(1)} %get-tuple-element.132), channel_id=1, source_target_pairs={{0,3},{1,2},{2,1},{3,0},{4,7},{5,6},{6,5},{7,4},{8,11},{9,10},{10,... | collective-permute-start | bytes 835592 | tf_op jit(solution)/shard_map/ppermute | solution.py:80
  75.9 10.0 %collective-permute-start.18 = (bf16[128,1536]{1,0:T(8,128)(2,1)S(1)}, bf16[128,1536]{1,0:T(8,128)(2,1)S(1)}, u32[]{:S(2)}, u32[]{:S(2)}) collective-permute-start(bf16[128,1536]{1,0:T(8,128)(2,1)S(1)} %slice.332), channel_id=1, source_target_pairs={{0,4},{8,0},{16,8},{24,16},{28,24},{20,28},{12,20},{4,12},{1,5},{9... | collective-permute-start | bytes 1179656 | tf_op jit(solution)/shard_map/ppermute | solution.py:63
  77.5 10.0 %collective-permute-start.17 = (bf16[128,1536]{1,0:T(8,128)(2,1)S(1)}, bf16[128,1536]{1,0:T(8,128)(2,1)S(1)}, u32[]{:S(2)}, u32[]{:S(2)}) collective-permute-start(bf16[128,1536]{1,0:T(8,128)(2,1)S(1)} %slice.331), channel_id=1, source_target_pairs={{0,8},{8,16},{16,24},{24,28},{28,20},{20,12},{12,4},{4,0},{1,9},{9... | collective-permute-start | bytes 1179656 | tf_op jit(solution)/shard_map/ppermute | solution.py:63
  91.6 4.2 %collective-permute-start.19 = (f32[3,8,512]{2,1,0:T(8,128)S(1)}, f32[3,8,512]{2,1,0:T(8,128)S(1)}, u32[]{:S(2)}, u32[]{:S(2)}) collective-permute-start(f32[3,8,512]{2,1,0:T(8,128)S(1)} %get-tuple-element.144), channel_id=1, source_target_pairs={{0,4},{4,0},{8,12},{12,8},{16,20},{20,16},{24,28},{28,24},{1,5},{5... | collective-permute-start | bytes 147464 | tf_op jit(solution)/shard_map/ppermute | solution.py:80
  95.8 4.6 %collective-permute-start.20 = (f32[3,8,512]{2,1,0:T(8,128)S(1)}, f32[3,8,512]{2,1,0:T(8,128)S(1)}, u32[]{:S(2)}, u32[]{:S(2)}) collective-permute-start(f32[3,8,512]{2,1,0:T(8,128)S(1)} %pad_maximum_fusion.3), channel_id=1, source_target_pairs={{0,8},{4,12},{8,0},{12,4},{16,24},{20,28},{24,16},{28,20},{1,9},{5... | collective-permute-start | bytes 147464 | tf_op jit(solution)/shard_map/ppermute | solution.py:80
  100.4 5.6 %collective-permute-start.21 = (f32[3,8,512]{2,1,0:T(8,128)S(1)}, f32[3,8,512]{2,1,0:T(8,128)S(1)}, u32[]{:S(2)}, u32[]{:S(2)}) collective-permute-start(f32[3,8,512]{2,1,0:T(8,128)S(1)} %pad_maximum_fusion.4), channel_id=1, source_target_pairs={{0,16},{4,20},{8,24},{12,28},{16,0},{20,4},{24,8},{28,12},{1,17},{... | collective-permute-start | bytes 147464 | tf_op jit(solution)/shard_map/ppermute | solution.py:80
  101.7 6.1 %collective-permute-start.22 = (f32[4,8,512]{2,1,0:T(8,128)S(1)}, f32[4,8,512]{2,1,0:T(8,128)S(1)}, u32[]{:S(2)}, u32[]{:S(2)}) collective-permute-start(f32[4,8,512]{2,1,0:T(8,128)S(1)} %get-tuple-element.151), channel_id=1, source_target_pairs={{4,0},{8,4},{12,8},{16,12},{20,16},{24,20},{28,24},{5,1},{9,5},{13... | collective-permute-start | bytes 196616 | tf_op jit(solution)/shard_map/ppermute | solution.py:742
  116.7 15.0 %collective-permute-start.25 = (bf16[2,2,128,512]{3,2,1,0:T(8,128)(2,1)S(1)}, bf16[2,2,128,512]{3,2,1,0:T(8,128)(2,1)S(1)}, u32[]{:S(2)}, u32[]{:S(2)}) collective-permute-start(bf16[2,2,128,512]{3,2,1,0:T(8,128)(2,1)S(1)} %get-tuple-element.159), channel_id=1, source_target_pairs={{0,1},{1,0},{2,3},{3,2},{4,5},{5,4},{6,7},{7,6},{8,9},{9,8},{10,11... | collective-permute-start | bytes 1572872 | tf_op jit(solution)/shard_map/ppermute | solution.py:80
  116.7 14.9 %collective-permute-start.26 = (bf16[2,2,128,512]{3,2,1,0:T(8,128)(2,1)S(1)}, bf16[2,2,128,512]{3,2,1,0:T(8,128)(2,1)S(1)}, u32[]{:S(2)}, u32[]{:S(2)}) collective-permute-start(bf16[2,2,128,512]{3,2,1,0:T(8,128)(2,1)S(1)} %get-tuple-element.160), channel_id=1, source_target_pairs={{0,2},{1,3},{2,0},{3,1},{4,6},{5,7},{6,4},{7,5},{8,10},{9,11},{10,... | collective-permute-start | bytes 1572872 | tf_op jit(solution)/shard_map/ppermute | solution.py:80
  119.1 12.3 %collective-permute-start.23 = (bf16[128,1536]{1,0:T(8,128)(2,1)S(1)}, bf16[128,1536]{1,0:T(8,128)(2,1)S(1)}, u32[]{:S(2)}, u32[]{:S(2)}) collective-permute-start(bf16[128,1536]{1,0:T(8,128)(2,1)S(1)} %get-tuple-element.220), channel_id=1, source_target_pairs={{0,8},{8,16},{16,24},{24,28},{28,20},{20,12},{12,4},{4,0},{1,9},{9... | collective-permute-start | bytes 1179656 | tf_op jit(solution)/shard_map/ppermute | solution.py:63
  120.3 11.1 %collective-permute-start.24 = (bf16[128,1536]{1,0:T(8,128)(2,1)S(1)}, bf16[128,1536]{1,0:T(8,128)(2,1)S(1)}, u32[]{:S(2)}, u32[]{:S(2)}) collective-permute-start(bf16[128,1536]{1,0:T(8,128)(2,1)S(1)} %get-tuple-element.219), channel_id=1, source_target_pairs={{0,4},{8,0},{16,8},{24,16},{28,24},{20,28},{12,20},{4,12},{1,5},{9... | collective-permute-start | bytes 1179656 | tf_op jit(solution)/shard_map/ppermute | solution.py:63
  131.6 19.1 %collective-permute-start.28 = (bf16[256,1536]{1,0:T(8,128)(2,1)S(1)}, bf16[256,1536]{1,0:T(8,128)(2,1)S(1)}, u32[]{:S(2)}, u32[]{:S(2)}) collective-permute-start(bf16[256,1536]{1,0:T(8,128)(2,1)S(1)} %get-tuple-element.167), channel_id=1, source_target_pairs={{0,4},{8,0},{16,8},{24,16},{28,24},{20,28},{12,20},{4,12},{1,5},{9... | collective-permute-start | bytes 2359304 | tf_op jit(solution)/shard_map/ppermute | solution.py:63
  133.9 18.8 %collective-permute-start.27 = (bf16[256,1536]{1,0:T(8,128)(2,1)S(1)}, bf16[256,1536]{1,0:T(8,128)(2,1)S(1)}, u32[]{:S(2)}, u32[]{:S(2)}) collective-permute-start(bf16[256,1536]{1,0:T(8,128)(2,1)S(1)} %get-tuple-element.165), channel_id=1, source_target_pairs={{0,8},{8,16},{16,24},{24,28},{28,20},{20,12},{12,4},{4,0},{1,9},{9... | collective-permute-start | bytes 2359304 | tf_op jit(solution)/shard_map/ppermute | solution.py:63
  133.9 14.2 %collective-permute-start.29 = (bf16[2,2,128,512]{3,2,1,0:T(8,128)(2,1)S(1)}, bf16[2,2,128,512]{3,2,1,0:T(8,128)(2,1)S(1)}, u32[]{:S(2)}, u32[]{:S(2)}) collective-permute-start(bf16[2,2,128,512]{3,2,1,0:T(8,128)(2,1)S(1)} %get-tuple-element.170), channel_id=1, source_target_pairs={{0,3},{1,2},{2,1},{3,0},{4,7},{5,6},{6,5},{7,4},{8,11},{9,10},{10,... | collective-permute-start | bytes 1572872 | tf_op jit(solution)/shard_map/ppermute | solution.py:80
  152.7 5.9 %collective-permute-start.32 = (bf16[256,2048]{1,0:T(8,128)(2,1)S(1)}, bf16[256,2048]{1,0:T(8,128)(2,1)S(1)}, u32[]{:S(2)}, u32[]{:S(2)}) collective-permute-start(bf16[256,2048]{1,0:T(8,128)(2,1)S(1)} %get-tuple-element.182), channel_id=1, source_target_pairs={{0,1},{1,0},{2,3},{3,2},{4,5},{5,4},{6,7},{7,6},{8,9},{9,8},{10,11... | collective-permute-start | bytes 3145736 | tf_op jit(solution)/shard_map/ppermute | solution.py:80
  152.8 23.7 %collective-permute-start.33 = (bf16[256,2048]{1,0:T(8,128)(2,1)S(1)}, bf16[256,2048]{1,0:T(8,128)(2,1)S(1)}, u32[]{:S(2)}, u32[]{:S(2)}) collective-permute-start(bf16[256,2048]{1,0:T(8,128)(2,1)S(1)} %get-tuple-element.184), channel_id=1, source_target_pairs={{0,1},{1,0},{2,3},{3,2},{4,5},{5,4},{6,7},{7,6},{8,9},{9,8},{10,11... | collective-permute-start | bytes 3145736 | tf_op jit(solution)/shard_map/ppermute | solution.py:80
  156.5 19.5 %collective-permute-start.31 = (bf16[256,1536]{1,0:T(8,128)(2,1)S(1)}, bf16[256,1536]{1,0:T(8,128)(2,1)S(1)}, u32[]{:S(2)}, u32[]{:S(2)}) collective-permute-start(bf16[256,1536]{1,0:T(8,128)(2,1)S(1)} %get-tuple-element.177), channel_id=1, source_target_pairs={{0,4},{8,0},{16,8},{24,16},{28,24},{20,28},{12,20},{4,12},{1,5},{9... | collective-permute-start | bytes 2359304 | tf_op jit(solution)/shard_map/ppermute | solution.py:63
  157.3 19.2 %collective-permute-start.30 = (bf16[256,1536]{1,0:T(8,128)(2,1)S(1)}, bf16[256,1536]{1,0:T(8,128)(2,1)S(1)}, u32[]{:S(2)}, u32[]{:S(2)}) collective-permute-start(bf16[256,1536]{1,0:T(8,128)(2,1)S(1)} %get-tuple-element.175), channel_id=1, source_target_pairs={{0,8},{8,16},{16,24},{24,28},{28,20},{20,12},{12,4},{4,0},{1,9},{9... | collective-permute-start | bytes 2359304 | tf_op jit(solution)/shard_map/ppermute | solution.py:63
  158.5 19.9 %collective-permute-start.34 = (f32[8,2048]{1,0:T(8,128)S(1)}, f32[8,2048]{1,0:T(8,128)S(1)}, u32[]{:S(2)}, u32[]{:S(2)}) collective-permute-start(f32[8,2048]{1,0:T(8,128)S(1)} %pad_maximum_fusion.2), channel_id=1, source_target_pairs={{0,1},{1,0},{2,3},{3,2},{4,5},{5,4},{6,7},{7,6},{8,9},{9,8},{10,11... | collective-permute-start | bytes 196616 | tf_op jit(solution)/shard_map/ppermute | solution.py:80
  176.5 14.9 %collective-permute-start.40 = (bf16[128,2048]{1,0:T(8,128)(2,1)S(1)}, bf16[128,2048]{1,0:T(8,128)(2,1)S(1)}, u32[]{:S(2)}, u32[]{:S(2)}) collective-permute-start(bf16[128,2048]{1,0:T(8,128)(2,1)S(1)} %get-tuple-element.204), channel_id=1, source_target_pairs={{0,2},{1,3},{2,0},{3,1},{4,6},{5,7},{6,4},{7,5},{8,10},{9,11},{10,... | collective-permute-start | bytes 1572872 | tf_op jit(solution)/shard_map/ppermute | solution.py:80
  177.9 22.5 %collective-permute-start.39 = (bf16[128,2048]{1,0:T(8,128)(2,1)S(1)}, bf16[128,2048]{1,0:T(8,128)(2,1)S(1)}, u32[]{:S(2)}, u32[]{:S(2)}) collective-permute-start(bf16[128,2048]{1,0:T(8,128)(2,1)S(1)} %get-tuple-element.203), channel_id=1, source_target_pairs={{0,2},{1,3},{2,0},{3,1},{4,6},{5,7},{6,4},{7,5},{8,10},{9,11},{10,... | collective-permute-start | bytes 1572872 | tf_op jit(solution)/shard_map/ppermute | solution.py:80
  178.5 4.3 %collective-permute-start.35 = (f32[6,2048]{1,0:T(8,128)S(1)}, f32[6,2048]{1,0:T(8,128)S(1)}, u32[]{:S(2)}, u32[]{:S(2)}) collective-permute-start(f32[6,2048]{1,0:T(8,128)S(1)} %slice_add_fusion.1), channel_id=1, source_target_pairs={{0,4},{4,0},{8,12},{12,8},{16,20},{20,16},{24,28},{28,24},{1,5},{5... | collective-permute-start | bytes 147464 | tf_op jit(solution)/shard_map/ppermute | solution.py:80
  182.8 7.1 %collective-permute-start.36 = (f32[6,2048]{1,0:T(8,128)S(1)}, f32[6,2048]{1,0:T(8,128)S(1)}, u32[]{:S(2)}, u32[]{:S(2)}) collective-permute-start(f32[6,2048]{1,0:T(8,128)S(1)} %add.306), channel_id=1, source_target_pairs={{0,8},{4,12},{8,0},{12,4},{16,24},{20,28},{24,16},{28,20},{1,9},{5... | collective-permute-start | bytes 147464 | tf_op jit(solution)/shard_map/ppermute | solution.py:80
  186.2 17.4 %collective-permute-start.38 = (bf16[256,1536]{1,0:T(8,128)(2,1)S(1)}, bf16[256,1536]{1,0:T(8,128)(2,1)S(1)}, u32[]{:S(2)}, u32[]{:S(2)}) collective-permute-start(bf16[256,1536]{1,0:T(8,128)(2,1)S(1)} %get-tuple-element.200), channel_id=1, source_target_pairs={{0,4},{8,0},{16,8},{24,16},{28,24},{20,28},{12,20},{4,12},{1,5},{9... | collective-permute-start | bytes 2359304 | tf_op jit(solution)/shard_map/ppermute | solution.py:63
  186.9 16.7 %collective-permute-start.37 = (bf16[256,1536]{1,0:T(8,128)(2,1)S(1)}, bf16[256,1536]{1,0:T(8,128)(2,1)S(1)}, u32[]{:S(2)}, u32[]{:S(2)}) collective-permute-start(bf16[256,1536]{1,0:T(8,128)(2,1)S(1)} %get-tuple-element.198), channel_id=1, source_target_pairs={{0,8},{8,16},{16,24},{24,28},{28,20},{20,12},{12,4},{4,0},{1,9},{9... | collective-permute-start | bytes 2359304 | tf_op jit(solution)/shard_map/ppermute | solution.py:63
  203.6 5.2 %collective-permute-start.41 = (f32[6,2048]{1,0:T(8,128)S(1)}, f32[6,2048]{1,0:T(8,128)S(1)}, u32[]{:S(2)}, u32[]{:S(2)}) collective-permute-start(f32[6,2048]{1,0:T(8,128)S(1)} %add.307), channel_id=1, source_target_pairs={{0,16},{4,20},{8,24},{12,28},{16,0},{20,4},{24,8},{28,12},{1,17},{... | collective-permute-start | bytes 147464 | tf_op jit(solution)/shard_map/ppermute | solution.py:80
  208.8 4.5 %collective-permute-start.42 = (f32[8,2048]{1,0:T(8,128)S(1)}, f32[8,2048]{1,0:T(8,128)S(1)}, u32[]{:S(2)}, u32[]{:S(2)}) collective-permute-start(f32[8,2048]{1,0:T(8,128)S(1)} %select_maximum_fusion), channel_id=1, source_target_pairs={{0,2},{1,3},{2,0},{3,1},{4,6},{5,7},{6,4},{7,5},{8,10},{9,11},{10,... | collective-permute-start | bytes 196616 | tf_op jit(solution)/shard_map/ppermute | solution.py:80
  210.0 6.4 %collective-permute-start.43 = (bf16[256,512]{1,0:T(8,128)(2,1)S(1)}, bf16[256,512]{1,0:T(8,128)(2,1)S(1)}, u32[]{:S(2)}, u32[]{:S(2)}) collective-permute-start(bf16[256,512]{1,0:T(8,128)(2,1)S(1)} %get-tuple-element.218), channel_id=1, source_target_pairs={{0,2},{1,3},{2,0},{3,1},{4,6},{5,7},{6,4},{7,5},{8,10},{9,11},{10,... | collective-permute-start | bytes 786440 | tf_op jit(solution)/shard_map/ppermute | solution.py:80
  211.0 3.5 %collective-permute-start.44 = (bf16[256,512]{1,0:T(8,128)(2,1)S(1)}, bf16[256,512]{1,0:T(8,128)(2,1)S(1)}, u32[]{:S(2)}, u32[]{:S(2)}) collective-permute-start(bf16[256,512]{1,0:T(8,128)(2,1)S(1)} %get-tuple-element.217), channel_id=1, source_target_pairs={{0,1},{1,0},{2,3},{3,2},{4,5},{5,4},{6,7},{7,6},{8,9},{9,8},{10,11... | collective-permute-start | bytes 786440 | tf_op jit(solution)/shard_map/ppermute | solution.py:80
  (7 other events, 90.8 us)

commit v4 on v3

--- a/solution.py
+++ b/solution.py
@@ -23,15 +23,16 @@
     return pl.BlockSpec(memory_space=pltpu.SMEM)
 
 
-def call(kernel, out_shape, operands, scratch=(), scalars=0, cost=0):
+def call(kernel, out_shape, operands, scratch=(), scalars=0, pinned=True):
+    held = jax.tree.map(lambda out: pltpu.VMEM(out.shape, out.dtype), out_shape)
     return pl.pallas_call(
         kernel,
-        out_shape=jax.tree.map(lambda out: pltpu.VMEM(out.shape, out.dtype), out_shape),
+        out_shape=held if pinned else out_shape,
         in_specs=[smem_spec()] * scalars + [vmem_spec()] * (len(operands) - scalars),
         out_specs=jax.tree.map(lambda _: vmem_spec(), out_shape),
         scratch_shapes=list(scratch),
         compiler_params=pltpu.CompilerParams(vmem_limit_bytes=lax.axis_size("stream") * ROOM),
-        cost_estimate=pl.CostEstimate(flops=int(cost * 1e9), bytes_accessed=0, transcendentals=0),
+        cost_estimate=pl.CostEstimate(flops=0, bytes_accessed=0, transcendentals=0),
     )(
         *operands[:scalars],
         *[pltpu.with_memory_space_constraint(x, pltpu.VMEM) for x in operands[scalars:]],
@@ -543,8 +544,10 @@
         own, rest = box["total"]
         near, distant = rest[:, :width], rest[:, width:]
         if dealing:
-            distant = swapped(distant.astype(bf16), "stream", 2).astype(f32)
-            near = swapped(near.astype(bf16), "stream", 1).astype(f32)
+            distant, near = distant.astype(bf16), near.astype(bf16)
+            rounds.before = [*rounds.before, distant, near]
+            distant = swapped(distant, "stream", 2).astype(f32)
+            near = swapped(near, "stream", 1).astype(f32)
             found = [jnp.where(even, own, distant), near, jnp.where(even, distant, own)]
         else:
             flat = lax.all_gather(
@@ -600,13 +603,17 @@
             sent = call(
                 functools.partial(merge_kernel, cuts_of),
                 [jax.ShapeDtypeStruct((depth, b - a), bf16) for a, b in cuts_of for _ in range(2)],
-                [*box["mine"], box["up"], box["down"]],
+                [*box["mine", step], box["up"], box["down"]],
             )
         came = [along_ring(take(value), 1 - 2 * (i % 2)) for i, value in enumerate(sent)]
+        rounds.before = [*rounds.before, *sent]
         box["up"], box["down"] = came
         give(*came)
-        box["mine"] = partials((far - step, step - far) if step < far else (0,), f32)
-        give(*box["mine"])
+
+    def sums_of(step):
+        distance = far + 1 - step
+        box["mine", step] = partials((distance, -distance) if distance else (0,), f32)
+        give(*box["mine", step])
 
     whole_part = [(0, rows + tail)]
     cuts = [(0, rows // 2), (rows // 2, rows + tail)]
@@ -849,18 +856,36 @@
             row = jnp.pad(row, ((0, 0), (0, model - row.shape[1])))
             summed = jnp.concatenate([summed, row], axis=0)
         got = swapped(take(summed), axis, bit)
+        give(got)
         box["summed"] = box["summed"][:6] + got[:6]
         for i, k in enumerate(going):
             states.pop(k)
             states[k ^ bit] = states[k ^ bit] + got[6:, i * share : (i + 1) * share]
 
     def assemble():
-        box["outputs"], box["direct"] = call(
+        box["outputs"], box["direct"] = found = call(
             functools.partial(assemble_kernel, slots, width),
             [jax.ShapeDtypeStruct((per, span, model), bf16)] * 2,
             [index["where"], *[take(box["moved", k]) for k in range(slots)]],
             scalars=1,
-        )
+            pinned=False,
+        )
+        give(*found)
+        give(*found)
+
+    def finish():
+        grad_normed = box["kept"][0]
+        source = inputs.astype(f32).reshape(rows, model)
+        scale = box["scales"][:rows, :1]
+        scaled = (source - box["means"][:rows, :1]) * scale
+        grad_scaled = grad_normed * norm_gain
+        grad_source = scale * (
+            grad_scaled
+            - jnp.mean(grad_scaled, axis=1, keepdims=True)
+            - scaled * jnp.mean(grad_scaled * scaled, axis=1, keepdims=True)
+        )
+        box["input_grad"] = (grad_source.reshape(per, span, model) + box["direct"].astype(f32)).astype(bf16)
+        give(box["input_grad"])
 
     part = functools.partial
     if dealing:
@@ -891,37 +916,35 @@
     late = [
         [part(moved, range(slots)[:3])],
         [part(moved, range(slots)[3:]), token_grads],
-        [part(token_sends, 1), part(sums, "stream", 1), part(sums, "seq", 1)],
-        [part(sums, "seq", 2), assemble],
+        [part(token_sends, 1)]
+        + [part(sums, "stream", bit) for bit in bits]
+        + [part(sums, "seq", 1)],
+        [part(sums, "seq", 2)],
     ]
+    for step in range(2, far + 2):
+        late_at = step - 2 if far > 4 or step < 3 else min(step - 3, 1)
+        while len(late) <= late_at:
+            late.append([])
+        late[late_at].insert(0, part(sums_of, step))
     if dealing:
-        late[3] += [part(token_part, 0, 2), part(token_part, 1, 2)]
+        late[2].append(part(token_part, 0, 2))
+        late[3] += [part(token_part, 1, 2)]
     else:
         late[3] += [part(token_sends, bit) for bit in bits[1:]]
+    late[2].append(assemble)
+    late[3].append(finish)
     for step in range(1, far + 1):
         scatter(step)
         for other in late[step - 1] if step <= len(late) else ():
             other()
         rounds.turn()
-    total = box["mine"][0] + box["up"].astype(f32) + box["down"].astype(f32)
+    total = box["mine", far + 1][0] + box["up"].astype(f32) + box["down"].astype(f32)
     box["total"] = total[:, :width], total[:, width:]
     weight_grad = stored()
     for bit in seq_bits[2:]:
         sums("seq", bit)
-    for bit in bits[1:]:
-        sums("stream", bit)
-
-    grad_normed = box["kept"][0]
-    source = inputs.astype(f32).reshape(rows, model)
-    scale = box["scales"][:rows, :1]
-    scaled = (source - box["means"][:rows, :1]) * scale
-    grad_scaled = grad_normed * norm_gain
-    grad_source = scale * (
-        grad_scaled
-        - jnp.mean(grad_scaled, axis=1, keepdims=True)
-        - scaled * jnp.mean(grad_scaled * scaled, axis=1, keepdims=True)
-    )
-    input_grad = (grad_source.reshape(per, span, model) + box["direct"].astype(f32)).astype(bf16)
+
+    input_grad = box["input_grad"]
     outputs, final_state, summed = box["outputs"], box["states"][0], box["summed"]
 
     return (

time: 218 us -> 207 us (0.950)
  waiting for transfers between devices: 116 us -> 107 us
    ppermute x27, waiting for transfers between devices: 70.6 us -> 62 us  [swapped(): lax.ppermute(value, axis, [(i, i ^ bit) for i in range(lax.axis_size(axis...]
  transfers between devices with their start and end apart: 45 -> 45, of which waited for: 31 -> 32; matrix products, arithmetic and copies ran while one was open for 4% -> 3% of each run, Pallas kernels for 15% -> 15%
where the time goes in v4:
time: 207 us; the launch traced here: 206 us
  waiting for transfers between devices  107 us (52%)
  Pallas kernels  45.8 us (22%)
  starting transfers between devices  42.4 us (20%)
  other arithmetic  7.34 us (4%)
  local copies, waits for them, and re-layouts  2.65 us (1%)
    ppermute x27, waiting for transfers between devices, swapped(): lax.ppermute(value, axis, [(i, i ^ bit) for i in range(lax.axis_size(axis...  62 us
    pallas_call x15, Pallas kernels, call(): pl.pallas_call(kernel, out_shape=held if pinned else out_shape, in_specs=...  45.8 us
    ppermute x16, waiting for transfers between devices, along_ring(): lax.ppermute(value, 'seq', [(order[i], order[(i + steps) % count]) for i...  43 us
    ppermute x27, starting transfers between devices, swapped(): lax.ppermute(value, axis, [(i, i ^ bit) for i in range(lax.axis_size(axis...  20.2 us
    ppermute x16, starting transfers between devices, along_ring(): lax.ppermute(value, 'seq', [(order[i], order[(i + steps) % count]) for i...  17.5 us
  transfers between devices with their start and end apart: 45, of which 32 were waited for; matrix products, arithmetic and copies ran while one was open for 3% of the time, Pallas kernels for 15%

profile of v4, /device:TPU:0, one launch (start us, length us, event | category | flops | bytes accessed | tf_op | source)
XLA Modules:
  0.0 206.4 jit_solution(16368710346243261788)
XLA Ops:
  3.0 2.6 %collective-permute-start.1 = (bf16[256,512]{1,0:T(8,128)(2,1)S(1)}, bf16[256,512]{1,0:T(8,128)(2,1)S(1)}, u32[]{:S(2)}, u32[]{:S(2)}) collective-permute-start(bf16[256,512]{1,0:T(8,128)(2,1)S(1)} %get-tuple-element.225), channel_id=1, source_target_pairs={{0,2},{1,3},{2,0},{3,1},{4,6},{5,7},{6,4},{7,5},{8,10},{9,11},{10,... | collective-permute-start | bytes 786440 | tf_op jit(solution)/shard_map/ppermute | solution.py:81
  6.7 3.4 %collective-permute-start.2 = (bf16[2,2048]{1,0:T(2,128)(2,1)S(1)}, bf16[2,2048]{1,0:T(2,128)(2,1)S(1)}, u32[]{:S(2)}, u32[]{:S(2)}) collective-permute-start(bf16[2,2048]{1,0:T(2,128)(2,1)S(1)} %slice_bitcast_fusion.1), channel_id=1, source_target_pairs={{0,4},{4,8},{8,12},{12,16},{16,20},{20,24},{24,28},{1,5},{5,9},{9,... | collective-permute-start | bytes 24584 | tf_op jit(solution)/shard_map/ppermute | solution.py:625
  10.1 2.4 %collective-permute-done.1 = bf16[256,512]{1,0:T(8,128)(2,1)S(1)} collective-permute-done((bf16[256,512]{1,0:T(8,128)(2,1)S(1)}, bf16[256,512]{1,0:T(8,128)(2,1)S(1)}, u32[]{:S(2)}, u32[]{:S(2)}) %collective-permute-start.1) | collective-permute-done | bytes 262176 | tf_op jit(solution)/shard_map/ppermute | solution.py:81
  12.6 2.1 %collective-permute-start.3 = (bf16[256,1536]{1,0:T(8,128)(2,1)S(1)}, bf16[256,1536]{1,0:T(8,128)(2,1)S(1)}, u32[]{:S(2)}, u32[]{:S(2)}) collective-permute-start(bf16[256,1536]{1,0:T(8,128)(2,1)S(1)} %pad_maximum_fusion.1.refs_0_), channel_id=1, source_target_pairs={{0,8},{8,16},{16,24},{24,28},{28,20},{20,12},{12,4},{4,0},{1,9},{9... | collective-permute-start | bytes 2359304 | tf_op jit(solution)/shard_map/ppermute | solution.py:64
  14.7 1.8 collective-permute-start.5
  16.9 11.0 %collective-permute-done.5.refs_2_.refs_11_ = bf16[128,2048]{1,0:T(8,128)(2,1)S(1)} collective-permute-done((bf16[128,2048]{1,0:T(8,128)(2,1)S(1)}, bf16[128,2048]{1,0:T(8,128)(2,1)S(1)}, u32[]{:S(2)}, u32[]{:S(2)}) %collective-permute-start.5) | collective-permute-done | bytes 524320 | tf_op jit(solution)/shard_map/ppermute | solution.py:81
  27.9 4.0 %collective-permute-done.3.refs_1_ = bf16[256,1536]{1,0:T(8,128)(2,1)S(1)} collective-permute-done((bf16[256,1536]{1,0:T(8,128)(2,1)S(1)}, bf16[256,1536]{1,0:T(8,128)(2,1)S(1)}, u32[]{:S(2)}, u32[]{:S(2)}) %collective-permute-start.3) | collective-permute-done | bytes 786464 | tf_op jit(solution)/shard_map/ppermute | solution.py:64
  33.7 1.6 collective-permute-start.6
  35.4 1.6 collective-permute-start.9
  38.9 11.7 %collective-permute-done.9.refs_3_.refs_12_ = bf16[144,2048]{1,0:T(8,128)(2,1)S(1)} collective-permute-done((bf16[144,2048]{1,0:T(8,128)(2,1)S(1)}, bf16[144,2048]{1,0:T(8,128)(2,1)S(1)}, u32[]{:S(2)}, u32[]{:S(2)}) %collective-permute-start.9) | collective-permute-done | bytes 589856 | tf_op jit(solution)/shard_map/ppermute | solution.py:81
  50.6 2.6 %collective-permute-done.7.refs_4_ = bf16[256,1536]{1,0:T(8,128)(2,1)S(1)} collective-permute-done((bf16[256,1536]{1,0:T(8,128)(2,1)S(1)}, bf16[256,1536]{1,0:T(8,128)(2,1)S(1)}, u32[]{:S(2)}, u32[]{:S(2)}) %collective-permute-start.7) | collective-permute-done | bytes 786464 | tf_op jit(solution)/shard_map/ppermute | solution.py:64
  53.4 1.6 collective-permute-start.12
  55.0 1.5 collective-permute-start.16
  57.7 5.2 %collective-permute-done.12.refs_4_.refs_2_ = bf16[272,512]{1,0:T(8,128)(2,1)S(1)} collective-permute-done((bf16[272,512]{1,0:T(8,128)(2,1)S(1)}, bf16[272,512]{1,0:T(8,128)(2,1)S(1)}, u32[]{:S(2)}, u32[]{:S(2)}) %collective-permute-start.12) | collective-permute-done | bytes 278560 | tf_op jit(solution)/shard_map/ppermute | solution.py:81
  62.9 5.0 %collective-permute-done.13.refs_5_.refs_3_ = bf16[272,512]{1,0:T(8,128)(2,1)S(1)} collective-permute-done((bf16[272,512]{1,0:T(8,128)(2,1)S(1)}, bf16[272,512]{1,0:T(8,128)(2,1)S(1)}, u32[]{:S(2)}, u32[]{:S(2)}) %collective-permute-start.13) | collective-permute-done | bytes 278560 | tf_op jit(solution)/shard_map/ppermute | solution.py:81
  68.0 3.7 %shard_map.187 = (bf16[1088,2048]{1,0:T(8,128)(2,1)S(1)}, f32[1024,128]{1,0:T(8,128)S(1)}, f32[1024,128]{1,0:T(8,128)S(1)}, bf16[1024,512]{1,0:T(8,128)(2,1)S(1)}) custom-call(s32[6]{0:T(128)S(1)} %stack.116.place, bf16[272,2048]{1,0:T(8,128)(2,1)S(1)} %maximum_maximum_fusion.refs_0_.refs_9_, bf16[272,2048]{1,0:T(8,128)(2,1)S(1)} %collective-permute-done.8.refs_1_.refs_10_, ...), custom_call_target="tpu_custom_call" | custom-call | tf_op jit(solution)/shard_map/pallas_call | solution.py:28
  71.7 3.0 %collective-permute-done.16.refs_6_ = bf16[256,1536]{1,0:T(8,128)(2,1)S(1)} collective-permute-done((bf16[256,1536]{1,0:T(8,128)(2,1)S(1)}, bf16[256,1536]{1,0:T(8,128)(2,1)S(1)}, u32[]{:S(2)}, u32[]{:S(2)}) %collective-permute-start.16) | collective-permute-done | bytes 786464 | tf_op jit(solution)/shard_map/ppermute | solution.py:64
  75.9 1.6 collective-permute-start.18
  78.3 6.8 %shard_map.188.begun = f32[1088,1536]{1,0:T(8,128)S(1)} custom-call(s32[8]{0:T(128)S(1)} %stack.120.sources, bf16[1088,2048]{1,0:T(8,128)(2,1)S(1)} %get-tuple-element.142.normed, bf16[256,1536]{1,0:T(8,128)(2,1)S(1)} %pad_maximum_fusion.1.refs_0_, bf16[256,1536]{1,0:T(8,128)(2,1)S(1)} %collective-permute-done.3.refs_1_, ...), custom_call_target="tpu_custom_call" | custom-call | tf_op jit(solution)/shard_map/pallas_call | solution.py:28
  85.9 1.6 collective-permute-done.17.refs_0_.refs_7_
  87.5 4.1 %shard_map.189 = (f32[3,4,1088,128]{3,2,1,0:T(8,128)S(1)}, f32[3,8,512]{2,1,0:T(8,128)S(1)}, f32[4,8,512]{2,1,0:T(8,128)S(1)}) custom-call(s32[8]{0:T(128)S(1)} %stack.120.sources, s32[6]{0:T(128)S(1)} %stack.116.place, bf16[1088,2048]{1,0:T(8,128)(2,1)S(1)} %get-tuple-element.142.normed, f32[8,512]{1,0:T(8,128)S(1)} %pad_maximum_fusion.7.start, ...), custom_call_target="tpu_custom_call" | custom-call | tf_op jit(solution)/shard_map/pallas_call | solution.py:28
  91.6 1.6 collective-permute-start.19
  93.2 2.5 %collective-permute-done.19 = f32[3,8,512]{2,1,0:T(8,128)S(1)} collective-permute-done((f32[3,8,512]{2,1,0:T(8,128)S(1)}, f32[3,8,512]{2,1,0:T(8,128)S(1)}, u32[]{:S(2)}, u32[]{:S(2)}) %collective-permute-start.19) | collective-permute-done | bytes 49184 | tf_op jit(solution)/shard_map/ppermute | solution.py:81
  96.9 3.5 %collective-permute-done.20 = f32[3,8,512]{2,1,0:T(8,128)S(1)} collective-permute-done((f32[3,8,512]{2,1,0:T(8,128)S(1)}, f32[3,8,512]{2,1,0:T(8,128)S(1)}, u32[]{:S(2)}, u32[]{:S(2)}) %collective-permute-start.20) | collective-permute-done | bytes 49184 | tf_op jit(solution)/shard_map/ppermute | solution.py:81
  103.0 3.0 %collective-permute-done.21 = f32[3,8,512]{2,1,0:T(8,128)S(1)} collective-permute-done((f32[3,8,512]{2,1,0:T(8,128)S(1)}, f32[3,8,512]{2,1,0:T(8,128)S(1)}, u32[]{:S(2)}, u32[]{:S(2)}) %collective-permute-start.21) | collective-permute-done | bytes 49184 | tf_op jit(solution)/shard_map/ppermute | solution.py:81
  106.1 1.8 collective-permute-done.22.linked
  107.8 8.8 %shard_map.190 = (bf16[1088,1536]{1,0:T(8,128)(2,1)S(1)}, bf16[2,2,128,512]{3,2,1,0:T(8,128)(2,1)S(1)}, bf16[2,2,128,512]{3,2,1,0:T(8,128)(2,1)S(1)}, bf16[2,2,1...) custom-call(s32[6]{0:T(128)S(1)} %stack.116.place, ...), custom_call_target="tpu_custom_call" | custom-call | tf_op jit(solution)/shard_map/pallas_call | solution.py:28
  116.7 1.8 shard_map.191
  120.2 1.7 collective-permute-start.24
  121.9 2.8 %shard_map.194 = (f32[256,1536]{1,0:T(8,128)S(1)}, f32[256,1536]{1,0:T(8,128)S(1)}) custom-call(s32[8]{0:T(128)S(1)} %stack.109.owners, s32[6]{0:T(128)S(1)} %stack.116.place, bf16[1088,2048]{1,0:T(8,128)(2,1)S(1)} %get-tuple-element.142.normed, bf16[1088,1536]{1,0:T(8,128)(2,1)S(1)} %get-tuple-element.171.grads), custom_call_target="tpu_custom_call" | custom-call | tf_op jit(solution)/shard_map/pallas_call | solution.py:28
  124.7 2.8 %shard_map.192 = (f32[256,1536]{1,0:T(8,128)S(1)}, f32[256,1536]{1,0:T(8,128)S(1)}) custom-call(s32[8]{0:T(128)S(1)} %stack.109.owners, s32[6]{0:T(128)S(1)} %stack.116.place, bf16[1088,2048]{1,0:T(8,128)(2,1)S(1)} %get-tuple-element.142.normed, bf16[1088,1536]{1,0:T(8,128)(2,1)S(1)} %get-tuple-element.171.grads), custom_call_target="tpu_custom_call" | custom-call | tf_op jit(solution)/shard_map/pallas_call | solution.py:28
  127.5 4.2 %collective-permute-done.23.up = bf16[128,1536]{1,0:T(8,128)(2,1)S(1)} collective-permute-done((bf16[128,1536]{1,0:T(8,128)(2,1)S(1)}, bf16[128,1536]{1,0:T(8,128)(2,1)S(1)}, u32[]{:S(2)}, u32[]{:S(2)}) %collective-permute-start.23) | collective-permute-done | bytes 393248 | tf_op jit(solution)/shard_map/ppermute | solution.py:64
  131.9 1.8 collective-permute-start.28
  134.5 2.8 %shard_map.196 = (f32[256,1536]{1,0:T(8,128)S(1)}, f32[256,1536]{1,0:T(8,128)S(1)}) custom-call(s32[8]{0:T(128)S(1)} %stack.109.owners, s32[6]{0:T(128)S(1)} %stack.116.place, bf16[1088,2048]{1,0:T(8,128)(2,1)S(1)} %get-tuple-element.142.normed, bf16[1088,1536]{1,0:T(8,128)(2,1)S(1)} %get-tuple-element.171.grads), custom_call_target="tpu_custom_call" | custom-call | tf_op jit(solution)/shard_map/pallas_call | solution.py:28
  137.3 1.8 shard_map.195
  139.1 7.5 %shard_map.197 = (f32[256,2048]{1,0:T(8,128)S(1)}, bf16[256,2048]{1,0:T(8,128)(2,1)S(1)}, bf16[256,2048]{1,0:T(8,128)(2,1)S(1)}, bf16[256,2048]{1,0:T(8,128)(2,1)S(1)}, f32[8,2048]{1,0:T(8,128)S(1)}) custom-call(s32[8]{0:T(128)S(1)} %stack.120.sources, s32[6]{0:T(128)S(1)} %stack.116.place, bf16[1088,1536]{1,0:T(8,128)(2,1)S(1)} %get-tuple-element.171.grads, ...), custom_call_target="tpu_custom_call" | custom-call | tf_op jit(solution)/shard_map/pallas_call | solution.py:28
  146.6 4.7 %collective-permute-done.28.down = bf16[256,1536]{1,0:T(8,128)(2,1)S(1)} collective-permute-done((bf16[256,1536]{1,0:T(8,128)(2,1)S(1)}, bf16[256,1536]{1,0:T(8,128)(2,1)S(1)}, u32[]{:S(2)}, u32[]{:S(2)}) %collective-permute-start.28) | collective-permute-done | bytes 786464 | tf_op jit(solution)/shard_map/ppermute | solution.py:64
  155.7 1.6 collective-permute-start.31
  158.4 1.8 collective-permute-done.31
  161.7 1.7 shard_map.199
  163.3 9.7 %collective-permute-done.36.down = bf16[256,1536]{1,0:T(8,128)(2,1)S(1)} collective-permute-done((bf16[256,1536]{1,0:T(8,128)(2,1)S(1)}, bf16[256,1536]{1,0:T(8,128)(2,1)S(1)}, u32[]{:S(2)}, u32[]{:S(2)}) %collective-permute-start.36) | collective-permute-done | bytes 786464 | tf_op jit(solution)/shard_map/ppermute | solution.py:64
  173.0 1.8 collective-permute-done.35.up
  177.4 2.1 collective-permute-start.39
  179.4 2.7 %collective-permute-done.43 = f32[6,2048]{1,0:T(8,128)S(1)} collective-permute-done((f32[6,2048]{1,0:T(8,128)S(1)}, f32[6,2048]{1,0:T(8,128)S(1)}, u32[]{:S(2)}, u32[]{:S(2)}) %collective-permute-start.43) | collective-permute-done | bytes 49184 | tf_op jit(solution)/shard_map/ppermute | solution.py:81
  182.1 6.2 %collective-permute-done.38 = bf16[128,2048]{1,0:T(8,128)(2,1)S(1)} collective-permute-done((bf16[128,2048]{1,0:T(8,128)(2,1)S(1)}, bf16[128,2048]{1,0:T(8,128)(2,1)S(1)}, u32[]{:S(2)}, u32[]{:S(2)}) %collective-permute-start.38) | collective-permute-done | bytes 524320 | tf_op jit(solution)/shard_map/ppermute | solution.py:81
  191.1 4.4 %collective-permute-done.39 = bf16[256,1536]{1,0:T(8,128)(2,1)S(1)} collective-permute-done((bf16[256,1536]{1,0:T(8,128)(2,1)S(1)}, bf16[256,1536]{1,0:T(8,128)(2,1)S(1)}, u32[]{:S(2)}, u32[]{:S(2)}) %collective-permute-start.39) | collective-permute-done | bytes 786464 | tf_op jit(solution)/shard_map/ppermute | solution.py:64
  195.5 2.2 %collective-permute-done.40 = bf16[256,1536]{1,0:T(8,128)(2,1)S(1)} collective-permute-done((bf16[256,1536]{1,0:T(8,128)(2,1)S(1)}, bf16[256,1536]{1,0:T(8,128)(2,1)S(1)}, u32[]{:S(2)}, u32[]{:S(2)}) %collective-permute-start.40) | collective-permute-done | bytes 786464 | tf_op jit(solution)/shard_map/ppermute | solution.py:64
  199.2 4.5 %collective-permute-done.44 = f32[6,2048]{1,0:T(8,128)S(1)} collective-permute-done((f32[6,2048]{1,0:T(8,128)S(1)}, f32[6,2048]{1,0:T(8,128)S(1)}, u32[]{:S(2)}, u32[]{:S(2)}) %collective-permute-start.44) | collective-permute-done | bytes 49184 | tf_op jit(solution)/shard_map/ppermute | solution.py:81
  (138 shorter events, 34.4 us)
Async XLA Ops:
  2.5 7.6 %collective-permute-start = (bf16[256,512]{1,0:T(8,128)(2,1)S(1)}, bf16[256,512]{1,0:T(8,128)(2,1)S(1)}, u32[]{:S(2)}, u32[]{:S(2)}) collective-permute-start(bf16[256,512]{1,0:T(8,128)(2,1)S(1)} %get-tuple-element.224), channel_id=1, source_target_pairs={{0,1},{1,0},{2,3},{3,2},{4,5},{5,4},{6,7},{7,6},{8,9},{9,8},{10,11... | collective-permute-start | bytes 786440 | tf_op jit(solution)/shard_map/ppermute | solution.py:81
  3.0 9.5 %collective-permute-start.1 = (bf16[256,512]{1,0:T(8,128)(2,1)S(1)}, bf16[256,512]{1,0:T(8,128)(2,1)S(1)}, u32[]{:S(2)}, u32[]{:S(2)}) collective-permute-start(bf16[256,512]{1,0:T(8,128)(2,1)S(1)} %get-tuple-element.225), channel_id=1, source_target_pairs={{0,2},{1,3},{2,0},{3,1},{4,6},{5,7},{6,4},{7,5},{8,10},{9,11},{10,... | collective-permute-start | bytes 786440 | tf_op jit(solution)/shard_map/ppermute | solution.py:81
  6.7 5.9 %collective-permute-start.2 = (bf16[2,2048]{1,0:T(2,128)(2,1)S(1)}, bf16[2,2048]{1,0:T(2,128)(2,1)S(1)}, u32[]{:S(2)}, u32[]{:S(2)}) collective-permute-start(bf16[2,2048]{1,0:T(2,128)(2,1)S(1)} %slice_bitcast_fusion.1), channel_id=1, source_target_pairs={{0,4},{4,8},{8,12},{12,16},{16,20},{20,24},{24,28},{1,5},{5,9},{9,... | collective-permute-start | bytes 24584 | tf_op jit(solution)/shard_map/ppermute | solution.py:625
  12.5 24.5 %copy-start = (bf16[2,128,2048]{2,1,0:T(8,128)(2,1)S(1)}, bf16[2,128,2048]{2,1,0:T(8,128)(2,1)}, u32[]{:S(2)}) copy-start(bf16[2,128,2048]{2,1,0:T(8,128)(2,1)} %param.21) | copy-start | bytes 3145732
  12.6 19.4 %collective-permute-start.3 = (bf16[256,1536]{1,0:T(8,128)(2,1)S(1)}, bf16[256,1536]{1,0:T(8,128)(2,1)S(1)}, u32[]{:S(2)}, u32[]{:S(2)}) collective-permute-start(bf16[256,1536]{1,0:T(8,128)(2,1)S(1)} %pad_maximum_fusion.1.refs_0_), channel_id=1, source_target_pairs={{0,8},{8,16},{16,24},{24,28},{28,20},{20,12},{12,4},{4,0},{1,9},{9... | collective-permute-start | bytes 2359304 | tf_op jit(solution)/shard_map/ppermute | solution.py:64
  14.7 18.6 %collective-permute-start.4 = (bf16[256,1536]{1,0:T(8,128)(2,1)S(1)}, bf16[256,1536]{1,0:T(8,128)(2,1)S(1)}, u32[]{:S(2)}, u32[]{:S(2)}) collective-permute-start(bf16[256,1536]{1,0:T(8,128)(2,1)S(1)} %pad_maximum_fusion.1.refs_0_), channel_id=1, source_target_pairs={{0,4},{8,0},{16,8},{24,16},{28,24},{20,28},{12,20},{4,12},{1,5},{9... | collective-permute-start | bytes 2359304 | tf_op jit(solution)/shard_map/ppermute | solution.py:64
  14.7 13.1 %collective-permute-start.5 = (bf16[128,2048]{1,0:T(8,128)(2,1)S(1)}, bf16[128,2048]{1,0:T(8,128)(2,1)S(1)}, u32[]{:S(2)}, u32[]{:S(2)}) collective-permute-start(bf16[128,2048]{1,0:T(8,128)(2,1)S(1)} %slice_bitcast_fusion), channel_id=1, source_target_pairs={{0,2},{1,3},{2,0},{3,1},{4,6},{5,7},{6,4},{7,5},{8,10},{9,11},{10,... | collective-permute-start | bytes 1572872 | tf_op jit(solution)/shard_map/ppermute | solution.py:81
  16.6 51.4 %copy-start.3 = (f32[2048]{0:T(1024)S(1)}, f32[2048]{0:T(1024)}, u32[]{:S(2)}) copy-start(f32[2048]{0:T(1024)} %param.19) | copy-start | bytes 24580
  16.6 51.4 %copy-start.7 = (f32[2048]{0:T(1024)S(1)}, f32[2048]{0:T(1024)}, u32[]{:S(2)}) copy-start(f32[2048]{0:T(1024)} %param.20) | copy-start | bytes 24580
  33.3 20.1 %collective-permute-start.8 = (bf16[272,2048]{1,0:T(8,128)(2,1)S(1)}, bf16[272,2048]{1,0:T(8,128)(2,1)S(1)}, u32[]{:S(2)}, u32[]{:S(2)}) collective-permute-start(bf16[272,2048]{1,0:T(8,128)(2,1)S(1)} %maximum_maximum_fusion.refs_0_.refs_9_), channel_id=1, source_target_pairs={{0,1},{1,0},{2,3},{3,2},{4,5},{5,4},{6,7},{7,6},{8,9},{9,8},{10,11... | collective-permute-start | bytes 3342344 | tf_op jit(solution)/shard_map/ppermute | solution.py:81
  33.3 20.0 %collective-permute-start.7 = (bf16[256,1536]{1,0:T(8,128)(2,1)S(1)}, bf16[256,1536]{1,0:T(8,128)(2,1)S(1)}, u32[]{:S(2)}, u32[]{:S(2)}) collective-permute-start(bf16[256,1536]{1,0:T(8,128)(2,1)S(1)} %collective-permute-done.4.refs_2_), channel_id=1, source_target_pairs={{0,4},{8,0},{16,8},{24,16},{28,24},{20,28},{12,20},{4,12},{1,5},{9... | collective-permute-start | bytes 2359304 | tf_op jit(solution)/shard_map/ppermute | solution.py:64
  33.7 19.7 %collective-permute-start.6 = (bf16[256,1536]{1,0:T(8,128)(2,1)S(1)}, bf16[256,1536]{1,0:T(8,128)(2,1)S(1)}, u32[]{:S(2)}, u32[]{:S(2)}) collective-permute-start(bf16[256,1536]{1,0:T(8,128)(2,1)S(1)} %collective-permute-done.3.refs_1_), channel_id=1, source_target_pairs={{0,8},{8,16},{16,24},{24,28},{28,20},{20,12},{12,4},{4,0},{1,9},{9... | collective-permute-start | bytes 2359304 | tf_op jit(solution)/shard_map/ppermute | solution.py:64
  35.4 15.2 %collective-permute-start.9 = (bf16[144,2048]{1,0:T(8,128)(2,1)S(1)}, bf16[144,2048]{1,0:T(8,128)(2,1)S(1)}, u32[]{:S(2)}, u32[]{:S(2)}) collective-permute-start(bf16[144,2048]{1,0:T(8,128)(2,1)S(1)} %slice.309), channel_id=1, source_target_pairs={{0,2},{1,3},{2,0},{3,1},{4,6},{5,7},{6,4},{7,5},{8,10},{9,11},{10,... | collective-permute-start | bytes 1769480 | tf_op jit(solution)/shard_map/ppermute | solution.py:81
  36.9 1.9 collective-permute-start.10
  53.4 3.7 %collective-permute-start.11 = (bf16[272,512]{1,0:T(8,128)(2,1)S(1)}, bf16[272,512]{1,0:T(8,128)(2,1)S(1)}, u32[]{:S(2)}, u32[]{:S(2)}) collective-permute-start(bf16[272,512]{1,0:T(8,128)(2,1)S(1)} %get-tuple-element.129), channel_id=1, source_target_pairs={{0,1},{1,0},{2,3},{3,2},{4,5},{5,4},{6,7},{7,6},{8,9},{9,8},{10,11... | collective-permute-start | bytes 835592 | tf_op jit(solution)/shard_map/ppermute | solution.py:81
  53.4 9.5 %collective-permute-start.12 = (bf16[272,512]{1,0:T(8,128)(2,1)S(1)}, bf16[272,512]{1,0:T(8,128)(2,1)S(1)}, u32[]{:S(2)}, u32[]{:S(2)}) collective-permute-start(bf16[272,512]{1,0:T(8,128)(2,1)S(1)} %get-tuple-element.131), channel_id=1, source_target_pairs={{0,2},{1,3},{2,0},{3,1},{4,6},{5,7},{6,4},{7,5},{8,10},{9,11},{10,... | collective-permute-start | bytes 835592 | tf_op jit(solution)/shard_map/ppermute | solution.py:81
  55.0 19.7 %collective-permute-start.16 = (bf16[256,1536]{1,0:T(8,128)(2,1)S(1)}, bf16[256,1536]{1,0:T(8,128)(2,1)S(1)}, u32[]{:S(2)}, u32[]{:S(2)}) collective-permute-start(bf16[256,1536]{1,0:T(8,128)(2,1)S(1)} %collective-permute-done.7.refs_4_), channel_id=1, source_target_pairs={{0,4},{8,0},{16,8},{24,16},{28,24},{20,28},{12,20},{4,12},{1,5},{9... | collective-permute-start | bytes 2359304 | tf_op jit(solution)/shard_map/ppermute | solution.py:64
  56.6 19.3 %collective-permute-start.15 = (bf16[256,1536]{1,0:T(8,128)(2,1)S(1)}, bf16[256,1536]{1,0:T(8,128)(2,1)S(1)}, u32[]{:S(2)}, u32[]{:S(2)}) collective-permute-start(bf16[256,1536]{1,0:T(8,128)(2,1)S(1)} %collective-permute-done.6.refs_3_), channel_id=1, source_target_pairs={{0,8},{8,16},{16,24},{24,28},{28,20},{20,12},{12,4},{4,0},{1,9},{9... | collective-permute-start | bytes 2359304 | tf_op jit(solution)/shard_map/ppermute | solution.py:64
  57.1 10.9 %collective-permute-start.14 = (bf16[144,2048]{1,0:T(8,128)(2,1)S(1)}, bf16[144,2048]{1,0:T(8,128)(2,1)S(1)}, u32[]{:S(2)}, u32[]{:S(2)}) collective-permute-start(bf16[144,2048]{1,0:T(8,128)(2,1)S(1)} %collective-permute-done.9.refs_3_.refs_12_), channel_id=1, source_target_pairs={{0,1},{1,0},{2,3},{3,2},{4,5},{5,4},{6,7},{7,6},{8,9},{9,8},{10,11... | collective-permute-start | bytes 1769480 | tf_op jit(solution)/shard_map/ppermute | solution.py:81
  57.1 10.8 %collective-permute-start.13 = (bf16[272,512]{1,0:T(8,128)(2,1)S(1)}, bf16[272,512]{1,0:T(8,128)(2,1)S(1)}, u32[]{:S(2)}, u32[]{:S(2)}) collective-permute-start(bf16[272,512]{1,0:T(8,128)(2,1)S(1)} %get-tuple-element.133), channel_id=1, source_target_pairs={{0,3},{1,2},{2,1},{3,0},{4,7},{5,6},{6,5},{7,4},{8,11},{9,10},{10,... | collective-permute-start | bytes 835592 | tf_op jit(solution)/shard_map/ppermute | solution.py:81
  75.9 10.0 %collective-permute-start.18 = (bf16[128,1536]{1,0:T(8,128)(2,1)S(1)}, bf16[128,1536]{1,0:T(8,128)(2,1)S(1)}, u32[]{:S(2)}, u32[]{:S(2)}) collective-permute-start(bf16[128,1536]{1,0:T(8,128)(2,1)S(1)} %slice.332), channel_id=1, source_target_pairs={{0,4},{8,0},{16,8},{24,16},{28,24},{20,28},{12,20},{4,12},{1,5},{9... | collective-permute-start | bytes 1179656 | tf_op jit(solution)/shard_map/ppermute | solution.py:64
  77.5 10.0 %collective-permute-start.17 = (bf16[128,1536]{1,0:T(8,128)(2,1)S(1)}, bf16[128,1536]{1,0:T(8,128)(2,1)S(1)}, u32[]{:S(2)}, u32[]{:S(2)}) collective-permute-start(bf16[128,1536]{1,0:T(8,128)(2,1)S(1)} %slice.331), channel_id=1, source_target_pairs={{0,8},{8,16},{16,24},{24,28},{28,20},{20,12},{12,4},{4,0},{1,9},{9... | collective-permute-start | bytes 1179656 | tf_op jit(solution)/shard_map/ppermute | solution.py:64
  91.6 4.2 %collective-permute-start.19 = (f32[3,8,512]{2,1,0:T(8,128)S(1)}, f32[3,8,512]{2,1,0:T(8,128)S(1)}, u32[]{:S(2)}, u32[]{:S(2)}) collective-permute-start(f32[3,8,512]{2,1,0:T(8,128)S(1)} %get-tuple-element.145), channel_id=1, source_target_pairs={{0,4},{4,0},{8,12},{12,8},{16,20},{20,16},{24,28},{28,24},{1,5},{5... | collective-permute-start | bytes 147464 | tf_op jit(solution)/shard_map/ppermute | solution.py:81
  95.8 4.6 %collective-permute-start.20 = (f32[3,8,512]{2,1,0:T(8,128)S(1)}, f32[3,8,512]{2,1,0:T(8,128)S(1)}, u32[]{:S(2)}, u32[]{:S(2)}) collective-permute-start(f32[3,8,512]{2,1,0:T(8,128)S(1)} %pad_maximum_fusion.3), channel_id=1, source_target_pairs={{0,8},{4,12},{8,0},{12,4},{16,24},{20,28},{24,16},{28,20},{1,9},{5... | collective-permute-start | bytes 147464 | tf_op jit(solution)/shard_map/ppermute | solution.py:81
  100.4 5.6 %collective-permute-start.21 = (f32[3,8,512]{2,1,0:T(8,128)S(1)}, f32[3,8,512]{2,1,0:T(8,128)S(1)}, u32[]{:S(2)}, u32[]{:S(2)}) collective-permute-start(f32[3,8,512]{2,1,0:T(8,128)S(1)} %pad_maximum_fusion.4), channel_id=1, source_target_pairs={{0,16},{4,20},{8,24},{12,28},{16,0},{20,4},{24,8},{28,12},{1,17},{... | collective-permute-start | bytes 147464 | tf_op jit(solution)/shard_map/ppermute | solution.py:81
  101.7 6.1 %collective-permute-start.22 = (f32[4,8,512]{2,1,0:T(8,128)S(1)}, f32[4,8,512]{2,1,0:T(8,128)S(1)}, u32[]{:S(2)}, u32[]{:S(2)}) collective-permute-start(f32[4,8,512]{2,1,0:T(8,128)S(1)} %get-tuple-element.152), channel_id=1, source_target_pairs={{4,0},{8,4},{12,8},{16,12},{20,16},{24,20},{28,24},{5,1},{9,5},{13... | collective-permute-start | bytes 196616 | tf_op jit(solution)/shard_map/ppermute | solution.py:749
  118.5 13.4 %collective-permute-start.26 = (bf16[2,2,128,512]{3,2,1,0:T(8,128)(2,1)S(1)}, bf16[2,2,128,512]{3,2,1,0:T(8,128)(2,1)S(1)}, u32[]{:S(2)}, u32[]{:S(2)}) collective-permute-start(bf16[2,2,128,512]{3,2,1,0:T(8,128)(2,1)S(1)} %get-tuple-element.167), channel_id=1, source_target_pairs={{0,2},{1,3},{2,0},{3,1},{4,6},{5,7},{6,4},{7,5},{8,10},{9,11},{10,... | collective-permute-start | bytes 1572872 | tf_op jit(solution)/shard_map/ppermute | solution.py:81
  119.1 12.8 %collective-permute-start.25 = (bf16[2,2,128,512]{3,2,1,0:T(8,128)(2,1)S(1)}, bf16[2,2,128,512]{3,2,1,0:T(8,128)(2,1)S(1)}, u32[]{:S(2)}, u32[]{:S(2)}) collective-permute-start(bf16[2,2,128,512]{3,2,1,0:T(8,128)(2,1)S(1)} %get-tuple-element.165), channel_id=1, source_target_pairs={{0,1},{1,0},{2,3},{3,2},{4,5},{5,4},{6,7},{7,6},{8,9},{9,8},{10,11... | collective-permute-start | bytes 1572872 | tf_op jit(solution)/shard_map/ppermute | solution.py:81
  119.1 12.6 %collective-permute-start.23 = (bf16[128,1536]{1,0:T(8,128)(2,1)S(1)}, bf16[128,1536]{1,0:T(8,128)(2,1)S(1)}, u32[]{:S(2)}, u32[]{:S(2)}) collective-permute-start(bf16[128,1536]{1,0:T(8,128)(2,1)S(1)} %get-tuple-element.222), channel_id=1, source_target_pairs={{0,8},{8,16},{16,24},{24,28},{28,20},{20,12},{12,4},{4,0},{1,9},{9... | collective-permute-start | bytes 1179656 | tf_op jit(solution)/shard_map/ppermute | solution.py:64
  120.2 11.5 %collective-permute-start.24 = (bf16[128,1536]{1,0:T(8,128)(2,1)S(1)}, bf16[128,1536]{1,0:T(8,128)(2,1)S(1)}, u32[]{:S(2)}, u32[]{:S(2)}) collective-permute-start(bf16[128,1536]{1,0:T(8,128)(2,1)S(1)} %get-tuple-element.221), channel_id=1, source_target_pairs={{0,4},{8,0},{16,8},{24,16},{28,24},{20,28},{12,20},{4,12},{1,5},{9... | collective-permute-start | bytes 1179656 | tf_op jit(solution)/shard_map/ppermute | solution.py:64
  131.9 19.4 %collective-permute-start.28 = (bf16[256,1536]{1,0:T(8,128)(2,1)S(1)}, bf16[256,1536]{1,0:T(8,128)(2,1)S(1)}, u32[]{:S(2)}, u32[]{:S(2)}) collective-permute-start(bf16[256,1536]{1,0:T(8,128)(2,1)S(1)} %get-tuple-element.170), channel_id=1, source_target_pairs={{0,4},{8,0},{16,8},{24,16},{28,24},{20,28},{12,20},{4,12},{1,5},{9... | collective-permute-start | bytes 2359304 | tf_op jit(solution)/shard_map/ppermute | solution.py:64
  133.7 18.9 %collective-permute-start.27 = (bf16[256,1536]{1,0:T(8,128)(2,1)S(1)}, bf16[256,1536]{1,0:T(8,128)(2,1)S(1)}, u32[]{:S(2)}, u32[]{:S(2)}) collective-permute-start(bf16[256,1536]{1,0:T(8,128)(2,1)S(1)} %get-tuple-element.168), channel_id=1, source_target_pairs={{0,8},{8,16},{16,24},{24,28},{28,20},{20,12},{12,4},{4,0},{1,9},{9... | collective-permute-start | bytes 2359304 | tf_op jit(solution)/shard_map/ppermute | solution.py:64
  134.0 18.9 %collective-permute-start.29 = (bf16[2,2,128,512]{3,2,1,0:T(8,128)(2,1)S(1)}, bf16[2,2,128,512]{3,2,1,0:T(8,128)(2,1)S(1)}, u32[]{:S(2)}, u32[]{:S(2)}) collective-permute-start(bf16[2,2,128,512]{3,2,1,0:T(8,128)(2,1)S(1)} %get-tuple-element.175), channel_id=1, source_target_pairs={{0,3},{1,2},{2,1},{3,0},{4,7},{5,6},{6,5},{7,4},{8,11},{9,10},{10,... | collective-permute-start | bytes 1572872 | tf_op jit(solution)/shard_map/ppermute | solution.py:81
  152.9 4.5 %collective-permute-start.33 = (bf16[256,2048]{1,0:T(8,128)(2,1)S(1)}, bf16[256,2048]{1,0:T(8,128)(2,1)S(1)}, u32[]{:S(2)}, u32[]{:S(2)}) collective-permute-start(bf16[256,2048]{1,0:T(8,128)(2,1)S(1)} %get-tuple-element.197), channel_id=1, source_target_pairs={{0,1},{1,0},{2,3},{3,2},{4,5},{5,4},{6,7},{7,6},{8,9},{9,8},{10,11... | collective-permute-start | bytes 3145736 | tf_op jit(solution)/shard_map/ppermute | solution.py:81
  153.0 2.7 %collective-permute-start.30 = (f32[8,2048]{1,0:T(8,128)S(1)}, f32[8,2048]{1,0:T(8,128)S(1)}, u32[]{:S(2)}, u32[]{:S(2)}) collective-permute-start(f32[8,2048]{1,0:T(8,128)S(1)} %pad_maximum_fusion.2), channel_id=1, source_target_pairs={{0,1},{1,0},{2,3},{3,2},{4,5},{5,4},{6,7},{7,6},{8,9},{9,8},{10,11... | collective-permute-start | bytes 196616 | tf_op jit(solution)/shard_map/ppermute | solution.py:81
  153.5 19.5 %collective-permute-start.36 = (bf16[256,1536]{1,0:T(8,128)(2,1)S(1)}, bf16[256,1536]{1,0:T(8,128)(2,1)S(1)}, u32[]{:S(2)}, u32[]{:S(2)}) collective-permute-start(bf16[256,1536]{1,0:T(8,128)(2,1)S(1)} %get-tuple-element.200), channel_id=1, source_target_pairs={{0,4},{8,0},{16,8},{24,16},{28,24},{20,28},{12,20},{4,12},{1,5},{9... | collective-permute-start | bytes 2359304 | tf_op jit(solution)/shard_map/ppermute | solution.py:64
  155.0 19.9 %collective-permute-start.35 = (bf16[256,1536]{1,0:T(8,128)(2,1)S(1)}, bf16[256,1536]{1,0:T(8,128)(2,1)S(1)}, u32[]{:S(2)}, u32[]{:S(2)}) collective-permute-start(bf16[256,1536]{1,0:T(8,128)(2,1)S(1)} %get-tuple-element.199), channel_id=1, source_target_pairs={{0,8},{8,16},{16,24},{24,28},{28,20},{20,12},{12,4},{4,0},{1,9},{9... | collective-permute-start | bytes 2359304 | tf_op jit(solution)/shard_map/ppermute | solution.py:64
  155.6 20.0 %collective-permute-start.32 = (bf16[256,2048]{1,0:T(8,128)(2,1)S(1)}, bf16[256,2048]{1,0:T(8,128)(2,1)S(1)}, u32[]{:S(2)}, u32[]{:S(2)}) collective-permute-start(bf16[256,2048]{1,0:T(8,128)(2,1)S(1)} %get-tuple-element.194), channel_id=1, source_target_pairs={{0,1},{1,0},{2,3},{3,2},{4,5},{5,4},{6,7},{7,6},{8,9},{9,8},{10,11... | collective-permute-start | bytes 3145736 | tf_op jit(solution)/shard_map/ppermute | solution.py:81
  155.7 4.5 %collective-permute-start.31 = (f32[8,2048]{1,0:T(8,128)S(1)}, f32[8,2048]{1,0:T(8,128)S(1)}, u32[]{:S(2)}, u32[]{:S(2)}) collective-permute-start(f32[8,2048]{1,0:T(8,128)S(1)} %select_maximum_fusion), channel_id=1, source_target_pairs={{0,2},{1,3},{2,0},{3,1},{4,6},{5,7},{6,4},{7,5},{8,10},{9,11},{10,... | collective-permute-start | bytes 196616 | tf_op jit(solution)/shard_map/ppermute | solution.py:81
  157.8 17.8 %collective-permute-start.34 = (bf16[128,2048]{1,0:T(8,128)(2,1)S(1)}, bf16[128,2048]{1,0:T(8,128)(2,1)S(1)}, u32[]{:S(2)}, u32[]{:S(2)}) collective-permute-start(bf16[128,2048]{1,0:T(8,128)(2,1)S(1)} %get-tuple-element.198), channel_id=1, source_target_pairs={{0,2},{1,3},{2,0},{3,1},{4,6},{5,7},{6,4},{7,5},{8,10},{9,11},{10,... | collective-permute-start | bytes 1572872 | tf_op jit(solution)/shard_map/ppermute | solution.py:81
  160.2 15.4 %collective-permute-start.37 = (f32[6,2048]{1,0:T(8,128)S(1)}, f32[6,2048]{1,0:T(8,128)S(1)}, u32[]{:S(2)}, u32[]{:S(2)}) collective-permute-start(f32[6,2048]{1,0:T(8,128)S(1)} %slice_add_fusion), channel_id=1, source_target_pairs={{0,4},{4,0},{8,12},{12,8},{16,20},{20,16},{24,28},{28,24},{1,5},{5... | collective-permute-start | bytes 147464 | tf_op jit(solution)/shard_map/ppermute | solution.py:81
  175.6 12.7 %collective-permute-start.38 = (bf16[128,2048]{1,0:T(8,128)(2,1)S(1)}, bf16[128,2048]{1,0:T(8,128)(2,1)S(1)}, u32[]{:S(2)}, u32[]{:S(2)}) collective-permute-start(bf16[128,2048]{1,0:T(8,128)(2,1)S(1)} %get-tuple-element.205), channel_id=1, source_target_pairs={{0,2},{1,3},{2,0},{3,1},{4,6},{5,7},{6,4},{7,5},{8,10},{9,11},{10,... | collective-permute-start | bytes 1572872 | tf_op jit(solution)/shard_map/ppermute | solution.py:81
  177.1 5.0 %collective-permute-start.43 = (f32[6,2048]{1,0:T(8,128)S(1)}, f32[6,2048]{1,0:T(8,128)S(1)}, u32[]{:S(2)}, u32[]{:S(2)}) collective-permute-start(f32[6,2048]{1,0:T(8,128)S(1)} %add.315), channel_id=1, source_target_pairs={{0,8},{4,12},{8,0},{12,4},{16,24},{20,28},{24,16},{28,20},{1,9},{5... | collective-permute-start | bytes 147464 | tf_op jit(solution)/shard_map/ppermute | solution.py:81
  177.4 18.1 %collective-permute-start.39 = (bf16[256,1536]{1,0:T(8,128)(2,1)S(1)}, bf16[256,1536]{1,0:T(8,128)(2,1)S(1)}, u32[]{:S(2)}, u32[]{:S(2)}) collective-permute-start(bf16[256,1536]{1,0:T(8,128)(2,1)S(1)} %get-tuple-element.206), channel_id=1, source_target_pairs={{0,8},{8,16},{16,24},{24,28},{28,20},{20,12},{12,4},{4,0},{1,9},{9... | collective-permute-start | bytes 2359304 | tf_op jit(solution)/shard_map/ppermute | solution.py:64
  179.4 18.2 %collective-permute-start.40 = (bf16[256,1536]{1,0:T(8,128)(2,1)S(1)}, bf16[256,1536]{1,0:T(8,128)(2,1)S(1)}, u32[]{:S(2)}, u32[]{:S(2)}) collective-permute-start(bf16[256,1536]{1,0:T(8,128)(2,1)S(1)} %get-tuple-element.207), channel_id=1, source_target_pairs={{0,4},{8,0},{16,8},{24,16},{28,24},{20,28},{12,20},{4,12},{1,5},{9... | collective-permute-start | bytes 2359304 | tf_op jit(solution)/shard_map/ppermute | solution.py:64
  198.0 5.7 %collective-permute-start.44 = (f32[6,2048]{1,0:T(8,128)S(1)}, f32[6,2048]{1,0:T(8,128)S(1)}, u32[]{:S(2)}, u32[]{:S(2)}) collective-permute-start(f32[6,2048]{1,0:T(8,128)S(1)} %add.316), channel_id=1, source_target_pairs={{0,16},{4,20},{8,24},{12,28},{16,0},{20,4},{24,8},{28,12},{1,17},{... | collective-permute-start | bytes 147464 | tf_op jit(solution)/shard_map/ppermute | solution.py:81
  198.7 6.4 %collective-permute-start.41 = (bf16[256,512]{1,0:T(8,128)(2,1)S(1)}, bf16[256,512]{1,0:T(8,128)(2,1)S(1)}, u32[]{:S(2)}, u32[]{:S(2)}) collective-permute-start(bf16[256,512]{1,0:T(8,128)(2,1)S(1)} %get-tuple-element.220), channel_id=1, source_target_pairs={{0,2},{1,3},{2,0},{3,1},{4,6},{5,7},{6,4},{7,5},{8,10},{9,11},{10,... | collective-permute-start | bytes 786440 | tf_op jit(solution)/shard_map/ppermute | solution.py:81
  199.2 5.1 %collective-permute-start.42 = (bf16[256,512]{1,0:T(8,128)(2,1)S(1)}, bf16[256,512]{1,0:T(8,128)(2,1)S(1)}, u32[]{:S(2)}, u32[]{:S(2)}) collective-permute-start(bf16[256,512]{1,0:T(8,128)(2,1)S(1)} %get-tuple-element.219), channel_id=1, source_target_pairs={{0,1},{1,0},{2,3},{3,2},{4,5},{5,4},{6,7},{7,6},{8,9},{9,8},{10,11... | collective-permute-start | bytes 786440 | tf_op jit(solution)/shard_map/ppermute | solution.py:81
  (7 other events, 90.8 us)

commit v5 on v4

--- a/solution.py
+++ b/solution.py
@@ -115,9 +115,9 @@
         ref[low + lane, pl.ds(row, seqs, stride=stride), :] = value[:, lane * 128 : (lane + 1) * 128]
 
 
-def put_rows(ref, row, count, value):
+def put_rows(ref, row, count, value, low=0):
     for lane in range(value.shape[1] // 128):
-        ref[lane, pl.ds(row, count), :] = value[:, lane * 128 : (lane + 1) * 128]
+        ref[low + lane, pl.ds(row, count), :] = value[:, lane * 128 : (lane + 1) * 128]
 
 
 def get_rows(ref, row, count):
@@ -146,10 +146,10 @@
 
 def merge_kernel(cuts, mine_up, mine_down, up, down, *outs):
     count, total = up.shape[0], mine_up.shape[0]
+    first, last = slice(0, count), slice(total - count, total)
     for n, (low, high) in enumerate(cuts):
         lanes = slice(low, high)
         out_up, out_down = outs[2 * n], outs[2 * n + 1]
-        first, last = slice(0, count), slice(total - count, total)
         out_up[first, :] = (mine_up[first, lanes] + up[:, lanes].astype(f32)).astype(bf16)
         out_down[last, :] = (mine_down[last, lanes] + down[:, lanes].astype(f32)).astype(bf16)
         if count < total:
@@ -166,12 +166,12 @@
 
 def spread_rows(dims, low, width, g_in, picked, gs, xs):
     seqs, span, slots = dims
-    per = seqs // slots
+    per, lane = seqs // slots, low // 128
     for n in range(seqs):
         to, lanes = n * (span + PAD) + PAD, slice(low, low + width)
         at = n % per * span
-        put_rows(gs, to, span, g_in[n // per][at : at + span, lanes].astype(f32))
-        put_rows(xs, to, span, picked[n * span : (n + 1) * span, lanes].astype(f32))
+        put_rows(gs, to, span, g_in[n // per][at : at + span, lanes].astype(f32), lane)
+        put_rows(xs, to, span, picked[n * span : (n + 1) * span, lanes].astype(f32), lane)
 
 
 def joined(refs):
@@ -195,8 +195,9 @@
     seqs, span, width, slots, blocks, depth, late, tail = dims
     stride = span + PAD
     g_in = refs[late : late + slots]
-    fields, maps, planes, gs, xs = refs[late + slots :]
-    cand, forg, rese = fields.at[0], fields.at[1], fields.at[2]
+    fields, known, scans, maps, planes = refs[late + slots :]
+    cand, forg, rese = (fields.at[i] for i in range(3))
+    gs, xs, products, sums = known.at[0], known.at[1], scans.at[0], scans.at[1]
     per = seqs // slots
     rows = per * span
     ext = rows + tail
@@ -240,17 +241,22 @@
             live = base + t < ends
             d = jnp.where(live, f, 1.0)
             inject = jnp.where(live, (1.0 - f) * c, 0.0)
-            pulled = jnp.where(live, r * strided(gs, row, seqs, stride), 0.0)
-            decays = decays * d
-            return c, decays, d * injects + inject, handed + decays * pulled
+            pulled = jnp.where(live, r * strided(gs, row, seqs, stride, lane, lanes), 0.0)
+            decays, injects = decays * d, d * injects + inject
+            put_strided(products, row, seqs, stride, decays, lane)
+            put_strided(sums, row, seqs, stride, injects, lane)
+            return c, decays, injects, handed + decays * pulled
 
         one, zero = jnp.ones((seqs, step), f32), jnp.zeros((seqs, step), f32)
+        put_strided(products, PAD - 1, seqs, stride, one, lane)
+        put_strided(sums, PAD - 1, seqs, stride, zero, lane)
         _, decays, injects, handed = lax.fori_loop(
             0, span, turn, (before[:, units], one, zero, zero), unroll=8
         )
         maps[0, :, units], maps[1, :, units], maps[2, :, units] = decays, injects, handed
-        c, f, r = (strided(ref, PAD, seqs, stride, lane, lanes) for ref in (cand, forg, rese))
-        g, x = (strided(ref, PAD, seqs, stride) for ref in (gs, xs))
+        c, f, r, g, x = (
+            strided(ref, PAD, seqs, stride, lane, lanes) for ref in (cand, forg, rese, gs, xs)
+        )
         live = base < ends
         d = jnp.where(live, f, 1.0)
         inject = jnp.where(live, (1.0 - f) * c, 0.0)
@@ -261,16 +267,15 @@
 
 
 def second_kernel(
-    dims, place, lens, v0, v1, earlier, later, start, linked, fields, picked, *refs
+    dims, place, lens, v0, v1, earlier, later, start, linked, fields, known, scans, *refs
 ):
     vecs = (v0, v1)
     seqs, span, width, slots, tail = dims
     stride = span + PAD
-    g_in = refs[:slots]
-    grads, moved = refs[slots], refs[slots + 1 : 2 * slots + 1]
-    final, sums = refs[2 * slots + 1 : 2 * slots + 3]
-    gs, xs, states, outs, gcs, fts, rts = refs[2 * slots + 3 :]
-    cand, forg, rese = fields.at[0], fields.at[1], fields.at[2]
+    grads, moved = refs[0], refs[1 : slots + 1]
+    final, sums, outs, directs, gcs, fts, rts = refs[slots + 1 :]
+    cand, forg, rese = (fields.at[i] for i in range(3))
+    gs, xs, products, injected = known.at[0], known.at[1], scans.at[0], scans.at[1]
     per = seqs // slots
     base = place[0]
     step = min(width, STEP)
@@ -282,49 +287,46 @@
     for low in range(0, width, step):
         units = slice(low, low + step)
         lane, lanes = low // 128, step // 128
-        spread_rows((seqs, span, slots), low, step, g_in, picked, gs, xs)
         own = pl.ds(pl.multiple_of(place[2] + low, 128), step)
-        peep_f, peep_r = (row[:, own] for row in vecs[:2])
+        peep_f, peep_r = (row[:, own] for row in vecs)
         begin = earlier[0, :, units] * start[:, units] + earlier[1, :, units]
         after = later[2, :, units]
-        put_strided(states, PAD - 1, seqs, stride, begin)
-
-        def forward(t, state):
-            row = t + PAD
-            c, f, r = (strided(ref, row, seqs, stride, lane, lanes) for ref in (cand, forg, rese))
-            x = strided(xs, row, seqs, stride)
-            live = base + t < ends
-            state = jnp.where(live, f * state + (1.0 - f) * c, state)
-            put_strided(states, row, seqs, stride, state)
-            put_strided(outs, row, seqs, stride, jnp.where(live, r * state + (1.0 - r) * x, x))
-            return state
-
-        end = lax.fori_loop(0, span, forward, begin, unroll=8)
+
+        def token(ref, row):
+            return strided(ref, row, seqs, stride, lane, lanes)
+
+        def state_at(row):
+            return token(products, row) * begin + token(injected, row)
+
+        end = state_at(span - 1 + PAD)
         final[:, units] = later[0, :, units] * end + later[1, :, units]
         link = [linked[i, :, units] for i in range(4)]
         upcoming = end * (link[0] * after + link[2]) - link[1] * after + link[3]
 
         def backward(i, carry):
-            reached, upcoming, pf, pr, bf, br = carry
+            reached, upcoming, state, c, pf, pr, bf, br = carry
             row = span - 1 - i + PAD
-            c, f, r = (strided(ref, row, seqs, stride, lane, lanes) for ref in (cand, forg, rese))
-            x, g, state = (strided(ref, row, seqs, stride) for ref in (xs, gs, states))
-            prior = strided(states, row - 1, seqs, stride)
-            previous = strided(cand, row - 1, seqs, stride, lane, lanes)
+            f, r, x, g = (token(ref, row) for ref in (forg, rese, xs, gs))
+            prior, previous = state_at(row - 1), token(cand, row - 1)
             live = base + (span - 1 - i) < ends
             zero = jnp.zeros_like(f)
-            adjoint = jnp.where(live, r * g, 0.0) + reached
+            pulled = r * g
+            adjoint = jnp.where(live, pulled, zero) + reached
             kept = jnp.where(live, (1.0 - f) * adjoint, zero)
             ft = f * kept * (prior - c)
-            rt = jnp.where(live, r * (1.0 - r) * g * (state - x), zero)
+            change = r * (state - x)
+            rt = jnp.where(live, (1.0 - r) * g * change, zero)
             put_strided(gcs, row, seqs, stride, kept + upcoming)
             put_strided(fts, row, seqs, stride, ft)
             put_strided(rts, row, seqs, stride, rt)
-            put_strided(gs, row, seqs, stride, jnp.where(live, (1.0 - r) * g, g))
+            put_strided(outs, row, seqs, stride, jnp.where(live, r * state + (1.0 - r) * x, x))
+            put_strided(directs, row, seqs, stride, jnp.where(live, (1.0 - r) * g, g))
             reached = jnp.where(live, f * adjoint, adjoint)
             return (
                 reached,
                 ft * peep_f + rt * peep_r,
+                prior,
+                previous,
                 pf + ft * previous,
                 pr + rt * previous,
                 bf + ft,
@@ -332,11 +334,12 @@
             )
 
         zero = jnp.zeros((seqs, step), f32)
+        last = token(cand, span - 1 + PAD)
         done = lax.fori_loop(
-            0, span, backward, (after, upcoming, zero, zero, zero, zero), unroll=4
+            0, span, backward, (after, upcoming, end, last, zero, zero, zero, zero), unroll=4
         )
         for i in range(4):
-            sums[i : i + 1, units] = jnp.sum(done[2 + i], axis=0, keepdims=True)
+            sums[i : i + 1, units] = jnp.sum(done[4 + i], axis=0, keepdims=True)
         for n in range(seqs):
             at = n * stride + PAD
             k, j = n // per, n % per
@@ -345,7 +348,7 @@
                 here = slice(gate * width + low, gate * width + low + step)
                 grads[to : to + span, here] = get_rows(ref, at, span).astype(bf16)
             moved[k][0, j, :, units] = get_rows(outs, at, span).astype(bf16)
-            moved[k][1, j, :, units] = get_rows(gs, at, span).astype(bf16)
+            moved[k][1, j, :, units] = get_rows(directs, at, span).astype(bf16)
 
 
 def partial_kernel(distances, depth, width, owners, place, normed, grads, *outs):
@@ -357,7 +360,11 @@
             sum_ = lax.dot_general(
                 columns, grads[:, gate], (((0,), (0,)), ((), ())), preferred_element_type=f32
             )
-            outs[i][:, piece * width : (piece + 1) * width] = sum_.astype(outs[i].dtype)
+            here = slice(piece * width, (piece + 1) * width)
+            split = len(outs) // len(distances)
+            count = depth // split
+            for n in range(split):
+                outs[split * i + n][:, here] = sum_[n * count : (n + 1) * count].astype(outs[0].dtype)
 
 
 def token_kernel(dims, parts, sources, place, grads, gate_sums, *refs):
@@ -517,7 +524,7 @@
     ]
     gain_row, bias_row = norm_gain.reshape(1, model), norm_bias.reshape(1, model)
     tall = seqs * (span + PAD)
-    fields = jax.ShapeDtypeStruct((3, width // 128, tall, 128), f32)
+    fields, two = (jax.ShapeDtypeStruct((n, width // 128, tall, 128), f32) for n in (3, 2))
     space = pltpu.VMEM((min(width, STEP) // 128, tall, 128), f32)
 
     rounds = Rounds()
@@ -540,18 +547,25 @@
         ]
         box["dealt"] = jnp.concatenate(found, axis=1)
 
+    def last_columns():
+        came = box["came"]
+        rest = box["mine", far + 1][0][:, width:] + came[0].astype(f32) + came[1].astype(f32)
+        box["rest"] = rest[:, :width], rest[:, width:]
+        if dealing:
+            near, distant = (part_of.astype(bf16) for part_of in box["rest"])
+            box["distant"] = swapped(distant, "stream", 2)
+            box["near"] = swapped(near, "stream", 1)
+            rounds.before = [*rounds.before, distant, near]
+
     def stored():
-        own, rest = box["total"]
-        near, distant = rest[:, :width], rest[:, width:]
+        came = box["came"]
+        own = box["mine", far + 1][0][:, :width] + came[2].astype(f32) + came[3].astype(f32)
         if dealing:
-            distant, near = distant.astype(bf16), near.astype(bf16)
-            rounds.before = [*rounds.before, distant, near]
-            distant = swapped(distant, "stream", 2).astype(f32)
-            near = swapped(near, "stream", 1).astype(f32)
+            distant, near = box["distant"].astype(f32), box["near"].astype(f32)
             found = [jnp.where(even, own, distant), near, jnp.where(even, distant, own)]
         else:
             flat = lax.all_gather(
-                jnp.concatenate(box["total"], axis=1).astype(bf16), "stream", axis=0
+                jnp.concatenate([own, *box["rest"]], axis=1).astype(bf16), "stream", axis=0
             ).astype(f32)
             flat = jnp.swapaxes(flat.reshape(slots, depth, 3, width), 0, 2)
             flat = jnp.swapaxes(flat, 1, 2).reshape(3 * slots, depth, width)
@@ -572,7 +586,7 @@
         box["blocks"] += [box["up"], box["down"]]
         give(box["up"], box["down"])
 
-    def partials(distances, kind):
+    def partials(distances, kind, split=1):
         grads = take(box["grads"])
         if depth % 128:
             found = []
@@ -584,21 +598,21 @@
                     (((0,), (0,)), ((), ())),
                     preferred_element_type=f32,
                 ).astype(kind)
-                found.append(sum_)
+                found += [sum_[n * depth // split :][: depth // split] for n in range(split)]
             return found
         return call(
             functools.partial(
                 partial_kernel, [distance % n_seq for distance in distances], depth, width
             ),
-            [jax.ShapeDtypeStruct((depth, 3 * width), kind)] * len(distances),
+            [jax.ShapeDtypeStruct((depth // split, 3 * width), kind)] * (split * len(distances)),
             [index["owners"], place, box["normed"], grads],
             scalars=2,
         )
 
     def scatter(step):
-        cuts_of = [(0, 3 * width)]
+        cuts_of = [(width, 3 * width), (0, width)] if step == far else [(0, 3 * width)]
         if step == 1:
-            sent = [box["farthest"][:half], box["farthest"][half:]]
+            sent = box["farthest"]
         else:
             sent = call(
                 functools.partial(merge_kernel, cuts_of),
@@ -607,7 +621,8 @@
             )
         came = [along_ring(take(value), 1 - 2 * (i % 2)) for i, value in enumerate(sent)]
         rounds.before = [*rounds.before, *sent]
-        box["up"], box["down"] = came
+        box["up"], box["down"] = came[:2]
+        box["came"] = came
         give(*came)
 
     def sums_of(step):
@@ -722,12 +737,14 @@
 
     def first():
         held, places, count, deep, split = in_order()
-        box["fields"], maps, planes = call(
+        *box["fields"], maps, planes = call(
             functools.partial(
                 first_kernel, (seqs, span, width, slots, count, deep, 2 if split else 1, tail)
             ),
             [
                 fields,
+                two,
+                two,
                 jax.ShapeDtypeStruct((3, seqs, width), f32),
                 jax.ShapeDtypeStruct((4, seqs, width), f32),
             ],
@@ -743,7 +760,6 @@
                 *held[count - 1 :],
                 *[box["g", k] for k in range(slots)],
             ],
-            scratch=[space, space],
             scalars=2,
         )
         box["linked"] = lax.ppermute(planes, "seq", [(i + 1, i) for i in range(n_seq - 1)])
@@ -780,17 +796,15 @@
                 jnp.stack(later),
                 box["start"],
                 box["linked"],
-                box["fields"],
-                box["picked"],
-                *[box["g", k] for k in range(slots)],
+                *box["fields"],
             ],
-            scratch=[space] * 7,
+            scratch=[space] * 5,
             scalars=1,
         )
         box["grads"], box["moving"] = out[0], out[1 : slots + 1]
         box["final"], box["sums"] = out[slots + 1], out[slots + 2]
         rounds.before = []
-        box["farthest"] = partials((far,), bf16)[0]
+        box["farthest"] = partials((far,), bf16, 2)
         box["grads"] = lax.optimization_barrier((box["grads"], box["farthest"]))[0]
 
     def moved(among):
@@ -876,7 +890,7 @@
     def finish():
         grad_normed = box["kept"][0]
         source = inputs.astype(f32).reshape(rows, model)
-        scale = box["scales"][:rows, :1]
+        scale = take(box["scales"])[:rows, :1]
         scaled = (source - box["means"][:rows, :1]) * scale
         grad_scaled = grad_normed * norm_gain
         grad_source = scale * (
@@ -928,19 +942,19 @@
         late[late_at].insert(0, part(sums_of, step))
     if dealing:
         late[2].append(part(token_part, 0, 2))
-        late[3] += [part(token_part, 1, 2)]
+        late[3].insert(0, part(token_part, 1, 2))
     else:
         late[3] += [part(token_sends, bit) for bit in bits[1:]]
     late[2].append(assemble)
-    late[3].append(finish)
+    late += [[] for _ in range(far - len(late))]
+    late[far - 1].insert(1, last_columns)
     for step in range(1, far + 1):
         scatter(step)
         for other in late[step - 1] if step <= len(late) else ():
             other()
         rounds.turn()
-    total = box["mine", far + 1][0] + box["up"].astype(f32) + box["down"].astype(f32)
-    box["total"] = total[:, :width], total[:, width:]
     weight_grad = stored()
+    finish()
     for bit in seq_bits[2:]:
         sums("seq", bit)
 

time: 207 us -> 204 us (0.986)
  waiting for transfers between devices: 107 us -> 98.3 us
  starting transfers between devices: 42.4 us -> 48 us
    ppermute x27, waiting for transfers between devices: 62 us -> 51.7 us  [swapped(): lax.ppermute(value, axis, [(i, i ^ bit) for i in range(lax.axis_size(axis...]
    ppermute x27, starting transfers between devices: 20.2 us -> 23.9 us  [swapped(): lax.ppermute(value, axis, [(i, i ^ bit) for i in range(lax.axis_size(axis...]
    ppermute x16 -> x18, starting transfers between devices: 17.5 us -> 19.4 us  [along_ring(): lax.ppermute(value, 'seq', [(order[i], order[(i + steps) % count]) for i...]
    ppermute x16 -> x18, waiting for transfers between devices: 43 us -> 44.9 us  [along_ring(): lax.ppermute(value, 'seq', [(order[i], order[(i + steps) % count]) for i...]
  transfers between devices with their start and end apart: 45 -> 47, of which waited for: 32 -> 30; matrix products, arithmetic and copies ran while one was open for 3% -> 4% of each run, Pallas kernels for 15% -> 16%
where the time goes in v5:
time: 204 us; the launch traced here: 203 us
  waiting for transfers between devices  98.3 us (48%)
  starting transfers between devices  48 us (24%)
  Pallas kernels  44.5 us (22%)
  other arithmetic  7.46 us (4%)
  local copies, waits for them, and re-layouts  3.59 us (2%)
    ppermute x27, waiting for transfers between devices, swapped(): lax.ppermute(value, axis, [(i, i ^ bit) for i in range(lax.axis_size(axis...  51.7 us
    ppermute x18, waiting for transfers between devices, along_ring(): lax.ppermute(value, 'seq', [(order[i], order[(i + steps) % count]) for i...  44.9 us
    pallas_call x15, Pallas kernels, call(): pl.pallas_call(kernel, out_shape=held if pinned else out_shape, in_specs=...  44.5 us
    ppermute x27, starting transfers between devices, swapped(): lax.ppermute(value, axis, [(i, i ^ bit) for i in range(lax.axis_size(axis...  23.9 us
    ppermute x18, starting transfers between devices, along_ring(): lax.ppermute(value, 'seq', [(order[i], order[(i + steps) % count]) for i...  19.4 us
  transfers between devices with their start and end apart: 47, of which 30 were waited for; matrix products, arithmetic and copies ran while one was open for 4% of the time, Pallas kernels for 16%

profile of v5, /device:TPU:0, one launch (start us, length us, event | category | flops | bytes accessed | tf_op | source)
XLA Modules:
  0.0 203.4 jit_solution(11684271573095679211)
XLA Ops:
  3.0 2.6 %collective-permute-start.1 = (bf16[256,512]{1,0:T(8,128)(2,1)S(1)}, bf16[256,512]{1,0:T(8,128)(2,1)S(1)}, u32[]{:S(2)}, u32[]{:S(2)}) collective-permute-start(bf16[256,512]{1,0:T(8,128)(2,1)S(1)} %get-tuple-element.237), channel_id=1, source_target_pairs={{0,2},{1,3},{2,0},{3,1},{4,6},{5,7},{6,4},{7,5},{8,10},{9,11},{10,... | collective-permute-start | bytes 786440 | tf_op jit(solution)/shard_map/ppermute | solution.py:81
  6.7 3.4 %collective-permute-start.2 = (bf16[2,2048]{1,0:T(2,128)(2,1)S(1)}, bf16[2,2048]{1,0:T(2,128)(2,1)S(1)}, u32[]{:S(2)}, u32[]{:S(2)}) collective-permute-start(bf16[2,2048]{1,0:T(2,128)(2,1)S(1)} %slice_bitcast_fusion.1), channel_id=1, source_target_pairs={{0,4},{4,8},{8,12},{12,16},{16,20},{20,24},{24,28},{1,5},{5,9},{9,... | collective-permute-start | bytes 24584 | tf_op jit(solution)/shard_map/ppermute | solution.py:640
  10.1 2.4 %collective-permute-done.1 = bf16[256,512]{1,0:T(8,128)(2,1)S(1)} collective-permute-done((bf16[256,512]{1,0:T(8,128)(2,1)S(1)}, bf16[256,512]{1,0:T(8,128)(2,1)S(1)}, u32[]{:S(2)}, u32[]{:S(2)}) %collective-permute-start.1) | collective-permute-done | bytes 262176 | tf_op jit(solution)/shard_map/ppermute | solution.py:81
  12.6 2.1 %collective-permute-start.3 = (bf16[256,1536]{1,0:T(8,128)(2,1)S(1)}, bf16[256,1536]{1,0:T(8,128)(2,1)S(1)}, u32[]{:S(2)}, u32[]{:S(2)}) collective-permute-start(bf16[256,1536]{1,0:T(8,128)(2,1)S(1)} %pad_maximum_fusion.1.refs_0_), channel_id=1, source_target_pairs={{0,8},{8,16},{16,24},{24,28},{28,20},{20,12},{12,4},{4,0},{1,9},{9... | collective-permute-start | bytes 2359304 | tf_op jit(solution)/shard_map/ppermute | solution.py:64
  14.8 1.8 collective-permute-start.5
  16.9 11.0 %collective-permute-done.5.refs_2_.refs_11_ = bf16[128,2048]{1,0:T(8,128)(2,1)S(1)} collective-permute-done((bf16[128,2048]{1,0:T(8,128)(2,1)S(1)}, bf16[128,2048]{1,0:T(8,128)(2,1)S(1)}, u32[]{:S(2)}, u32[]{:S(2)}) %collective-permute-start.5) | collective-permute-done | bytes 524320 | tf_op jit(solution)/shard_map/ppermute | solution.py:81
  27.9 4.0 %collective-permute-done.3.refs_1_ = bf16[256,1536]{1,0:T(8,128)(2,1)S(1)} collective-permute-done((bf16[256,1536]{1,0:T(8,128)(2,1)S(1)}, bf16[256,1536]{1,0:T(8,128)(2,1)S(1)}, u32[]{:S(2)}, u32[]{:S(2)}) %collective-permute-start.3) | collective-permute-done | bytes 786464 | tf_op jit(solution)/shard_map/ppermute | solution.py:64
  33.7 1.6 collective-permute-start.6
  35.4 1.6 collective-permute-start.9
  38.8 11.7 %collective-permute-done.9.refs_3_.refs_12_ = bf16[144,2048]{1,0:T(8,128)(2,1)S(1)} collective-permute-done((bf16[144,2048]{1,0:T(8,128)(2,1)S(1)}, bf16[144,2048]{1,0:T(8,128)(2,1)S(1)}, u32[]{:S(2)}, u32[]{:S(2)}) %collective-permute-start.9) | collective-permute-done | bytes 589856 | tf_op jit(solution)/shard_map/ppermute | solution.py:81
  50.6 2.6 %collective-permute-done.7.refs_4_ = bf16[256,1536]{1,0:T(8,128)(2,1)S(1)} collective-permute-done((bf16[256,1536]{1,0:T(8,128)(2,1)S(1)}, bf16[256,1536]{1,0:T(8,128)(2,1)S(1)}, u32[]{:S(2)}, u32[]{:S(2)}) %collective-permute-start.7) | collective-permute-done | bytes 786464 | tf_op jit(solution)/shard_map/ppermute | solution.py:64
  53.4 1.6 collective-permute-start.12
  55.0 1.5 collective-permute-start.16
  57.7 5.2 %collective-permute-done.12.refs_4_ = bf16[272,512]{1,0:T(8,128)(2,1)S(1)} collective-permute-done((bf16[272,512]{1,0:T(8,128)(2,1)S(1)}, bf16[272,512]{1,0:T(8,128)(2,1)S(1)}, u32[]{:S(2)}, u32[]{:S(2)}) %collective-permute-start.12) | collective-permute-done | bytes 278560 | tf_op jit(solution)/shard_map/ppermute | solution.py:81
  62.9 5.0 %collective-permute-done.13.refs_5_ = bf16[272,512]{1,0:T(8,128)(2,1)S(1)} collective-permute-done((bf16[272,512]{1,0:T(8,128)(2,1)S(1)}, bf16[272,512]{1,0:T(8,128)(2,1)S(1)}, u32[]{:S(2)}, u32[]{:S(2)}) %collective-permute-start.13) | collective-permute-done | bytes 278560 | tf_op jit(solution)/shard_map/ppermute | solution.py:81
  68.0 3.7 %shard_map.187 = (bf16[1088,2048]{1,0:T(8,128)(2,1)S(1)}, f32[1024,128]{1,0:T(8,128)S(1)}, f32[1024,128]{1,0:T(8,128)S(1)}, bf16[1024,512]{1,0:T(8,128)(2,1)S(1)}) custom-call(s32[6]{0:T(128)S(1)} %stack.116.place, bf16[272,2048]{1,0:T(8,128)(2,1)S(1)} %maximum_maximum_fusion.refs_0_.refs_9_, bf16[272,2048]{1,0:T(8,128)(2,1)S(1)} %collective-permute-done.8.refs_1_.refs_10_, ...), custom_call_target="tpu_custom_call" | custom-call | tf_op jit(solution)/shard_map/pallas_call | solution.py:28
  71.7 3.0 %collective-permute-done.16.refs_6_ = bf16[256,1536]{1,0:T(8,128)(2,1)S(1)} collective-permute-done((bf16[256,1536]{1,0:T(8,128)(2,1)S(1)}, bf16[256,1536]{1,0:T(8,128)(2,1)S(1)}, u32[]{:S(2)}, u32[]{:S(2)}) %collective-permute-start.16) | collective-permute-done | bytes 786464 | tf_op jit(solution)/shard_map/ppermute | solution.py:64
  75.9 1.6 collective-permute-start.18
  78.3 6.8 %shard_map.188.begun = f32[1088,1536]{1,0:T(8,128)S(1)} custom-call(s32[8]{0:T(128)S(1)} %stack.120.sources, bf16[1088,2048]{1,0:T(8,128)(2,1)S(1)} %get-tuple-element.151.normed, bf16[256,1536]{1,0:T(8,128)(2,1)S(1)} %pad_maximum_fusion.1.refs_0_, bf16[256,1536]{1,0:T(8,128)(2,1)S(1)} %collective-permute-done.3.refs_1_, ...), custom_call_target="tpu_custom_call" | custom-call | tf_op jit(solution)/shard_map/pallas_call | solution.py:28
  85.9 1.6 collective-permute-done.17.refs_0_.refs_7_
  87.5 4.8 %shard_map.189 = (f32[3,4,1088,128]{3,2,1,0:T(8,128)S(1)}, f32[2,4,1088,128]{3,2,1,0:T(8,128)S(1)}, f32[2,4,1088,128]{3,2,1,0:T(8,128)S(1)}, f32[3,8,512]{2,1,0:T(8,128)S(1)}, f32[4,8,512]{2,1,0:T(8,128)S(1)}) custom-call(s32[8]{0:T(128)S(1)} %stack.120.sources, s32[6]{0:T(128)S(1)} %stack.116.place, bf16[1088,2048]{1,0:T(8,128)(2,1)S(1)} %get-tuple-element.151.normed, ...), custom_call_target="tpu_custom_call" | custom-call | tf_op jit(solution)/shard_map/pallas_call | solution.py:28
  92.3 1.6 collective-permute-start.19
  93.9 2.5 %collective-permute-done.19 = f32[3,8,512]{2,1,0:T(8,128)S(1)} collective-permute-done((f32[3,8,512]{2,1,0:T(8,128)S(1)}, f32[3,8,512]{2,1,0:T(8,128)S(1)}, u32[]{:S(2)}, u32[]{:S(2)}) %collective-permute-start.19) | collective-permute-done | bytes 49184 | tf_op jit(solution)/shard_map/ppermute | solution.py:81
  97.6 3.5 %collective-permute-done.20 = f32[3,8,512]{2,1,0:T(8,128)S(1)} collective-permute-done((f32[3,8,512]{2,1,0:T(8,128)S(1)}, f32[3,8,512]{2,1,0:T(8,128)S(1)}, u32[]{:S(2)}, u32[]{:S(2)}) %collective-permute-start.20) | collective-permute-done | bytes 49184 | tf_op jit(solution)/shard_map/ppermute | solution.py:81
  103.7 3.0 %collective-permute-done.21 = f32[3,8,512]{2,1,0:T(8,128)S(1)} collective-permute-done((f32[3,8,512]{2,1,0:T(8,128)S(1)}, f32[3,8,512]{2,1,0:T(8,128)S(1)}, u32[]{:S(2)}, u32[]{:S(2)}) %collective-permute-start.21) | collective-permute-done | bytes 49184 | tf_op jit(solution)/shard_map/ppermute | solution.py:81
  106.8 1.8 collective-permute-done.22.linked
  108.5 6.1 %shard_map.190 = (bf16[1088,1536]{1,0:T(8,128)(2,1)S(1)}, bf16[2,2,128,512]{3,2,1,0:T(8,128)(2,1)S(1)}, bf16[2,2,128,512]{3,2,1,0:T(8,128)(2,1)S(1)}, bf16[2,2,1...) custom-call(s32[6]{0:T(128)S(1)} %stack.116.place, ...), custom_call_target="tpu_custom_call" | custom-call | tf_op jit(solution)/shard_map/pallas_call | solution.py:28
  114.7 1.8 shard_map.191
  118.2 1.7 collective-permute-start.24
  119.9 2.8 %shard_map.194 = (f32[256,1536]{1,0:T(8,128)S(1)}, f32[256,1536]{1,0:T(8,128)S(1)}) custom-call(s32[8]{0:T(128)S(1)} %stack.109.owners, s32[6]{0:T(128)S(1)} %stack.116.place, bf16[1088,2048]{1,0:T(8,128)(2,1)S(1)} %get-tuple-element.151.normed, bf16[1088,1536]{1,0:T(8,128)(2,1)S(1)} %get-tuple-element.184.grads), custom_call_target="tpu_custom_call" | custom-call | tf_op jit(solution)/shard_map/pallas_call | solution.py:28
  122.7 2.8 %shard_map.192 = (f32[256,1536]{1,0:T(8,128)S(1)}, f32[256,1536]{1,0:T(8,128)S(1)}) custom-call(s32[8]{0:T(128)S(1)} %stack.109.owners, s32[6]{0:T(128)S(1)} %stack.116.place, bf16[1088,2048]{1,0:T(8,128)(2,1)S(1)} %get-tuple-element.151.normed, bf16[1088,1536]{1,0:T(8,128)(2,1)S(1)} %get-tuple-element.184.grads), custom_call_target="tpu_custom_call" | custom-call | tf_op jit(solution)/shard_map/pallas_call | solution.py:28
  125.5 4.2 %collective-permute-done.23.up = bf16[128,1536]{1,0:T(8,128)(2,1)S(1)} collective-permute-done((bf16[128,1536]{1,0:T(8,128)(2,1)S(1)}, bf16[128,1536]{1,0:T(8,128)(2,1)S(1)}, u32[]{:S(2)}, u32[]{:S(2)}) %collective-permute-start.23) | collective-permute-done | bytes 393248 | tf_op jit(solution)/shard_map/ppermute | solution.py:64
  129.9 1.8 collective-permute-start.28
  132.6 2.8 %shard_map.196 = (f32[256,1536]{1,0:T(8,128)S(1)}, f32[256,1536]{1,0:T(8,128)S(1)}) custom-call(s32[8]{0:T(128)S(1)} %stack.109.owners, s32[6]{0:T(128)S(1)} %stack.116.place, bf16[1088,2048]{1,0:T(8,128)(2,1)S(1)} %get-tuple-element.151.normed, bf16[1088,1536]{1,0:T(8,128)(2,1)S(1)} %get-tuple-element.184.grads), custom_call_target="tpu_custom_call" | custom-call | tf_op jit(solution)/shard_map/pallas_call | solution.py:28
  135.4 1.8 shard_map.195
  137.2 8.0 %shard_map.197 = (f32[256,2048]{1,0:T(8,128)S(1)}, bf16[256,2048]{1,0:T(8,128)(2,1)S(1)}, bf16[256,2048]{1,0:T(8,128)(2,1)S(1)}, bf16[256,2048]{1,0:T(8,128)(2,1)S(1)}, f32[8,2048]{1,0:T(8,128)S(1)}) custom-call(s32[8]{0:T(128)S(1)} %stack.120.sources, s32[6]{0:T(128)S(1)} %stack.116.place, bf16[1088,1536]{1,0:T(8,128)(2,1)S(1)} %get-tuple-element.184.grads, ...), custom_call_target="tpu_custom_call" | custom-call | tf_op jit(solution)/shard_map/pallas_call | solution.py:28
  145.2 4.1 %collective-permute-done.28.down = bf16[256,1536]{1,0:T(8,128)(2,1)S(1)} collective-permute-done((bf16[256,1536]{1,0:T(8,128)(2,1)S(1)}, bf16[256,1536]{1,0:T(8,128)(2,1)S(1)}, u32[]{:S(2)}, u32[]{:S(2)}) %collective-permute-start.28) | collective-permute-done | bytes 786464 | tf_op jit(solution)/shard_map/ppermute | solution.py:64
  153.8 1.6 collective-permute-start.31
  156.4 1.7 collective-permute-done.31
  159.6 1.7 shard_map.199
  161.3 10.3 %collective-permute-done.33.down = bf16[256,1536]{1,0:T(8,128)(2,1)S(1)} collective-permute-done((bf16[256,1536]{1,0:T(8,128)(2,1)S(1)}, bf16[256,1536]{1,0:T(8,128)(2,1)S(1)}, u32[]{:S(2)}, u32[]{:S(2)}) %collective-permute-start.33) | collective-permute-done | bytes 786464 | tf_op jit(solution)/shard_map/ppermute | solution.py:64
  171.5 1.8 collective-permute-done.32.up
  174.4 1.7 collective-permute-start.38
  177.2 1.6 collective-permute-start.42
  179.0 1.7 collective-permute-start.40
  180.8 8.2 %collective-permute-done.39 = bf16[256,1024]{1,0:T(8,128)(2,1)S(1)} collective-permute-done((bf16[256,1024]{1,0:T(8,128)(2,1)S(1)}, bf16[256,1024]{1,0:T(8,128)(2,1)S(1)}, u32[]{:S(2)}, u32[]{:S(2)}) %collective-permute-start.39) | collective-permute-done | bytes 524320 | tf_op jit(solution)/shard_map/ppermute | solution.py:64
  189.6 1.8 collective-permute-start.43
  198.2 3.0 %collective-permute-done.46 = f32[6,2048]{1,0:T(8,128)S(1)} collective-permute-done((f32[6,2048]{1,0:T(8,128)S(1)}, f32[6,2048]{1,0:T(8,128)S(1)}, u32[]{:S(2)}, u32[]{:S(2)}) %collective-permute-start.46) | collective-permute-done | bytes 49184 | tf_op jit(solution)/shard_map/ppermute | solution.py:81
  (145 shorter events, 36.7 us)
Async XLA Ops:
  2.5 7.6 %collective-permute-start = (bf16[256,512]{1,0:T(8,128)(2,1)S(1)}, bf16[256,512]{1,0:T(8,128)(2,1)S(1)}, u32[]{:S(2)}, u32[]{:S(2)}) collective-permute-start(bf16[256,512]{1,0:T(8,128)(2,1)S(1)} %get-tuple-element.236), channel_id=1, source_target_pairs={{0,1},{1,0},{2,3},{3,2},{4,5},{5,4},{6,7},{7,6},{8,9},{9,8},{10,11... | collective-permute-start | bytes 786440 | tf_op jit(solution)/shard_map/ppermute | solution.py:81
  3.0 9.5 %collective-permute-start.1 = (bf16[256,512]{1,0:T(8,128)(2,1)S(1)}, bf16[256,512]{1,0:T(8,128)(2,1)S(1)}, u32[]{:S(2)}, u32[]{:S(2)}) collective-permute-start(bf16[256,512]{1,0:T(8,128)(2,1)S(1)} %get-tuple-element.237), channel_id=1, source_target_pairs={{0,2},{1,3},{2,0},{3,1},{4,6},{5,7},{6,4},{7,5},{8,10},{9,11},{10,... | collective-permute-start | bytes 786440 | tf_op jit(solution)/shard_map/ppermute | solution.py:81
  6.7 5.9 %collective-permute-start.2 = (bf16[2,2048]{1,0:T(2,128)(2,1)S(1)}, bf16[2,2048]{1,0:T(2,128)(2,1)S(1)}, u32[]{:S(2)}, u32[]{:S(2)}) collective-permute-start(bf16[2,2048]{1,0:T(2,128)(2,1)S(1)} %slice_bitcast_fusion.1), channel_id=1, source_target_pairs={{0,4},{4,8},{8,12},{12,16},{16,20},{20,24},{24,28},{1,5},{5,9},{9,... | collective-permute-start | bytes 24584 | tf_op jit(solution)/shard_map/ppermute | solution.py:640
  12.6 19.4 %collective-permute-start.3 = (bf16[256,1536]{1,0:T(8,128)(2,1)S(1)}, bf16[256,1536]{1,0:T(8,128)(2,1)S(1)}, u32[]{:S(2)}, u32[]{:S(2)}) collective-permute-start(bf16[256,1536]{1,0:T(8,128)(2,1)S(1)} %pad_maximum_fusion.1.refs_0_), channel_id=1, source_target_pairs={{0,8},{8,16},{16,24},{24,28},{28,20},{20,12},{12,4},{4,0},{1,9},{9... | collective-permute-start | bytes 2359304 | tf_op jit(solution)/shard_map/ppermute | solution.py:64
  14.7 18.6 %collective-permute-start.4 = (bf16[256,1536]{1,0:T(8,128)(2,1)S(1)}, bf16[256,1536]{1,0:T(8,128)(2,1)S(1)}, u32[]{:S(2)}, u32[]{:S(2)}) collective-permute-start(bf16[256,1536]{1,0:T(8,128)(2,1)S(1)} %pad_maximum_fusion.1.refs_0_), channel_id=1, source_target_pairs={{0,4},{8,0},{16,8},{24,16},{28,24},{20,28},{12,20},{4,12},{1,5},{9... | collective-permute-start | bytes 2359304 | tf_op jit(solution)/shard_map/ppermute | solution.py:64
  14.8 13.1 %collective-permute-start.5 = (bf16[128,2048]{1,0:T(8,128)(2,1)S(1)}, bf16[128,2048]{1,0:T(8,128)(2,1)S(1)}, u32[]{:S(2)}, u32[]{:S(2)}) collective-permute-start(bf16[128,2048]{1,0:T(8,128)(2,1)S(1)} %slice_bitcast_fusion), channel_id=1, source_target_pairs={{0,2},{1,3},{2,0},{3,1},{4,6},{5,7},{6,4},{7,5},{8,10},{9,11},{10,... | collective-permute-start | bytes 1572872 | tf_op jit(solution)/shard_map/ppermute | solution.py:81
  33.3 20.1 %collective-permute-start.8 = (bf16[272,2048]{1,0:T(8,128)(2,1)S(1)}, bf16[272,2048]{1,0:T(8,128)(2,1)S(1)}, u32[]{:S(2)}, u32[]{:S(2)}) collective-permute-start(bf16[272,2048]{1,0:T(8,128)(2,1)S(1)} %maximum_maximum_fusion.refs_0_.refs_9_), channel_id=1, source_target_pairs={{0,1},{1,0},{2,3},{3,2},{4,5},{5,4},{6,7},{7,6},{8,9},{9,8},{10,11... | collective-permute-start | bytes 3342344 | tf_op jit(solution)/shard_map/ppermute | solution.py:81
  33.3 20.0 %collective-permute-start.7 = (bf16[256,1536]{1,0:T(8,128)(2,1)S(1)}, bf16[256,1536]{1,0:T(8,128)(2,1)S(1)}, u32[]{:S(2)}, u32[]{:S(2)}) collective-permute-start(bf16[256,1536]{1,0:T(8,128)(2,1)S(1)} %collective-permute-done.4.refs_2_), channel_id=1, source_target_pairs={{0,4},{8,0},{16,8},{24,16},{28,24},{20,28},{12,20},{4,12},{1,5},{9... | collective-permute-start | bytes 2359304 | tf_op jit(solution)/shard_map/ppermute | solution.py:64
  33.7 19.7 %collective-permute-start.6 = (bf16[256,1536]{1,0:T(8,128)(2,1)S(1)}, bf16[256,1536]{1,0:T(8,128)(2,1)S(1)}, u32[]{:S(2)}, u32[]{:S(2)}) collective-permute-start(bf16[256,1536]{1,0:T(8,128)(2,1)S(1)} %collective-permute-done.3.refs_1_), channel_id=1, source_target_pairs={{0,8},{8,16},{16,24},{24,28},{28,20},{20,12},{12,4},{4,0},{1,9},{9... | collective-permute-start | bytes 2359304 | tf_op jit(solution)/shard_map/ppermute | solution.py:64
  35.4 15.2 %collective-permute-start.9 = (bf16[144,2048]{1,0:T(8,128)(2,1)S(1)}, bf16[144,2048]{1,0:T(8,128)(2,1)S(1)}, u32[]{:S(2)}, u32[]{:S(2)}) collective-permute-start(bf16[144,2048]{1,0:T(8,128)(2,1)S(1)} %slice.302), channel_id=1, source_target_pairs={{0,2},{1,3},{2,0},{3,1},{4,6},{5,7},{6,4},{7,5},{8,10},{9,11},{10,... | collective-permute-start | bytes 1769480 | tf_op jit(solution)/shard_map/ppermute | solution.py:81
  36.9 1.9 collective-permute-start.10
  53.4 3.7 %collective-permute-start.11 = (bf16[272,512]{1,0:T(8,128)(2,1)S(1)}, bf16[272,512]{1,0:T(8,128)(2,1)S(1)}, u32[]{:S(2)}, u32[]{:S(2)}) collective-permute-start(bf16[272,512]{1,0:T(8,128)(2,1)S(1)} %get-tuple-element.138), channel_id=1, source_target_pairs={{0,1},{1,0},{2,3},{3,2},{4,5},{5,4},{6,7},{7,6},{8,9},{9,8},{10,11... | collective-permute-start | bytes 835592 | tf_op jit(solution)/shard_map/ppermute | solution.py:81
  53.4 9.5 %collective-permute-start.12 = (bf16[272,512]{1,0:T(8,128)(2,1)S(1)}, bf16[272,512]{1,0:T(8,128)(2,1)S(1)}, u32[]{:S(2)}, u32[]{:S(2)}) collective-permute-start(bf16[272,512]{1,0:T(8,128)(2,1)S(1)} %get-tuple-element.140), channel_id=1, source_target_pairs={{0,2},{1,3},{2,0},{3,1},{4,6},{5,7},{6,4},{7,5},{8,10},{9,11},{10,... | collective-permute-start | bytes 835592 | tf_op jit(solution)/shard_map/ppermute | solution.py:81
  55.0 19.7 %collective-permute-start.16 = (bf16[256,1536]{1,0:T(8,128)(2,1)S(1)}, bf16[256,1536]{1,0:T(8,128)(2,1)S(1)}, u32[]{:S(2)}, u32[]{:S(2)}) collective-permute-start(bf16[256,1536]{1,0:T(8,128)(2,1)S(1)} %collective-permute-done.7.refs_4_), channel_id=1, source_target_pairs={{0,4},{8,0},{16,8},{24,16},{28,24},{20,28},{12,20},{4,12},{1,5},{9... | collective-permute-start | bytes 2359304 | tf_op jit(solution)/shard_map/ppermute | solution.py:64
  56.6 19.3 %collective-permute-start.15 = (bf16[256,1536]{1,0:T(8,128)(2,1)S(1)}, bf16[256,1536]{1,0:T(8,128)(2,1)S(1)}, u32[]{:S(2)}, u32[]{:S(2)}) collective-permute-start(bf16[256,1536]{1,0:T(8,128)(2,1)S(1)} %collective-permute-done.6.refs_3_), channel_id=1, source_target_pairs={{0,8},{8,16},{16,24},{24,28},{28,20},{20,12},{12,4},{4,0},{1,9},{9... | collective-permute-start | bytes 2359304 | tf_op jit(solution)/shard_map/ppermute | solution.py:64
  57.1 10.9 %collective-permute-start.14 = (bf16[144,2048]{1,0:T(8,128)(2,1)S(1)}, bf16[144,2048]{1,0:T(8,128)(2,1)S(1)}, u32[]{:S(2)}, u32[]{:S(2)}) collective-permute-start(bf16[144,2048]{1,0:T(8,128)(2,1)S(1)} %collective-permute-done.9.refs_3_.refs_12_), channel_id=1, source_target_pairs={{0,1},{1,0},{2,3},{3,2},{4,5},{5,4},{6,7},{7,6},{8,9},{9,8},{10,11... | collective-permute-start | bytes 1769480 | tf_op jit(solution)/shard_map/ppermute | solution.py:81
  57.1 10.8 %collective-permute-start.13 = (bf16[272,512]{1,0:T(8,128)(2,1)S(1)}, bf16[272,512]{1,0:T(8,128)(2,1)S(1)}, u32[]{:S(2)}, u32[]{:S(2)}) collective-permute-start(bf16[272,512]{1,0:T(8,128)(2,1)S(1)} %get-tuple-element.142), channel_id=1, source_target_pairs={{0,3},{1,2},{2,1},{3,0},{4,7},{5,6},{6,5},{7,4},{8,11},{9,10},{10,... | collective-permute-start | bytes 835592 | tf_op jit(solution)/shard_map/ppermute | solution.py:81
  71.7 65.5 %copy-start.1 = (f32[1024,128]{1,0:T(8,128)}, f32[1024,128]{1,0:T(8,128)S(1)}, u32[]{:S(2)}) copy-start(f32[1024,128]{1,0:T(8,128)S(1)} %get-tuple-element.190.refs_15_) | copy-start | bytes 1572868
  75.9 10.0 %collective-permute-start.18 = (bf16[128,1536]{1,0:T(8,128)(2,1)S(1)}, bf16[128,1536]{1,0:T(8,128)(2,1)S(1)}, u32[]{:S(2)}, u32[]{:S(2)}) collective-permute-start(bf16[128,1536]{1,0:T(8,128)(2,1)S(1)} %slice.325), channel_id=1, source_target_pairs={{0,4},{8,0},{16,8},{24,16},{28,24},{20,28},{12,20},{4,12},{1,5},{9... | collective-permute-start | bytes 1179656 | tf_op jit(solution)/shard_map/ppermute | solution.py:64
  77.5 10.0 %collective-permute-start.17 = (bf16[128,1536]{1,0:T(8,128)(2,1)S(1)}, bf16[128,1536]{1,0:T(8,128)(2,1)S(1)}, u32[]{:S(2)}, u32[]{:S(2)}) collective-permute-start(bf16[128,1536]{1,0:T(8,128)(2,1)S(1)} %slice.324), channel_id=1, source_target_pairs={{0,8},{8,16},{16,24},{24,28},{28,20},{20,12},{12,4},{4,0},{1,9},{9... | collective-permute-start | bytes 1179656 | tf_op jit(solution)/shard_map/ppermute | solution.py:64
  92.3 4.2 %collective-permute-start.19 = (f32[3,8,512]{2,1,0:T(8,128)S(1)}, f32[3,8,512]{2,1,0:T(8,128)S(1)}, u32[]{:S(2)}, u32[]{:S(2)}) collective-permute-start(f32[3,8,512]{2,1,0:T(8,128)S(1)} %get-tuple-element.154), channel_id=1, source_target_pairs={{0,4},{4,0},{8,12},{12,8},{16,20},{20,16},{24,28},{28,24},{1,5},{5... | collective-permute-start | bytes 147464 | tf_op jit(solution)/shard_map/ppermute | solution.py:81
  96.5 4.6 %collective-permute-start.20 = (f32[3,8,512]{2,1,0:T(8,128)S(1)}, f32[3,8,512]{2,1,0:T(8,128)S(1)}, u32[]{:S(2)}, u32[]{:S(2)}) collective-permute-start(f32[3,8,512]{2,1,0:T(8,128)S(1)} %pad_maximum_fusion.3), channel_id=1, source_target_pairs={{0,8},{4,12},{8,0},{12,4},{16,24},{20,28},{24,16},{28,20},{1,9},{5... | collective-permute-start | bytes 147464 | tf_op jit(solution)/shard_map/ppermute | solution.py:81
  101.1 5.6 %collective-permute-start.21 = (f32[3,8,512]{2,1,0:T(8,128)S(1)}, f32[3,8,512]{2,1,0:T(8,128)S(1)}, u32[]{:S(2)}, u32[]{:S(2)}) collective-permute-start(f32[3,8,512]{2,1,0:T(8,128)S(1)} %pad_maximum_fusion.4), channel_id=1, source_target_pairs={{0,16},{4,20},{8,24},{12,28},{16,0},{20,4},{24,8},{28,12},{1,17},{... | collective-permute-start | bytes 147464 | tf_op jit(solution)/shard_map/ppermute | solution.py:81
  102.4 6.1 %collective-permute-start.22 = (f32[4,8,512]{2,1,0:T(8,128)S(1)}, f32[4,8,512]{2,1,0:T(8,128)S(1)}, u32[]{:S(2)}, u32[]{:S(2)}) collective-permute-start(f32[4,8,512]{2,1,0:T(8,128)S(1)} %get-tuple-element.161), channel_id=1, source_target_pairs={{4,0},{8,4},{12,8},{16,12},{20,16},{24,20},{28,24},{5,1},{9,5},{13... | collective-permute-start | bytes 196616 | tf_op jit(solution)/shard_map/ppermute | solution.py:765
  116.5 13.4 %collective-permute-start.26 = (bf16[2,2,128,512]{3,2,1,0:T(8,128)(2,1)S(1)}, bf16[2,2,128,512]{3,2,1,0:T(8,128)(2,1)S(1)}, u32[]{:S(2)}, u32[]{:S(2)}) collective-permute-start(bf16[2,2,128,512]{3,2,1,0:T(8,128)(2,1)S(1)} %get-tuple-element.180), channel_id=1, source_target_pairs={{0,2},{1,3},{2,0},{3,1},{4,6},{5,7},{6,4},{7,5},{8,10},{9,11},{10,... | collective-permute-start | bytes 1572872 | tf_op jit(solution)/shard_map/ppermute | solution.py:81
  117.0 12.8 %collective-permute-start.25 = (bf16[2,2,128,512]{3,2,1,0:T(8,128)(2,1)S(1)}, bf16[2,2,128,512]{3,2,1,0:T(8,128)(2,1)S(1)}, u32[]{:S(2)}, u32[]{:S(2)}) collective-permute-start(bf16[2,2,128,512]{3,2,1,0:T(8,128)(2,1)S(1)} %get-tuple-element.178), channel_id=1, source_target_pairs={{0,1},{1,0},{2,3},{3,2},{4,5},{5,4},{6,7},{7,6},{8,9},{9,8},{10,11... | collective-permute-start | bytes 1572872 | tf_op jit(solution)/shard_map/ppermute | solution.py:81
  117.1 12.6 %collective-permute-start.23 = (bf16[128,1536]{1,0:T(8,128)(2,1)S(1)}, bf16[128,1536]{1,0:T(8,128)(2,1)S(1)}, u32[]{:S(2)}, u32[]{:S(2)}) collective-permute-start(bf16[128,1536]{1,0:T(8,128)(2,1)S(1)} %get-tuple-element.168), channel_id=1, source_target_pairs={{0,8},{8,16},{16,24},{24,28},{28,20},{20,12},{12,4},{4,0},{1,9},{9... | collective-permute-start | bytes 1179656 | tf_op jit(solution)/shard_map/ppermute | solution.py:64
  118.2 11.5 %collective-permute-start.24 = (bf16[128,1536]{1,0:T(8,128)(2,1)S(1)}, bf16[128,1536]{1,0:T(8,128)(2,1)S(1)}, u32[]{:S(2)}, u32[]{:S(2)}) collective-permute-start(bf16[128,1536]{1,0:T(8,128)(2,1)S(1)} %get-tuple-element.169), channel_id=1, source_target_pairs={{0,4},{8,0},{16,8},{24,16},{28,24},{20,28},{12,20},{4,12},{1,5},{9... | collective-permute-start | bytes 1179656 | tf_op jit(solution)/shard_map/ppermute | solution.py:64
  129.9 19.4 %collective-permute-start.28 = (bf16[256,1536]{1,0:T(8,128)(2,1)S(1)}, bf16[256,1536]{1,0:T(8,128)(2,1)S(1)}, u32[]{:S(2)}, u32[]{:S(2)}) collective-permute-start(bf16[256,1536]{1,0:T(8,128)(2,1)S(1)} %get-tuple-element.183), channel_id=1, source_target_pairs={{0,4},{8,0},{16,8},{24,16},{28,24},{20,28},{12,20},{4,12},{1,5},{9... | collective-permute-start | bytes 2359304 | tf_op jit(solution)/shard_map/ppermute | solution.py:64
  131.7 18.9 %collective-permute-start.27 = (bf16[256,1536]{1,0:T(8,128)(2,1)S(1)}, bf16[256,1536]{1,0:T(8,128)(2,1)S(1)}, u32[]{:S(2)}, u32[]{:S(2)}) collective-permute-start(bf16[256,1536]{1,0:T(8,128)(2,1)S(1)} %get-tuple-element.181), channel_id=1, source_target_pairs={{0,8},{8,16},{16,24},{24,28},{28,20},{20,12},{12,4},{4,0},{1,9},{9... | collective-permute-start | bytes 2359304 | tf_op jit(solution)/shard_map/ppermute | solution.py:64
  132.0 18.9 %collective-permute-start.29 = (bf16[2,2,128,512]{3,2,1,0:T(8,128)(2,1)S(1)}, bf16[2,2,128,512]{3,2,1,0:T(8,128)(2,1)S(1)}, u32[]{:S(2)}, u32[]{:S(2)}) collective-permute-start(bf16[2,2,128,512]{3,2,1,0:T(8,128)(2,1)S(1)} %get-tuple-element.188), channel_id=1, source_target_pairs={{0,3},{1,2},{2,1},{3,0},{4,7},{5,6},{6,5},{7,4},{8,11},{9,10},{10,... | collective-permute-start | bytes 1572872 | tf_op jit(solution)/shard_map/ppermute | solution.py:81
  150.9 4.4 %collective-permute-start.34 = (bf16[256,2048]{1,0:T(8,128)(2,1)S(1)}, bf16[256,2048]{1,0:T(8,128)(2,1)S(1)}, u32[]{:S(2)}, u32[]{:S(2)}) collective-permute-start(bf16[256,2048]{1,0:T(8,128)(2,1)S(1)} %get-tuple-element.210), channel_id=1, source_target_pairs={{0,1},{1,0},{2,3},{3,2},{4,5},{5,4},{6,7},{7,6},{8,9},{9,8},{10,11... | collective-permute-start | bytes 3145736 | tf_op jit(solution)/shard_map/ppermute | solution.py:81
  151.0 2.7 %collective-permute-start.30 = (f32[8,2048]{1,0:T(8,128)S(1)}, f32[8,2048]{1,0:T(8,128)S(1)}, u32[]{:S(2)}, u32[]{:S(2)}) collective-permute-start(f32[8,2048]{1,0:T(8,128)S(1)} %pad_maximum_fusion.2), channel_id=1, source_target_pairs={{0,1},{1,0},{2,3},{3,2},{4,5},{5,4},{6,7},{7,6},{8,9},{9,8},{10,11... | collective-permute-start | bytes 196616 | tf_op jit(solution)/shard_map/ppermute | solution.py:81
  151.6 22.5 %collective-permute-start.35 = (bf16[256,2048]{1,0:T(8,128)(2,1)S(1)}, bf16[256,2048]{1,0:T(8,128)(2,1)S(1)}, u32[]{:S(2)}, u32[]{:S(2)}) collective-permute-start(bf16[256,2048]{1,0:T(8,128)(2,1)S(1)} %get-tuple-element.212), channel_id=1, source_target_pairs={{0,1},{1,0},{2,3},{3,2},{4,5},{5,4},{6,7},{7,6},{8,9},{9,8},{10,11... | collective-permute-start | bytes 3145736 | tf_op jit(solution)/shard_map/ppermute | solution.py:81
  151.6 19.9 %collective-permute-start.33 = (bf16[256,1536]{1,0:T(8,128)(2,1)S(1)}, bf16[256,1536]{1,0:T(8,128)(2,1)S(1)}, u32[]{:S(2)}, u32[]{:S(2)}) collective-permute-start(bf16[256,1536]{1,0:T(8,128)(2,1)S(1)} %get-tuple-element.207), channel_id=1, source_target_pairs={{0,4},{8,0},{16,8},{24,16},{28,24},{20,28},{12,20},{4,12},{1,5},{9... | collective-permute-start | bytes 2359304 | tf_op jit(solution)/shard_map/ppermute | solution.py:64
  153.1 20.3 %collective-permute-start.32 = (bf16[256,1536]{1,0:T(8,128)(2,1)S(1)}, bf16[256,1536]{1,0:T(8,128)(2,1)S(1)}, u32[]{:S(2)}, u32[]{:S(2)}) collective-permute-start(bf16[256,1536]{1,0:T(8,128)(2,1)S(1)} %get-tuple-element.206), channel_id=1, source_target_pairs={{0,8},{8,16},{16,24},{24,28},{28,20},{20,12},{12,4},{4,0},{1,9},{9... | collective-permute-start | bytes 2359304 | tf_op jit(solution)/shard_map/ppermute | solution.py:64
  153.8 4.3 %collective-permute-start.31 = (f32[8,2048]{1,0:T(8,128)S(1)}, f32[8,2048]{1,0:T(8,128)S(1)}, u32[]{:S(2)}, u32[]{:S(2)}) collective-permute-start(f32[8,2048]{1,0:T(8,128)S(1)} %select_maximum_fusion), channel_id=1, source_target_pairs={{0,2},{1,3},{2,0},{3,1},{4,6},{5,7},{6,4},{7,5},{8,10},{9,11},{10,... | collective-permute-start | bytes 196616 | tf_op jit(solution)/shard_map/ppermute | solution.py:81
  155.9 18.2 %collective-permute-start.37 = (bf16[128,2048]{1,0:T(8,128)(2,1)S(1)}, bf16[128,2048]{1,0:T(8,128)(2,1)S(1)}, u32[]{:S(2)}, u32[]{:S(2)}) collective-permute-start(bf16[128,2048]{1,0:T(8,128)(2,1)S(1)} %get-tuple-element.215), channel_id=1, source_target_pairs={{0,2},{1,3},{2,0},{3,1},{4,6},{5,7},{6,4},{7,5},{8,10},{9,11},{10,... | collective-permute-start | bytes 1572872 | tf_op jit(solution)/shard_map/ppermute | solution.py:81
  158.1 16.0 %collective-permute-start.36 = (f32[6,2048]{1,0:T(8,128)S(1)}, f32[6,2048]{1,0:T(8,128)S(1)}, u32[]{:S(2)}, u32[]{:S(2)}) collective-permute-start(f32[6,2048]{1,0:T(8,128)S(1)} %slice_add_fusion.2), channel_id=1, source_target_pairs={{0,4},{4,0},{8,12},{12,8},{16,20},{20,16},{24,28},{28,24},{1,5},{5... | collective-permute-start | bytes 147464 | tf_op jit(solution)/shard_map/ppermute | solution.py:81
  174.1 14.9 %collective-permute-start.39 = (bf16[256,1024]{1,0:T(8,128)(2,1)S(1)}, bf16[256,1024]{1,0:T(8,128)(2,1)S(1)}, u32[]{:S(2)}, u32[]{:S(2)}) collective-permute-start(bf16[256,1024]{1,0:T(8,128)(2,1)S(1)} %get-tuple-element.219), channel_id=1, source_target_pairs={{0,4},{8,0},{16,8},{24,16},{28,24},{20,28},{12,20},{4,12},{1,5},{9... | collective-permute-start | bytes 1572872 | tf_op jit(solution)/shard_map/ppermute | solution.py:64
  174.4 14.9 %collective-permute-start.38 = (bf16[256,1024]{1,0:T(8,128)(2,1)S(1)}, bf16[256,1024]{1,0:T(8,128)(2,1)S(1)}, u32[]{:S(2)}, u32[]{:S(2)}) collective-permute-start(bf16[256,1024]{1,0:T(8,128)(2,1)S(1)} %get-tuple-element.217), channel_id=1, source_target_pairs={{0,8},{8,16},{16,24},{24,28},{28,20},{20,12},{12,4},{4,0},{1,9},{9... | collective-permute-start | bytes 1572872 | tf_op jit(solution)/shard_map/ppermute | solution.py:64
  177.2 17.2 %collective-permute-start.42 = (bf16[128,2048]{1,0:T(8,128)(2,1)S(1)}, bf16[128,2048]{1,0:T(8,128)(2,1)S(1)}, u32[]{:S(2)}, u32[]{:S(2)}) collective-permute-start(bf16[128,2048]{1,0:T(8,128)(2,1)S(1)} %get-tuple-element.224), channel_id=1, source_target_pairs={{0,2},{1,3},{2,0},{3,1},{4,6},{5,7},{6,4},{7,5},{8,10},{9,11},{10,... | collective-permute-start | bytes 1572872 | tf_op jit(solution)/shard_map/ppermute | solution.py:81
  178.7 15.6 %collective-permute-start.41 = (bf16[256,512]{1,0:T(8,128)(2,1)S(1)}, bf16[256,512]{1,0:T(8,128)(2,1)S(1)}, u32[]{:S(2)}, u32[]{:S(2)}) collective-permute-start(bf16[256,512]{1,0:T(8,128)(2,1)S(1)} %get-tuple-element.223), channel_id=1, source_target_pairs={{0,4},{8,0},{16,8},{24,16},{28,24},{20,28},{12,20},{4,12},{1,5},{9... | collective-permute-start | bytes 786440 | tf_op jit(solution)/shard_map/ppermute | solution.py:64
  179.0 15.3 %collective-permute-start.40 = (bf16[256,512]{1,0:T(8,128)(2,1)S(1)}, bf16[256,512]{1,0:T(8,128)(2,1)S(1)}, u32[]{:S(2)}, u32[]{:S(2)}) collective-permute-start(bf16[256,512]{1,0:T(8,128)(2,1)S(1)} %get-tuple-element.221), channel_id=1, source_target_pairs={{0,8},{8,16},{16,24},{24,28},{28,20},{20,12},{12,4},{4,0},{1,9},{9... | collective-permute-start | bytes 786440 | tf_op jit(solution)/shard_map/ppermute | solution.py:64
  189.6 4.7 %collective-permute-start.43 = (f32[6,2048]{1,0:T(8,128)S(1)}, f32[6,2048]{1,0:T(8,128)S(1)}, u32[]{:S(2)}, u32[]{:S(2)}) collective-permute-start(f32[6,2048]{1,0:T(8,128)S(1)} %add.316), channel_id=1, source_target_pairs={{0,8},{4,12},{8,0},{12,4},{16,24},{20,28},{24,16},{28,20},{1,9},{5... | collective-permute-start | bytes 147464 | tf_op jit(solution)/shard_map/ppermute | solution.py:81
  192.0 9.9 %collective-permute-start.44 = (bf16[256,512]{1,0:T(8,128)(2,1)S(1)}, bf16[256,512]{1,0:T(8,128)(2,1)S(1)}, u32[]{:S(2)}, u32[]{:S(2)}) collective-permute-start(bf16[256,512]{1,0:T(8,128)(2,1)S(1)} %get-tuple-element.239), channel_id=1, source_target_pairs={{0,2},{1,3},{2,0},{3,1},{4,6},{5,7},{6,4},{7,5},{8,10},{9,11},{10,... | collective-permute-start | bytes 786440 | tf_op jit(solution)/shard_map/ppermute | solution.py:81
  194.3 7.8 %collective-permute-start.45 = (bf16[256,512]{1,0:T(8,128)(2,1)S(1)}, bf16[256,512]{1,0:T(8,128)(2,1)S(1)}, u32[]{:S(2)}, u32[]{:S(2)}) collective-permute-start(bf16[256,512]{1,0:T(8,128)(2,1)S(1)} %get-tuple-element.238), channel_id=1, source_target_pairs={{0,1},{1,0},{2,3},{3,2},{4,5},{5,4},{6,7},{7,6},{8,9},{9,8},{10,11... | collective-permute-start | bytes 786440 | tf_op jit(solution)/shard_map/ppermute | solution.py:81
  194.3 6.9 %collective-permute-start.46 = (f32[6,2048]{1,0:T(8,128)S(1)}, f32[6,2048]{1,0:T(8,128)S(1)}, u32[]{:S(2)}, u32[]{:S(2)}) collective-permute-start(f32[6,2048]{1,0:T(8,128)S(1)} %add.324), channel_id=1, source_target_pairs={{0,16},{4,20},{8,24},{12,28},{16,0},{20,4},{24,8},{28,12},{1,17},{... | collective-permute-start | bytes 147464 | tf_op jit(solution)/shard_map/ppermute | solution.py:81
  (11 other events, 236.0 us)

commit v6 on v5

--- a/solution.py
+++ b/solution.py
@@ -23,7 +23,7 @@
     return pl.BlockSpec(memory_space=pltpu.SMEM)
 
 
-def call(kernel, out_shape, operands, scratch=(), scalars=0, pinned=True):
+def call(kernel, out_shape, operands, scratch=(), scalars=0, pinned=True, aliases=None):
     held = jax.tree.map(lambda out: pltpu.VMEM(out.shape, out.dtype), out_shape)
     return pl.pallas_call(
         kernel,
@@ -31,6 +31,7 @@
         in_specs=[smem_spec()] * scalars + [vmem_spec()] * (len(operands) - scalars),
         out_specs=jax.tree.map(lambda _: vmem_spec(), out_shape),
         scratch_shapes=list(scratch),
+        input_output_aliases=aliases or {},
         compiler_params=pltpu.CompilerParams(vmem_limit_bytes=lax.axis_size("stream") * ROOM),
         cost_estimate=pl.CostEstimate(flops=0, bytes_accessed=0, transcendentals=0),
     )(
@@ -267,13 +268,13 @@
 
 
 def second_kernel(
-    dims, place, lens, v0, v1, earlier, later, start, linked, fields, known, scans, *refs
+    dims, place, lens, v0, v1, earlier, later, start, fields, known, scans, *refs
 ):
     vecs = (v0, v1)
     seqs, span, width, slots, tail = dims
     stride = span + PAD
     grads, moved = refs[0], refs[1 : slots + 1]
-    final, sums, outs, directs, gcs, fts, rts = refs[slots + 1 :]
+    final, sums, ending, ends_kept, outs, directs, gcs, fts, rts = refs[slots + 1 :]
     cand, forg, rese = (fields.at[i] for i in range(3))
     gs, xs, products, injected = known.at[0], known.at[1], scans.at[0], scans.at[1]
     per = seqs // slots
@@ -295,13 +296,15 @@
         def token(ref, row):
             return strided(ref, row, seqs, stride, lane, lanes)
 
+        def token_of(ref, row):
+            return strided(ref, row, seqs, stride)
+
         def state_at(row):
             return token(products, row) * begin + token(injected, row)
 
         end = state_at(span - 1 + PAD)
         final[:, units] = later[0, :, units] * end + later[1, :, units]
-        link = [linked[i, :, units] for i in range(4)]
-        upcoming = end * (link[0] * after + link[2]) - link[1] * after + link[3]
+        ending[:, units] = end
 
         def backward(i, carry):
             reached, upcoming, state, c, pf, pr, bf, br = carry
@@ -336,8 +339,9 @@
         zero = jnp.zeros((seqs, step), f32)
         last = token(cand, span - 1 + PAD)
         done = lax.fori_loop(
-            0, span, backward, (after, upcoming, end, last, zero, zero, zero, zero), unroll=4
-        )
+            0, span, backward, (after, zero, end, last, zero, zero, zero, zero), unroll=4
+        )
+        ends_kept[:, units] = token_of(gcs, span - 1 + PAD)
         for i in range(4):
             sums[i : i + 1, units] = jnp.sum(done[4 + i], axis=0, keepdims=True)
         for n in range(seqs):
@@ -349,6 +353,19 @@
                 grads[to : to + span, here] = get_rows(ref, at, span).astype(bf16)
             moved[k][0, j, :, units] = get_rows(outs, at, span).astype(bf16)
             moved[k][1, j, :, units] = get_rows(directs, at, span).astype(bf16)
+
+
+def mend_kernel(dims, grads, ending, kept, later, linked, out):
+    per, span, width, ext = dims
+    after = later[2]
+    upcoming = ending[...] * (linked[0] * after + linked[2]) - linked[1] * after + linked[3]
+    value = (kept[...] + upcoming).astype(bf16)
+    last = lax.broadcasted_iota(jnp.int32, (16, width), 0) == 15
+    for n in range(ending.shape[0]):
+        at = n // per * ext + n % per * span + span - 16
+        rows = slice(at, at + 16)
+        row = jnp.broadcast_to(value[n : n + 1, :].astype(f32), (16, width))
+        out[rows, :width] = jnp.where(last, row, grads[rows, :width].astype(f32)).astype(bf16)
 
 
 def partial_kernel(distances, depth, width, owners, place, normed, grads, *outs):
@@ -780,6 +797,7 @@
 
     def second():
         _, earlier, later = box["known"]
+        later = jnp.stack(later)
         out = call(
             functools.partial(second_kernel, (seqs, span, width, slots, tail)),
             [
@@ -787,15 +805,16 @@
                 *[jax.ShapeDtypeStruct((2, per, span, width), bf16)] * slots,
                 jax.ShapeDtypeStruct((seqs, width), f32),
                 jax.ShapeDtypeStruct((8, width), f32),
+                jax.ShapeDtypeStruct((seqs, width), f32),
+                jax.ShapeDtypeStruct((seqs, width), f32),
             ],
             [
                 place,
                 take(box["ends"]),
                 *vectors[:2],
                 jnp.stack(earlier),
-                jnp.stack(later),
+                later,
                 box["start"],
-                box["linked"],
                 *box["fields"],
             ],
             scratch=[space] * 5,
@@ -803,6 +822,12 @@
         )
         box["grads"], box["moving"] = out[0], out[1 : slots + 1]
         box["final"], box["sums"] = out[slots + 1], out[slots + 2]
+        box["grads"] = call(
+            functools.partial(mend_kernel, (per, span, width, rows + tail)),
+            jax.ShapeDtypeStruct((slots * (rows + tail), 3 * width), bf16),
+            [out[0], *out[slots + 3 :], later, box["linked"]],
+            aliases={0: 0},
+        )
         rounds.before = []
         box["farthest"] = partials((far,), bf16, 2)
         box["grads"] = lax.optimization_barrier((box["grads"], box["farthest"]))[0]

time: 204 us -> 200 us (0.980)
    pallas_call x15 -> x16, Pallas kernels: 44.5 us -> 44.6 us  [call(): pl.pallas_call(kernel, out_shape=held if pinned else out_shape, in_specs=...]
  transfers between devices with their start and end apart: 47 -> 47, of which waited for: 30 -> 30; matrix products, arithmetic and copies ran while one was open for 4% -> 4% of each run, Pallas kernels for 16% -> 19%
where the time goes in v6:
time: 200 us
  waiting for transfers between devices  96.4 us (48%)
  starting transfers between devices  46.3 us (23%)
  Pallas kernels  44.6 us (22%)
  other arithmetic  7.47 us (4%)
  local copies, waits for them, and re-layouts  3.59 us (2%)
    ppermute x27, waiting for transfers between devices, swapped(): lax.ppermute(value, axis, [(i, i ^ bit) for i in range(lax.axis_size(axis...  51.6 us
    ppermute x18, waiting for transfers between devices, along_ring(): lax.ppermute(value, 'seq', [(order[i], order[(i + steps) % count]) for i...  44.8 us
    pallas_call x16, Pallas kernels, call(): pl.pallas_call(kernel, out_shape=held if pinned else out_shape, in_specs=...  44.6 us
    ppermute x27, starting transfers between devices, swapped(): lax.ppermute(value, axis, [(i, i ^ bit) for i in range(lax.axis_size(axis...  23 us
    ppermute x18, starting transfers between devices, along_ring(): lax.ppermute(value, 'seq', [(order[i], order[(i + steps) % count]) for i...  18.7 us
  transfers between devices with their start and end apart: 47, of which 30 were waited for; matrix products, arithmetic and copies ran while one was open for 4% of the time, Pallas kernels for 19%

profile of v6, /device:TPU:0, one launch (start us, length us, event | category | flops | bytes accessed | tf_op | source)
XLA Modules:
  0.0 199.9 jit_solution(9891906002610279407)
XLA Ops:
  3.0 2.6 %collective-permute-start.1 = (bf16[256,512]{1,0:T(8,128)(2,1)S(1)}, bf16[256,512]{1,0:T(8,128)(2,1)S(1)}, u32[]{:S(2)}, u32[]{:S(2)}) collective-permute-start(bf16[256,512]{1,0:T(8,128)(2,1)S(1)} %get-tuple-element.241), channel_id=1, source_target_pairs={{0,2},{1,3},{2,0},{3,1},{4,6},{5,7},{6,4},{7,5},{8,10},{9,11},{10,... | collective-permute-start | bytes 786440 | tf_op jit(solution)/shard_map/ppermute | solution.py:82
  6.7 3.4 %collective-permute-start.2 = (bf16[2,2048]{1,0:T(2,128)(2,1)S(1)}, bf16[2,2048]{1,0:T(2,128)(2,1)S(1)}, u32[]{:S(2)}, u32[]{:S(2)}) collective-permute-start(bf16[2,2048]{1,0:T(2,128)(2,1)S(1)} %slice_bitcast_fusion.1), channel_id=1, source_target_pairs={{0,4},{4,8},{8,12},{12,16},{16,20},{20,24},{24,28},{1,5},{5,9},{9,... | collective-permute-start | bytes 24584 | tf_op jit(solution)/shard_map/ppermute | solution.py:657
  10.1 2.4 %collective-permute-done.1 = bf16[256,512]{1,0:T(8,128)(2,1)S(1)} collective-permute-done((bf16[256,512]{1,0:T(8,128)(2,1)S(1)}, bf16[256,512]{1,0:T(8,128)(2,1)S(1)}, u32[]{:S(2)}, u32[]{:S(2)}) %collective-permute-start.1) | collective-permute-done | bytes 262176 | tf_op jit(solution)/shard_map/ppermute | solution.py:82
  12.6 2.1 %collective-permute-start.3 = (bf16[256,1536]{1,0:T(8,128)(2,1)S(1)}, bf16[256,1536]{1,0:T(8,128)(2,1)S(1)}, u32[]{:S(2)}, u32[]{:S(2)}) collective-permute-start(bf16[256,1536]{1,0:T(8,128)(2,1)S(1)} %pad_maximum_fusion.1.refs_0_), channel_id=1, source_target_pairs={{0,8},{8,16},{16,24},{24,28},{28,20},{20,12},{12,4},{4,0},{1,9},{9... | collective-permute-start | bytes 2359304 | tf_op jit(solution)/shard_map/ppermute | solution.py:65
  14.8 1.8 collective-permute-start.5
  16.9 11.0 %collective-permute-done.5.refs_2_.refs_11_ = bf16[128,2048]{1,0:T(8,128)(2,1)S(1)} collective-permute-done((bf16[128,2048]{1,0:T(8,128)(2,1)S(1)}, bf16[128,2048]{1,0:T(8,128)(2,1)S(1)}, u32[]{:S(2)}, u32[]{:S(2)}) %collective-permute-start.5) | collective-permute-done | bytes 524320 | tf_op jit(solution)/shard_map/ppermute | solution.py:82
  27.9 4.0 %collective-permute-done.3.refs_1_ = bf16[256,1536]{1,0:T(8,128)(2,1)S(1)} collective-permute-done((bf16[256,1536]{1,0:T(8,128)(2,1)S(1)}, bf16[256,1536]{1,0:T(8,128)(2,1)S(1)}, u32[]{:S(2)}, u32[]{:S(2)}) %collective-permute-start.3) | collective-permute-done | bytes 786464 | tf_op jit(solution)/shard_map/ppermute | solution.py:65
  31.9 1.3 collective-permute-done.4.refs_2_
  33.7 1.6 collective-permute-start.6
  35.4 1.6 collective-permute-start.9
  38.8 11.7 %collective-permute-done.9.refs_3_.refs_12_ = bf16[144,2048]{1,0:T(8,128)(2,1)S(1)} collective-permute-done((bf16[144,2048]{1,0:T(8,128)(2,1)S(1)}, bf16[144,2048]{1,0:T(8,128)(2,1)S(1)}, u32[]{:S(2)}, u32[]{:S(2)}) %collective-permute-start.9) | collective-permute-done | bytes 589856 | tf_op jit(solution)/shard_map/ppermute | solution.py:82
  50.6 2.6 %collective-permute-done.7.refs_4_ = bf16[256,1536]{1,0:T(8,128)(2,1)S(1)} collective-permute-done((bf16[256,1536]{1,0:T(8,128)(2,1)S(1)}, bf16[256,1536]{1,0:T(8,128)(2,1)S(1)}, u32[]{:S(2)}, u32[]{:S(2)}) %collective-permute-start.7) | collective-permute-done | bytes 786464 | tf_op jit(solution)/shard_map/ppermute | solution.py:65
  53.4 1.6 collective-permute-start.12
  55.0 1.5 collective-permute-start.16
  57.7 5.2 %collective-permute-done.12.refs_4_ = bf16[272,512]{1,0:T(8,128)(2,1)S(1)} collective-permute-done((bf16[272,512]{1,0:T(8,128)(2,1)S(1)}, bf16[272,512]{1,0:T(8,128)(2,1)S(1)}, u32[]{:S(2)}, u32[]{:S(2)}) %collective-permute-start.12) | collective-permute-done | bytes 278560 | tf_op jit(solution)/shard_map/ppermute | solution.py:82
  62.9 5.0 %collective-permute-done.13.refs_5_ = bf16[272,512]{1,0:T(8,128)(2,1)S(1)} collective-permute-done((bf16[272,512]{1,0:T(8,128)(2,1)S(1)}, bf16[272,512]{1,0:T(8,128)(2,1)S(1)}, u32[]{:S(2)}, u32[]{:S(2)}) %collective-permute-start.13) | collective-permute-done | bytes 278560 | tf_op jit(solution)/shard_map/ppermute | solution.py:82
  68.0 3.7 %shard_map.187 = (bf16[1088,2048]{1,0:T(8,128)(2,1)S(1)}, f32[1024,128]{1,0:T(8,128)S(1)}, f32[1024,128]{1,0:T(8,128)S(1)}, bf16[1024,512]{1,0:T(8,128)(2,1)S(1)}) custom-call(s32[6]{0:T(128)S(1)} %stack.116.place, bf16[272,2048]{1,0:T(8,128)(2,1)S(1)} %maximum_maximum_fusion.refs_0_.refs_9_, bf16[272,2048]{1,0:T(8,128)(2,1)S(1)} %collective-permute-done.8.refs_1_.refs_10_, ...), custom_call_target="tpu_custom_call" | custom-call | tf_op jit(solution)/shard_map/pallas_call | solution.py:28
  71.7 3.0 %collective-permute-done.16.refs_6_ = bf16[256,1536]{1,0:T(8,128)(2,1)S(1)} collective-permute-done((bf16[256,1536]{1,0:T(8,128)(2,1)S(1)}, bf16[256,1536]{1,0:T(8,128)(2,1)S(1)}, u32[]{:S(2)}, u32[]{:S(2)}) %collective-permute-start.16) | collective-permute-done | bytes 786464 | tf_op jit(solution)/shard_map/ppermute | solution.py:65
  75.9 1.6 collective-permute-start.18
  78.3 6.8 %shard_map.188.begun = f32[1088,1536]{1,0:T(8,128)S(1)} custom-call(s32[8]{0:T(128)S(1)} %stack.120.sources, bf16[1088,2048]{1,0:T(8,128)(2,1)S(1)} %get-tuple-element.153.normed, bf16[256,1536]{1,0:T(8,128)(2,1)S(1)} %pad_maximum_fusion.1.refs_0_, bf16[256,1536]{1,0:T(8,128)(2,1)S(1)} %collective-permute-done.3.refs_1_, ...), custom_call_target="tpu_custom_call" | custom-call | tf_op jit(solution)/shard_map/pallas_call | solution.py:28
  85.9 1.6 collective-permute-done.17.refs_0_.refs_7_
  87.5 4.8 %shard_map.189 = (f32[3,4,1088,128]{3,2,1,0:T(8,128)S(1)}, f32[2,4,1088,128]{3,2,1,0:T(8,128)S(1)}, f32[2,4,1088,128]{3,2,1,0:T(8,128)S(1)}, f32[3,8,512]{2,1,0:T(8,128)S(1)}, f32[4,8,512]{2,1,0:T(8,128)S(1)}) custom-call(s32[8]{0:T(128)S(1)} %stack.120.sources, s32[6]{0:T(128)S(1)} %stack.116.place, bf16[1088,2048]{1,0:T(8,128)(2,1)S(1)} %get-tuple-element.153.normed, ...), custom_call_target="tpu_custom_call" | custom-call | tf_op jit(solution)/shard_map/pallas_call | solution.py:28
  92.3 1.6 collective-permute-start.19
  93.9 2.5 %collective-permute-done.19 = f32[3,8,512]{2,1,0:T(8,128)S(1)} collective-permute-done((f32[3,8,512]{2,1,0:T(8,128)S(1)}, f32[3,8,512]{2,1,0:T(8,128)S(1)}, u32[]{:S(2)}, u32[]{:S(2)}) %collective-permute-start.19) | collective-permute-done | bytes 49184 | tf_op jit(solution)/shard_map/ppermute | solution.py:82
  97.6 3.5 %collective-permute-done.20 = f32[3,8,512]{2,1,0:T(8,128)S(1)} collective-permute-done((f32[3,8,512]{2,1,0:T(8,128)S(1)}, f32[3,8,512]{2,1,0:T(8,128)S(1)}, u32[]{:S(2)}, u32[]{:S(2)}) %collective-permute-start.20) | collective-permute-done | bytes 49184 | tf_op jit(solution)/shard_map/ppermute | solution.py:82
  102.4 1.3 collective-permute-start.22
  103.7 3.0 %collective-permute-done.21 = f32[3,8,512]{2,1,0:T(8,128)S(1)} collective-permute-done((f32[3,8,512]{2,1,0:T(8,128)S(1)}, f32[3,8,512]{2,1,0:T(8,128)S(1)}, u32[]{:S(2)}, u32[]{:S(2)}) %collective-permute-start.21) | collective-permute-done | bytes 49184 | tf_op jit(solution)/shard_map/ppermute | solution.py:82
  106.8 6.2 %shard_map.190 = (bf16[1088,1536]{1,0:T(8,128)(2,1)S(1)}, bf16[2,2,128,512]{3,2,1,0:T(8,128)(2,1)S(1)}, bf16[2,2,128,512]{3,2,1,0:T(8,128)(2,1)S(1)}, bf16[2,2,1...) custom-call(s32[6]{0:T(128)S(1)} %stack.116.place, ...), custom_call_target="tpu_custom_call" | custom-call | tf_op jit(solution)/shard_map/pallas_call | solution.py:28
  113.0 1.8 shard_map.192
  117.4 2.8 %shard_map.195 = (f32[256,1536]{1,0:T(8,128)S(1)}, f32[256,1536]{1,0:T(8,128)S(1)}) custom-call(s32[8]{0:T(128)S(1)} %stack.109.owners, s32[6]{0:T(128)S(1)} %stack.116.place, bf16[1088,2048]{1,0:T(8,128)(2,1)S(1)} %get-tuple-element.153.normed, bf16[1088,1536]{1,0:T(8,128)(2,1)S(1)} %shard_map.191.grads), custom_call_target="tpu_custom_call" | custom-call | tf_op jit(solution)/shard_map/pallas_call | solution.py:28
  120.2 2.8 %shard_map.193 = (f32[256,1536]{1,0:T(8,128)S(1)}, f32[256,1536]{1,0:T(8,128)S(1)}) custom-call(s32[8]{0:T(128)S(1)} %stack.109.owners, s32[6]{0:T(128)S(1)} %stack.116.place, bf16[1088,2048]{1,0:T(8,128)(2,1)S(1)} %get-tuple-element.153.normed, bf16[1088,1536]{1,0:T(8,128)(2,1)S(1)} %shard_map.191.grads), custom_call_target="tpu_custom_call" | custom-call | tf_op jit(solution)/shard_map/pallas_call | solution.py:28
  123.0 3.9 %collective-permute-done.23.up = bf16[128,1536]{1,0:T(8,128)(2,1)S(1)} collective-permute-done((bf16[128,1536]{1,0:T(8,128)(2,1)S(1)}, bf16[128,1536]{1,0:T(8,128)(2,1)S(1)}, u32[]{:S(2)}, u32[]{:S(2)}) %collective-permute-start.23) | collective-permute-done | bytes 393248 | tf_op jit(solution)/shard_map/ppermute | solution.py:65
  130.0 2.8 %shard_map.197 = (f32[256,1536]{1,0:T(8,128)S(1)}, f32[256,1536]{1,0:T(8,128)S(1)}) custom-call(s32[8]{0:T(128)S(1)} %stack.109.owners, s32[6]{0:T(128)S(1)} %stack.116.place, bf16[1088,2048]{1,0:T(8,128)(2,1)S(1)} %get-tuple-element.153.normed, bf16[1088,1536]{1,0:T(8,128)(2,1)S(1)} %shard_map.191.grads), custom_call_target="tpu_custom_call" | custom-call | tf_op jit(solution)/shard_map/pallas_call | solution.py:28
  132.8 1.8 shard_map.196
  134.6 8.0 %shard_map.198 = (f32[256,2048]{1,0:T(8,128)S(1)}, bf16[256,2048]{1,0:T(8,128)(2,1)S(1)}, bf16[256,2048]{1,0:T(8,128)(2,1)S(1)}, bf16[256,2048]{1,0:T(8,128)(2,1)S(1)}, f32[8,2048]{1,0:T(8,128)S(1)}) custom-call(s32[8]{0:T(128)S(1)} %stack.120.sources, s32[6]{0:T(128)S(1)} %stack.116.place, bf16[1088,1536]{1,0:T(8,128)(2,1)S(1)} %shard_map.191.grads, ...), custom_call_target="tpu_custom_call" | custom-call | tf_op jit(solution)/shard_map/pallas_call | solution.py:28
  142.6 4.1 %collective-permute-done.28.down = bf16[256,1536]{1,0:T(8,128)(2,1)S(1)} collective-permute-done((bf16[256,1536]{1,0:T(8,128)(2,1)S(1)}, bf16[256,1536]{1,0:T(8,128)(2,1)S(1)}, u32[]{:S(2)}, u32[]{:S(2)}) %collective-permute-start.28) | collective-permute-done | bytes 786464 | tf_op jit(solution)/shard_map/ppermute | solution.py:65
  150.7 1.6 collective-permute-start.31
  153.4 1.7 collective-permute-done.31
  156.2 1.7 shard_map.200
  157.8 10.7 %collective-permute-done.33.down = bf16[256,1536]{1,0:T(8,128)(2,1)S(1)} collective-permute-done((bf16[256,1536]{1,0:T(8,128)(2,1)S(1)}, bf16[256,1536]{1,0:T(8,128)(2,1)S(1)}, u32[]{:S(2)}, u32[]{:S(2)}) %collective-permute-start.33) | collective-permute-done | bytes 786464 | tf_op jit(solution)/shard_map/ppermute | solution.py:65
  168.5 1.4 collective-permute-done.32.up
  170.9 1.7 collective-permute-start.38
  173.7 1.6 collective-permute-start.42
  175.6 1.7 collective-permute-start.40
  177.3 8.2 %collective-permute-done.39 = bf16[256,1024]{1,0:T(8,128)(2,1)S(1)} collective-permute-done((bf16[256,1024]{1,0:T(8,128)(2,1)S(1)}, bf16[256,1024]{1,0:T(8,128)(2,1)S(1)}, u32[]{:S(2)}, u32[]{:S(2)}) %collective-permute-start.39) | collective-permute-done | bytes 524320 | tf_op jit(solution)/shard_map/ppermute | solution.py:65
  186.1 1.8 collective-permute-start.43
  188.5 1.5 collective-permute-start.44
  194.7 3.0 %collective-permute-done.46 = f32[6,2048]{1,0:T(8,128)S(1)} collective-permute-done((f32[6,2048]{1,0:T(8,128)S(1)}, f32[6,2048]{1,0:T(8,128)S(1)}, u32[]{:S(2)}, u32[]{:S(2)}) %collective-permute-start.46) | collective-permute-done | bytes 49184 | tf_op jit(solution)/shard_map/ppermute | solution.py:82
  (146 shorter events, 34.6 us)
Async XLA Ops:
  2.5 7.6 %collective-permute-start = (bf16[256,512]{1,0:T(8,128)(2,1)S(1)}, bf16[256,512]{1,0:T(8,128)(2,1)S(1)}, u32[]{:S(2)}, u32[]{:S(2)}) collective-permute-start(bf16[256,512]{1,0:T(8,128)(2,1)S(1)} %get-tuple-element.240), channel_id=1, source_target_pairs={{0,1},{1,0},{2,3},{3,2},{4,5},{5,4},{6,7},{7,6},{8,9},{9,8},{10,11... | collective-permute-start | bytes 786440 | tf_op jit(solution)/shard_map/ppermute | solution.py:82
  3.0 9.5 %collective-permute-start.1 = (bf16[256,512]{1,0:T(8,128)(2,1)S(1)}, bf16[256,512]{1,0:T(8,128)(2,1)S(1)}, u32[]{:S(2)}, u32[]{:S(2)}) collective-permute-start(bf16[256,512]{1,0:T(8,128)(2,1)S(1)} %get-tuple-element.241), channel_id=1, source_target_pairs={{0,2},{1,3},{2,0},{3,1},{4,6},{5,7},{6,4},{7,5},{8,10},{9,11},{10,... | collective-permute-start | bytes 786440 | tf_op jit(solution)/shard_map/ppermute | solution.py:82
  6.7 5.9 %collective-permute-start.2 = (bf16[2,2048]{1,0:T(2,128)(2,1)S(1)}, bf16[2,2048]{1,0:T(2,128)(2,1)S(1)}, u32[]{:S(2)}, u32[]{:S(2)}) collective-permute-start(bf16[2,2048]{1,0:T(2,128)(2,1)S(1)} %slice_bitcast_fusion.1), channel_id=1, source_target_pairs={{0,4},{4,8},{8,12},{12,16},{16,20},{20,24},{24,28},{1,5},{5,9},{9,... | collective-permute-start | bytes 24584 | tf_op jit(solution)/shard_map/ppermute | solution.py:657
  12.6 19.4 %collective-permute-start.3 = (bf16[256,1536]{1,0:T(8,128)(2,1)S(1)}, bf16[256,1536]{1,0:T(8,128)(2,1)S(1)}, u32[]{:S(2)}, u32[]{:S(2)}) collective-permute-start(bf16[256,1536]{1,0:T(8,128)(2,1)S(1)} %pad_maximum_fusion.1.refs_0_), channel_id=1, source_target_pairs={{0,8},{8,16},{16,24},{24,28},{28,20},{20,12},{12,4},{4,0},{1,9},{9... | collective-permute-start | bytes 2359304 | tf_op jit(solution)/shard_map/ppermute | solution.py:65
  14.7 18.6 %collective-permute-start.4 = (bf16[256,1536]{1,0:T(8,128)(2,1)S(1)}, bf16[256,1536]{1,0:T(8,128)(2,1)S(1)}, u32[]{:S(2)}, u32[]{:S(2)}) collective-permute-start(bf16[256,1536]{1,0:T(8,128)(2,1)S(1)} %pad_maximum_fusion.1.refs_0_), channel_id=1, source_target_pairs={{0,4},{8,0},{16,8},{24,16},{28,24},{20,28},{12,20},{4,12},{1,5},{9... | collective-permute-start | bytes 2359304 | tf_op jit(solution)/shard_map/ppermute | solution.py:65
  14.8 13.1 %collective-permute-start.5 = (bf16[128,2048]{1,0:T(8,128)(2,1)S(1)}, bf16[128,2048]{1,0:T(8,128)(2,1)S(1)}, u32[]{:S(2)}, u32[]{:S(2)}) collective-permute-start(bf16[128,2048]{1,0:T(8,128)(2,1)S(1)} %slice_bitcast_fusion), channel_id=1, source_target_pairs={{0,2},{1,3},{2,0},{3,1},{4,6},{5,7},{6,4},{7,5},{8,10},{9,11},{10,... | collective-permute-start | bytes 1572872 | tf_op jit(solution)/shard_map/ppermute | solution.py:82
  33.3 20.1 %collective-permute-start.8 = (bf16[272,2048]{1,0:T(8,128)(2,1)S(1)}, bf16[272,2048]{1,0:T(8,128)(2,1)S(1)}, u32[]{:S(2)}, u32[]{:S(2)}) collective-permute-start(bf16[272,2048]{1,0:T(8,128)(2,1)S(1)} %maximum_maximum_fusion.refs_0_.refs_9_), channel_id=1, source_target_pairs={{0,1},{1,0},{2,3},{3,2},{4,5},{5,4},{6,7},{7,6},{8,9},{9,8},{10,11... | collective-permute-start | bytes 3342344 | tf_op jit(solution)/shard_map/ppermute | solution.py:82
  33.3 20.0 %collective-permute-start.7 = (bf16[256,1536]{1,0:T(8,128)(2,1)S(1)}, bf16[256,1536]{1,0:T(8,128)(2,1)S(1)}, u32[]{:S(2)}, u32[]{:S(2)}) collective-permute-start(bf16[256,1536]{1,0:T(8,128)(2,1)S(1)} %collective-permute-done.4.refs_2_), channel_id=1, source_target_pairs={{0,4},{8,0},{16,8},{24,16},{28,24},{20,28},{12,20},{4,12},{1,5},{9... | collective-permute-start | bytes 2359304 | tf_op jit(solution)/shard_map/ppermute | solution.py:65
  33.7 19.7 %collective-permute-start.6 = (bf16[256,1536]{1,0:T(8,128)(2,1)S(1)}, bf16[256,1536]{1,0:T(8,128)(2,1)S(1)}, u32[]{:S(2)}, u32[]{:S(2)}) collective-permute-start(bf16[256,1536]{1,0:T(8,128)(2,1)S(1)} %collective-permute-done.3.refs_1_), channel_id=1, source_target_pairs={{0,8},{8,16},{16,24},{24,28},{28,20},{20,12},{12,4},{4,0},{1,9},{9... | collective-permute-start | bytes 2359304 | tf_op jit(solution)/shard_map/ppermute | solution.py:65
  35.4 15.2 %collective-permute-start.9 = (bf16[144,2048]{1,0:T(8,128)(2,1)S(1)}, bf16[144,2048]{1,0:T(8,128)(2,1)S(1)}, u32[]{:S(2)}, u32[]{:S(2)}) collective-permute-start(bf16[144,2048]{1,0:T(8,128)(2,1)S(1)} %slice.302), channel_id=1, source_target_pairs={{0,2},{1,3},{2,0},{3,1},{4,6},{5,7},{6,4},{7,5},{8,10},{9,11},{10,... | collective-permute-start | bytes 1769480 | tf_op jit(solution)/shard_map/ppermute | solution.py:82
  36.9 1.9 collective-permute-start.10
  53.4 3.7 %collective-permute-start.11 = (bf16[272,512]{1,0:T(8,128)(2,1)S(1)}, bf16[272,512]{1,0:T(8,128)(2,1)S(1)}, u32[]{:S(2)}, u32[]{:S(2)}) collective-permute-start(bf16[272,512]{1,0:T(8,128)(2,1)S(1)} %get-tuple-element.140), channel_id=1, source_target_pairs={{0,1},{1,0},{2,3},{3,2},{4,5},{5,4},{6,7},{7,6},{8,9},{9,8},{10,11... | collective-permute-start | bytes 835592 | tf_op jit(solution)/shard_map/ppermute | solution.py:82
  53.4 9.5 %collective-permute-start.12 = (bf16[272,512]{1,0:T(8,128)(2,1)S(1)}, bf16[272,512]{1,0:T(8,128)(2,1)S(1)}, u32[]{:S(2)}, u32[]{:S(2)}) collective-permute-start(bf16[272,512]{1,0:T(8,128)(2,1)S(1)} %get-tuple-element.142), channel_id=1, source_target_pairs={{0,2},{1,3},{2,0},{3,1},{4,6},{5,7},{6,4},{7,5},{8,10},{9,11},{10,... | collective-permute-start | bytes 835592 | tf_op jit(solution)/shard_map/ppermute | solution.py:82
  55.0 19.7 %collective-permute-start.16 = (bf16[256,1536]{1,0:T(8,128)(2,1)S(1)}, bf16[256,1536]{1,0:T(8,128)(2,1)S(1)}, u32[]{:S(2)}, u32[]{:S(2)}) collective-permute-start(bf16[256,1536]{1,0:T(8,128)(2,1)S(1)} %collective-permute-done.7.refs_4_), channel_id=1, source_target_pairs={{0,4},{8,0},{16,8},{24,16},{28,24},{20,28},{12,20},{4,12},{1,5},{9... | collective-permute-start | bytes 2359304 | tf_op jit(solution)/shard_map/ppermute | solution.py:65
  56.6 19.3 %collective-permute-start.15 = (bf16[256,1536]{1,0:T(8,128)(2,1)S(1)}, bf16[256,1536]{1,0:T(8,128)(2,1)S(1)}, u32[]{:S(2)}, u32[]{:S(2)}) collective-permute-start(bf16[256,1536]{1,0:T(8,128)(2,1)S(1)} %collective-permute-done.6.refs_3_), channel_id=1, source_target_pairs={{0,8},{8,16},{16,24},{24,28},{28,20},{20,12},{12,4},{4,0},{1,9},{9... | collective-permute-start | bytes 2359304 | tf_op jit(solution)/shard_map/ppermute | solution.py:65
  57.1 10.9 %collective-permute-start.14 = (bf16[144,2048]{1,0:T(8,128)(2,1)S(1)}, bf16[144,2048]{1,0:T(8,128)(2,1)S(1)}, u32[]{:S(2)}, u32[]{:S(2)}) collective-permute-start(bf16[144,2048]{1,0:T(8,128)(2,1)S(1)} %collective-permute-done.9.refs_3_.refs_12_), channel_id=1, source_target_pairs={{0,1},{1,0},{2,3},{3,2},{4,5},{5,4},{6,7},{7,6},{8,9},{9,8},{10,11... | collective-permute-start | bytes 1769480 | tf_op jit(solution)/shard_map/ppermute | solution.py:82
  57.1 10.8 %collective-permute-start.13 = (bf16[272,512]{1,0:T(8,128)(2,1)S(1)}, bf16[272,512]{1,0:T(8,128)(2,1)S(1)}, u32[]{:S(2)}, u32[]{:S(2)}) collective-permute-start(bf16[272,512]{1,0:T(8,128)(2,1)S(1)} %get-tuple-element.144), channel_id=1, source_target_pairs={{0,3},{1,2},{2,1},{3,0},{4,7},{5,6},{6,5},{7,4},{8,11},{9,10},{10,... | collective-permute-start | bytes 835592 | tf_op jit(solution)/shard_map/ppermute | solution.py:82
  71.7 63.0 %copy-start.1 = (f32[1024,128]{1,0:T(8,128)}, f32[1024,128]{1,0:T(8,128)S(1)}, u32[]{:S(2)}) copy-start(f32[1024,128]{1,0:T(8,128)S(1)} %get-tuple-element.194.refs_15_) | copy-start | bytes 1572868
  75.9 10.0 %collective-permute-start.18 = (bf16[128,1536]{1,0:T(8,128)(2,1)S(1)}, bf16[128,1536]{1,0:T(8,128)(2,1)S(1)}, u32[]{:S(2)}, u32[]{:S(2)}) collective-permute-start(bf16[128,1536]{1,0:T(8,128)(2,1)S(1)} %slice.325), channel_id=1, source_target_pairs={{0,4},{8,0},{16,8},{24,16},{28,24},{20,28},{12,20},{4,12},{1,5},{9... | collective-permute-start | bytes 1179656 | tf_op jit(solution)/shard_map/ppermute | solution.py:65
  77.5 10.0 %collective-permute-start.17 = (bf16[128,1536]{1,0:T(8,128)(2,1)S(1)}, bf16[128,1536]{1,0:T(8,128)(2,1)S(1)}, u32[]{:S(2)}, u32[]{:S(2)}) collective-permute-start(bf16[128,1536]{1,0:T(8,128)(2,1)S(1)} %slice.324), channel_id=1, source_target_pairs={{0,8},{8,16},{16,24},{24,28},{28,20},{20,12},{12,4},{4,0},{1,9},{9... | collective-permute-start | bytes 1179656 | tf_op jit(solution)/shard_map/ppermute | solution.py:65
  92.3 4.2 %collective-permute-start.19 = (f32[3,8,512]{2,1,0:T(8,128)S(1)}, f32[3,8,512]{2,1,0:T(8,128)S(1)}, u32[]{:S(2)}, u32[]{:S(2)}) collective-permute-start(f32[3,8,512]{2,1,0:T(8,128)S(1)} %get-tuple-element.156), channel_id=1, source_target_pairs={{0,4},{4,0},{8,12},{12,8},{16,20},{20,16},{24,28},{28,24},{1,5},{5... | collective-permute-start | bytes 147464 | tf_op jit(solution)/shard_map/ppermute | solution.py:82
  96.5 4.6 %collective-permute-start.20 = (f32[3,8,512]{2,1,0:T(8,128)S(1)}, f32[3,8,512]{2,1,0:T(8,128)S(1)}, u32[]{:S(2)}, u32[]{:S(2)}) collective-permute-start(f32[3,8,512]{2,1,0:T(8,128)S(1)} %pad_maximum_fusion.3), channel_id=1, source_target_pairs={{0,8},{4,12},{8,0},{12,4},{16,24},{20,28},{24,16},{28,20},{1,9},{5... | collective-permute-start | bytes 147464 | tf_op jit(solution)/shard_map/ppermute | solution.py:82
  101.1 5.6 %collective-permute-start.21 = (f32[3,8,512]{2,1,0:T(8,128)S(1)}, f32[3,8,512]{2,1,0:T(8,128)S(1)}, u32[]{:S(2)}, u32[]{:S(2)}) collective-permute-start(f32[3,8,512]{2,1,0:T(8,128)S(1)} %pad_maximum_fusion.4), channel_id=1, source_target_pairs={{0,16},{4,20},{8,24},{12,28},{16,0},{20,4},{24,8},{28,12},{1,17},{... | collective-permute-start | bytes 147464 | tf_op jit(solution)/shard_map/ppermute | solution.py:82
  102.4 10.6 %collective-permute-start.22 = (f32[4,8,512]{2,1,0:T(8,128)S(1)}, f32[4,8,512]{2,1,0:T(8,128)S(1)}, u32[]{:S(2)}, u32[]{:S(2)}) collective-permute-start(f32[4,8,512]{2,1,0:T(8,128)S(1)} %get-tuple-element.171), channel_id=1, source_target_pairs={{4,0},{8,4},{12,8},{16,12},{20,16},{24,20},{28,24},{5,1},{9,5},{13... | collective-permute-start | bytes 196616 | tf_op jit(solution)/shard_map/ppermute | solution.py:782
  114.8 13.0 %collective-permute-start.26 = (bf16[2,2,128,512]{3,2,1,0:T(8,128)(2,1)S(1)}, bf16[2,2,128,512]{3,2,1,0:T(8,128)(2,1)S(1)}, u32[]{:S(2)}, u32[]{:S(2)}) collective-permute-start(bf16[2,2,128,512]{3,2,1,0:T(8,128)(2,1)S(1)} %get-tuple-element.184), channel_id=1, source_target_pairs={{0,2},{1,3},{2,0},{3,1},{4,6},{5,7},{6,4},{7,5},{8,10},{9,11},{10,... | collective-permute-start | bytes 1572872 | tf_op jit(solution)/shard_map/ppermute | solution.py:82
  115.4 12.4 %collective-permute-start.25 = (bf16[2,2,128,512]{3,2,1,0:T(8,128)(2,1)S(1)}, bf16[2,2,128,512]{3,2,1,0:T(8,128)(2,1)S(1)}, u32[]{:S(2)}, u32[]{:S(2)}) collective-permute-start(bf16[2,2,128,512]{3,2,1,0:T(8,128)(2,1)S(1)} %get-tuple-element.182), channel_id=1, source_target_pairs={{0,1},{1,0},{2,3},{3,2},{4,5},{5,4},{6,7},{7,6},{8,9},{9,8},{10,11... | collective-permute-start | bytes 1572872 | tf_op jit(solution)/shard_map/ppermute | solution.py:82
  115.4 11.5 %collective-permute-start.23 = (bf16[128,1536]{1,0:T(8,128)(2,1)S(1)}, bf16[128,1536]{1,0:T(8,128)(2,1)S(1)}, u32[]{:S(2)}, u32[]{:S(2)}) collective-permute-start(bf16[128,1536]{1,0:T(8,128)(2,1)S(1)} %get-tuple-element.172), channel_id=1, source_target_pairs={{0,8},{8,16},{16,24},{24,28},{28,20},{20,12},{12,4},{4,0},{1,9},{9... | collective-permute-start | bytes 1179656 | tf_op jit(solution)/shard_map/ppermute | solution.py:65
  116.3 11.2 %collective-permute-start.24 = (bf16[128,1536]{1,0:T(8,128)(2,1)S(1)}, bf16[128,1536]{1,0:T(8,128)(2,1)S(1)}, u32[]{:S(2)}, u32[]{:S(2)}) collective-permute-start(bf16[128,1536]{1,0:T(8,128)(2,1)S(1)} %get-tuple-element.173), channel_id=1, source_target_pairs={{0,4},{8,0},{16,8},{24,16},{28,24},{20,28},{12,20},{4,12},{1,5},{9... | collective-permute-start | bytes 1179656 | tf_op jit(solution)/shard_map/ppermute | solution.py:65
  127.8 18.9 %collective-permute-start.28 = (bf16[256,1536]{1,0:T(8,128)(2,1)S(1)}, bf16[256,1536]{1,0:T(8,128)(2,1)S(1)}, u32[]{:S(2)}, u32[]{:S(2)}) collective-permute-start(bf16[256,1536]{1,0:T(8,128)(2,1)S(1)} %get-tuple-element.187), channel_id=1, source_target_pairs={{0,4},{8,0},{16,8},{24,16},{28,24},{20,28},{12,20},{4,12},{1,5},{9... | collective-permute-start | bytes 2359304 | tf_op jit(solution)/shard_map/ppermute | solution.py:65
  129.0 18.6 %collective-permute-start.27 = (bf16[256,1536]{1,0:T(8,128)(2,1)S(1)}, bf16[256,1536]{1,0:T(8,128)(2,1)S(1)}, u32[]{:S(2)}, u32[]{:S(2)}) collective-permute-start(bf16[256,1536]{1,0:T(8,128)(2,1)S(1)} %get-tuple-element.185), channel_id=1, source_target_pairs={{0,8},{8,16},{16,24},{24,28},{28,20},{20,12},{12,4},{4,0},{1,9},{9... | collective-permute-start | bytes 2359304 | tf_op jit(solution)/shard_map/ppermute | solution.py:65
  129.9 17.9 %collective-permute-start.29 = (bf16[2,2,128,512]{3,2,1,0:T(8,128)(2,1)S(1)}, bf16[2,2,128,512]{3,2,1,0:T(8,128)(2,1)S(1)}, u32[]{:S(2)}, u32[]{:S(2)}) collective-permute-start(bf16[2,2,128,512]{3,2,1,0:T(8,128)(2,1)S(1)} %get-tuple-element.192), channel_id=1, source_target_pairs={{0,3},{1,2},{2,1},{3,0},{4,7},{5,6},{6,5},{7,4},{8,11},{9,10},{10,... | collective-permute-start | bytes 1572872 | tf_op jit(solution)/shard_map/ppermute | solution.py:82
  147.9 4.5 %collective-permute-start.34 = (bf16[256,2048]{1,0:T(8,128)(2,1)S(1)}, bf16[256,2048]{1,0:T(8,128)(2,1)S(1)}, u32[]{:S(2)}, u32[]{:S(2)}) collective-permute-start(bf16[256,2048]{1,0:T(8,128)(2,1)S(1)} %get-tuple-element.214), channel_id=1, source_target_pairs={{0,1},{1,0},{2,3},{3,2},{4,5},{5,4},{6,7},{7,6},{8,9},{9,8},{10,11... | collective-permute-start | bytes 3145736 | tf_op jit(solution)/shard_map/ppermute | solution.py:82
  148.0 2.7 %collective-permute-start.30 = (f32[8,2048]{1,0:T(8,128)S(1)}, f32[8,2048]{1,0:T(8,128)S(1)}, u32[]{:S(2)}, u32[]{:S(2)}) collective-permute-start(f32[8,2048]{1,0:T(8,128)S(1)} %pad_maximum_fusion.2), channel_id=1, source_target_pairs={{0,1},{1,0},{2,3},{3,2},{4,5},{5,4},{6,7},{7,6},{8,9},{9,8},{10,11... | collective-permute-start | bytes 196616 | tf_op jit(solution)/shard_map/ppermute | solution.py:82
  148.5 22.1 %collective-permute-start.35 = (bf16[256,2048]{1,0:T(8,128)(2,1)S(1)}, bf16[256,2048]{1,0:T(8,128)(2,1)S(1)}, u32[]{:S(2)}, u32[]{:S(2)}) collective-permute-start(bf16[256,2048]{1,0:T(8,128)(2,1)S(1)} %get-tuple-element.216), channel_id=1, source_target_pairs={{0,1},{1,0},{2,3},{3,2},{4,5},{5,4},{6,7},{7,6},{8,9},{9,8},{10,11... | collective-permute-start | bytes 3145736 | tf_op jit(solution)/shard_map/ppermute | solution.py:82
  148.6 19.9 %collective-permute-start.33 = (bf16[256,1536]{1,0:T(8,128)(2,1)S(1)}, bf16[256,1536]{1,0:T(8,128)(2,1)S(1)}, u32[]{:S(2)}, u32[]{:S(2)}) collective-permute-start(bf16[256,1536]{1,0:T(8,128)(2,1)S(1)} %get-tuple-element.211), channel_id=1, source_target_pairs={{0,4},{8,0},{16,8},{24,16},{28,24},{20,28},{12,20},{4,12},{1,5},{9... | collective-permute-start | bytes 2359304 | tf_op jit(solution)/shard_map/ppermute | solution.py:65
  149.6 20.3 %collective-permute-start.32 = (bf16[256,1536]{1,0:T(8,128)(2,1)S(1)}, bf16[256,1536]{1,0:T(8,128)(2,1)S(1)}, u32[]{:S(2)}, u32[]{:S(2)}) collective-permute-start(bf16[256,1536]{1,0:T(8,128)(2,1)S(1)} %get-tuple-element.210), channel_id=1, source_target_pairs={{0,8},{8,16},{16,24},{24,28},{28,20},{20,12},{12,4},{4,0},{1,9},{9... | collective-permute-start | bytes 2359304 | tf_op jit(solution)/shard_map/ppermute | solution.py:65
  150.7 4.3 %collective-permute-start.31 = (f32[8,2048]{1,0:T(8,128)S(1)}, f32[8,2048]{1,0:T(8,128)S(1)}, u32[]{:S(2)}, u32[]{:S(2)}) collective-permute-start(f32[8,2048]{1,0:T(8,128)S(1)} %select_maximum_fusion), channel_id=1, source_target_pairs={{0,2},{1,3},{2,0},{3,1},{4,6},{5,7},{6,4},{7,5},{8,10},{9,11},{10,... | collective-permute-start | bytes 196616 | tf_op jit(solution)/shard_map/ppermute | solution.py:82
  152.8 17.8 %collective-permute-start.37 = (bf16[128,2048]{1,0:T(8,128)(2,1)S(1)}, bf16[128,2048]{1,0:T(8,128)(2,1)S(1)}, u32[]{:S(2)}, u32[]{:S(2)}) collective-permute-start(bf16[128,2048]{1,0:T(8,128)(2,1)S(1)} %get-tuple-element.219), channel_id=1, source_target_pairs={{0,2},{1,3},{2,0},{3,1},{4,6},{5,7},{6,4},{7,5},{8,10},{9,11},{10,... | collective-permute-start | bytes 1572872 | tf_op jit(solution)/shard_map/ppermute | solution.py:82
  155.1 15.6 %collective-permute-start.36 = (f32[6,2048]{1,0:T(8,128)S(1)}, f32[6,2048]{1,0:T(8,128)S(1)}, u32[]{:S(2)}, u32[]{:S(2)}) collective-permute-start(f32[6,2048]{1,0:T(8,128)S(1)} %slice_add_fusion.2), channel_id=1, source_target_pairs={{0,4},{4,0},{8,12},{12,8},{16,20},{20,16},{24,28},{28,24},{1,5},{5... | collective-permute-start | bytes 147464 | tf_op jit(solution)/shard_map/ppermute | solution.py:82
  170.7 14.9 %collective-permute-start.39 = (bf16[256,1024]{1,0:T(8,128)(2,1)S(1)}, bf16[256,1024]{1,0:T(8,128)(2,1)S(1)}, u32[]{:S(2)}, u32[]{:S(2)}) collective-permute-start(bf16[256,1024]{1,0:T(8,128)(2,1)S(1)} %get-tuple-element.223), channel_id=1, source_target_pairs={{0,4},{8,0},{16,8},{24,16},{28,24},{20,28},{12,20},{4,12},{1,5},{9... | collective-permute-start | bytes 1572872 | tf_op jit(solution)/shard_map/ppermute | solution.py:65
  170.9 14.9 %collective-permute-start.38 = (bf16[256,1024]{1,0:T(8,128)(2,1)S(1)}, bf16[256,1024]{1,0:T(8,128)(2,1)S(1)}, u32[]{:S(2)}, u32[]{:S(2)}) collective-permute-start(bf16[256,1024]{1,0:T(8,128)(2,1)S(1)} %get-tuple-element.221), channel_id=1, source_target_pairs={{0,8},{8,16},{16,24},{24,28},{28,20},{20,12},{12,4},{4,0},{1,9},{9... | collective-permute-start | bytes 1572872 | tf_op jit(solution)/shard_map/ppermute | solution.py:65
  173.7 17.2 %collective-permute-start.42 = (bf16[128,2048]{1,0:T(8,128)(2,1)S(1)}, bf16[128,2048]{1,0:T(8,128)(2,1)S(1)}, u32[]{:S(2)}, u32[]{:S(2)}) collective-permute-start(bf16[128,2048]{1,0:T(8,128)(2,1)S(1)} %get-tuple-element.228), channel_id=1, source_target_pairs={{0,2},{1,3},{2,0},{3,1},{4,6},{5,7},{6,4},{7,5},{8,10},{9,11},{10,... | collective-permute-start | bytes 1572872 | tf_op jit(solution)/shard_map/ppermute | solution.py:82
  175.3 15.6 %collective-permute-start.41 = (bf16[256,512]{1,0:T(8,128)(2,1)S(1)}, bf16[256,512]{1,0:T(8,128)(2,1)S(1)}, u32[]{:S(2)}, u32[]{:S(2)}) collective-permute-start(bf16[256,512]{1,0:T(8,128)(2,1)S(1)} %get-tuple-element.227), channel_id=1, source_target_pairs={{0,4},{8,0},{16,8},{24,16},{28,24},{20,28},{12,20},{4,12},{1,5},{9... | collective-permute-start | bytes 786440 | tf_op jit(solution)/shard_map/ppermute | solution.py:65
  175.6 15.3 %collective-permute-start.40 = (bf16[256,512]{1,0:T(8,128)(2,1)S(1)}, bf16[256,512]{1,0:T(8,128)(2,1)S(1)}, u32[]{:S(2)}, u32[]{:S(2)}) collective-permute-start(bf16[256,512]{1,0:T(8,128)(2,1)S(1)} %get-tuple-element.225), channel_id=1, source_target_pairs={{0,8},{8,16},{16,24},{24,28},{28,20},{20,12},{12,4},{4,0},{1,9},{9... | collective-permute-start | bytes 786440 | tf_op jit(solution)/shard_map/ppermute | solution.py:65
  186.1 4.7 %collective-permute-start.43 = (f32[6,2048]{1,0:T(8,128)S(1)}, f32[6,2048]{1,0:T(8,128)S(1)}, u32[]{:S(2)}, u32[]{:S(2)}) collective-permute-start(f32[6,2048]{1,0:T(8,128)S(1)} %add.316), channel_id=1, source_target_pairs={{0,8},{4,12},{8,0},{12,4},{16,24},{20,28},{24,16},{28,20},{1,9},{5... | collective-permute-start | bytes 147464 | tf_op jit(solution)/shard_map/ppermute | solution.py:82
  188.5 9.9 %collective-permute-start.44 = (bf16[256,512]{1,0:T(8,128)(2,1)S(1)}, bf16[256,512]{1,0:T(8,128)(2,1)S(1)}, u32[]{:S(2)}, u32[]{:S(2)}) collective-permute-start(bf16[256,512]{1,0:T(8,128)(2,1)S(1)} %get-tuple-element.243), channel_id=1, source_target_pairs={{0,2},{1,3},{2,0},{3,1},{4,6},{5,7},{6,4},{7,5},{8,10},{9,11},{10,... | collective-permute-start | bytes 786440 | tf_op jit(solution)/shard_map/ppermute | solution.py:82
  190.9 7.8 %collective-permute-start.45 = (bf16[256,512]{1,0:T(8,128)(2,1)S(1)}, bf16[256,512]{1,0:T(8,128)(2,1)S(1)}, u32[]{:S(2)}, u32[]{:S(2)}) collective-permute-start(bf16[256,512]{1,0:T(8,128)(2,1)S(1)} %get-tuple-element.242), channel_id=1, source_target_pairs={{0,1},{1,0},{2,3},{3,2},{4,5},{5,4},{6,7},{7,6},{8,9},{9,8},{10,11... | collective-permute-start | bytes 786440 | tf_op jit(solution)/shard_map/ppermute | solution.py:82
  190.9 6.9 %collective-permute-start.46 = (f32[6,2048]{1,0:T(8,128)S(1)}, f32[6,2048]{1,0:T(8,128)S(1)}, u32[]{:S(2)}, u32[]{:S(2)}) collective-permute-start(f32[6,2048]{1,0:T(8,128)S(1)} %add.324), channel_id=1, source_target_pairs={{0,16},{4,20},{8,24},{12,28},{16,0},{20,4},{24,8},{28,12},{1,17},{... | collective-permute-start | bytes 147464 | tf_op jit(solution)/shard_map/ppermute | solution.py:82
  (11 other events, 236.0 us)

commit v7 on v6

--- a/solution.py
+++ b/solution.py
@@ -156,6 +156,14 @@
         if count < total:
             out_up[count:, :] = mine_up[count:, lanes].astype(bf16)
             out_down[: total - count, :] = mine_down[: total - count, lanes].astype(bf16)
+
+
+def stored_kernel(width, place, mine, up, down, near, distant, out):
+    own = mine[...] + up[...].astype(f32) + down[...].astype(f32)
+    shift = place[0] * 2 * width
+    out[:, pl.ds(pl.multiple_of(shift, width), width)] = own
+    out[:, width : 2 * width] = near[...].astype(f32)
+    out[:, pl.ds(pl.multiple_of(2 * width - shift, width), width)] = distant[...].astype(f32)
 
 
 def assemble_kernel(slots, width, where, *refs):
@@ -339,7 +347,7 @@
         zero = jnp.zeros((seqs, step), f32)
         last = token(cand, span - 1 + PAD)
         done = lax.fori_loop(
-            0, span, backward, (after, zero, end, last, zero, zero, zero, zero), unroll=4
+            0, span, backward, (after, zero, end, last, zero, zero, zero, zero), unroll=8
         )
         ends_kept[:, units] = token_of(gcs, span - 1 + PAD)
         for i in range(4):
@@ -528,6 +536,7 @@
         "rows": [(at_stream ^ k) * per for k in range(slots)],
         "first": [(at_seq & bit) == 0 for bit in seq_bits],
         "even": at_stream % 2 == 0,
+        "odd": (at_stream & 1).reshape(1).astype(jnp.int32),
         "share": at_seq * share % width,
         "holds": at_stream == at_seq * share // width,
     }
@@ -578,8 +587,13 @@
         came = box["came"]
         own = box["mine", far + 1][0][:, :width] + came[2].astype(f32) + came[3].astype(f32)
         if dealing:
-            distant, near = box["distant"].astype(f32), box["near"].astype(f32)
-            found = [jnp.where(even, own, distant), near, jnp.where(even, distant, own)]
+            return call(
+                functools.partial(stored_kernel, width),
+                jax.ShapeDtypeStruct((depth, 3 * width), f32),
+                [index["odd"], box["mine", far + 1][0][:, :width], *came[2:], box["near"], box["distant"]],
+                scalars=1,
+                pinned=False,
+            )
         else:
             flat = lax.all_gather(
                 jnp.concatenate([own, *box["rest"]], axis=1).astype(bf16), "stream", axis=0
@@ -700,12 +714,16 @@
             scalars=1,
         )
 
-    def out_grads():
+    def out_grads(behind=()):
         for k in range(slots):
             box["g", k] = box["messages"][k]
             if k:
-                box["g", k] = swapped(take(box["g", k]), "stream", k)
-                give(box["g", k])
+                message = take(box["g", k])
+                if behind:
+                    message = lax.optimization_barrier((message, behind[-1]))[0]
+                box["g", k] = swapped(message, "stream", k)
+                if not behind:
+                    give(box["g", k])
 
     def normalise():
         flat = [piece for slot in tokens_of for piece in slot]
@@ -723,6 +741,7 @@
         give(box["normed"])
 
     def from_others():
+        give(*[box["g", k] for k in range(1, slots)])
         extra = [box["g", k][rows : rows + 5 * per].astype(f32) for k in range(slots)]
         extra = [x.reshape(5, per, width) for x in extra]
         box["start"] = jnp.concatenate([x[0] + x[1] + x[2] for x in extra], axis=0)
@@ -931,7 +950,7 @@
         early = [
             [part(far_tokens, 0)],
             [near_tokens, part(far_tokens, 1), part(passed_tokens, 0), messages],
-            [part(passed_tokens, 1), out_grads, normalise],
+            [part(passed_tokens, 1), part(out_grads, tokens_of[3]), normalise],
         ]
     else:
         early = [[everyones_tokens], [messages], [out_grads, normalise]]

time: 200 us -> 199 us (level)
    ppermute x18, waiting for transfers between devices: 44.8 us -> 54.8 us  [along_ring(): lax.ppermute(value, 'seq', [(order[i], order[(i + steps) % count]) for i...]
    ppermute x27, waiting for transfers between devices: 51.6 us -> 42.3 us  [swapped(): lax.ppermute(value, axis, [(i, i ^ bit) for i in range(lax.axis_size(axis...]
    pallas_call x16 -> x17, Pallas kernels: 44.6 us -> 45.9 us  [call(): pl.pallas_call(kernel, out_shape=held if pinned else out_shape, in_specs=...]
  transfers between devices with their start and end apart: 47 -> 47, of which waited for: 30 -> 29; matrix products, arithmetic and copies ran while one was open for 4% -> 4% of each run, Pallas kernels for 19% -> 19%
where the time goes in v7:
time: 199 us
  waiting for transfers between devices  97.2 us (49%)
  Pallas kernels  45.9 us (23%)
  starting transfers between devices  44.8 us (23%)
  other arithmetic  5.98 us (3%)
  local copies, waits for them, and re-layouts  3.63 us (2%)
    ppermute x18, waiting for transfers between devices, along_ring(): lax.ppermute(value, 'seq', [(order[i], order[(i + steps) % count]) for i...  54.8 us
    pallas_call x17, Pallas kernels, call(): pl.pallas_call(kernel, out_shape=held if pinned else out_shape, in_specs=...  45.9 us
    ppermute x27, waiting for transfers between devices, swapped(): lax.ppermute(value, axis, [(i, i ^ bit) for i in range(lax.axis_size(axis...  42.3 us
    ppermute x27, starting transfers between devices, swapped(): lax.ppermute(value, axis, [(i, i ^ bit) for i in range(lax.axis_size(axis...  21.5 us
    ppermute x18, starting transfers between devices, along_ring(): lax.ppermute(value, 'seq', [(order[i], order[(i + steps) % count]) for i...  18.7 us
  transfers between devices with their start and end apart: 47, of which 29 were waited for; matrix products, arithmetic and copies ran while one was open for 4% of the time, Pallas kernels for 19%

profile of v7, /device:TPU:0, one launch (start us, length us, event | category | flops | bytes accessed | tf_op | source)
XLA Modules:
  0.0 199.2 jit_solution(9942513275976854039)
XLA Ops:
  3.0 2.6 %collective-permute-start.1 = (bf16[256,512]{1,0:T(8,128)(2,1)S(1)}, bf16[256,512]{1,0:T(8,128)(2,1)S(1)}, u32[]{:S(2)}, u32[]{:S(2)}) collective-permute-start(bf16[256,512]{1,0:T(8,128)(2,1)S(1)} %get-tuple-element.247), channel_id=1, source_target_pairs={{0,2},{1,3},{2,0},{3,1},{4,6},{5,7},{6,4},{7,5},{8,10},{9,11},{10,... | collective-permute-start | bytes 786440 | tf_op jit(solution)/shard_map/ppermute | solution.py:82
  6.7 3.4 %collective-permute-start.2 = (bf16[2,2048]{1,0:T(2,128)(2,1)S(1)}, bf16[2,2048]{1,0:T(2,128)(2,1)S(1)}, u32[]{:S(2)}, u32[]{:S(2)}) collective-permute-start(bf16[2,2048]{1,0:T(2,128)(2,1)S(1)} %slice_bitcast_fusion.1), channel_id=1, source_target_pairs={{0,4},{4,8},{8,12},{12,16},{16,20},{20,24},{24,28},{1,5},{5,9},{9,... | collective-permute-start | bytes 24584 | tf_op jit(solution)/shard_map/ppermute | solution.py:671
  10.1 2.4 %collective-permute-done.1 = bf16[256,512]{1,0:T(8,128)(2,1)S(1)} collective-permute-done((bf16[256,512]{1,0:T(8,128)(2,1)S(1)}, bf16[256,512]{1,0:T(8,128)(2,1)S(1)}, u32[]{:S(2)}, u32[]{:S(2)}) %collective-permute-start.1) | collective-permute-done | bytes 262176 | tf_op jit(solution)/shard_map/ppermute | solution.py:82
  12.6 2.1 %collective-permute-start.3 = (bf16[256,1536]{1,0:T(8,128)(2,1)S(1)}, bf16[256,1536]{1,0:T(8,128)(2,1)S(1)}, u32[]{:S(2)}, u32[]{:S(2)}) collective-permute-start(bf16[256,1536]{1,0:T(8,128)(2,1)S(1)} %pad_maximum_fusion.refs_0_), channel_id=1, source_target_pairs={{0,8},{8,16},{16,24},{24,28},{28,20},{20,12},{12,4},{4,0},{1,9},{9... | collective-permute-start | bytes 2359304 | tf_op jit(solution)/shard_map/ppermute | solution.py:65
  14.8 1.8 collective-permute-start.5
  16.9 11.0 %collective-permute-done.5.refs_2_.refs_11_ = bf16[128,2048]{1,0:T(8,128)(2,1)S(1)} collective-permute-done((bf16[128,2048]{1,0:T(8,128)(2,1)S(1)}, bf16[128,2048]{1,0:T(8,128)(2,1)S(1)}, u32[]{:S(2)}, u32[]{:S(2)}) %collective-permute-start.5) | collective-permute-done | bytes 524320 | tf_op jit(solution)/shard_map/ppermute | solution.py:82
  27.9 4.0 %collective-permute-done.3.refs_1_ = bf16[256,1536]{1,0:T(8,128)(2,1)S(1)} collective-permute-done((bf16[256,1536]{1,0:T(8,128)(2,1)S(1)}, bf16[256,1536]{1,0:T(8,128)(2,1)S(1)}, u32[]{:S(2)}, u32[]{:S(2)}) %collective-permute-start.3) | collective-permute-done | bytes 786464 | tf_op jit(solution)/shard_map/ppermute | solution.py:65
  31.9 1.3 collective-permute-done.4.refs_2_
  33.7 1.6 collective-permute-start.6
  35.4 1.6 collective-permute-start.9
  36.9 1.9 collective-permute-done.10.refs_4_.refs_13_
  38.9 11.7 %collective-permute-done.9.refs_3_.refs_12_ = bf16[144,2048]{1,0:T(8,128)(2,1)S(1)} collective-permute-done((bf16[144,2048]{1,0:T(8,128)(2,1)S(1)}, bf16[144,2048]{1,0:T(8,128)(2,1)S(1)}, u32[]{:S(2)}, u32[]{:S(2)}) %collective-permute-start.9) | collective-permute-done | bytes 589856 | tf_op jit(solution)/shard_map/ppermute | solution.py:82
  50.6 2.6 %collective-permute-done.7.refs_4_ = bf16[256,1536]{1,0:T(8,128)(2,1)S(1)} collective-permute-done((bf16[256,1536]{1,0:T(8,128)(2,1)S(1)}, bf16[256,1536]{1,0:T(8,128)(2,1)S(1)}, u32[]{:S(2)}, u32[]{:S(2)}) %collective-permute-start.7) | collective-permute-done | bytes 786464 | tf_op jit(solution)/shard_map/ppermute | solution.py:65
  53.4 1.5 collective-permute-start.16
  56.2 1.6 collective-permute-start.13
  58.1 3.7 %shard_map.187 = (bf16[1088,2048]{1,0:T(8,128)(2,1)S(1)}, f32[1024,128]{1,0:T(8,128)S(1)}, f32[1024,128]{1,0:T(8,128)S(1)}, bf16[1024,512]{1,0:T(8,128)(2,1)S(1)}) custom-call(s32[6]{0:T(128)S(1)} %stack.116.place, bf16[272,2048]{1,0:T(8,128)(2,1)S(1)} %maximum_maximum_fusion.refs_0_.refs_9_, bf16[272,2048]{1,0:T(8,128)(2,1)S(1)} %collective-permute-done.8.refs_1_.refs_10_, ...), custom_call_target="tpu_custom_call" | custom-call | tf_op jit(solution)/shard_map/pallas_call | solution.py:28
  61.8 11.5 %collective-permute-done.16.refs_6_ = bf16[256,1536]{1,0:T(8,128)(2,1)S(1)} collective-permute-done((bf16[256,1536]{1,0:T(8,128)(2,1)S(1)}, bf16[256,1536]{1,0:T(8,128)(2,1)S(1)}, u32[]{:S(2)}, u32[]{:S(2)}) %collective-permute-start.16) | collective-permute-done | bytes 786464 | tf_op jit(solution)/shard_map/ppermute | solution.py:65
  74.6 1.6 collective-permute-start.18
  77.0 6.8 %shard_map.188.begun = f32[1088,1536]{1,0:T(8,128)S(1)} custom-call(s32[8]{0:T(128)S(1)} %stack.120.sources, bf16[1088,2048]{1,0:T(8,128)(2,1)S(1)} %get-tuple-element.160.normed, bf16[256,1536]{1,0:T(8,128)(2,1)S(1)} %pad_maximum_fusion.refs_0_, bf16[256,1536]{1,0:T(8,128)(2,1)S(1)} %collective-permute-done.3.refs_1_, ...), custom_call_target="tpu_custom_call" | custom-call | tf_op jit(solution)/shard_map/pallas_call | solution.py:28
  85.1 1.6 collective-permute-done.17.refs_0_.refs_7_
  86.7 4.8 %shard_map.189 = (f32[3,4,1088,128]{3,2,1,0:T(8,128)S(1)}, f32[2,4,1088,128]{3,2,1,0:T(8,128)S(1)}, f32[2,4,1088,128]{3,2,1,0:T(8,128)S(1)}, f32[3,8,512]{2,1,0:T(8,128)S(1)}, f32[4,8,512]{2,1,0:T(8,128)S(1)}) custom-call(s32[8]{0:T(128)S(1)} %stack.120.sources, s32[6]{0:T(128)S(1)} %stack.116.place, bf16[1088,2048]{1,0:T(8,128)(2,1)S(1)} %get-tuple-element.160.normed, ...), custom_call_target="tpu_custom_call" | custom-call | tf_op jit(solution)/shard_map/pallas_call | solution.py:28
  91.5 1.6 collective-permute-start.19
  93.2 2.5 %collective-permute-done.19 = f32[3,8,512]{2,1,0:T(8,128)S(1)} collective-permute-done((f32[3,8,512]{2,1,0:T(8,128)S(1)}, f32[3,8,512]{2,1,0:T(8,128)S(1)}, u32[]{:S(2)}, u32[]{:S(2)}) %collective-permute-start.19) | collective-permute-done | bytes 49184 | tf_op jit(solution)/shard_map/ppermute | solution.py:82
  96.9 3.6 %collective-permute-done.20 = f32[3,8,512]{2,1,0:T(8,128)S(1)} collective-permute-done((f32[3,8,512]{2,1,0:T(8,128)S(1)}, f32[3,8,512]{2,1,0:T(8,128)S(1)}, u32[]{:S(2)}, u32[]{:S(2)}) %collective-permute-start.20) | collective-permute-done | bytes 49184 | tf_op jit(solution)/shard_map/ppermute | solution.py:82
  101.4 1.3 collective-permute-start.22
  102.7 3.3 %collective-permute-done.21 = f32[3,8,512]{2,1,0:T(8,128)S(1)} collective-permute-done((f32[3,8,512]{2,1,0:T(8,128)S(1)}, f32[3,8,512]{2,1,0:T(8,128)S(1)}, u32[]{:S(2)}, u32[]{:S(2)}) %collective-permute-start.21) | collective-permute-done | bytes 49184 | tf_op jit(solution)/shard_map/ppermute | solution.py:82
  106.1 6.2 %shard_map.190 = (bf16[1088,1536]{1,0:T(8,128)(2,1)S(1)}, bf16[2,2,128,512]{3,2,1,0:T(8,128)(2,1)S(1)}, bf16[2,2,128,512]{3,2,1,0:T(8,128)(2,1)S(1)}, bf16[2,2,1...) custom-call(s32[6]{0:T(128)S(1)} %stack.116.place, ...), custom_call_target="tpu_custom_call" | custom-call | tf_op jit(solution)/shard_map/pallas_call | solution.py:28
  112.4 1.8 shard_map.192
  114.2 1.6 collective-permute-start.26
  117.8 2.8 %shard_map.195 = (f32[256,1536]{1,0:T(8,128)S(1)}, f32[256,1536]{1,0:T(8,128)S(1)}) custom-call(s32[8]{0:T(128)S(1)} %stack.109.owners, s32[6]{0:T(128)S(1)} %stack.116.place, bf16[1088,2048]{1,0:T(8,128)(2,1)S(1)} %get-tuple-element.160.normed, bf16[1088,1536]{1,0:T(8,128)(2,1)S(1)} %shard_map.191.grads), custom_call_target="tpu_custom_call" | custom-call | tf_op jit(solution)/shard_map/pallas_call | solution.py:28
  120.6 2.8 %shard_map.193 = (f32[256,1536]{1,0:T(8,128)S(1)}, f32[256,1536]{1,0:T(8,128)S(1)}) custom-call(s32[8]{0:T(128)S(1)} %stack.109.owners, s32[6]{0:T(128)S(1)} %stack.116.place, bf16[1088,2048]{1,0:T(8,128)(2,1)S(1)} %get-tuple-element.160.normed, bf16[1088,1536]{1,0:T(8,128)(2,1)S(1)} %shard_map.191.grads), custom_call_target="tpu_custom_call" | custom-call | tf_op jit(solution)/shard_map/pallas_call | solution.py:28
  123.4 3.9 %collective-permute-done.23.up = bf16[128,1536]{1,0:T(8,128)(2,1)S(1)} collective-permute-done((bf16[128,1536]{1,0:T(8,128)(2,1)S(1)}, bf16[128,1536]{1,0:T(8,128)(2,1)S(1)}, u32[]{:S(2)}, u32[]{:S(2)}) %collective-permute-start.23) | collective-permute-done | bytes 393248 | tf_op jit(solution)/shard_map/ppermute | solution.py:65
  130.4 2.8 %shard_map.197 = (f32[256,1536]{1,0:T(8,128)S(1)}, f32[256,1536]{1,0:T(8,128)S(1)}) custom-call(s32[8]{0:T(128)S(1)} %stack.109.owners, s32[6]{0:T(128)S(1)} %stack.116.place, bf16[1088,2048]{1,0:T(8,128)(2,1)S(1)} %get-tuple-element.160.normed, bf16[1088,1536]{1,0:T(8,128)(2,1)S(1)} %shard_map.191.grads), custom_call_target="tpu_custom_call" | custom-call | tf_op jit(solution)/shard_map/pallas_call | solution.py:28
  133.3 1.8 shard_map.196
  135.1 8.0 %shard_map.198 = (f32[256,2048]{1,0:T(8,128)S(1)}, bf16[256,2048]{1,0:T(8,128)(2,1)S(1)}, bf16[256,2048]{1,0:T(8,128)(2,1)S(1)}, bf16[256,2048]{1,0:T(8,128)(2,1)S(1)}, f32[8,2048]{1,0:T(8,128)S(1)}) custom-call(s32[8]{0:T(128)S(1)} %stack.120.sources, s32[6]{0:T(128)S(1)} %stack.116.place, bf16[1088,1536]{1,0:T(8,128)(2,1)S(1)} %shard_map.191.grads, ...), custom_call_target="tpu_custom_call" | custom-call | tf_op jit(solution)/shard_map/pallas_call | solution.py:28
  143.0 4.1 %collective-permute-done.28.down = bf16[256,1536]{1,0:T(8,128)(2,1)S(1)} collective-permute-done((bf16[256,1536]{1,0:T(8,128)(2,1)S(1)}, bf16[256,1536]{1,0:T(8,128)(2,1)S(1)}, u32[]{:S(2)}, u32[]{:S(2)}) %collective-permute-start.28) | collective-permute-done | bytes 786464 | tf_op jit(solution)/shard_map/ppermute | solution.py:65
  152.2 1.6 collective-permute-start.37
  153.7 2.4 %collective-permute-done.31 = f32[8,2048]{1,0:T(8,128)S(1)} collective-permute-done((f32[8,2048]{1,0:T(8,128)S(1)}, f32[8,2048]{1,0:T(8,128)S(1)}, u32[]{:S(2)}, u32[]{:S(2)}) %collective-permute-start.31) | collective-permute-done | bytes 65568 | tf_op jit(solution)/shard_map/ppermute | solution.py:82
  157.2 1.7 shard_map.200
  158.9 10.0 %collective-permute-done.33.down = bf16[256,1536]{1,0:T(8,128)(2,1)S(1)} collective-permute-done((bf16[256,1536]{1,0:T(8,128)(2,1)S(1)}, bf16[256,1536]{1,0:T(8,128)(2,1)S(1)}, u32[]{:S(2)}, u32[]{:S(2)}) %collective-permute-start.33) | collective-permute-done | bytes 786464 | tf_op jit(solution)/shard_map/ppermute | solution.py:65
  168.9 1.5 collective-permute-done.32.up
  171.3 1.7 collective-permute-start.38
  174.1 1.7 collective-permute-start.40
  175.8 10.0 %collective-permute-done.39 = bf16[256,1024]{1,0:T(8,128)(2,1)S(1)} collective-permute-done((bf16[256,1024]{1,0:T(8,128)(2,1)S(1)}, bf16[256,1024]{1,0:T(8,128)(2,1)S(1)}, u32[]{:S(2)}, u32[]{:S(2)}) %collective-permute-start.39) | collective-permute-done | bytes 524320 | tf_op jit(solution)/shard_map/ppermute | solution.py:65
  186.5 1.8 collective-permute-start.43
  188.9 2.3 %collective-permute-done.43 = f32[6,2048]{1,0:T(8,128)S(1)} collective-permute-done((f32[6,2048]{1,0:T(8,128)S(1)}, f32[6,2048]{1,0:T(8,128)S(1)}, u32[]{:S(2)}, u32[]{:S(2)}) %collective-permute-start.43) | collective-permute-done | bytes 49184 | tf_op jit(solution)/shard_map/ppermute | solution.py:82
  195.3 1.3 add_convert_fusion
  197.8 1.3 shard_map.202
  (149 shorter events, 30.9 us)
Async XLA Ops:
  2.5 7.6 %collective-permute-start = (bf16[256,512]{1,0:T(8,128)(2,1)S(1)}, bf16[256,512]{1,0:T(8,128)(2,1)S(1)}, u32[]{:S(2)}, u32[]{:S(2)}) collective-permute-start(bf16[256,512]{1,0:T(8,128)(2,1)S(1)} %get-tuple-element.246), channel_id=1, source_target_pairs={{0,1},{1,0},{2,3},{3,2},{4,5},{5,4},{6,7},{7,6},{8,9},{9,8},{10,11... | collective-permute-start | bytes 786440 | tf_op jit(solution)/shard_map/ppermute | solution.py:82
  3.0 9.5 %collective-permute-start.1 = (bf16[256,512]{1,0:T(8,128)(2,1)S(1)}, bf16[256,512]{1,0:T(8,128)(2,1)S(1)}, u32[]{:S(2)}, u32[]{:S(2)}) collective-permute-start(bf16[256,512]{1,0:T(8,128)(2,1)S(1)} %get-tuple-element.247), channel_id=1, source_target_pairs={{0,2},{1,3},{2,0},{3,1},{4,6},{5,7},{6,4},{7,5},{8,10},{9,11},{10,... | collective-permute-start | bytes 786440 | tf_op jit(solution)/shard_map/ppermute | solution.py:82
  6.7 5.9 %collective-permute-start.2 = (bf16[2,2048]{1,0:T(2,128)(2,1)S(1)}, bf16[2,2048]{1,0:T(2,128)(2,1)S(1)}, u32[]{:S(2)}, u32[]{:S(2)}) collective-permute-start(bf16[2,2048]{1,0:T(2,128)(2,1)S(1)} %slice_bitcast_fusion.1), channel_id=1, source_target_pairs={{0,4},{4,8},{8,12},{12,16},{16,20},{20,24},{24,28},{1,5},{5,9},{9,... | collective-permute-start | bytes 24584 | tf_op jit(solution)/shard_map/ppermute | solution.py:671
  12.6 19.4 %collective-permute-start.3 = (bf16[256,1536]{1,0:T(8,128)(2,1)S(1)}, bf16[256,1536]{1,0:T(8,128)(2,1)S(1)}, u32[]{:S(2)}, u32[]{:S(2)}) collective-permute-start(bf16[256,1536]{1,0:T(8,128)(2,1)S(1)} %pad_maximum_fusion.refs_0_), channel_id=1, source_target_pairs={{0,8},{8,16},{16,24},{24,28},{28,20},{20,12},{12,4},{4,0},{1,9},{9... | collective-permute-start | bytes 2359304 | tf_op jit(solution)/shard_map/ppermute | solution.py:65
  14.7 18.6 %collective-permute-start.4 = (bf16[256,1536]{1,0:T(8,128)(2,1)S(1)}, bf16[256,1536]{1,0:T(8,128)(2,1)S(1)}, u32[]{:S(2)}, u32[]{:S(2)}) collective-permute-start(bf16[256,1536]{1,0:T(8,128)(2,1)S(1)} %pad_maximum_fusion.refs_0_), channel_id=1, source_target_pairs={{0,4},{8,0},{16,8},{24,16},{28,24},{20,28},{12,20},{4,12},{1,5},{9... | collective-permute-start | bytes 2359304 | tf_op jit(solution)/shard_map/ppermute | solution.py:65
  14.8 13.1 %collective-permute-start.5 = (bf16[128,2048]{1,0:T(8,128)(2,1)S(1)}, bf16[128,2048]{1,0:T(8,128)(2,1)S(1)}, u32[]{:S(2)}, u32[]{:S(2)}) collective-permute-start(bf16[128,2048]{1,0:T(8,128)(2,1)S(1)} %slice_bitcast_fusion), channel_id=1, source_target_pairs={{0,2},{1,3},{2,0},{3,1},{4,6},{5,7},{6,4},{7,5},{8,10},{9,11},{10,... | collective-permute-start | bytes 1572872 | tf_op jit(solution)/shard_map/ppermute | solution.py:82
  33.3 20.1 %collective-permute-start.8 = (bf16[272,2048]{1,0:T(8,128)(2,1)S(1)}, bf16[272,2048]{1,0:T(8,128)(2,1)S(1)}, u32[]{:S(2)}, u32[]{:S(2)}) collective-permute-start(bf16[272,2048]{1,0:T(8,128)(2,1)S(1)} %maximum_maximum_fusion.refs_0_.refs_9_), channel_id=1, source_target_pairs={{0,1},{1,0},{2,3},{3,2},{4,5},{5,4},{6,7},{7,6},{8,9},{9,8},{10,11... | collective-permute-start | bytes 3342344 | tf_op jit(solution)/shard_map/ppermute | solution.py:82
  33.3 20.0 %collective-permute-start.7 = (bf16[256,1536]{1,0:T(8,128)(2,1)S(1)}, bf16[256,1536]{1,0:T(8,128)(2,1)S(1)}, u32[]{:S(2)}, u32[]{:S(2)}) collective-permute-start(bf16[256,1536]{1,0:T(8,128)(2,1)S(1)} %collective-permute-done.4.refs_2_), channel_id=1, source_target_pairs={{0,4},{8,0},{16,8},{24,16},{28,24},{20,28},{12,20},{4,12},{1,5},{9... | collective-permute-start | bytes 2359304 | tf_op jit(solution)/shard_map/ppermute | solution.py:65
  33.7 19.7 %collective-permute-start.6 = (bf16[256,1536]{1,0:T(8,128)(2,1)S(1)}, bf16[256,1536]{1,0:T(8,128)(2,1)S(1)}, u32[]{:S(2)}, u32[]{:S(2)}) collective-permute-start(bf16[256,1536]{1,0:T(8,128)(2,1)S(1)} %collective-permute-done.3.refs_1_), channel_id=1, source_target_pairs={{0,8},{8,16},{16,24},{24,28},{28,20},{20,12},{12,4},{4,0},{1,9},{9... | collective-permute-start | bytes 2359304 | tf_op jit(solution)/shard_map/ppermute | solution.py:65
  35.4 15.2 %collective-permute-start.9 = (bf16[144,2048]{1,0:T(8,128)(2,1)S(1)}, bf16[144,2048]{1,0:T(8,128)(2,1)S(1)}, u32[]{:S(2)}, u32[]{:S(2)}) collective-permute-start(bf16[144,2048]{1,0:T(8,128)(2,1)S(1)} %slice.302), channel_id=1, source_target_pairs={{0,2},{1,3},{2,0},{3,1},{4,6},{5,7},{6,4},{7,5},{8,10},{9,11},{10,... | collective-permute-start | bytes 1769480 | tf_op jit(solution)/shard_map/ppermute | solution.py:82
  36.9 1.9 collective-permute-start.10
  53.4 2.8 %collective-permute-start.11 = (bf16[144,2048]{1,0:T(8,128)(2,1)S(1)}, bf16[144,2048]{1,0:T(8,128)(2,1)S(1)}, u32[]{:S(2)}, u32[]{:S(2)}) collective-permute-start(bf16[144,2048]{1,0:T(8,128)(2,1)S(1)} %collective-permute-done.9.refs_3_.refs_12_), channel_id=1, source_target_pairs={{0,1},{1,0},{2,3},{3,2},{4,5},{5,4},{6,7},{7,6},{8,9},{9,8},{10,11... | collective-permute-start | bytes 1769480 | tf_op jit(solution)/shard_map/ppermute | solution.py:82
  53.4 20.0 %collective-permute-start.16 = (bf16[256,1536]{1,0:T(8,128)(2,1)S(1)}, bf16[256,1536]{1,0:T(8,128)(2,1)S(1)}, u32[]{:S(2)}, u32[]{:S(2)}) collective-permute-start(bf16[256,1536]{1,0:T(8,128)(2,1)S(1)} %collective-permute-done.7.refs_4_), channel_id=1, source_target_pairs={{0,4},{8,0},{16,8},{24,16},{28,24},{20,28},{12,20},{4,12},{1,5},{9... | collective-permute-start | bytes 2359304 | tf_op jit(solution)/shard_map/ppermute | solution.py:65
  54.9 19.7 %collective-permute-start.15 = (bf16[256,1536]{1,0:T(8,128)(2,1)S(1)}, bf16[256,1536]{1,0:T(8,128)(2,1)S(1)}, u32[]{:S(2)}, u32[]{:S(2)}) collective-permute-start(bf16[256,1536]{1,0:T(8,128)(2,1)S(1)} %collective-permute-done.6.refs_3_), channel_id=1, source_target_pairs={{0,8},{8,16},{16,24},{24,28},{28,20},{20,12},{12,4},{4,0},{1,9},{9... | collective-permute-start | bytes 2359304 | tf_op jit(solution)/shard_map/ppermute | solution.py:65
  56.1 27.7 %collective-permute-start.12 = (bf16[272,512]{1,0:T(8,128)(2,1)S(1)}, bf16[272,512]{1,0:T(8,128)(2,1)S(1)}, u32[]{:S(2)}, u32[]{:S(2)}) collective-permute-start(bf16[272,512]{1,0:T(8,128)(2,1)S(1)} %get-tuple-element.146), channel_id=1, source_target_pairs={{0,1},{1,0},{2,3},{3,2},{4,5},{5,4},{6,7},{7,6},{8,9},{9,8},{10,11... | collective-permute-start | bytes 835592 | tf_op jit(solution)/shard_map/ppermute | solution.py:82
  56.2 27.6 %collective-permute-start.13 = (bf16[272,512]{1,0:T(8,128)(2,1)S(1)}, bf16[272,512]{1,0:T(8,128)(2,1)S(1)}, u32[]{:S(2)}, u32[]{:S(2)}) collective-permute-start(bf16[272,512]{1,0:T(8,128)(2,1)S(1)} %get-tuple-element.149), channel_id=1, source_target_pairs={{0,2},{1,3},{2,0},{3,1},{4,6},{5,7},{6,4},{7,5},{8,10},{9,11},{10,... | collective-permute-start | bytes 835592 | tf_op jit(solution)/shard_map/ppermute | solution.py:82
  57.9 26.0 %collective-permute-start.14 = (bf16[272,512]{1,0:T(8,128)(2,1)S(1)}, bf16[272,512]{1,0:T(8,128)(2,1)S(1)}, u32[]{:S(2)}, u32[]{:S(2)}) collective-permute-start(bf16[272,512]{1,0:T(8,128)(2,1)S(1)} %get-tuple-element.152), channel_id=1, source_target_pairs={{0,3},{1,2},{2,1},{3,0},{4,7},{5,6},{6,5},{7,4},{8,11},{9,10},{10,... | collective-permute-start | bytes 835592 | tf_op jit(solution)/shard_map/ppermute | solution.py:82
  61.8 73.2 %copy-start.1 = (f32[1024,128]{1,0:T(8,128)}, f32[1024,128]{1,0:T(8,128)S(1)}, u32[]{:S(2)}) copy-start(f32[1024,128]{1,0:T(8,128)S(1)} %get-tuple-element.237.refs_16_) | copy-start | bytes 1572868
  74.6 10.5 %collective-permute-start.18 = (bf16[128,1536]{1,0:T(8,128)(2,1)S(1)}, bf16[128,1536]{1,0:T(8,128)(2,1)S(1)}, u32[]{:S(2)}, u32[]{:S(2)}) collective-permute-start(bf16[128,1536]{1,0:T(8,128)(2,1)S(1)} %slice.325), channel_id=1, source_target_pairs={{0,4},{8,0},{16,8},{24,16},{28,24},{20,28},{12,20},{4,12},{1,5},{9... | collective-permute-start | bytes 1179656 | tf_op jit(solution)/shard_map/ppermute | solution.py:65
  76.3 10.4 %collective-permute-start.17 = (bf16[128,1536]{1,0:T(8,128)(2,1)S(1)}, bf16[128,1536]{1,0:T(8,128)(2,1)S(1)}, u32[]{:S(2)}, u32[]{:S(2)}) collective-permute-start(bf16[128,1536]{1,0:T(8,128)(2,1)S(1)} %slice.324), channel_id=1, source_target_pairs={{0,8},{8,16},{16,24},{24,28},{28,20},{20,12},{12,4},{4,0},{1,9},{9... | collective-permute-start | bytes 1179656 | tf_op jit(solution)/shard_map/ppermute | solution.py:65
  91.5 4.2 %collective-permute-start.19 = (f32[3,8,512]{2,1,0:T(8,128)S(1)}, f32[3,8,512]{2,1,0:T(8,128)S(1)}, u32[]{:S(2)}, u32[]{:S(2)}) collective-permute-start(f32[3,8,512]{2,1,0:T(8,128)S(1)} %get-tuple-element.163), channel_id=1, source_target_pairs={{0,4},{4,0},{8,12},{12,8},{16,20},{20,16},{24,28},{28,24},{1,5},{5... | collective-permute-start | bytes 147464 | tf_op jit(solution)/shard_map/ppermute | solution.py:82
  95.7 4.7 %collective-permute-start.20 = (f32[3,8,512]{2,1,0:T(8,128)S(1)}, f32[3,8,512]{2,1,0:T(8,128)S(1)}, u32[]{:S(2)}, u32[]{:S(2)}) collective-permute-start(f32[3,8,512]{2,1,0:T(8,128)S(1)} %pad_maximum_fusion.2), channel_id=1, source_target_pairs={{0,8},{4,12},{8,0},{12,4},{16,24},{20,28},{24,16},{28,20},{1,9},{5... | collective-permute-start | bytes 147464 | tf_op jit(solution)/shard_map/ppermute | solution.py:82
  100.4 5.6 %collective-permute-start.21 = (f32[3,8,512]{2,1,0:T(8,128)S(1)}, f32[3,8,512]{2,1,0:T(8,128)S(1)}, u32[]{:S(2)}, u32[]{:S(2)}) collective-permute-start(f32[3,8,512]{2,1,0:T(8,128)S(1)} %pad_maximum_fusion.3), channel_id=1, source_target_pairs={{0,16},{4,20},{8,24},{12,28},{16,0},{20,4},{24,8},{28,12},{1,17},{... | collective-permute-start | bytes 147464 | tf_op jit(solution)/shard_map/ppermute | solution.py:82
  101.4 10.9 %collective-permute-start.22 = (f32[4,8,512]{2,1,0:T(8,128)S(1)}, f32[4,8,512]{2,1,0:T(8,128)S(1)}, u32[]{:S(2)}, u32[]{:S(2)}) collective-permute-start(f32[4,8,512]{2,1,0:T(8,128)S(1)} %get-tuple-element.178), channel_id=1, source_target_pairs={{4,0},{8,4},{12,8},{16,12},{20,16},{24,20},{28,24},{5,1},{9,5},{13... | collective-permute-start | bytes 196616 | tf_op jit(solution)/shard_map/ppermute | solution.py:801
  114.2 14.1 %collective-permute-start.26 = (bf16[2,2,128,512]{3,2,1,0:T(8,128)(2,1)S(1)}, bf16[2,2,128,512]{3,2,1,0:T(8,128)(2,1)S(1)}, u32[]{:S(2)}, u32[]{:S(2)}) collective-permute-start(bf16[2,2,128,512]{3,2,1,0:T(8,128)(2,1)S(1)} %get-tuple-element.191), channel_id=1, source_target_pairs={{0,2},{1,3},{2,0},{3,1},{4,6},{5,7},{6,4},{7,5},{8,10},{9,11},{10,... | collective-permute-start | bytes 1572872 | tf_op jit(solution)/shard_map/ppermute | solution.py:82
  115.8 12.5 %collective-permute-start.25 = (bf16[2,2,128,512]{3,2,1,0:T(8,128)(2,1)S(1)}, bf16[2,2,128,512]{3,2,1,0:T(8,128)(2,1)S(1)}, u32[]{:S(2)}, u32[]{:S(2)}) collective-permute-start(bf16[2,2,128,512]{3,2,1,0:T(8,128)(2,1)S(1)} %get-tuple-element.189), channel_id=1, source_target_pairs={{0,1},{1,0},{2,3},{3,2},{4,5},{5,4},{6,7},{7,6},{8,9},{9,8},{10,11... | collective-permute-start | bytes 1572872 | tf_op jit(solution)/shard_map/ppermute | solution.py:82
  115.8 11.5 %collective-permute-start.23 = (bf16[128,1536]{1,0:T(8,128)(2,1)S(1)}, bf16[128,1536]{1,0:T(8,128)(2,1)S(1)}, u32[]{:S(2)}, u32[]{:S(2)}) collective-permute-start(bf16[128,1536]{1,0:T(8,128)(2,1)S(1)} %get-tuple-element.179), channel_id=1, source_target_pairs={{0,8},{8,16},{16,24},{24,28},{28,20},{20,12},{12,4},{4,0},{1,9},{9... | collective-permute-start | bytes 1179656 | tf_op jit(solution)/shard_map/ppermute | solution.py:65
  116.8 11.2 %collective-permute-start.24 = (bf16[128,1536]{1,0:T(8,128)(2,1)S(1)}, bf16[128,1536]{1,0:T(8,128)(2,1)S(1)}, u32[]{:S(2)}, u32[]{:S(2)}) collective-permute-start(bf16[128,1536]{1,0:T(8,128)(2,1)S(1)} %get-tuple-element.180), channel_id=1, source_target_pairs={{0,4},{8,0},{16,8},{24,16},{28,24},{20,28},{12,20},{4,12},{1,5},{9... | collective-permute-start | bytes 1179656 | tf_op jit(solution)/shard_map/ppermute | solution.py:65
  128.3 18.9 %collective-permute-start.28 = (bf16[256,1536]{1,0:T(8,128)(2,1)S(1)}, bf16[256,1536]{1,0:T(8,128)(2,1)S(1)}, u32[]{:S(2)}, u32[]{:S(2)}) collective-permute-start(bf16[256,1536]{1,0:T(8,128)(2,1)S(1)} %get-tuple-element.194), channel_id=1, source_target_pairs={{0,4},{8,0},{16,8},{24,16},{28,24},{20,28},{12,20},{4,12},{1,5},{9... | collective-permute-start | bytes 2359304 | tf_op jit(solution)/shard_map/ppermute | solution.py:65
  129.3 18.6 %collective-permute-start.27 = (bf16[256,1536]{1,0:T(8,128)(2,1)S(1)}, bf16[256,1536]{1,0:T(8,128)(2,1)S(1)}, u32[]{:S(2)}, u32[]{:S(2)}) collective-permute-start(bf16[256,1536]{1,0:T(8,128)(2,1)S(1)} %get-tuple-element.192), channel_id=1, source_target_pairs={{0,8},{8,16},{16,24},{24,28},{28,20},{20,12},{12,4},{4,0},{1,9},{9... | collective-permute-start | bytes 2359304 | tf_op jit(solution)/shard_map/ppermute | solution.py:65
  130.3 17.9 %collective-permute-start.29 = (bf16[2,2,128,512]{3,2,1,0:T(8,128)(2,1)S(1)}, bf16[2,2,128,512]{3,2,1,0:T(8,128)(2,1)S(1)}, u32[]{:S(2)}, u32[]{:S(2)}) collective-permute-start(bf16[2,2,128,512]{3,2,1,0:T(8,128)(2,1)S(1)} %get-tuple-element.199), channel_id=1, source_target_pairs={{0,3},{1,2},{2,1},{3,0},{4,7},{5,6},{6,5},{7,4},{8,11},{9,10},{10,... | collective-permute-start | bytes 1572872 | tf_op jit(solution)/shard_map/ppermute | solution.py:82
  148.2 3.4 %collective-permute-start.34 = (bf16[256,2048]{1,0:T(8,128)(2,1)S(1)}, bf16[256,2048]{1,0:T(8,128)(2,1)S(1)}, u32[]{:S(2)}, u32[]{:S(2)}) collective-permute-start(bf16[256,2048]{1,0:T(8,128)(2,1)S(1)} %get-tuple-element.221), channel_id=1, source_target_pairs={{0,1},{1,0},{2,3},{3,2},{4,5},{5,4},{6,7},{7,6},{8,9},{9,8},{10,11... | collective-permute-start | bytes 3145736 | tf_op jit(solution)/shard_map/ppermute | solution.py:82
  148.3 2.7 %collective-permute-start.30 = (f32[8,2048]{1,0:T(8,128)S(1)}, f32[8,2048]{1,0:T(8,128)S(1)}, u32[]{:S(2)}, u32[]{:S(2)}) collective-permute-start(f32[8,2048]{1,0:T(8,128)S(1)} %pad_maximum_fusion.1), channel_id=1, source_target_pairs={{0,1},{1,0},{2,3},{3,2},{4,5},{5,4},{6,7},{7,6},{8,9},{9,8},{10,11... | collective-permute-start | bytes 196616 | tf_op jit(solution)/shard_map/ppermute | solution.py:82
  148.9 22.1 %collective-permute-start.35 = (bf16[256,2048]{1,0:T(8,128)(2,1)S(1)}, bf16[256,2048]{1,0:T(8,128)(2,1)S(1)}, u32[]{:S(2)}, u32[]{:S(2)}) collective-permute-start(bf16[256,2048]{1,0:T(8,128)(2,1)S(1)} %get-tuple-element.223), channel_id=1, source_target_pairs={{0,1},{1,0},{2,3},{3,2},{4,5},{5,4},{6,7},{7,6},{8,9},{9,8},{10,11... | collective-permute-start | bytes 3145736 | tf_op jit(solution)/shard_map/ppermute | solution.py:82
  149.0 19.9 %collective-permute-start.33 = (bf16[256,1536]{1,0:T(8,128)(2,1)S(1)}, bf16[256,1536]{1,0:T(8,128)(2,1)S(1)}, u32[]{:S(2)}, u32[]{:S(2)}) collective-permute-start(bf16[256,1536]{1,0:T(8,128)(2,1)S(1)} %get-tuple-element.218), channel_id=1, source_target_pairs={{0,4},{8,0},{16,8},{24,16},{28,24},{20,28},{12,20},{4,12},{1,5},{9... | collective-permute-start | bytes 2359304 | tf_op jit(solution)/shard_map/ppermute | solution.py:65
  150.0 20.3 %collective-permute-start.32 = (bf16[256,1536]{1,0:T(8,128)(2,1)S(1)}, bf16[256,1536]{1,0:T(8,128)(2,1)S(1)}, u32[]{:S(2)}, u32[]{:S(2)}) collective-permute-start(bf16[256,1536]{1,0:T(8,128)(2,1)S(1)} %get-tuple-element.217), channel_id=1, source_target_pairs={{0,8},{8,16},{16,24},{24,28},{28,20},{20,12},{12,4},{4,0},{1,9},{9... | collective-permute-start | bytes 2359304 | tf_op jit(solution)/shard_map/ppermute | solution.py:65
  151.1 5.0 %collective-permute-start.31 = (f32[8,2048]{1,0:T(8,128)S(1)}, f32[8,2048]{1,0:T(8,128)S(1)}, u32[]{:S(2)}, u32[]{:S(2)}) collective-permute-start(f32[8,2048]{1,0:T(8,128)S(1)} %select_maximum_fusion), channel_id=1, source_target_pairs={{0,2},{1,3},{2,0},{3,1},{4,6},{5,7},{6,4},{7,5},{8,10},{9,11},{10,... | collective-permute-start | bytes 196616 | tf_op jit(solution)/shard_map/ppermute | solution.py:82
  152.2 18.9 %collective-permute-start.37 = (bf16[128,2048]{1,0:T(8,128)(2,1)S(1)}, bf16[128,2048]{1,0:T(8,128)(2,1)S(1)}, u32[]{:S(2)}, u32[]{:S(2)}) collective-permute-start(bf16[128,2048]{1,0:T(8,128)(2,1)S(1)} %get-tuple-element.226), channel_id=1, source_target_pairs={{0,2},{1,3},{2,0},{3,1},{4,6},{5,7},{6,4},{7,5},{8,10},{9,11},{10,... | collective-permute-start | bytes 1572872 | tf_op jit(solution)/shard_map/ppermute | solution.py:82
  156.1 14.9 %collective-permute-start.36 = (f32[6,2048]{1,0:T(8,128)S(1)}, f32[6,2048]{1,0:T(8,128)S(1)}, u32[]{:S(2)}, u32[]{:S(2)}) collective-permute-start(f32[6,2048]{1,0:T(8,128)S(1)} %slice_add_fusion.1), channel_id=1, source_target_pairs={{0,4},{4,0},{8,12},{12,8},{16,20},{20,16},{24,28},{28,24},{1,5},{5... | collective-permute-start | bytes 147464 | tf_op jit(solution)/shard_map/ppermute | solution.py:82
  171.0 14.9 %collective-permute-start.39 = (bf16[256,1024]{1,0:T(8,128)(2,1)S(1)}, bf16[256,1024]{1,0:T(8,128)(2,1)S(1)}, u32[]{:S(2)}, u32[]{:S(2)}) collective-permute-start(bf16[256,1024]{1,0:T(8,128)(2,1)S(1)} %get-tuple-element.230), channel_id=1, source_target_pairs={{0,4},{8,0},{16,8},{24,16},{28,24},{20,28},{12,20},{4,12},{1,5},{9... | collective-permute-start | bytes 1572872 | tf_op jit(solution)/shard_map/ppermute | solution.py:65
  171.3 14.9 %collective-permute-start.38 = (bf16[256,1024]{1,0:T(8,128)(2,1)S(1)}, bf16[256,1024]{1,0:T(8,128)(2,1)S(1)}, u32[]{:S(2)}, u32[]{:S(2)}) collective-permute-start(bf16[256,1024]{1,0:T(8,128)(2,1)S(1)} %get-tuple-element.228), channel_id=1, source_target_pairs={{0,8},{8,16},{16,24},{24,28},{28,20},{20,12},{12,4},{4,0},{1,9},{9... | collective-permute-start | bytes 1572872 | tf_op jit(solution)/shard_map/ppermute | solution.py:65
  173.2 18.5 %collective-permute-start.42 = (bf16[128,2048]{1,0:T(8,128)(2,1)S(1)}, bf16[128,2048]{1,0:T(8,128)(2,1)S(1)}, u32[]{:S(2)}, u32[]{:S(2)}) collective-permute-start(bf16[128,2048]{1,0:T(8,128)(2,1)S(1)} %get-tuple-element.235), channel_id=1, source_target_pairs={{0,2},{1,3},{2,0},{3,1},{4,6},{5,7},{6,4},{7,5},{8,10},{9,11},{10,... | collective-permute-start | bytes 1572872 | tf_op jit(solution)/shard_map/ppermute | solution.py:82
  173.8 17.9 %collective-permute-start.41 = (bf16[256,512]{1,0:T(8,128)(2,1)S(1)}, bf16[256,512]{1,0:T(8,128)(2,1)S(1)}, u32[]{:S(2)}, u32[]{:S(2)}) collective-permute-start(bf16[256,512]{1,0:T(8,128)(2,1)S(1)} %get-tuple-element.234), channel_id=1, source_target_pairs={{0,4},{8,0},{16,8},{24,16},{28,24},{20,28},{12,20},{4,12},{1,5},{9... | collective-permute-start | bytes 786440 | tf_op jit(solution)/shard_map/ppermute | solution.py:65
  174.1 17.7 %collective-permute-start.40 = (bf16[256,512]{1,0:T(8,128)(2,1)S(1)}, bf16[256,512]{1,0:T(8,128)(2,1)S(1)}, u32[]{:S(2)}, u32[]{:S(2)}) collective-permute-start(bf16[256,512]{1,0:T(8,128)(2,1)S(1)} %get-tuple-element.232), channel_id=1, source_target_pairs={{0,8},{8,16},{16,24},{24,28},{28,20},{20,12},{12,4},{4,0},{1,9},{9... | collective-permute-start | bytes 786440 | tf_op jit(solution)/shard_map/ppermute | solution.py:65
  186.5 4.7 %collective-permute-start.43 = (f32[6,2048]{1,0:T(8,128)S(1)}, f32[6,2048]{1,0:T(8,128)S(1)}, u32[]{:S(2)}, u32[]{:S(2)}) collective-permute-start(f32[6,2048]{1,0:T(8,128)S(1)} %add.310), channel_id=1, source_target_pairs={{0,8},{4,12},{8,0},{12,4},{16,24},{20,28},{24,16},{28,20},{1,9},{5... | collective-permute-start | bytes 147464 | tf_op jit(solution)/shard_map/ppermute | solution.py:82
  188.9 8.8 %collective-permute-start.44 = (bf16[256,512]{1,0:T(8,128)(2,1)S(1)}, bf16[256,512]{1,0:T(8,128)(2,1)S(1)}, u32[]{:S(2)}, u32[]{:S(2)}) collective-permute-start(bf16[256,512]{1,0:T(8,128)(2,1)S(1)} %get-tuple-element.248), channel_id=1, source_target_pairs={{0,1},{1,0},{2,3},{3,2},{4,5},{5,4},{6,7},{7,6},{8,9},{9,8},{10,11... | collective-permute-start | bytes 786440 | tf_op jit(solution)/shard_map/ppermute | solution.py:82
  191.2 6.6 %collective-permute-start.45 = (bf16[256,512]{1,0:T(8,128)(2,1)S(1)}, bf16[256,512]{1,0:T(8,128)(2,1)S(1)}, u32[]{:S(2)}, u32[]{:S(2)}) collective-permute-start(bf16[256,512]{1,0:T(8,128)(2,1)S(1)} %get-tuple-element.249), channel_id=1, source_target_pairs={{0,2},{1,3},{2,0},{3,1},{4,6},{5,7},{6,4},{7,5},{8,10},{9,11},{10,... | collective-permute-start | bytes 786440 | tf_op jit(solution)/shard_map/ppermute | solution.py:82
  191.8 5.2 %collective-permute-start.46 = (f32[6,2048]{1,0:T(8,128)S(1)}, f32[6,2048]{1,0:T(8,128)S(1)}, u32[]{:S(2)}, u32[]{:S(2)}) collective-permute-start(f32[6,2048]{1,0:T(8,128)S(1)} %add.316), channel_id=1, source_target_pairs={{0,16},{4,20},{8,24},{12,28},{16,0},{20,4},{24,8},{28,12},{1,17},{... | collective-permute-start | bytes 147464 | tf_op jit(solution)/shard_map/ppermute | solution.py:82
  (13 other events, 302.5 us)

commit v8 on v7

--- a/solution.py
+++ b/solution.py
@@ -260,7 +260,7 @@
         put_strided(products, PAD - 1, seqs, stride, one, lane)
         put_strided(sums, PAD - 1, seqs, stride, zero, lane)
         _, decays, injects, handed = lax.fori_loop(
-            0, span, turn, (before[:, units], one, zero, zero), unroll=8
+            0, span, turn, (before[:, units], one, zero, zero), unroll=16
         )
         maps[0, :, units], maps[1, :, units], maps[2, :, units] = decays, injects, handed
         c, f, r, g, x = (

time: 199 us -> 199 us (level)
  no operation moved by 1% of the time
where the time goes in v8:
time: 199 us
  waiting for transfers between devices  97.2 us (49%)
  Pallas kernels  45.8 us (23%)
  starting transfers between devices  44.8 us (23%)
  other arithmetic  5.98 us (3%)
  local copies, waits for them, and re-layouts  3.63 us (2%)
    ppermute x18, waiting for transfers between devices, along_ring(): lax.ppermute(value, 'seq', [(order[i], order[(i + steps) % count]) for i...  54.8 us
    pallas_call x17, Pallas kernels, call(): pl.pallas_call(kernel, out_shape=held if pinned else out_shape, in_specs=...  45.8 us
    ppermute x27, waiting for transfers between devices, swapped(): lax.ppermute(value, axis, [(i, i ^ bit) for i in range(lax.axis_size(axis...  42.3 us
    ppermute x27, starting transfers between devices, swapped(): lax.ppermute(value, axis, [(i, i ^ bit) for i in range(lax.axis_size(axis...  21.5 us
    ppermute x18, starting transfers between devices, along_ring(): lax.ppermute(value, 'seq', [(order[i], order[(i + steps) % count]) for i...  18.7 us
  transfers between devices with their start and end apart: 47, of which 29 were waited for; matrix products, arithmetic and copies ran while one was open for 4% of the time, Pallas kernels for 19%

profile of v8, /device:TPU:0, one launch (start us, length us, event | category | flops | bytes accessed | tf_op | source)
XLA Modules:
  0.0 199.1 jit_solution(11518526835766418380)
XLA Ops:
  3.0 2.6 %collective-permute-start.1 = (bf16[256,512]{1,0:T(8,128)(2,1)S(1)}, bf16[256,512]{1,0:T(8,128)(2,1)S(1)}, u32[]{:S(2)}, u32[]{:S(2)}) collective-permute-start(bf16[256,512]{1,0:T(8,128)(2,1)S(1)} %get-tuple-element.247), channel_id=1, source_target_pairs={{0,2},{1,3},{2,0},{3,1},{4,6},{5,7},{6,4},{7,5},{8,10},{9,11},{10,... | collective-permute-start | bytes 786440 | tf_op jit(solution)/shard_map/ppermute | solution.py:82
  6.7 3.4 %collective-permute-start.2 = (bf16[2,2048]{1,0:T(2,128)(2,1)S(1)}, bf16[2,2048]{1,0:T(2,128)(2,1)S(1)}, u32[]{:S(2)}, u32[]{:S(2)}) collective-permute-start(bf16[2,2048]{1,0:T(2,128)(2,1)S(1)} %slice_bitcast_fusion.1), channel_id=1, source_target_pairs={{0,4},{4,8},{8,12},{12,16},{16,20},{20,24},{24,28},{1,5},{5,9},{9,... | collective-permute-start | bytes 24584 | tf_op jit(solution)/shard_map/ppermute | solution.py:671
  10.1 2.4 %collective-permute-done.1 = bf16[256,512]{1,0:T(8,128)(2,1)S(1)} collective-permute-done((bf16[256,512]{1,0:T(8,128)(2,1)S(1)}, bf16[256,512]{1,0:T(8,128)(2,1)S(1)}, u32[]{:S(2)}, u32[]{:S(2)}) %collective-permute-start.1) | collective-permute-done | bytes 262176 | tf_op jit(solution)/shard_map/ppermute | solution.py:82
  12.6 2.1 %collective-permute-start.3 = (bf16[256,1536]{1,0:T(8,128)(2,1)S(1)}, bf16[256,1536]{1,0:T(8,128)(2,1)S(1)}, u32[]{:S(2)}, u32[]{:S(2)}) collective-permute-start(bf16[256,1536]{1,0:T(8,128)(2,1)S(1)} %pad_maximum_fusion.refs_0_), channel_id=1, source_target_pairs={{0,8},{8,16},{16,24},{24,28},{28,20},{20,12},{12,4},{4,0},{1,9},{9... | collective-permute-start | bytes 2359304 | tf_op jit(solution)/shard_map/ppermute | solution.py:65
  14.8 1.8 collective-permute-start.5
  16.9 11.0 %collective-permute-done.5.refs_2_.refs_11_ = bf16[128,2048]{1,0:T(8,128)(2,1)S(1)} collective-permute-done((bf16[128,2048]{1,0:T(8,128)(2,1)S(1)}, bf16[128,2048]{1,0:T(8,128)(2,1)S(1)}, u32[]{:S(2)}, u32[]{:S(2)}) %collective-permute-start.5) | collective-permute-done | bytes 524320 | tf_op jit(solution)/shard_map/ppermute | solution.py:82
  27.9 4.0 %collective-permute-done.3.refs_1_ = bf16[256,1536]{1,0:T(8,128)(2,1)S(1)} collective-permute-done((bf16[256,1536]{1,0:T(8,128)(2,1)S(1)}, bf16[256,1536]{1,0:T(8,128)(2,1)S(1)}, u32[]{:S(2)}, u32[]{:S(2)}) %collective-permute-start.3) | collective-permute-done | bytes 786464 | tf_op jit(solution)/shard_map/ppermute | solution.py:65
  31.9 1.3 collective-permute-done.4.refs_2_
  33.7 1.6 collective-permute-start.6
  35.4 1.6 collective-permute-start.9
  36.9 1.9 collective-permute-done.10.refs_4_.refs_13_
  38.9 11.7 %collective-permute-done.9.refs_3_.refs_12_ = bf16[144,2048]{1,0:T(8,128)(2,1)S(1)} collective-permute-done((bf16[144,2048]{1,0:T(8,128)(2,1)S(1)}, bf16[144,2048]{1,0:T(8,128)(2,1)S(1)}, u32[]{:S(2)}, u32[]{:S(2)}) %collective-permute-start.9) | collective-permute-done | bytes 589856 | tf_op jit(solution)/shard_map/ppermute | solution.py:82
  50.6 2.6 %collective-permute-done.7.refs_4_ = bf16[256,1536]{1,0:T(8,128)(2,1)S(1)} collective-permute-done((bf16[256,1536]{1,0:T(8,128)(2,1)S(1)}, bf16[256,1536]{1,0:T(8,128)(2,1)S(1)}, u32[]{:S(2)}, u32[]{:S(2)}) %collective-permute-start.7) | collective-permute-done | bytes 786464 | tf_op jit(solution)/shard_map/ppermute | solution.py:65
  53.4 1.5 collective-permute-start.16
  56.2 1.6 collective-permute-start.13
  58.1 3.7 %shard_map.187 = (bf16[1088,2048]{1,0:T(8,128)(2,1)S(1)}, f32[1024,128]{1,0:T(8,128)S(1)}, f32[1024,128]{1,0:T(8,128)S(1)}, bf16[1024,512]{1,0:T(8,128)(2,1)S(1)}) custom-call(s32[6]{0:T(128)S(1)} %stack.116.place, bf16[272,2048]{1,0:T(8,128)(2,1)S(1)} %maximum_maximum_fusion.refs_0_.refs_9_, bf16[272,2048]{1,0:T(8,128)(2,1)S(1)} %collective-permute-done.8.refs_1_.refs_10_, ...), custom_call_target="tpu_custom_call" | custom-call | tf_op jit(solution)/shard_map/pallas_call | solution.py:28
  61.8 11.5 %collective-permute-done.16.refs_6_ = bf16[256,1536]{1,0:T(8,128)(2,1)S(1)} collective-permute-done((bf16[256,1536]{1,0:T(8,128)(2,1)S(1)}, bf16[256,1536]{1,0:T(8,128)(2,1)S(1)}, u32[]{:S(2)}, u32[]{:S(2)}) %collective-permute-start.16) | collective-permute-done | bytes 786464 | tf_op jit(solution)/shard_map/ppermute | solution.py:65
  74.6 1.6 collective-permute-start.18
  77.0 6.8 %shard_map.188.begun = f32[1088,1536]{1,0:T(8,128)S(1)} custom-call(s32[8]{0:T(128)S(1)} %stack.120.sources, bf16[1088,2048]{1,0:T(8,128)(2,1)S(1)} %get-tuple-element.160.normed, bf16[256,1536]{1,0:T(8,128)(2,1)S(1)} %pad_maximum_fusion.refs_0_, bf16[256,1536]{1,0:T(8,128)(2,1)S(1)} %collective-permute-done.3.refs_1_, ...), custom_call_target="tpu_custom_call" | custom-call | tf_op jit(solution)/shard_map/pallas_call | solution.py:28
  85.1 1.6 collective-permute-done.17.refs_0_.refs_7_
  86.7 4.7 %shard_map.189 = (f32[3,4,1088,128]{3,2,1,0:T(8,128)S(1)}, f32[2,4,1088,128]{3,2,1,0:T(8,128)S(1)}, f32[2,4,1088,128]{3,2,1,0:T(8,128)S(1)}, f32[3,8,512]{2,1,0:T(8,128)S(1)}, f32[4,8,512]{2,1,0:T(8,128)S(1)}) custom-call(s32[8]{0:T(128)S(1)} %stack.120.sources, s32[6]{0:T(128)S(1)} %stack.116.place, bf16[1088,2048]{1,0:T(8,128)(2,1)S(1)} %get-tuple-element.160.normed, ...), custom_call_target="tpu_custom_call" | custom-call | tf_op jit(solution)/shard_map/pallas_call | solution.py:28
  91.5 1.6 collective-permute-start.19
  93.1 2.5 %collective-permute-done.19 = f32[3,8,512]{2,1,0:T(8,128)S(1)} collective-permute-done((f32[3,8,512]{2,1,0:T(8,128)S(1)}, f32[3,8,512]{2,1,0:T(8,128)S(1)}, u32[]{:S(2)}, u32[]{:S(2)}) %collective-permute-start.19) | collective-permute-done | bytes 49184 | tf_op jit(solution)/shard_map/ppermute | solution.py:82
  96.8 3.6 %collective-permute-done.20 = f32[3,8,512]{2,1,0:T(8,128)S(1)} collective-permute-done((f32[3,8,512]{2,1,0:T(8,128)S(1)}, f32[3,8,512]{2,1,0:T(8,128)S(1)}, u32[]{:S(2)}, u32[]{:S(2)}) %collective-permute-start.20) | collective-permute-done | bytes 49184 | tf_op jit(solution)/shard_map/ppermute | solution.py:82
  101.3 1.3 collective-permute-start.22
  102.6 3.3 %collective-permute-done.21 = f32[3,8,512]{2,1,0:T(8,128)S(1)} collective-permute-done((f32[3,8,512]{2,1,0:T(8,128)S(1)}, f32[3,8,512]{2,1,0:T(8,128)S(1)}, u32[]{:S(2)}, u32[]{:S(2)}) %collective-permute-start.21) | collective-permute-done | bytes 49184 | tf_op jit(solution)/shard_map/ppermute | solution.py:82
  106.0 6.2 %shard_map.190 = (bf16[1088,1536]{1,0:T(8,128)(2,1)S(1)}, bf16[2,2,128,512]{3,2,1,0:T(8,128)(2,1)S(1)}, bf16[2,2,128,512]{3,2,1,0:T(8,128)(2,1)S(1)}, bf16[2,2,1...) custom-call(s32[6]{0:T(128)S(1)} %stack.116.place, ...), custom_call_target="tpu_custom_call" | custom-call | tf_op jit(solution)/shard_map/pallas_call | solution.py:28
  112.3 1.8 shard_map.192
  114.1 1.6 collective-permute-start.26
  117.7 2.8 %shard_map.195 = (f32[256,1536]{1,0:T(8,128)S(1)}, f32[256,1536]{1,0:T(8,128)S(1)}) custom-call(s32[8]{0:T(128)S(1)} %stack.109.owners, s32[6]{0:T(128)S(1)} %stack.116.place, bf16[1088,2048]{1,0:T(8,128)(2,1)S(1)} %get-tuple-element.160.normed, bf16[1088,1536]{1,0:T(8,128)(2,1)S(1)} %shard_map.191.grads), custom_call_target="tpu_custom_call" | custom-call | tf_op jit(solution)/shard_map/pallas_call | solution.py:28
  120.5 2.8 %shard_map.193 = (f32[256,1536]{1,0:T(8,128)S(1)}, f32[256,1536]{1,0:T(8,128)S(1)}) custom-call(s32[8]{0:T(128)S(1)} %stack.109.owners, s32[6]{0:T(128)S(1)} %stack.116.place, bf16[1088,2048]{1,0:T(8,128)(2,1)S(1)} %get-tuple-element.160.normed, bf16[1088,1536]{1,0:T(8,128)(2,1)S(1)} %shard_map.191.grads), custom_call_target="tpu_custom_call" | custom-call | tf_op jit(solution)/shard_map/pallas_call | solution.py:28
  123.3 3.9 %collective-permute-done.23.up = bf16[128,1536]{1,0:T(8,128)(2,1)S(1)} collective-permute-done((bf16[128,1536]{1,0:T(8,128)(2,1)S(1)}, bf16[128,1536]{1,0:T(8,128)(2,1)S(1)}, u32[]{:S(2)}, u32[]{:S(2)}) %collective-permute-start.23) | collective-permute-done | bytes 393248 | tf_op jit(solution)/shard_map/ppermute | solution.py:65
  130.4 2.8 %shard_map.197 = (f32[256,1536]{1,0:T(8,128)S(1)}, f32[256,1536]{1,0:T(8,128)S(1)}) custom-call(s32[8]{0:T(128)S(1)} %stack.109.owners, s32[6]{0:T(128)S(1)} %stack.116.place, bf16[1088,2048]{1,0:T(8,128)(2,1)S(1)} %get-tuple-element.160.normed, bf16[1088,1536]{1,0:T(8,128)(2,1)S(1)} %shard_map.191.grads), custom_call_target="tpu_custom_call" | custom-call | tf_op jit(solution)/shard_map/pallas_call | solution.py:28
  133.2 1.8 shard_map.196
  135.0 8.0 %shard_map.198 = (f32[256,2048]{1,0:T(8,128)S(1)}, bf16[256,2048]{1,0:T(8,128)(2,1)S(1)}, bf16[256,2048]{1,0:T(8,128)(2,1)S(1)}, bf16[256,2048]{1,0:T(8,128)(2,1)S(1)}, f32[8,2048]{1,0:T(8,128)S(1)}) custom-call(s32[8]{0:T(128)S(1)} %stack.120.sources, s32[6]{0:T(128)S(1)} %stack.116.place, bf16[1088,1536]{1,0:T(8,128)(2,1)S(1)} %shard_map.191.grads, ...), custom_call_target="tpu_custom_call" | custom-call | tf_op jit(solution)/shard_map/pallas_call | solution.py:28
  143.0 4.1 %collective-permute-done.28.down = bf16[256,1536]{1,0:T(8,128)(2,1)S(1)} collective-permute-done((bf16[256,1536]{1,0:T(8,128)(2,1)S(1)}, bf16[256,1536]{1,0:T(8,128)(2,1)S(1)}, u32[]{:S(2)}, u32[]{:S(2)}) %collective-permute-start.28) | collective-permute-done | bytes 786464 | tf_op jit(solution)/shard_map/ppermute | solution.py:65
  152.1 1.6 collective-permute-start.37
  153.7 2.4 %collective-permute-done.31 = f32[8,2048]{1,0:T(8,128)S(1)} collective-permute-done((f32[8,2048]{1,0:T(8,128)S(1)}, f32[8,2048]{1,0:T(8,128)S(1)}, u32[]{:S(2)}, u32[]{:S(2)}) %collective-permute-start.31) | collective-permute-done | bytes 65568 | tf_op jit(solution)/shard_map/ppermute | solution.py:82
  157.2 1.7 shard_map.200
  158.8 10.0 %collective-permute-done.33.down = bf16[256,1536]{1,0:T(8,128)(2,1)S(1)} collective-permute-done((bf16[256,1536]{1,0:T(8,128)(2,1)S(1)}, bf16[256,1536]{1,0:T(8,128)(2,1)S(1)}, u32[]{:S(2)}, u32[]{:S(2)}) %collective-permute-start.33) | collective-permute-done | bytes 786464 | tf_op jit(solution)/shard_map/ppermute | solution.py:65
  168.8 1.5 collective-permute-done.32.up
  171.2 1.7 collective-permute-start.38
  174.0 1.7 collective-permute-start.40
  175.8 10.0 %collective-permute-done.39 = bf16[256,1024]{1,0:T(8,128)(2,1)S(1)} collective-permute-done((bf16[256,1024]{1,0:T(8,128)(2,1)S(1)}, bf16[256,1024]{1,0:T(8,128)(2,1)S(1)}, u32[]{:S(2)}, u32[]{:S(2)}) %collective-permute-start.39) | collective-permute-done | bytes 524320 | tf_op jit(solution)/shard_map/ppermute | solution.py:65
  186.4 1.8 collective-permute-start.43
  188.8 2.3 %collective-permute-done.43 = f32[6,2048]{1,0:T(8,128)S(1)} collective-permute-done((f32[6,2048]{1,0:T(8,128)S(1)}, f32[6,2048]{1,0:T(8,128)S(1)}, u32[]{:S(2)}, u32[]{:S(2)}) %collective-permute-start.43) | collective-permute-done | bytes 49184 | tf_op jit(solution)/shard_map/ppermute | solution.py:82
  195.2 1.3 add_convert_fusion
  197.8 1.3 shard_map.202
  (149 shorter events, 30.9 us)
Async XLA Ops:
  2.5 7.6 %collective-permute-start = (bf16[256,512]{1,0:T(8,128)(2,1)S(1)}, bf16[256,512]{1,0:T(8,128)(2,1)S(1)}, u32[]{:S(2)}, u32[]{:S(2)}) collective-permute-start(bf16[256,512]{1,0:T(8,128)(2,1)S(1)} %get-tuple-element.246), channel_id=1, source_target_pairs={{0,1},{1,0},{2,3},{3,2},{4,5},{5,4},{6,7},{7,6},{8,9},{9,8},{10,11... | collective-permute-start | bytes 786440 | tf_op jit(solution)/shard_map/ppermute | solution.py:82
  3.0 9.5 %collective-permute-start.1 = (bf16[256,512]{1,0:T(8,128)(2,1)S(1)}, bf16[256,512]{1,0:T(8,128)(2,1)S(1)}, u32[]{:S(2)}, u32[]{:S(2)}) collective-permute-start(bf16[256,512]{1,0:T(8,128)(2,1)S(1)} %get-tuple-element.247), channel_id=1, source_target_pairs={{0,2},{1,3},{2,0},{3,1},{4,6},{5,7},{6,4},{7,5},{8,10},{9,11},{10,... | collective-permute-start | bytes 786440 | tf_op jit(solution)/shard_map/ppermute | solution.py:82
  6.7 5.9 %collective-permute-start.2 = (bf16[2,2048]{1,0:T(2,128)(2,1)S(1)}, bf16[2,2048]{1,0:T(2,128)(2,1)S(1)}, u32[]{:S(2)}, u32[]{:S(2)}) collective-permute-start(bf16[2,2048]{1,0:T(2,128)(2,1)S(1)} %slice_bitcast_fusion.1), channel_id=1, source_target_pairs={{0,4},{4,8},{8,12},{12,16},{16,20},{20,24},{24,28},{1,5},{5,9},{9,... | collective-permute-start | bytes 24584 | tf_op jit(solution)/shard_map/ppermute | solution.py:671
  12.6 19.4 %collective-permute-start.3 = (bf16[256,1536]{1,0:T(8,128)(2,1)S(1)}, bf16[256,1536]{1,0:T(8,128)(2,1)S(1)}, u32[]{:S(2)}, u32[]{:S(2)}) collective-permute-start(bf16[256,1536]{1,0:T(8,128)(2,1)S(1)} %pad_maximum_fusion.refs_0_), channel_id=1, source_target_pairs={{0,8},{8,16},{16,24},{24,28},{28,20},{20,12},{12,4},{4,0},{1,9},{9... | collective-permute-start | bytes 2359304 | tf_op jit(solution)/shard_map/ppermute | solution.py:65
  14.7 18.6 %collective-permute-start.4 = (bf16[256,1536]{1,0:T(8,128)(2,1)S(1)}, bf16[256,1536]{1,0:T(8,128)(2,1)S(1)}, u32[]{:S(2)}, u32[]{:S(2)}) collective-permute-start(bf16[256,1536]{1,0:T(8,128)(2,1)S(1)} %pad_maximum_fusion.refs_0_), channel_id=1, source_target_pairs={{0,4},{8,0},{16,8},{24,16},{28,24},{20,28},{12,20},{4,12},{1,5},{9... | collective-permute-start | bytes 2359304 | tf_op jit(solution)/shard_map/ppermute | solution.py:65
  14.8 13.1 %collective-permute-start.5 = (bf16[128,2048]{1,0:T(8,128)(2,1)S(1)}, bf16[128,2048]{1,0:T(8,128)(2,1)S(1)}, u32[]{:S(2)}, u32[]{:S(2)}) collective-permute-start(bf16[128,2048]{1,0:T(8,128)(2,1)S(1)} %slice_bitcast_fusion), channel_id=1, source_target_pairs={{0,2},{1,3},{2,0},{3,1},{4,6},{5,7},{6,4},{7,5},{8,10},{9,11},{10,... | collective-permute-start | bytes 1572872 | tf_op jit(solution)/shard_map/ppermute | solution.py:82
  33.3 20.1 %collective-permute-start.8 = (bf16[272,2048]{1,0:T(8,128)(2,1)S(1)}, bf16[272,2048]{1,0:T(8,128)(2,1)S(1)}, u32[]{:S(2)}, u32[]{:S(2)}) collective-permute-start(bf16[272,2048]{1,0:T(8,128)(2,1)S(1)} %maximum_maximum_fusion.refs_0_.refs_9_), channel_id=1, source_target_pairs={{0,1},{1,0},{2,3},{3,2},{4,5},{5,4},{6,7},{7,6},{8,9},{9,8},{10,11... | collective-permute-start | bytes 3342344 | tf_op jit(solution)/shard_map/ppermute | solution.py:82
  33.3 20.0 %collective-permute-start.7 = (bf16[256,1536]{1,0:T(8,128)(2,1)S(1)}, bf16[256,1536]{1,0:T(8,128)(2,1)S(1)}, u32[]{:S(2)}, u32[]{:S(2)}) collective-permute-start(bf16[256,1536]{1,0:T(8,128)(2,1)S(1)} %collective-permute-done.4.refs_2_), channel_id=1, source_target_pairs={{0,4},{8,0},{16,8},{24,16},{28,24},{20,28},{12,20},{4,12},{1,5},{9... | collective-permute-start | bytes 2359304 | tf_op jit(solution)/shard_map/ppermute | solution.py:65
  33.7 19.7 %collective-permute-start.6 = (bf16[256,1536]{1,0:T(8,128)(2,1)S(1)}, bf16[256,1536]{1,0:T(8,128)(2,1)S(1)}, u32[]{:S(2)}, u32[]{:S(2)}) collective-permute-start(bf16[256,1536]{1,0:T(8,128)(2,1)S(1)} %collective-permute-done.3.refs_1_), channel_id=1, source_target_pairs={{0,8},{8,16},{16,24},{24,28},{28,20},{20,12},{12,4},{4,0},{1,9},{9... | collective-permute-start | bytes 2359304 | tf_op jit(solution)/shard_map/ppermute | solution.py:65
  35.4 15.2 %collective-permute-start.9 = (bf16[144,2048]{1,0:T(8,128)(2,1)S(1)}, bf16[144,2048]{1,0:T(8,128)(2,1)S(1)}, u32[]{:S(2)}, u32[]{:S(2)}) collective-permute-start(bf16[144,2048]{1,0:T(8,128)(2,1)S(1)} %slice.302), channel_id=1, source_target_pairs={{0,2},{1,3},{2,0},{3,1},{4,6},{5,7},{6,4},{7,5},{8,10},{9,11},{10,... | collective-permute-start | bytes 1769480 | tf_op jit(solution)/shard_map/ppermute | solution.py:82
  36.9 1.9 collective-permute-start.10
  53.4 2.8 %collective-permute-start.11 = (bf16[144,2048]{1,0:T(8,128)(2,1)S(1)}, bf16[144,2048]{1,0:T(8,128)(2,1)S(1)}, u32[]{:S(2)}, u32[]{:S(2)}) collective-permute-start(bf16[144,2048]{1,0:T(8,128)(2,1)S(1)} %collective-permute-done.9.refs_3_.refs_12_), channel_id=1, source_target_pairs={{0,1},{1,0},{2,3},{3,2},{4,5},{5,4},{6,7},{7,6},{8,9},{9,8},{10,11... | collective-permute-start | bytes 1769480 | tf_op jit(solution)/shard_map/ppermute | solution.py:82
  53.4 20.0 %collective-permute-start.16 = (bf16[256,1536]{1,0:T(8,128)(2,1)S(1)}, bf16[256,1536]{1,0:T(8,128)(2,1)S(1)}, u32[]{:S(2)}, u32[]{:S(2)}) collective-permute-start(bf16[256,1536]{1,0:T(8,128)(2,1)S(1)} %collective-permute-done.7.refs_4_), channel_id=1, source_target_pairs={{0,4},{8,0},{16,8},{24,16},{28,24},{20,28},{12,20},{4,12},{1,5},{9... | collective-permute-start | bytes 2359304 | tf_op jit(solution)/shard_map/ppermute | solution.py:65
  54.9 19.7 %collective-permute-start.15 = (bf16[256,1536]{1,0:T(8,128)(2,1)S(1)}, bf16[256,1536]{1,0:T(8,128)(2,1)S(1)}, u32[]{:S(2)}, u32[]{:S(2)}) collective-permute-start(bf16[256,1536]{1,0:T(8,128)(2,1)S(1)} %collective-permute-done.6.refs_3_), channel_id=1, source_target_pairs={{0,8},{8,16},{16,24},{24,28},{28,20},{20,12},{12,4},{4,0},{1,9},{9... | collective-permute-start | bytes 2359304 | tf_op jit(solution)/shard_map/ppermute | solution.py:65
  56.1 27.7 %collective-permute-start.12 = (bf16[272,512]{1,0:T(8,128)(2,1)S(1)}, bf16[272,512]{1,0:T(8,128)(2,1)S(1)}, u32[]{:S(2)}, u32[]{:S(2)}) collective-permute-start(bf16[272,512]{1,0:T(8,128)(2,1)S(1)} %get-tuple-element.146), channel_id=1, source_target_pairs={{0,1},{1,0},{2,3},{3,2},{4,5},{5,4},{6,7},{7,6},{8,9},{9,8},{10,11... | collective-permute-start | bytes 835592 | tf_op jit(solution)/shard_map/ppermute | solution.py:82
  56.2 27.6 %collective-permute-start.13 = (bf16[272,512]{1,0:T(8,128)(2,1)S(1)}, bf16[272,512]{1,0:T(8,128)(2,1)S(1)}, u32[]{:S(2)}, u32[]{:S(2)}) collective-permute-start(bf16[272,512]{1,0:T(8,128)(2,1)S(1)} %get-tuple-element.149), channel_id=1, source_target_pairs={{0,2},{1,3},{2,0},{3,1},{4,6},{5,7},{6,4},{7,5},{8,10},{9,11},{10,... | collective-permute-start | bytes 835592 | tf_op jit(solution)/shard_map/ppermute | solution.py:82
  57.9 26.0 %collective-permute-start.14 = (bf16[272,512]{1,0:T(8,128)(2,1)S(1)}, bf16[272,512]{1,0:T(8,128)(2,1)S(1)}, u32[]{:S(2)}, u32[]{:S(2)}) collective-permute-start(bf16[272,512]{1,0:T(8,128)(2,1)S(1)} %get-tuple-element.152), channel_id=1, source_target_pairs={{0,3},{1,2},{2,1},{3,0},{4,7},{5,6},{6,5},{7,4},{8,11},{9,10},{10,... | collective-permute-start | bytes 835592 | tf_op jit(solution)/shard_map/ppermute | solution.py:82
  61.8 73.2 %copy-start.1 = (f32[1024,128]{1,0:T(8,128)}, f32[1024,128]{1,0:T(8,128)S(1)}, u32[]{:S(2)}) copy-start(f32[1024,128]{1,0:T(8,128)S(1)} %get-tuple-element.237.refs_16_) | copy-start | bytes 1572868
  74.6 10.5 %collective-permute-start.18 = (bf16[128,1536]{1,0:T(8,128)(2,1)S(1)}, bf16[128,1536]{1,0:T(8,128)(2,1)S(1)}, u32[]{:S(2)}, u32[]{:S(2)}) collective-permute-start(bf16[128,1536]{1,0:T(8,128)(2,1)S(1)} %slice.325), channel_id=1, source_target_pairs={{0,4},{8,0},{16,8},{24,16},{28,24},{20,28},{12,20},{4,12},{1,5},{9... | collective-permute-start | bytes 1179656 | tf_op jit(solution)/shard_map/ppermute | solution.py:65
  76.3 10.4 %collective-permute-start.17 = (bf16[128,1536]{1,0:T(8,128)(2,1)S(1)}, bf16[128,1536]{1,0:T(8,128)(2,1)S(1)}, u32[]{:S(2)}, u32[]{:S(2)}) collective-permute-start(bf16[128,1536]{1,0:T(8,128)(2,1)S(1)} %slice.324), channel_id=1, source_target_pairs={{0,8},{8,16},{16,24},{24,28},{28,20},{20,12},{12,4},{4,0},{1,9},{9... | collective-permute-start | bytes 1179656 | tf_op jit(solution)/shard_map/ppermute | solution.py:65
  91.5 4.2 %collective-permute-start.19 = (f32[3,8,512]{2,1,0:T(8,128)S(1)}, f32[3,8,512]{2,1,0:T(8,128)S(1)}, u32[]{:S(2)}, u32[]{:S(2)}) collective-permute-start(f32[3,8,512]{2,1,0:T(8,128)S(1)} %get-tuple-element.163), channel_id=1, source_target_pairs={{0,4},{4,0},{8,12},{12,8},{16,20},{20,16},{24,28},{28,24},{1,5},{5... | collective-permute-start | bytes 147464 | tf_op jit(solution)/shard_map/ppermute | solution.py:82
  95.6 4.7 %collective-permute-start.20 = (f32[3,8,512]{2,1,0:T(8,128)S(1)}, f32[3,8,512]{2,1,0:T(8,128)S(1)}, u32[]{:S(2)}, u32[]{:S(2)}) collective-permute-start(f32[3,8,512]{2,1,0:T(8,128)S(1)} %pad_maximum_fusion.2), channel_id=1, source_target_pairs={{0,8},{4,12},{8,0},{12,4},{16,24},{20,28},{24,16},{28,20},{1,9},{5... | collective-permute-start | bytes 147464 | tf_op jit(solution)/shard_map/ppermute | solution.py:82
  100.4 5.6 %collective-permute-start.21 = (f32[3,8,512]{2,1,0:T(8,128)S(1)}, f32[3,8,512]{2,1,0:T(8,128)S(1)}, u32[]{:S(2)}, u32[]{:S(2)}) collective-permute-start(f32[3,8,512]{2,1,0:T(8,128)S(1)} %pad_maximum_fusion.3), channel_id=1, source_target_pairs={{0,16},{4,20},{8,24},{12,28},{16,0},{20,4},{24,8},{28,12},{1,17},{... | collective-permute-start | bytes 147464 | tf_op jit(solution)/shard_map/ppermute | solution.py:82
  101.3 10.9 %collective-permute-start.22 = (f32[4,8,512]{2,1,0:T(8,128)S(1)}, f32[4,8,512]{2,1,0:T(8,128)S(1)}, u32[]{:S(2)}, u32[]{:S(2)}) collective-permute-start(f32[4,8,512]{2,1,0:T(8,128)S(1)} %get-tuple-element.178), channel_id=1, source_target_pairs={{4,0},{8,4},{12,8},{16,12},{20,16},{24,20},{28,24},{5,1},{9,5},{13... | collective-permute-start | bytes 196616 | tf_op jit(solution)/shard_map/ppermute | solution.py:801
  114.1 14.1 %collective-permute-start.26 = (bf16[2,2,128,512]{3,2,1,0:T(8,128)(2,1)S(1)}, bf16[2,2,128,512]{3,2,1,0:T(8,128)(2,1)S(1)}, u32[]{:S(2)}, u32[]{:S(2)}) collective-permute-start(bf16[2,2,128,512]{3,2,1,0:T(8,128)(2,1)S(1)} %get-tuple-element.191), channel_id=1, source_target_pairs={{0,2},{1,3},{2,0},{3,1},{4,6},{5,7},{6,4},{7,5},{8,10},{9,11},{10,... | collective-permute-start | bytes 1572872 | tf_op jit(solution)/shard_map/ppermute | solution.py:82
  115.7 12.5 %collective-permute-start.25 = (bf16[2,2,128,512]{3,2,1,0:T(8,128)(2,1)S(1)}, bf16[2,2,128,512]{3,2,1,0:T(8,128)(2,1)S(1)}, u32[]{:S(2)}, u32[]{:S(2)}) collective-permute-start(bf16[2,2,128,512]{3,2,1,0:T(8,128)(2,1)S(1)} %get-tuple-element.189), channel_id=1, source_target_pairs={{0,1},{1,0},{2,3},{3,2},{4,5},{5,4},{6,7},{7,6},{8,9},{9,8},{10,11... | collective-permute-start | bytes 1572872 | tf_op jit(solution)/shard_map/ppermute | solution.py:82
  115.7 11.5 %collective-permute-start.23 = (bf16[128,1536]{1,0:T(8,128)(2,1)S(1)}, bf16[128,1536]{1,0:T(8,128)(2,1)S(1)}, u32[]{:S(2)}, u32[]{:S(2)}) collective-permute-start(bf16[128,1536]{1,0:T(8,128)(2,1)S(1)} %get-tuple-element.179), channel_id=1, source_target_pairs={{0,8},{8,16},{16,24},{24,28},{28,20},{20,12},{12,4},{4,0},{1,9},{9... | collective-permute-start | bytes 1179656 | tf_op jit(solution)/shard_map/ppermute | solution.py:65
  116.7 11.2 %collective-permute-start.24 = (bf16[128,1536]{1,0:T(8,128)(2,1)S(1)}, bf16[128,1536]{1,0:T(8,128)(2,1)S(1)}, u32[]{:S(2)}, u32[]{:S(2)}) collective-permute-start(bf16[128,1536]{1,0:T(8,128)(2,1)S(1)} %get-tuple-element.180), channel_id=1, source_target_pairs={{0,4},{8,0},{16,8},{24,16},{28,24},{20,28},{12,20},{4,12},{1,5},{9... | collective-permute-start | bytes 1179656 | tf_op jit(solution)/shard_map/ppermute | solution.py:65
  128.2 18.9 %collective-permute-start.28 = (bf16[256,1536]{1,0:T(8,128)(2,1)S(1)}, bf16[256,1536]{1,0:T(8,128)(2,1)S(1)}, u32[]{:S(2)}, u32[]{:S(2)}) collective-permute-start(bf16[256,1536]{1,0:T(8,128)(2,1)S(1)} %get-tuple-element.194), channel_id=1, source_target_pairs={{0,4},{8,0},{16,8},{24,16},{28,24},{20,28},{12,20},{4,12},{1,5},{9... | collective-permute-start | bytes 2359304 | tf_op jit(solution)/shard_map/ppermute | solution.py:65
  129.3 18.6 %collective-permute-start.27 = (bf16[256,1536]{1,0:T(8,128)(2,1)S(1)}, bf16[256,1536]{1,0:T(8,128)(2,1)S(1)}, u32[]{:S(2)}, u32[]{:S(2)}) collective-permute-start(bf16[256,1536]{1,0:T(8,128)(2,1)S(1)} %get-tuple-element.192), channel_id=1, source_target_pairs={{0,8},{8,16},{16,24},{24,28},{28,20},{20,12},{12,4},{4,0},{1,9},{9... | collective-permute-start | bytes 2359304 | tf_op jit(solution)/shard_map/ppermute | solution.py:65
  130.3 17.9 %collective-permute-start.29 = (bf16[2,2,128,512]{3,2,1,0:T(8,128)(2,1)S(1)}, bf16[2,2,128,512]{3,2,1,0:T(8,128)(2,1)S(1)}, u32[]{:S(2)}, u32[]{:S(2)}) collective-permute-start(bf16[2,2,128,512]{3,2,1,0:T(8,128)(2,1)S(1)} %get-tuple-element.199), channel_id=1, source_target_pairs={{0,3},{1,2},{2,1},{3,0},{4,7},{5,6},{6,5},{7,4},{8,11},{9,10},{10,... | collective-permute-start | bytes 1572872 | tf_op jit(solution)/shard_map/ppermute | solution.py:82
  148.2 3.4 %collective-permute-start.34 = (bf16[256,2048]{1,0:T(8,128)(2,1)S(1)}, bf16[256,2048]{1,0:T(8,128)(2,1)S(1)}, u32[]{:S(2)}, u32[]{:S(2)}) collective-permute-start(bf16[256,2048]{1,0:T(8,128)(2,1)S(1)} %get-tuple-element.221), channel_id=1, source_target_pairs={{0,1},{1,0},{2,3},{3,2},{4,5},{5,4},{6,7},{7,6},{8,9},{9,8},{10,11... | collective-permute-start | bytes 3145736 | tf_op jit(solution)/shard_map/ppermute | solution.py:82
  148.3 2.7 %collective-permute-start.30 = (f32[8,2048]{1,0:T(8,128)S(1)}, f32[8,2048]{1,0:T(8,128)S(1)}, u32[]{:S(2)}, u32[]{:S(2)}) collective-permute-start(f32[8,2048]{1,0:T(8,128)S(1)} %pad_maximum_fusion.1), channel_id=1, source_target_pairs={{0,1},{1,0},{2,3},{3,2},{4,5},{5,4},{6,7},{7,6},{8,9},{9,8},{10,11... | collective-permute-start | bytes 196616 | tf_op jit(solution)/shard_map/ppermute | solution.py:82
  148.8 22.1 %collective-permute-start.35 = (bf16[256,2048]{1,0:T(8,128)(2,1)S(1)}, bf16[256,2048]{1,0:T(8,128)(2,1)S(1)}, u32[]{:S(2)}, u32[]{:S(2)}) collective-permute-start(bf16[256,2048]{1,0:T(8,128)(2,1)S(1)} %get-tuple-element.223), channel_id=1, source_target_pairs={{0,1},{1,0},{2,3},{3,2},{4,5},{5,4},{6,7},{7,6},{8,9},{9,8},{10,11... | collective-permute-start | bytes 3145736 | tf_op jit(solution)/shard_map/ppermute | solution.py:82
  148.9 19.9 %collective-permute-start.33 = (bf16[256,1536]{1,0:T(8,128)(2,1)S(1)}, bf16[256,1536]{1,0:T(8,128)(2,1)S(1)}, u32[]{:S(2)}, u32[]{:S(2)}) collective-permute-start(bf16[256,1536]{1,0:T(8,128)(2,1)S(1)} %get-tuple-element.218), channel_id=1, source_target_pairs={{0,4},{8,0},{16,8},{24,16},{28,24},{20,28},{12,20},{4,12},{1,5},{9... | collective-permute-start | bytes 2359304 | tf_op jit(solution)/shard_map/ppermute | solution.py:65
  149.9 20.3 %collective-permute-start.32 = (bf16[256,1536]{1,0:T(8,128)(2,1)S(1)}, bf16[256,1536]{1,0:T(8,128)(2,1)S(1)}, u32[]{:S(2)}, u32[]{:S(2)}) collective-permute-start(bf16[256,1536]{1,0:T(8,128)(2,1)S(1)} %get-tuple-element.217), channel_id=1, source_target_pairs={{0,8},{8,16},{16,24},{24,28},{28,20},{20,12},{12,4},{4,0},{1,9},{9... | collective-permute-start | bytes 2359304 | tf_op jit(solution)/shard_map/ppermute | solution.py:65
  151.0 5.0 %collective-permute-start.31 = (f32[8,2048]{1,0:T(8,128)S(1)}, f32[8,2048]{1,0:T(8,128)S(1)}, u32[]{:S(2)}, u32[]{:S(2)}) collective-permute-start(f32[8,2048]{1,0:T(8,128)S(1)} %select_maximum_fusion), channel_id=1, source_target_pairs={{0,2},{1,3},{2,0},{3,1},{4,6},{5,7},{6,4},{7,5},{8,10},{9,11},{10,... | collective-permute-start | bytes 196616 | tf_op jit(solution)/shard_map/ppermute | solution.py:82
  152.1 18.9 %collective-permute-start.37 = (bf16[128,2048]{1,0:T(8,128)(2,1)S(1)}, bf16[128,2048]{1,0:T(8,128)(2,1)S(1)}, u32[]{:S(2)}, u32[]{:S(2)}) collective-permute-start(bf16[128,2048]{1,0:T(8,128)(2,1)S(1)} %get-tuple-element.226), channel_id=1, source_target_pairs={{0,2},{1,3},{2,0},{3,1},{4,6},{5,7},{6,4},{7,5},{8,10},{9,11},{10,... | collective-permute-start | bytes 1572872 | tf_op jit(solution)/shard_map/ppermute | solution.py:82
  156.1 14.9 %collective-permute-start.36 = (f32[6,2048]{1,0:T(8,128)S(1)}, f32[6,2048]{1,0:T(8,128)S(1)}, u32[]{:S(2)}, u32[]{:S(2)}) collective-permute-start(f32[6,2048]{1,0:T(8,128)S(1)} %slice_add_fusion.1), channel_id=1, source_target_pairs={{0,4},{4,0},{8,12},{12,8},{16,20},{20,16},{24,28},{28,24},{1,5},{5... | collective-permute-start | bytes 147464 | tf_op jit(solution)/shard_map/ppermute | solution.py:82
  171.0 14.9 %collective-permute-start.39 = (bf16[256,1024]{1,0:T(8,128)(2,1)S(1)}, bf16[256,1024]{1,0:T(8,128)(2,1)S(1)}, u32[]{:S(2)}, u32[]{:S(2)}) collective-permute-start(bf16[256,1024]{1,0:T(8,128)(2,1)S(1)} %get-tuple-element.230), channel_id=1, source_target_pairs={{0,4},{8,0},{16,8},{24,16},{28,24},{20,28},{12,20},{4,12},{1,5},{9... | collective-permute-start | bytes 1572872 | tf_op jit(solution)/shard_map/ppermute | solution.py:65
  171.2 14.9 %collective-permute-start.38 = (bf16[256,1024]{1,0:T(8,128)(2,1)S(1)}, bf16[256,1024]{1,0:T(8,128)(2,1)S(1)}, u32[]{:S(2)}, u32[]{:S(2)}) collective-permute-start(bf16[256,1024]{1,0:T(8,128)(2,1)S(1)} %get-tuple-element.228), channel_id=1, source_target_pairs={{0,8},{8,16},{16,24},{24,28},{28,20},{20,12},{12,4},{4,0},{1,9},{9... | collective-permute-start | bytes 1572872 | tf_op jit(solution)/shard_map/ppermute | solution.py:65
  173.2 18.5 %collective-permute-start.42 = (bf16[128,2048]{1,0:T(8,128)(2,1)S(1)}, bf16[128,2048]{1,0:T(8,128)(2,1)S(1)}, u32[]{:S(2)}, u32[]{:S(2)}) collective-permute-start(bf16[128,2048]{1,0:T(8,128)(2,1)S(1)} %get-tuple-element.235), channel_id=1, source_target_pairs={{0,2},{1,3},{2,0},{3,1},{4,6},{5,7},{6,4},{7,5},{8,10},{9,11},{10,... | collective-permute-start | bytes 1572872 | tf_op jit(solution)/shard_map/ppermute | solution.py:82
  173.7 17.9 %collective-permute-start.41 = (bf16[256,512]{1,0:T(8,128)(2,1)S(1)}, bf16[256,512]{1,0:T(8,128)(2,1)S(1)}, u32[]{:S(2)}, u32[]{:S(2)}) collective-permute-start(bf16[256,512]{1,0:T(8,128)(2,1)S(1)} %get-tuple-element.234), channel_id=1, source_target_pairs={{0,4},{8,0},{16,8},{24,16},{28,24},{20,28},{12,20},{4,12},{1,5},{9... | collective-permute-start | bytes 786440 | tf_op jit(solution)/shard_map/ppermute | solution.py:65
  174.0 17.7 %collective-permute-start.40 = (bf16[256,512]{1,0:T(8,128)(2,1)S(1)}, bf16[256,512]{1,0:T(8,128)(2,1)S(1)}, u32[]{:S(2)}, u32[]{:S(2)}) collective-permute-start(bf16[256,512]{1,0:T(8,128)(2,1)S(1)} %get-tuple-element.232), channel_id=1, source_target_pairs={{0,8},{8,16},{16,24},{24,28},{28,20},{20,12},{12,4},{4,0},{1,9},{9... | collective-permute-start | bytes 786440 | tf_op jit(solution)/shard_map/ppermute | solution.py:65
  186.4 4.7 %collective-permute-start.43 = (f32[6,2048]{1,0:T(8,128)S(1)}, f32[6,2048]{1,0:T(8,128)S(1)}, u32[]{:S(2)}, u32[]{:S(2)}) collective-permute-start(f32[6,2048]{1,0:T(8,128)S(1)} %add.310), channel_id=1, source_target_pairs={{0,8},{4,12},{8,0},{12,4},{16,24},{20,28},{24,16},{28,20},{1,9},{5... | collective-permute-start | bytes 147464 | tf_op jit(solution)/shard_map/ppermute | solution.py:82
  188.8 8.8 %collective-permute-start.44 = (bf16[256,512]{1,0:T(8,128)(2,1)S(1)}, bf16[256,512]{1,0:T(8,128)(2,1)S(1)}, u32[]{:S(2)}, u32[]{:S(2)}) collective-permute-start(bf16[256,512]{1,0:T(8,128)(2,1)S(1)} %get-tuple-element.248), channel_id=1, source_target_pairs={{0,1},{1,0},{2,3},{3,2},{4,5},{5,4},{6,7},{7,6},{8,9},{9,8},{10,11... | collective-permute-start | bytes 786440 | tf_op jit(solution)/shard_map/ppermute | solution.py:82
  191.1 6.6 %collective-permute-start.45 = (bf16[256,512]{1,0:T(8,128)(2,1)S(1)}, bf16[256,512]{1,0:T(8,128)(2,1)S(1)}, u32[]{:S(2)}, u32[]{:S(2)}) collective-permute-start(bf16[256,512]{1,0:T(8,128)(2,1)S(1)} %get-tuple-element.249), channel_id=1, source_target_pairs={{0,2},{1,3},{2,0},{3,1},{4,6},{5,7},{6,4},{7,5},{8,10},{9,11},{10,... | collective-permute-start | bytes 786440 | tf_op jit(solution)/shard_map/ppermute | solution.py:82
  191.7 5.2 %collective-permute-start.46 = (f32[6,2048]{1,0:T(8,128)S(1)}, f32[6,2048]{1,0:T(8,128)S(1)}, u32[]{:S(2)}, u32[]{:S(2)}) collective-permute-start(f32[6,2048]{1,0:T(8,128)S(1)} %add.316), channel_id=1, source_target_pairs={{0,16},{4,20},{8,24},{12,28},{16,0},{20,4},{24,8},{28,12},{1,17},{... | collective-permute-start | bytes 147464 | tf_op jit(solution)/shard_map/ppermute | solution.py:82
  (13 other events, 302.5 us)
